TPU v7x, 32 devices: a whole 2x2x4 slice. The times are simulated.
32 devices in a mesh: dp: 8 (over y, x, core), tensor: 4 (over z).
Axes of the slice: x: 2, y: 2, z: 4, core: 2. Of those that a mesh axis runs over, the one named last changes fastest.
Arguments:
- activations: bfloat16 [16, 256, 2560], P('dp', 'tensor'), may hold values from -6 to 6
- norm_gain: float32 [2560], replicated, may hold values from 0.5 to 1.5
- gelu_proj: bfloat16 [2560, 2560], P('dp', 'tensor'), may hold values from -0.125 to 0.125
- input_proj: bfloat16 [2560, 2560], P('dp', 'tensor'), may hold values from -0.125 to 0.125
- conv_weight: float32 [4, 2560], P(None, 'tensor'), may hold values from -3 to 3
- gate_input: bfloat16 [256, 2560], P('dp', 'tensor'), may hold values from -0.375 to 0.375
- gate_decay: bfloat16 [256, 2560], P('dp', 'tensor'), may hold values from -0.375 to 0.375
- decay_rate: float32 [2560], P('tensor'), may hold values from 0.00025 to 0.01
- out_proj: bfloat16 [2560, 2560], P('tensor', 'dp'), may hold values from -0.25 to 0.25
- mlp_gain: float32 [2560], replicated, may hold values from 0.5 to 1.5
- feed_gate: bfloat16 [2560, 7680], P('dp', 'tensor'), may hold values from -0.125 to 0.125
- feed_up: bfloat16 [2560, 7680], P('dp', 'tensor'), may hold values from -0.125 to 0.125
- feed_down: bfloat16 [7680, 2560], P('tensor', 'dp'), may hold values from -0.125 to 0.125
- cotangent: bfloat16 [16, 256, 2560], P('dp', 'tensor'), may hold values from -6 to 6
- lengths: int32 [16], replicated, may hold values from 64 to 256, as said below
- batch_of: int32 [16], replicated, may hold values from 0 to 3, as said below
Outputs:
- output: bfloat16 [16, 256, 2560], P('dp', 'tensor')
- input_grad: float32 [16, 256, 2560], P('dp', 'tensor')
- norm_gain_grad: float32 [2560], replicated
- gelu_proj_grad: float32 [2560, 2560], P('dp', 'tensor')
- input_proj_grad: float32 [2560, 2560], P('dp', 'tensor')
- conv_grad: float32 [4, 2560], P(None, 'tensor')
- gate_input_grad: float32 [256, 2560], P('dp', 'tensor')
- gate_decay_grad: float32 [256, 2560], P('dp', 'tensor')
- decay_grad: float32 [2560], P('tensor')
- out_proj_grad: float32 [2560, 2560], P('tensor', 'dp')
- mlp_gain_grad: float32 [2560], replicated
- feed_gate_grad: float32 [2560, 7680], P('dp', 'tensor')
- feed_up_grad: float32 [2560, 7680], P('dp', 'tensor')
- feed_down_grad: float32 [7680, 2560], P('tensor', 'dp')
Inputs may be any that keep to these rules, and one draw needn't show every extreme that they name: `lengths`: a sequence's valid positions are its first ones; in each aligned group of 2 sequences (one index of dp) one sequence has all 256. `batch_of`: every micro-batch holds at least one sequence.
All inputs are finite; a program needn't handle non-finite values.
Results may differ from a plain program's by a relative error of at most 0.024.
Values may be sent and summed in bfloat16 or wider, within the bound.
A program may use at most 256 MiB of HBM per device.

v0:
```python
import jax
import jax.numpy as jnp
from jax import lax
from jax.sharding import PartitionSpec as P

MICRO = 4
SBLK = 64


EPS = 1e-06


def swapped(block, axis, apart):
    count = lax.axis_size(axis)
    route = []
    for low in range(count):
        high = low | 1 << apart
        if high != low and high < count:
            route += [(low, high), (high, low)]
    return lax.ppermute(block, axis, route)


def normalize(value_entries, scale_gain):
    return (
        value_entries
        * lax.rsqrt(jnp.mean(value_entries * value_entries, axis=-1, keepdims=True) + EPS)
        * scale_gain
    )


def causal_conv(value_entries, kernel):
    summed = value_entries * kernel[0]
    for offset in range(1, kernel.shape[0]):
        shifted = jnp.concatenate(
            [jnp.zeros_like(value_entries[:, :offset]), value_entries[:, :-offset]], axis=1
        )
        summed = summed + shifted * kernel[offset]
    return summed


def decay_inputs(input_pre, decay_pre, conv_vals, decay_rate):
    log_decay = -8.0 * jax.nn.sigmoid(decay_pre) * decay_rate
    scaled = jnp.sqrt(-jnp.expm1(2.0 * log_decay))
    return (log_decay, scaled * jax.nn.sigmoid(input_pre) * conv_vals)


def blocked_recurrence(log_steps, inputs, block_len):
    seq_count, length, channels = log_steps.shape
    block_num = length // block_len
    log_blocks = jnp.swapaxes(log_steps.reshape(seq_count, block_num, block_len, channels), 0, 1)
    input_blocks = jnp.swapaxes(inputs.reshape(seq_count, block_num, block_len, channels), 0, 1)
    lower_mask = jnp.arange(block_len)[:, None] >= jnp.arange(block_len)[None, :]

    def advance(carried, pieces):
        log_block, input_block = pieces
        cumul = jnp.cumsum(log_block, axis=1)
        spread = cumul[:, :, None, :] - cumul[:, None, :, :]
        factor = jnp.where(lower_mask[None, :, :, None], jnp.exp(jnp.minimum(spread, 0.0)), 0.0)
        states = (
            jnp.sum(factor * input_block[:, None, :, :], axis=2)
            + jnp.exp(cumul) * carried[:, None, :]
        )
        return (states[:, -1, :], states)

    start = jnp.zeros((seq_count, channels), jnp.float32)
    _, states = lax.scan(advance, start, (log_blocks, input_blocks))
    return jnp.swapaxes(states, 0, 1).reshape(seq_count, length, channels)


def reduce_feed(
    second_normalized_every, gate_gradient_rows, lift_gradient, hidden_rows, cotangent_every
):
    down_weight_gradient = jnp.einsum(
        "pkr,pku->ru", hidden_rows, cotangent_every, preferred_element_type=jnp.float32
    )
    grad_gate_w = jnp.einsum(
        "gor,goa->ra",
        second_normalized_every,
        gate_gradient_rows,
        preferred_element_type=jnp.float32,
    )
    grad_lift_w = jnp.einsum(
        "gor,goa->ra", second_normalized_every, lift_gradient, preferred_element_type=jnp.float32
    )
    return (
        lax.psum_scatter(
            grad_gate_w.astype(jnp.bfloat16), "dp", scatter_dimension=0, tiled=True
        ).astype(jnp.float32),
        lax.psum_scatter(
            grad_lift_w.astype(jnp.bfloat16), "dp", scatter_dimension=0, tiled=True
        ).astype(jnp.float32),
        lax.psum_scatter(
            down_weight_gradient.astype(jnp.bfloat16), "dp", scatter_dimension=1, tiled=True
        ).astype(jnp.float32),
    )


def shards(
    activations,
    norm_gain,
    gelu_proj,
    input_proj,
    conv_weight,
    gate_input,
    gate_decay,
    decay_rate,
    out_proj,
    mlp_gain,
    feed_gate,
    feed_up,
    feed_down,
    cotangent,
    lengths,
    batch_of,
):
    tensor_count = lax.axis_size("tensor")
    tensor_index = lax.axis_index("tensor")
    data_index = lax.axis_index("dp")
    seq_count, row_count, model_width = activations.shape
    full_length = row_count * tensor_count
    weights = (
        lax.all_gather(gelu_proj, "dp", axis=0, tiled=True),
        lax.all_gather(input_proj, "dp", axis=0, tiled=True),
        lax.all_gather(out_proj, "dp", axis=1, tiled=True),
        lax.all_gather(gate_input, "dp", axis=0, tiled=True),
        lax.all_gather(gate_decay, "dp", axis=0, tiled=True),
        lax.all_gather(feed_gate, "dp", axis=0, tiled=True),
        lax.all_gather(feed_up, "dp", axis=0, tiled=True),
        lax.all_gather(feed_down, "dp", axis=1, tiled=True),
    )
    (
        gelu_activation_all,
        input_every_token,
        output_every_token,
        gate_in_full,
        gate_dec_full,
        feed_gate_matrix,
        feed_up_matrix,
        feed_down_matrix,
    ) = weights
    channels = gelu_activation_all.shape[1]
    block_size = gate_in_full.shape[0]
    half_block = block_size // 2
    window_width = channels + half_block
    window_count = window_width // block_size
    parity = tensor_index % 2
    members = (batch_of[:, None] == jnp.arange(MICRO)[None, :]).astype(jnp.float32)
    counts = jnp.sum(members * lengths[:, None].astype(jnp.float32), axis=0)
    total_seqs = lengths.shape[0]
    per_batch = float(total_seqs * full_length) / (MICRO * counts)
    weight_all = jnp.sum(members * per_batch[None, :], axis=1)
    my_weight = lax.dynamic_slice_in_dim(weight_all, data_index * seq_count, seq_count)
    my_length = lax.dynamic_slice_in_dim(lengths, data_index * seq_count, seq_count)
    places = tensor_index * row_count + jnp.arange(row_count)
    valid_mask = (places[None, :] < my_length[:, None]).astype(jnp.float32)
    scaled_cot = cotangent.astype(jnp.float32) * (valid_mask * my_weight[:, None])[:, :, None]
    resid_in = activations.astype(jnp.float32)
    normed = normalize(resid_in, norm_gain).astype(jnp.bfloat16)
    normalized_every = lax.all_gather(normed, "tensor", axis=1, tiled=True)
    gelu_preactivation = jnp.einsum(
        "kqg,ga->kqa", normalized_every, gelu_activation_all, preferred_element_type=jnp.float32
    )
    input_pre = jnp.einsum(
        "kqg,ga->kqa", normalized_every, input_every_token, preferred_element_type=jnp.float32
    )
    gelu_out, gelu_back = jax.vjp(jax.nn.gelu, gelu_preactivation)
    conv_out, conv_back = jax.vjp(causal_conv, input_pre, conv_weight)
    conv_bf = conv_out.astype(jnp.bfloat16)
    rim_send = lax.dynamic_slice_in_dim(
        conv_bf, (1 - parity) * (channels - half_block), half_block, 2
    )
    rim_recv = swapped(rim_send, "tensor", 0)
    window = jnp.zeros((seq_count, full_length, window_width), jnp.bfloat16)
    window = lax.dynamic_update_slice_in_dim(window, conv_bf, parity * half_block, 2)
    window = lax.dynamic_update_slice_in_dim(window, rim_recv, (1 - parity) * channels, 2)
    tile_view = window.reshape(seq_count, full_length, window_count, block_size)
    gate_pair = jnp.stack([gate_in_full, gate_dec_full])
    placed = lax.dynamic_update_slice_in_dim(
        jnp.zeros((2, block_size, window_width), jnp.bfloat16), gate_pair, parity * half_block, 2
    )
    placed = placed.reshape(2, block_size, window_count, block_size)
    gate_wide = jnp.einsum(
        "slbk,gkbc->gslbc", tile_view, placed, preferred_element_type=jnp.float32
    )
    gate_wide = gate_wide.reshape(2, seq_count, full_length, window_width)
    gate_own = lax.dynamic_slice_in_dim(gate_wide, parity * half_block, channels, 3)
    (log_decay, drive_in), gate_back = jax.vjp(
        decay_inputs, gate_own[0], gate_own[1], conv_bf.astype(jnp.float32), decay_rate
    )
    states = blocked_recurrence(log_decay, drive_in, SBLK)
    mixer_output = (gelu_out * states).astype(jnp.bfloat16)
    partial_value = jnp.einsum(
        "xgq,qp->xgp", mixer_output, output_every_token, preferred_element_type=jnp.float32
    )
    branch = lax.psum_scatter(
        partial_value.astype(jnp.bfloat16), "tensor", scatter_dimension=1, tiled=True
    ).astype(jnp.float32)
    middle = resid_in + branch
    normed_two = normalize(middle, mlp_gain).astype(jnp.bfloat16)
    second_normalized_every = lax.all_gather(normed_two, "tensor", axis=1, tiled=True)
    gate_pre = jnp.einsum(
        "nwo,ob->nwb", second_normalized_every, feed_gate_matrix, preferred_element_type=jnp.float32
    )
    lift_pre = jnp.einsum(
        "nwo,ob->nwb", second_normalized_every, feed_up_matrix, preferred_element_type=jnp.float32
    )
    gate_act, activ_back = jax.vjp(jax.nn.gelu, gate_pre)
    hidden_rows = (gate_act * lift_pre).astype(jnp.bfloat16)
    partial_two = jnp.einsum(
        "xav,vt->xat", hidden_rows, feed_down_matrix, preferred_element_type=jnp.float32
    )
    feed_out = lax.psum_scatter(
        partial_two.astype(jnp.bfloat16), "tensor", scatter_dimension=1, tiled=True
    ).astype(jnp.float32)
    output = (middle + feed_out).astype(jnp.bfloat16)
    cotangent_every = lax.all_gather(scaled_cot.astype(jnp.bfloat16), "tensor", axis=1, tiled=True)
    grad_hidden = jnp.einsum(
        "gre,ue->gru", cotangent_every, feed_down_matrix, preferred_element_type=jnp.float32
    )
    gate_gradient_rows = activ_back(grad_hidden * lift_pre)[0].astype(jnp.bfloat16)
    lift_gradient = (grad_hidden * gate_act).astype(jnp.bfloat16)
    back_two = jnp.einsum(
        "mqa,ya->mqy", gate_gradient_rows, feed_gate_matrix, preferred_element_type=jnp.float32
    )
    back_two = back_two + jnp.einsum(
        "mqa,ya->mqy", lift_gradient, feed_up_matrix, preferred_element_type=jnp.float32
    )
    grad_normed_two = lax.psum_scatter(
        back_two.astype(jnp.bfloat16), "tensor", scatter_dimension=1, tiled=True
    ).astype(jnp.float32)
    _, second_back = jax.vjp(normalize, middle, mlp_gain)
    grad_middle_norm, grad_mlp_gain = second_back(grad_normed_two)
    grad_middle = scaled_cot + grad_middle_norm
    branch_gradient_every = lax.all_gather(
        grad_middle.astype(jnp.bfloat16), "tensor", axis=1, tiled=True
    )
    grad_mixed = jnp.einsum(
        "xtz,mz->xtm", branch_gradient_every, output_every_token, preferred_element_type=jnp.float32
    )
    grad_out_w = jnp.einsum(
        "iqy,iqk->yk", mixer_output, branch_gradient_every, preferred_element_type=jnp.float32
    )
    grad_states = grad_mixed * gelu_out
    gelu_preactivation_gradient = gelu_back(grad_mixed * states)[0].astype(jnp.bfloat16)
    later_logs = jnp.concatenate([log_decay[:, 1:], jnp.zeros_like(log_decay[:, :1])], axis=1)
    grad_drive = jnp.flip(
        blocked_recurrence(jnp.flip(later_logs, 1), jnp.flip(grad_states, 1), SBLK), 1
    )
    earlier = jnp.concatenate([jnp.zeros_like(states[:, :1]), states[:, :-1]], axis=1)
    grad_log = grad_drive * jnp.exp(log_decay) * earlier
    grad_in_pre, grad_dec_pre, grad_conv_val, grad_rate = gate_back((grad_log, grad_drive))
    grad_pair = jnp.stack([grad_in_pre, grad_dec_pre]).astype(jnp.bfloat16)
    grad_wide = lax.dynamic_update_slice_in_dim(
        jnp.zeros((2, seq_count, full_length, window_width), jnp.bfloat16),
        grad_pair,
        parity * half_block,
        3,
    )
    grad_wide = grad_wide.reshape(2, seq_count, full_length, window_count, block_size)
    grad_window = jnp.einsum(
        "gslbc,gkbc->slbk", grad_wide, placed, preferred_element_type=jnp.float32
    )
    grad_window = grad_window.reshape(seq_count, full_length, window_width)
    grad_placed = jnp.einsum(
        "slbk,gslbc->gkbc", tile_view, grad_wide, preferred_element_type=jnp.float32
    )
    grad_placed = grad_placed.reshape(2, block_size, window_width)
    grad_gates = lax.dynamic_slice_in_dim(grad_placed, parity * half_block, channels, 2)
    rim_grad = lax.dynamic_slice_in_dim(grad_window, (1 - parity) * channels, half_block, 2)
    rim_return = swapped(rim_grad.astype(jnp.bfloat16), "tensor", 0).astype(rim_grad.dtype)
    grad_conv = grad_conv_val + lax.dynamic_slice_in_dim(
        grad_window, parity * half_block, channels, 2
    )
    rim_start = (1 - parity) * (channels - half_block)
    rim_sum = lax.dynamic_slice_in_dim(grad_conv, rim_start, half_block, 2) + rim_return
    grad_conv = lax.dynamic_update_slice_in_dim(grad_conv, rim_sum, rim_start, 2)
    input_preactivation_gradient, grad_taps = conv_back(grad_conv)
    input_preactivation_gradient = input_preactivation_gradient.astype(jnp.bfloat16)
    grad_gelu_w = jnp.einsum(
        "qgv,qgp->vp",
        normalized_every,
        gelu_preactivation_gradient,
        preferred_element_type=jnp.float32,
    )
    grad_input_w = jnp.einsum(
        "qgv,qgp->vp",
        normalized_every,
        input_preactivation_gradient,
        preferred_element_type=jnp.float32,
    )
    back_one = jnp.einsum(
        "mzf,af->mza",
        gelu_preactivation_gradient,
        gelu_activation_all,
        preferred_element_type=jnp.float32,
    )
    back_one = back_one + jnp.einsum(
        "mzf,af->mza",
        input_preactivation_gradient,
        input_every_token,
        preferred_element_type=jnp.float32,
    )
    grad_normed = lax.psum_scatter(
        back_one.astype(jnp.bfloat16), "tensor", scatter_dimension=1, tiled=True
    ).astype(jnp.float32)
    _, first_back = jax.vjp(normalize, resid_in, norm_gain)
    grad_resid_norm, grad_norm_gain = first_back(grad_normed)
    input_grad = grad_middle + grad_resid_norm
    rate_full = lax.dynamic_update_slice_in_dim(
        jnp.zeros((model_width,), jnp.float32), grad_rate, tensor_index * channels, 0
    )
    taps_full = lax.dynamic_update_slice_in_dim(
        jnp.zeros((conv_weight.shape[0], model_width), jnp.float32),
        grad_taps,
        tensor_index * channels,
        1,
    )
    norm_total, mlp_total, rate_total, taps_total = lax.psum(
        (grad_norm_gain, grad_mlp_gain, rate_full, taps_full), ("dp", "tensor")
    )
    mixer_grads = (
        lax.psum_scatter(
            grad_gelu_w.astype(jnp.bfloat16), "dp", scatter_dimension=0, tiled=True
        ).astype(jnp.float32),
        lax.psum_scatter(
            grad_input_w.astype(jnp.bfloat16), "dp", scatter_dimension=0, tiled=True
        ).astype(jnp.float32),
        lax.psum_scatter(
            grad_out_w.astype(jnp.bfloat16), "dp", scatter_dimension=1, tiled=True
        ).astype(jnp.float32),
        lax.psum_scatter(
            grad_gates[0].astype(jnp.bfloat16), "dp", scatter_dimension=0, tiled=True
        ).astype(jnp.float32),
        lax.psum_scatter(
            grad_gates[1].astype(jnp.bfloat16), "dp", scatter_dimension=0, tiled=True
        ).astype(jnp.float32),
    )
    feed_grads = reduce_feed(
        second_normalized_every, gate_gradient_rows, lift_gradient, hidden_rows, cotangent_every
    )
    rate_own = lax.dynamic_slice_in_dim(rate_total, tensor_index * channels, channels, 0)
    taps_own = lax.dynamic_slice_in_dim(taps_total, tensor_index * channels, channels, 1)
    return (
        output,
        input_grad,
        norm_total,
        mixer_grads[0],
        mixer_grads[1],
        taps_own,
        mixer_grads[3],
        mixer_grads[4],
        rate_own,
        mixer_grads[2],
        mlp_total,
        feed_grads[0],
        feed_grads[1],
        feed_grads[2],
    )


def solution(mesh):
    placed = (
        P("dp", "tensor", None),
        P(),
        P("dp", "tensor"),
        P("dp", "tensor"),
        P(None, "tensor"),
        P("dp", "tensor"),
        P("dp", "tensor"),
        P("tensor"),
        P("tensor", "dp"),
        P(),
        P("dp", "tensor"),
        P("dp", "tensor"),
        P("tensor", "dp"),
        P("dp", "tensor", None),
        P(),
        P(),
    )
    return jax.shard_map(
        shards,
        mesh=mesh,
        in_specs=placed,
        out_specs=(
            P("dp", "tensor", None),
            P("dp", "tensor", None),
            P(),
            P("dp", "tensor"),
            P("dp", "tensor"),
            P(None, "tensor"),
            P("dp", "tensor"),
            P("dp", "tensor"),
            P("tensor"),
            P("tensor", "dp"),
            P(),
            P("dp", "tensor"),
            P("dp", "tensor"),
            P("tensor", "dp"),
        ),
        check_vma=False,
    )
```

profile of v0, /device:TPU:0, one launch (start us, length us, event | category | flops | bytes accessed | tf_op | source)
XLA Modules:
  0.0 1493.5 jit_solution(6766571753044502844)
XLA Ops:
  13.0 10.9 all_gather.39
  24.1 9.4 all_gather.38
  33.8 34.6 %all-gather.11.cloned.1.call-done = bf16[2,256,2560]{2,1,0:T(8,128)(2,1)} async-done(((bf16[2,64,2560]{2,1,0:T(8,128)(2,1)}), bf16[2,256,2560]{2,1,0:T(8,128)(2,1)}) %all-gather.11.cloned.1.call-update) | async-done | bytes 2621456 | tf_op jit(solution)/shard_map/all_gather | solution.py:159
  68.4 33.6 %all-gather.15.cloned.1.call-done = bf16[2560,640]{1,0:T(8,128)(2,1)} async-done(((bf16[320,640]{1,0:T(8,128)(2,1)}), bf16[2560,640]{1,0:T(8,128)(2,1)}) %all-gather.15.cloned.1.call-update) | async-done | bytes 3276816 | tf_op jit(solution)/shard_map/all_gather | solution.py:123
  129.4 37.6 %while.26 = (s32[]{:T(128)}, f32[2,640]{1,0:T(2,128)S(1)}, f32[4,2,64,640]{3,2,1,0:T(8,128)}, f32[4,2,64,640]{3,2,1,0:T(8,128)}, f32[4,2,64,640]{3,2,1,0:T(8,128)}, /*index=5*/s32[]{:T(128)}, f32[]{:T(128)}) while((s32[]{:T(128)}, f32[2,640]{1,0:T(2,128)S(1)}, f32[4,2,64,640]{3,2,1,0:T(8,128)}, f32[4,2,64,640]{3,2,1,0:T(8,128)}, ...), condition=%wide.region_4.5_spmd.clone, body=%wide.region_1.0_spmd.clone.sunk | while | flops 31463936 | bytes 4631649 | solution.py:66
  131.2 7.0 multiply_reduce_fusion.9
  140.5 7.0 multiply_reduce_fusion.9
  149.8 7.0 multiply_reduce_fusion.9
  159.1 7.0 multiply_reduce_fusion.9
  168.5 6.6 multiply_convert_fusion.3
  175.1 6.0 convolution_convert_fusion
  184.0 49.4 %reduce-scatter.17.cloned.1.call-done = bf16[2,64,2560]{2,1,0:T(8,128)(2,1)} async-done(((bf16[2,256,2560]{2,1,0:T(8,128)(2,1)}), bf16[2,64,2560]{2,1,0:T(8,128)(2,1)}) %reduce-scatter.17.cloned.1.call-update) | async-done | bytes 655376 | tf_op jit(solution)/shard_map/reduce_scatter | solution.py:195
  237.4 52.5 %all-gather.27.cloned.1.call-done = bf16[2,256,2560]{2,1,0:T(8,128)(2,1)} async-done(((bf16[2,64,2560]{2,1,0:T(8,128)(2,1)}), bf16[2,256,2560]{2,1,0:T(8,128)(2,1)}) %all-gather.27.cloned.1.call-update) | async-done | bytes 2621456 | tf_op jit(solution)/shard_map/all_gather | solution.py:216
  289.9 61.2 %all-gather.25.cloned.1.call-done = bf16[1920,2560]{0,1:T(8,128)(2,1)} async-done(((bf16[1920,320]{0,1:T(8,128)(2,1)}), bf16[1920,2560]{0,1:T(8,128)(2,1)}) %all-gather.25.cloned.1.call-update) | async-done | bytes 9830416 | tf_op jit(solution)/shard_map/all_gather | solution.py:129
  351.1 11.8 fusion.8
  362.9 45.2 %all-gather.19.cloned.1.call-done = bf16[2,256,2560]{2,1,0:T(8,128)(2,1)} async-done(((bf16[2,64,2560]{2,1,0:T(8,128)(2,1)}), bf16[2,256,2560]{2,1,0:T(8,128)(2,1)}) %all-gather.19.cloned.1.call-update) | async-done | bytes 2621456 | tf_op jit(solution)/shard_map/all_gather | solution.py:200
  408.0 61.2 %all-gather.23.cloned.1.call-done = bf16[2560,1920]{1,0:T(8,128)(2,1)} async-done(((bf16[320,1920]{1,0:T(8,128)(2,1)}), bf16[2560,1920]{1,0:T(8,128)(2,1)}) %all-gather.23.cloned.1.call-update) | async-done | bytes 9830416 | tf_op jit(solution)/shard_map/all_gather | solution.py:128
  469.2 11.3 fusion.14
  480.5 51.0 %all-gather.21.cloned.1.call-done = bf16[2560,1920]{1,0:T(8,128)(2,1)} async-done(((bf16[320,1920]{1,0:T(8,128)(2,1)}), bf16[2560,1920]{1,0:T(8,128)(2,1)}) %all-gather.21.cloned.1.call-update) | async-done | bytes 9830416 | tf_op jit(solution)/shard_map/all_gather | solution.py:127
  531.5 15.2 %fusion.31 = (bf16[2,256,1920]{2,1,0:T(8,128)(2,1)S(1)}, bf16[2,256,1920]{2,1,0:T(8,128)(2,1)}, bf16[2,256,1920]{2,1,0:T(8,128)(2,1)}) fusion(f32[2,256,1920]{2,1,0:T(8,128)} %fusion.8, f32[2,256,1920]{2,1,0:T(8,128)} %fusion.14, bf16[2,256,2560]{2,1,0:T(8,128)(2,1)} %all-gather.19.cloned.1.call-done, bf16[2560,1920]{1,0:T(8,128)(2,1)} %all-gather.21.cloned.1.call-done), kind=kOutput, calls=%fused_computation.52 | convolution fusion | flops 5058723840 | bytes 26214400 | tf_op jit(solution)/shard_map/nwo,ob->nwb/dot_general | solution.py:201
  546.8 9.3 fusion.12
  556.1 8.7 add_convert_fusion.1
  565.1 52.0 %reduce-scatter.21.cloned.1.call-done = bf16[2,64,2560]{2,1,0:T(8,128)(2,1)} async-done(((bf16[2,256,2560]{2,1,0:T(8,128)(2,1)}), bf16[2,64,2560]{2,1,0:T(8,128)(2,1)}) %reduce-scatter.21.cloned.1.call-update) | async-done | bytes 655376 | tf_op jit(solution)/shard_map/reduce_scatter | solution.py:228
  622.6 6.5 rev.10
  631.9 45.1 %all-gather.29.cloned.1.call-done = bf16[2,256,2560]{2,1,0:T(8,128)(2,1)} async-done(((bf16[2,64,2560]{2,1,0:T(8,128)(2,1)}), bf16[2,256,2560]{2,1,0:T(8,128)(2,1)}) %all-gather.29.cloned.1.call-update) | async-done | bytes 2621456 | tf_op jit(solution)/shard_map/all_gather | solution.py:234
  677.0 7.4 fusion.90
  684.4 8.5 rev.11
  695.3 37.3 %while.27 = (s32[]{:T(128)}, f32[2,640]{1,0:T(2,128)S(1)}, f32[4,2,64,640]{3,2,1,0:T(8,128)}, f32[4,2,64,640]{3,2,1,0:T(8,128)}, f32[4,2,64,640]{3,2,1,0:T(8,128)}, /*index=5*/s32[]{:T(128)}, f32[]{:T(128)}) while((s32[]{:T(128)}, f32[2,640]{1,0:T(2,128)S(1)}, f32[4,2,64,640]{3,2,1,0:T(8,128)}, f32[4,2,64,640]{3,2,1,0:T(8,128)}, ...), condition=%wide.region_15.16_spmd.clone, body=%wide.region_12.15_spmd.clone.sunk | while | flops 31463936 | bytes 4631649 | solution.py:66
  696.7 7.0 multiply_reduce_fusion.10
  706.0 7.0 multiply_reduce_fusion.10
  715.4 7.0 multiply_reduce_fusion.10
  724.7 7.0 multiply_reduce_fusion.10
  735.1 10.8 rev.12
  793.6 5.7 bitcast_convert_fusion.4
  800.9 10.7 fusion.22
  812.6 16.2 %reduce-scatter.23.cloned.1.call-done = bf16[2,64,2560]{2,1,0:T(8,128)(2,1)} async-done(((bf16[2,256,2560]{2,1,0:T(8,128)(2,1)}), bf16[2,64,2560]{2,1,0:T(8,128)(2,1)}) %reduce-scatter.23.cloned.1.call-update) | async-done | bytes 655376 | tf_op jit(solution)/shard_map/reduce_scatter | solution.py:303
  831.3 9.7 bitcast_convert_fusion.2
  841.3 9.6 bitcast_convert_fusion.1
  852.7 9.7 bitcast_convert_fusion
  867.4 35.5 %reduce-scatter.39.cloned.1.call-done = bf16[32,640]{1,0:T(8,128)(2,1)} async-done(((bf16[256,640]{1,0:T(8,128)(2,1)}), bf16[32,640]{1,0:T(8,128)(2,1)}) %reduce-scatter.39.cloned.1.call-update) | async-done | bytes 40976
  904.6 48.5 %reduce-scatter.25.cloned.1.call-done = bf16[320,640]{1,0:T(8,128)(2,1)} async-done(((bf16[2560,640]{1,0:T(8,128)(2,1)}), bf16[320,640]{1,0:T(8,128)(2,1)}) %reduce-scatter.25.cloned.1.call-update) | async-done | bytes 409616 | tf_op jit(solution)/shard_map/reduce_scatter | solution.py:322
  955.2 48.1 %reduce-scatter.29.cloned.1.call-done = bf16[640,320]{0,1:T(8,128)(2,1)} async-done(((bf16[640,2560]{0,1:T(8,128)(2,1)}), bf16[640,320]{0,1:T(8,128)(2,1)}) %reduce-scatter.29.cloned.1.call-update) | async-done | bytes 409616 | tf_op jit(solution)/shard_map/reduce_scatter | solution.py:328
  1005.3 48.2 %reduce-scatter.27.cloned.1.call-done = bf16[320,640]{1,0:T(8,128)(2,1)} async-done(((bf16[2560,640]{1,0:T(8,128)(2,1)}), bf16[320,640]{1,0:T(8,128)(2,1)}) %reduce-scatter.27.cloned.1.call-update) | async-done | bytes 409616 | tf_op jit(solution)/shard_map/reduce_scatter | solution.py:325
  1055.5 52.5 %reduce-scatter.19.cloned.1.call-done = bf16[2,64,2560]{2,1,0:T(8,128)(2,1)} async-done(((bf16[2,256,2560]{2,1,0:T(8,128)(2,1)}), bf16[2,64,2560]{2,1,0:T(8,128)(2,1)}) %reduce-scatter.19.cloned.1.call-update) | async-done | bytes 655376 | tf_op jit(solution)/shard_map/reduce_scatter | solution.py:212
  1111.4 123.9 %all-reduce.15.cloned.1.call-done = (f32[2560]{0:T(1024)}, f32[4,2560]{1,0:T(4,128)}, f32[2560]{0:T(1024)}, f32[2560]{0:T(1024)}) async-done(((f32[2560]{0:T(1024)}, f32[4,2560]{1,0:T(4,128)}, f32[2560]{0:T(1024)}, f32[2560]{0:T(1024)}), (f32[2560]{0:T(1024)}, f32[4,2560]{1,0:T(4,128)}, f32[2560]{0:T(1024)}, f32[2560]{0:T(1024)})) %all-reduce.15.cloned.1.call-update) | async-done | bytes 71696 | tf_op jit(solution)/shard_map/psum | solution.py:318
  1238.0 81.0 %reduce-scatter.31.cloned.1.call-done = bf16[320,1920]{1,0:T(8,128)(2,1)} async-done(((bf16[2560,1920]{1,0:T(8,128)(2,1)}), bf16[320,1920]{1,0:T(8,128)(2,1)}) %reduce-scatter.31.cloned.1.call-update) | async-done | bytes 1228816 | tf_op jit(solution)/shard_map/reduce_scatter | solution.py:86
  1321.8 79.0 %reduce-scatter.33.cloned.1.call-done = bf16[320,1920]{1,0:T(8,128)(2,1)} async-done(((bf16[2560,1920]{1,0:T(8,128)(2,1)}), bf16[320,1920]{1,0:T(8,128)(2,1)}) %reduce-scatter.33.cloned.1.call-update) | async-done | bytes 1228816 | tf_op jit(solution)/shard_map/reduce_scatter | solution.py:89
  1403.7 79.0 %reduce-scatter.35.cloned.1.call-done = bf16[1920,320]{0,1:T(8,128)(2,1)} async-done(((bf16[1920,2560]{0,1:T(8,128)(2,1)}), bf16[1920,320]{0,1:T(8,128)(2,1)}) %reduce-scatter.35.cloned.1.call-update) | async-done | bytes 1228816 | tf_op jit(solution)/shard_map/reduce_scatter | solution.py:92
  (357 shorter events, 156.1 us)
Async XLA Ops:
  7.2 61.2 %all-gather.11.cloned.1.call-start = ((), (), s32[]{:S(2)}) async-start(), calls=%async_computation.12 | async-start | bytes 3276800 | tf_op jit(solution)/shard_map/all_gather | solution.py:159
  10.8 91.2 %all-gather.15.cloned.1.call-start = ((), (), s32[]{:S(2)}) async-start(), calls=%async_computation.14 | async-start | bytes 3686400 | tf_op jit(solution)/shard_map/all_gather | solution.py:123
  11.5 157.0 %all-gather.13.cloned.1.call-start = ((), (), s32[]{:S(2)}) async-start(), calls=%async_computation.13 | async-start | bytes 3686400 | tf_op jit(solution)/shard_map/all_gather | solution.py:122
  12.3 21.5 %copy-start.44 = (f32[640]{0:T(1024)S(1)}, f32[640]{0:T(1024)}, u32[]{:S(2)}) copy-start(f32[640]{0:T(1024)} %param.27) | copy-start | bytes 7684
  12.3 162.8 %all-gather.17.cloned.1.call-start = ((), (), s32[]{:S(2)}) async-start(), calls=%async_computation.15 | async-start | bytes 3686400 | tf_op jit(solution)/shard_map/all_gather | solution.py:124
  12.8 220.6 %reduce-scatter.17.cloned.1.call-start = ((), (), s32[]{:S(2)}) async-start(), calls=%async_computation.16 | async-start | bytes 3276800 | tf_op jit(solution)/shard_map/reduce_scatter | solution.py:195
  13.0 93.9 %copy-start.32 = (f32[640]{0:T(1024)}, f32[640]{0:T(1024)S(1)}, u32[]{:S(2)}) copy-start(f32[640]{0:T(1024)S(1)} %get-tuple-element.156) | copy-start | bytes 7684
  13.0 93.9 %copy-start.34 = (f32[640]{0:T(1024)}, f32[640]{0:T(1024)S(1)}, u32[]{:S(2)}) copy-start(f32[640]{0:T(1024)S(1)} %get-tuple-element.157) | copy-start | bytes 7684
  13.0 93.9 %copy-start.36 = (f32[640]{0:T(1024)}, f32[640]{0:T(1024)S(1)}, u32[]{:S(2)}) copy-start(f32[640]{0:T(1024)S(1)} %get-tuple-element.155) | copy-start | bytes 7684
  108.3 6.0 collective-permute-start
  181.1 108.8 %all-gather.27.cloned.1.call-start = ((), (), s32[]{:S(2)}) async-start(), calls=%async_computation.22 | async-start | bytes 3276800 | tf_op jit(solution)/shard_map/all_gather | solution.py:216
  182.2 437.3 %copy-start.47 = (f32[2,64]{1,0:T(2,128)}, f32[2,64]{1,0:T(2,128)S(1)}, u32[]{:S(2)}) copy-start(f32[2,64]{1,0:T(2,128)S(1)} %compare_select_fusion) | copy-start | bytes 1540
  182.2 51.2 %copy-start = (bf16[2,64,2560]{2,1,0:T(8,128)(2,1)S(1)}, bf16[2,64,2560]{2,1,0:T(8,128)(2,1)}, u32[]{:S(2)}) copy-start(bf16[2,64,2560]{2,1,0:T(8,128)(2,1)} %param.20) | copy-start | bytes 1966084
  183.2 51.7 %copy-start.26 = (f32[2560]{0:T(1024)S(1)}, f32[2560]{0:T(1024)}, u32[]{:S(2)}) copy-start(f32[2560]{0:T(1024)} %param.29) | copy-start | bytes 30724
  183.2 167.9 %all-gather.25.cloned.1.call-start = ((), (), s32[]{:S(2)}) async-start(), calls=%async_computation.20 | async-start | bytes 11059200 | tf_op jit(solution)/shard_map/all_gather | solution.py:129
  184.0 224.1 %all-gather.19.cloned.1.call-start = ((), (), s32[]{:S(2)}) async-start(), calls=%async_computation.17 | async-start | bytes 3276800 | tf_op jit(solution)/shard_map/all_gather | solution.py:200
  234.9 384.6 %copy-start.38 = (f32[2,64]{1,0:T(2,128)}, f32[2,64]{1,0:T(2,128)S(1)}, u32[]{:S(2)}) copy-start(f32[2,64]{1,0:T(2,128)S(1)} %fusion.93) | copy-start | bytes 1540
  236.0 233.2 %all-gather.23.cloned.1.call-start = ((), (), s32[]{:S(2)}) async-start(), calls=%async_computation.19 | async-start | bytes 11059200 | tf_op jit(solution)/shard_map/all_gather | solution.py:128
  236.7 294.8 %all-gather.21.cloned.1.call-start = ((), (), s32[]{:S(2)}) async-start(), calls=%async_computation.18 | async-start | bytes 11059200 | tf_op jit(solution)/shard_map/all_gather | solution.py:127
  237.3 379.8 %reduce-scatter.21.cloned.1.call-start = ((), (), s32[]{:S(2)}) async-start(), calls=%async_computation.23 | async-start | bytes 3276800 | tf_op jit(solution)/shard_map/reduce_scatter | solution.py:228
  531.5 24.6 %slice-start = ((s8[9830400]{0:T(1024)(128)(4,1)}), s8[4194304]{0:T(1024)(128)(4,1)S(1)}, s32[]{:S(2)}) async-start(s8[9830400]{0:T(1024)(128)(4,1)} %bitcast.244), calls=%async_computation.35 | async-start | bytes 8388608
  531.5 24.6 %slice-start.1 = ((s8[9830400]{0:T(1024)(128)(4,1)}), s8[4194304]{0:T(1024)(128)(4,1)S(1)}, s32[]{:S(2)}) async-start(s8[9830400]{0:T(1024)(128)(4,1)} %bitcast.244), calls=%async_computation.36 | async-start | bytes 8388608
  564.9 112.1 %all-gather.29.cloned.1.call-start = ((), (), s32[]{:S(2)}) async-start(), calls=%async_computation.24 | async-start | bytes 3276800 | tf_op jit(solution)/shard_map/all_gather | solution.py:234
  622.4 206.4 %reduce-scatter.23.cloned.1.call-start = ((), (), s32[]{:S(2)}) async-start(), calls=%async_computation.25 | async-start | bytes 3276800 | tf_op jit(solution)/shard_map/reduce_scatter | solution.py:303
  629.1 47.9 %copy-start.20 = (f32[2,4,64,640]{3,2,1,0:T(8,128)S(1)}, f32[2,4,64,640]{3,2,1,0:T(8,128)}, u32[]{:S(2)}) copy-start(f32[2,4,64,640]{3,2,1,0:T(8,128)} %copy-done.19) | copy-start | bytes 3932164
  763.0 5.6 collective-permute-start.1
  776.3 89.4 %reduce-scatter.37.cloned.1.call-start = ((), (), s32[]{:S(2)}) async-start(), calls=%async_computation.32 | async-start | bytes 368640
  779.1 123.8 %reduce-scatter.39.cloned.1.call-start = ((), (), s32[]{:S(2)}) async-start(), calls=%async_computation.33 | async-start | bytes 368640
  780.1 173.1 %reduce-scatter.25.cloned.1.call-start = ((), (), s32[]{:S(2)}) async-start(), calls=%async_computation.26 | async-start | bytes 3686400 | tf_op jit(solution)/shard_map/reduce_scatter | solution.py:322
  785.8 217.5 %reduce-scatter.29.cloned.1.call-start = ((), (), s32[]{:S(2)}) async-start(), calls=%async_computation.28 | async-start | bytes 3686400 | tf_op jit(solution)/shard_map/reduce_scatter | solution.py:328
  792.6 260.9 %reduce-scatter.27.cloned.1.call-start = ((), (), s32[]{:S(2)}) async-start(), calls=%async_computation.27 | async-start | bytes 3686400 | tf_op jit(solution)/shard_map/reduce_scatter | solution.py:325
  799.3 308.6 %reduce-scatter.19.cloned.1.call-start = ((), (), s32[]{:S(2)}) async-start(), calls=%async_computation.21 | async-start | bytes 3276800 | tf_op jit(solution)/shard_map/reduce_scatter | solution.py:212
  811.6 19.6 %copy-start.61 = (bf16[2,256,2560]{2,1,0:T(8,128)(2,1)S(1)}, bf16[2,256,2560]{2,1,0:T(8,128)(2,1)}, u32[]{:S(2)}) copy-start(bf16[2,256,2560]{2,1,0:T(8,128)(2,1)} %all-gather.19.cloned.1.call-done) | copy-start | bytes 7864324
  811.7 423.6 %all-reduce.15.cloned.1.call-start = ((), (), s32[]{:S(2)}) async-start(), calls=%async_computation.34 | async-start | bytes 155648 | tf_op jit(solution)/shard_map/psum | solution.py:318
  812.4 18.7 %copy-start.29 = (f32[2560]{0:T(1024)}, f32[2560]{0:T(1024)S(1)}, u32[]{:S(2)}) copy-start(f32[2560]{0:T(1024)S(1)} %dynamic_update_slice.34) | copy-start | bytes 30724
  831.2 487.7 %reduce-scatter.31.cloned.1.call-start = ((), (), s32[]{:S(2)}) async-start(), calls=%async_computation.29 | async-start | bytes 11059200 | tf_op jit(solution)/shard_map/reduce_scatter | solution.py:86
  841.0 559.8 %reduce-scatter.33.cloned.1.call-start = ((), (), s32[]{:S(2)}) async-start(), calls=%async_computation.30 | async-start | bytes 11059200 | tf_op jit(solution)/shard_map/reduce_scatter | solution.py:89
  850.9 631.8 %reduce-scatter.35.cloned.1.call-start = ((), (), s32[]{:S(2)}) async-start(), calls=%async_computation.31 | async-start | bytes 11059200 | tf_op jit(solution)/shard_map/reduce_scatter | solution.py:92
  953.1 154.8 %copy-start.23 = (bf16[2,64,2560]{2,1,0:T(8,128)(2,1)S(1)}, bf16[2,64,2560]{2,1,0:T(8,128)(2,1)}, u32[]{:S(2)}) copy-start(bf16[2,64,2560]{2,1,0:T(8,128)(2,1)} %reduce-scatter.23.cloned.1.call-done) | copy-start | bytes 1966084
  955.2 100.3 %copy-start.55 = (f32[2,64]{1,0:T(2,128)S(1)}, f32[2,64]{1,0:T(2,128)}, u32[]{:S(2)}) copy-start(f32[2,64]{1,0:T(2,128)} %copy-done.54) | copy-start | bytes 1540
  955.2 152.8 %copy-start.8 = (bf16[2,64,2560]{2,1,0:T(8,128)(2,1)S(1)}, bf16[2,64,2560]{2,1,0:T(8,128)(2,1)}, u32[]{:S(2)}) copy-start(bf16[2,64,2560]{2,1,0:T(8,128)(2,1)} %reduce-scatter.17.cloned.1.call-done) | copy-start | bytes 1966084
  955.2 152.8 %copy-start.14 = (bf16[2,64,2560]{2,1,0:T(8,128)(2,1)S(1)}, bf16[2,64,2560]{2,1,0:T(8,128)(2,1)}, u32[]{:S(2)}) copy-start(bf16[2,64,2560]{2,1,0:T(8,128)(2,1)} %reduce-scatter.21.cloned.1.call-done) | copy-start | bytes 1966084
  955.2 152.8 %copy-start.16 = (bf16[2,64,2560]{2,1,0:T(8,128)(2,1)S(1)}, bf16[2,64,2560]{2,1,0:T(8,128)(2,1)}, u32[]{:S(2)}) copy-start(bf16[2,64,2560]{2,1,0:T(8,128)(2,1)} %param.33) | copy-start | bytes 1966084
  955.2 152.8 %copy-start.39 = (f32[2,64]{1,0:T(2,128)S(1)}, f32[2,64]{1,0:T(2,128)}, u32[]{:S(2)}) copy-start(f32[2,64]{1,0:T(2,128)} %copy-done.38) | copy-start | bytes 1540
  955.2 152.8 %copy-start.48 = (f32[2,64]{1,0:T(2,128)S(1)}, f32[2,64]{1,0:T(2,128)}, u32[]{:S(2)}) copy-start(f32[2,64]{1,0:T(2,128)} %copy-done.47) | copy-start | bytes 1540
  955.2 152.8 %copy-start.57 = (f32[2,64]{1,0:T(2,128)S(1)}, f32[2,64]{1,0:T(2,128)}, u32[]{:S(2)}) copy-start(f32[2,64]{1,0:T(2,128)} %copy-done.56) | copy-start | bytes 1540
  1403.7 81.9 %copy-start.52 = (f32[2560]{0:T(1024)S(1)}, f32[2560]{0:T(1024)}, u32[]{:S(2)}) copy-start(f32[2560]{0:T(1024)} %get-tuple-element.321) | copy-start | bytes 30724
  1403.7 82.5 %copy-start.51 = (f32[2560]{0:T(1024)S(1)}, f32[2560]{0:T(1024)}, u32[]{:S(2)}) copy-start(f32[2560]{0:T(1024)} %get-tuple-element.329) | copy-start | bytes 30724
  (49 other events, 220.1 us)
Sparse Core Ops, SparseCore 0:
  10.9 57.4 all-gather.10
  70.3 31.6 all-gather.14
  103.9 32.8 all-gather.12
  138.5 32.8 all-gather.16
  181.2 52.1 reduce-scatter.16
  235.4 54.4 all-gather.26
  291.7 59.2 all-gather.24
  353.2 54.7 all-gather.18
  409.9 59.2 all-gather.22
  471.0 60.4 all-gather.20
  565.0 52.0 reduce-scatter.20
  622.5 54.4 all-gather.28
  776.4 52.3 reduce-scatter.22
  832.3 33.3 reduce-scatter.36
  869.2 33.7 reduce-scatter.38
  906.2 46.8 reduce-scatter.24
  956.4 46.8 reduce-scatter.28
  1006.6 46.8 reduce-scatter.26
  1055.8 52.0 reduce-scatter.18
  1115.0 120.2 all-reduce.14
  1238.9 80.0 reduce-scatter.30
  1322.5 78.2 reduce-scatter.32
  1404.4 78.2 reduce-scatter.34
where the time goes:
time: 1500 us; the launch traced here: 1490 us
  waiting for transfers between devices  1110 us (74%)
  matrix products  147 us (10%)
  other arithmetic  112 us (7%)
  local copies, waits for them, and re-layouts  87.9 us (6%)
  blocking collectives  20.3 us (1%)
  between operations  15.2 us (1%)
    psum x1, waiting for transfers between devices, shards(): lax.psum((grad_norm_gain, grad_mlp_gain, rate_full, taps_full), ('dp', 't...  124 us
    reduce_scatter x1, waiting for transfers between devices, reduce_feed(): lax.psum_scatter(grad_gate_w.astype(jnp.bfloat16), 'dp', scatter_dimensio...  81 us
    reduce_scatter x1, waiting for transfers between devices, reduce_feed(): lax.psum_scatter(down_weight_gradient.astype(jnp.bfloat16), 'dp', scatter...  79 us
    reduce_scatter x1, waiting for transfers between devices, reduce_feed(): lax.psum_scatter(grad_lift_w.astype(jnp.bfloat16), 'dp', scatter_dimensio...  79 us
    all_gather x1, waiting for transfers between devices, shards(): lax.all_gather(feed_up, 'dp', axis=0, tiled=True)  61.2 us
    all_gather x1, waiting for transfers between devices, shards(): lax.all_gather(feed_down, 'dp', axis=1, tiled=True)  61.2 us
    reduce_sum x8, other arithmetic, advance(): jnp.sum(factor * input_block[:, None, :, :], axis=2)  55.9 us
    all_gather x1, waiting for transfers between devices, shards(): lax.all_gather(scaled_cot.astype(jnp.bfloat16), 'tensor', axis=1, tiled=T...  52.5 us
  transfers between devices with their start and end apart: 25, of which 22 were waited for; matrix products, arithmetic and copies ran while one was open for 13% of the time, Pallas kernels for 0%

commit v1 on v0

v1 whole, which is shorter than its diff:
```python
import functools

import jax
import jax.numpy as jnp
from jax import lax
from jax.experimental import pallas as pl
from jax.experimental.pallas import tpu as pltpu
from jax.sharding import PartitionSpec as P

MICRO = 4
EPS = 1e-06
MESH = pl.DeviceIdType.MESH
ANY = pl.BlockSpec(memory_space=pl.ANY)
VMEM = pl.BlockSpec(memory_space=pltpu.VMEM)
DMA = pltpu.SemaphoreType.DMA
BF16 = jnp.bfloat16
F32 = jnp.float32


def place():
    return lax.axis_index("dp"), lax.axis_index("tensor")


def greet(d, t, depth, dp_masks=(1, 2, 4), z_all=False):
    barrier = pltpu.get_barrier_semaphore()
    for mask in dp_masks:
        pl.semaphore_signal(barrier, inc=1, device_id=(d ^ mask, t), device_id_type=MESH)
    if z_all:
        for step in range(1, depth):
            pl.semaphore_signal(
                barrier, inc=1, device_id=(d, lax.rem(t + step, depth)), device_id_type=MESH
            )
        pl.semaphore_wait(barrier, len(dp_masks) + depth - 1)
        return

    @pl.when(t > 0)
    def _():
        pl.semaphore_signal(barrier, inc=1, device_id=(d, t - 1), device_id_type=MESH)

    @pl.when(t < depth - 1)
    def _():
        pl.semaphore_signal(barrier, inc=1, device_id=(d, t + 1), device_id_type=MESH)

    ends = jnp.where((t == 0) | (t == depth - 1), 1, 2)
    pl.semaphore_wait(barrier, len(dp_masks) + ends)


def add_rows(total, term, rows, step=32):
    step = min(step, rows)

    @pl.loop(0, rows, step=step)
    def _(start):
        part = pl.ds(pl.multiple_of(start, step), step)
        total[part, :] = (total[part, :].astype(F32) + term[part, :].astype(F32)).astype(BF16)


class WeightGather:
    def __init__(self, shard, out, local, send, recv, d, t):
        rows = shard.shape[0]
        half = rows // 2
        top, low = pl.ds(0, half), pl.ds(half, half)
        plan = [
            (shard.at[top], d, top, 2),
            (shard.at[low], d, low, 4),
            (shard.at[low], d, low, 2),
            (shard.at[top], d, top, 4),
            (out.at[d ^ 2, top], d ^ 2, top, 4),
            (out.at[d ^ 4, low], d ^ 4, low, 2),
            (shard.at[top], d, top, 1),
            (shard.at[low], d, low, 1),
            (out.at[d ^ 2, top], d ^ 2, top, 1),
            (out.at[d ^ 4, low], d ^ 4, low, 1),
            (out.at[d ^ 2, low], d ^ 2, low, 1),
            (out.at[d ^ 4, top], d ^ 4, top, 1),
            (out.at[d ^ 6, top], d ^ 6, top, 1),
            (out.at[d ^ 6, low], d ^ 6, low, 1),
        ]
        self.copies = [
            pltpu.make_async_remote_copy(
                src_ref=src,
                dst_ref=out.at[slot, part],
                send_sem=send.at[i],
                recv_sem=recv.at[i],
                device_id=(d ^ mask, t),
                device_id_type=MESH,
            )
            for i, (src, slot, part, mask) in enumerate(plan)
        ]
        self.own = pltpu.make_async_copy(shard, out.at[d], local)

    def start(self):
        for i in (0, 1, 2, 3):
            self.copies[i].start()
        self.own.start()

    def relay(self):
        c = self.copies
        for i in (6, 7):
            c[i].start()
        c[0].wait_recv()
        c[4].start()
        c[1].wait_recv()
        c[5].start()
        c[8].start()
        c[9].start()

    def relay_two(self):
        c = self.copies
        c[2].wait_recv()
        c[10].start()
        c[3].wait_recv()
        c[11].start()

    def relay_last(self):
        c = self.copies
        c[4].wait_recv()
        c[12].start()
        c[5].wait_recv()
        c[13].start()

    def end(self):
        for i in range(6, 14):
            self.copies[i].wait_recv()
        for i in range(14):
            self.copies[i].wait_send()
        self.own.wait()


def gather_scratch(count):
    return [DMA((count,)), DMA((count, 14)), DMA((count, 14))]


class GradScatter:
    ORDER = (6, 2, 4, 0)

    def __init__(self, grad, out, own, core, diag, last, local, send, recv, d, t):
        self.out, self.own, self.core, self.diag, self.last = out, own, core, diag, last
        self.rows = rows = grad.shape[1]
        half = rows // 2
        self.half = half
        self.top, self.low = pl.ds(0, half), pl.ds(half, half)
        self.loads = [
            pltpu.make_async_copy(grad.at[d ^ r], own.at[i], local.at[i])
            for i, r in enumerate(self.ORDER)
        ]
        top, low = self.top, self.low
        plan = [(grad.at[d ^ 1 ^ r], core.at[i], 1) for i, r in enumerate(self.ORDER)] + [
            (own.at[0, top], diag.at[0], 2),
            (own.at[0, low], diag.at[1], 4),
            (own.at[1, top], last.at[0, top], 2),
            (own.at[2, low], last.at[1, low], 4),
            (own.at[2, top], last.at[1, top], 4),
            (own.at[1, low], last.at[0, low], 2),
        ]
        self.copies = [
            pltpu.make_async_remote_copy(
                src_ref=src,
                dst_ref=dst,
                send_sem=send.at[i],
                recv_sem=recv.at[i],
                device_id=(d ^ mask, t),
                device_id_type=MESH,
            )
            for i, (src, dst, mask) in enumerate(plan)
        ]

    def start(self):
        for i in range(4):
            self.copies[i].start()
            self.loads[i].start()

    def pair(self, i):
        self.loads[i].wait()
        self.copies[i].wait_recv()
        add_rows(self.own.at[i], self.core.at[i], self.rows)

    def first(self):
        self.pair(0)
        self.copies[4].start()
        self.copies[5].start()

    def second(self):
        self.pair(1)
        self.copies[6].start()
        self.pair(2)
        self.copies[7].start()
        self.pair(3)

    def third(self):
        c = self.copies
        c[4].wait_recv()
        add_rows(self.own.at[2, self.top], self.diag.at[0], self.half)
        c[8].start()
        c[5].wait_recv()
        add_rows(self.own.at[1, self.low], self.diag.at[1], self.half)
        c[9].start()

    def end(self):
        for i in (6, 7, 8, 9):
            self.copies[i].wait_recv()
        step = 16

        @pl.loop(0, self.rows, step=step)
        def _(start):
            part = pl.ds(pl.multiple_of(start, step), step)
            self.out[part, :] = (
                self.own[3, part, :].astype(F32)
                + self.last[0, part, :].astype(F32)
                + self.last[1, part, :].astype(F32)
            )

        for i in range(10):
            self.copies[i].wait_send()


def scatter_scratch(shapes):
    own = [pltpu.VMEM((4,) + s, BF16) for s in shapes]
    core = [pltpu.VMEM((4,) + s, BF16) for s in shapes]
    diag = [pltpu.VMEM((2, s[0] // 2, s[1]), BF16) for s in shapes]
    last = [pltpu.VMEM((2,) + s, BF16) for s in shapes]
    n = len(shapes)
    return own + core + diag + last + [DMA((n, 4)), DMA((n, 10)), DMA((n, 10))]


def make_scatters(grads, outs, scratch, d, t):
    n = len(grads)
    own, core, diag, last = (scratch[i * n : (i + 1) * n] for i in range(4))
    local, send, recv = scratch[4 * n :]
    return [
        GradScatter(
            grads[i],
            outs[i],
            own[i],
            core[i],
            diag[i],
            last[i],
            local.at[i],
            send.at[i],
            recv.at[i],
            d,
            t,
        )
        for i in range(n)
    ]


class LineGather:
    def __init__(self, block, out, local, send, recv, d, t, depth):
        self.block, self.out, self.send, self.recv = block, out, send, recv
        self.d, self.t, self.depth = d, t, depth
        self.rows = block.shape[1]
        self.own = pltpu.make_async_copy(block, self.slot(t), local)

    def slot(self, j):
        return self.out.at[:, pl.ds(pl.multiple_of(j * self.rows, self.rows), self.rows)]

    def copy(self, way, step, j, to):
        return pltpu.make_async_remote_copy(
            src_ref=self.block if step == 0 else self.slot(j),
            dst_ref=self.slot(j),
            send_sem=self.send.at[way, step],
            recv_sem=self.recv.at[way, step],
            device_id=(self.d, to),
            device_id_type=MESH,
        )

    def step(self, s):
        t, depth = self.t, self.depth
        if s == 0:
            self.own.start()
        if s > 0:

            @pl.when(t - s >= 0)
            def _():
                self.copy(0, s - 1, t, t).wait_recv()

        if s < depth - 1:

            @pl.when((t - s >= 0) & (t < depth - 1))
            def _():
                self.copy(0, s, t - s, t + 1).start()

        if s > 0:

            @pl.when(t + s < depth)
            def _():
                self.copy(1, s - 1, t, t).wait_recv()

        if s < depth - 1:

            @pl.when((t + s < depth) & (t > 0))
            def _():
                self.copy(1, s, t + s, t - 1).start()

    def end(self):
        t, depth = self.t, self.depth
        for s in range(depth - 1):

            @pl.when((t - s >= 0) & (t < depth - 1))
            def _():
                self.copy(0, s, t, t).wait_send()

            @pl.when((t + s < depth) & (t > 0))
            def _():
                self.copy(1, s, t, t).wait_send()

        self.own.wait()


def line_gather_scratch(depth):
    return [DMA, DMA((2, depth - 1)), DMA((2, depth - 1))]


class LineScatter:
    def __init__(self, part, got, send, recv, d, t, depth):
        self.part, self.got, self.send, self.recv = part, got, send, recv
        self.d, self.t, self.depth = d, t, depth
        self.seqs = part.shape[0]
        self.rows = part.shape[1] // depth

    def copy(self, way, j, s, src, to):
        return pltpu.make_async_remote_copy(
            src_ref=src,
            dst_ref=self.got.at[way, j, s],
            send_sem=self.send.at[way, j, s],
            recv_sem=self.recv.at[way, j, s],
            device_id=(self.d, to),
            device_id_type=MESH,
        )

    def move(self, way, j):
        t, depth = self.t, self.depth
        rows = pl.ds(j * self.rows, self.rows)
        if way == 0:
            source, hears, sends, to = t == 0, (t > 0) & (j >= t), j > t, t + 1
        else:
            source, hears, sends, to = t == depth - 1, (t < depth - 1) & (j <= t), j < t, t - 1
        for s in range(self.seqs):
            mine = self.got.at[way, j, s]

            @pl.when(hears)
            def _():
                self.copy(way, j, s, mine, t).wait_recv()

            @pl.when(sends & source)
            def _():
                self.copy(way, j, s, self.part.at[s, rows], to).start()

            @pl.when(sends & jnp.logical_not(source))
            def _():
                add_rows(mine, self.part.at[s, rows], self.rows)
                self.copy(way, j, s, mine, to).start()

    def step(self, k):
        depth, t = self.depth, self.t
        right, left = depth - 1 - k, k

        @pl.when(t < depth // 2)
        def _():
            self.move(0, right)

        self.move(1, left)

        @pl.when(t >= depth // 2)
        def _():
            self.move(0, right)

    def total(self, out):
        t, depth = self.t, self.depth
        mine = pl.ds(pl.multiple_of(t * self.rows, self.rows), self.rows)
        out[...] = self.part[:, mine, :].astype(F32)

        @pl.when(t > 0)
        def _():
            out[...] += self.got[0, t].astype(F32)

        @pl.when(t < depth - 1)
        def _():
            out[...] += self.got[1, t].astype(F32)

    def end(self):
        t, depth = self.t, self.depth
        for j in range(depth):
            for s in range(self.seqs):
                mine = self.got.at[0, j, s]

                @pl.when((j > t) & (t < depth - 1))
                def _():
                    self.copy(0, j, s, mine, t).wait_send()

                @pl.when((j < t) & (t > 0))
                def _():
                    self.copy(1, j, s, mine, t).wait_send()


def line_scatter_scratch(seqs, rows, width, depth):
    return [
        pltpu.VMEM((2, depth, seqs, rows, width), BF16),
        DMA((2, depth, seqs)),
        DMA((2, depth, seqs)),
    ]


def call(kernel, name, number, ins, outs, scratch, args, vmem=60 * 1024 * 1024):
    return pl.pallas_call(
        kernel,
        name=name,
        out_shape=[o[0] for o in outs],
        in_specs=ins,
        out_specs=[o[1] for o in outs],
        scratch_shapes=scratch,
        compiler_params=pltpu.CompilerParams(
            collective_id=number, has_side_effects=True, vmem_limit_bytes=vmem
        ),
    )(*args)


def shaped(shape, dtype, spec):
    return (jax.ShapeDtypeStruct(shape, dtype), spec)


def gather_kernel(depth, n_weights, *refs):
    blocks = refs[:2]
    shards = refs[2 : 2 + n_weights]
    outs = refs[2 + n_weights :]
    wide, full = outs[:2], outs[2 : 2 + n_weights]
    scratch = outs[2 + n_weights :]
    d, t = place()
    greet(d, t, depth)
    local, send, recv = scratch[:3]
    lines = [
        LineGather(blocks[i], wide[i], *scratch[3 + 3 * i : 6 + 3 * i], d, t, depth)
        for i in range(2)
    ]
    gathers = [
        WeightGather(shards[i], full[i], local.at[i], send.at[i], recv.at[i], d, t)
        for i in range(n_weights)
    ]
    lines[0].step(0)
    for g in gathers:
        g.start()
    early, late = gathers[:-1], gathers[-1:]
    lines[0].step(1)
    for g in early:
        g.relay()
    lines[0].step(2)
    lines[1].step(0)
    for g in early:
        g.relay_two()
    lines[0].step(3)
    for g in early:
        g.relay_last()
    lines[1].step(1)
    for g in late:
        g.relay()
    lines[1].step(2)
    for g in late:
        g.relay_two()
    lines[1].step(3)
    for g in late:
        g.relay_last()
    for g in gathers:
        g.end()
    for line in lines:
        line.end()


def gather_first(normed, cot, weights, depth):
    seqs, rows, width = normed.shape
    n = len(weights)
    outs = [shaped((seqs, rows * depth, width), BF16, ANY)] * 2
    outs += [shaped((8,) + w.shape, BF16, ANY) for w in weights]
    scratch = gather_scratch(n) + line_gather_scratch(depth) * 2
    res = call(
        functools.partial(gather_kernel, depth, n),
        "gather_first",
        0,
        [ANY] * (2 + n),
        outs,
        scratch,
        (normed, cot) + tuple(weights),
    )
    return res[0], res[1], res[2:]


def middle_kernel(depth, part, act, gain, w0, w1, middle, wide, f0, f1, *scratch):
    local, send, recv = scratch[:3]
    got, ssem, rsem = scratch[3:6]
    block = scratch[6]
    lsem = scratch[7:10]
    d, t = place()
    greet(d, t, depth)
    gathers = [
        WeightGather(w, f, local.at[i], send.at[i], recv.at[i], d, t)
        for i, (w, f) in enumerate(((w0, f0), (w1, f1)))
    ]
    scatter = LineScatter(part, got, ssem, rsem, d, t, depth)
    scatter.step(0)
    for g in gathers:
        g.start()
    scatter.step(1)
    gathers[0].relay()
    scatter.step(2)
    gathers[0].relay_two()
    scatter.step(3)
    scatter.total(middle)
    seqs, rows, width = act.shape
    for s in range(seqs):
        value = middle[s] + act[s].astype(F32)
        middle[s] = value
        inverse = lax.rsqrt(jnp.mean(value * value, axis=-1, keepdims=True) + EPS)
        block[s] = (value * inverse * gain[...]).astype(BF16)
    line = LineGather(block, wide, *lsem, d, t, depth)
    line.step(0)
    gathers[0].relay_last()
    gathers[1].relay()
    line.step(1)
    gathers[1].relay_two()
    line.step(2)
    gathers[1].relay_last()
    line.step(3)
    for g in gathers:
        g.end()
    scatter.end()
    line.end()


def middle_phase(part, act, gain, w0, w1, depth):
    seqs, rows, width = act.shape
    outs = [
        shaped(act.shape, F32, VMEM),
        shaped((seqs, rows * depth, width), BF16, ANY),
        shaped((8,) + w0.shape, BF16, ANY),
        shaped((8,) + w1.shape, BF16, ANY),
    ]
    scratch = (
        gather_scratch(2)
        + line_scatter_scratch(seqs, rows, width, depth)
        + [pltpu.VMEM(act.shape, BF16)]
        + line_gather_scratch(depth)
    )
    return call(
        functools.partial(middle_kernel, depth),
        "middle_phase",
        1,
        [VMEM, VMEM, VMEM, ANY, ANY],
        outs,
        scratch,
        (part, act, gain.reshape(1, width), w0, w1),
    )


def norm_back(value, gain, error):
    inverse = lax.rsqrt(jnp.mean(value * value, axis=-1, keepdims=True) + EPS)
    scaled = error * gain
    mean = jnp.mean(scaled * value, axis=-1, keepdims=True)
    grad = inverse * scaled - value * (inverse * inverse * inverse * mean)
    return grad, jnp.sum(error * value * inverse, axis=0, keepdims=True)


def back_kernel(depth, part, middle, gain, cot, g0, g1, grad, wide, gain_grad, o0, o1, *scratch):
    got, ssem, rsem = scratch[:3]
    block = scratch[3]
    lsem = scratch[4:7]
    d, t = place()
    greet(d, t, depth)
    scatters = make_scatters((g0, g1), (o0, o1), scratch[7:], d, t)
    scatter = LineScatter(part, got, ssem, rsem, d, t, depth)
    scatter.step(0)
    for g in scatters:
        g.start()
    scatters[0].first()
    scatters[0].second()
    scatter.step(1)
    scatters[1].first()
    scatters[0].third()
    scatter.step(2)
    scatters[1].second()
    scatter.step(3)
    scatter.total(grad)
    seqs, rows, width = middle.shape
    for s in range(seqs):
        change, gain_part = norm_back(middle[s], gain[...], grad[s])
        change = change + cot[s]
        grad[s] = change
        block[s] = change.astype(BF16)
        if s == 0:
            gain_grad[...] = gain_part
        else:
            gain_grad[...] += gain_part
    line = LineGather(block, wide, *lsem, d, t, depth)
    line.step(0)
    scatters[1].third()
    line.step(1)
    scatters[0].end()
    line.step(2)
    line.step(3)
    scatters[1].end()
    scatter.end()
    line.end()


def back_phase(part, middle, gain, cot, g0, g1, depth):
    seqs, rows, width = middle.shape
    shapes = [g0.shape[1:], g1.shape[1:]]
    outs = [
        shaped(middle.shape, F32, VMEM),
        shaped((seqs, rows * depth, width), BF16, ANY),
        shaped((1, width), F32, VMEM),
        shaped(shapes[0], F32, VMEM),
        shaped(shapes[1], F32, VMEM),
    ]
    scratch = (
        line_scatter_scratch(seqs, rows, width, depth)
        + [pltpu.VMEM(middle.shape, BF16)]
        + line_gather_scratch(depth)
        + scatter_scratch(shapes)
    )
    return call(
        functools.partial(back_kernel, depth),
        "back_phase",
        2,
        [VMEM, VMEM, VMEM, VMEM, ANY, ANY],
        outs,
        scratch,
        (part, middle, gain.reshape(1, width), cot, g0, g1),
    )


def last_kernel(depth, n_grads, part, feed, act, gain, middle, grad_middle, mlp_part, small, *refs):
    grads = refs[:n_grads]
    refs = refs[n_grads:]
    output, input_grad, gains, smalls = refs[:4]
    outs = refs[4 : 4 + n_grads]
    scratch = refs[4 + n_grads :]
    got0, ssem0, rsem0, got1, ssem1, rsem1 = scratch[:6]
    pack, packs, small_all, line_pack, line_packs = scratch[6:11]
    psend, precv, qsend, qrecv, zsend, zrecv = scratch[11:17]
    total = scratch[17]
    d, t = place()
    greet(d, t, depth, dp_masks=(1, 2, 3, 4, 5, 6, 7), z_all=True)
    scatters = make_scatters(grads, outs, scratch[18:], d, t)
    first = LineScatter(part, got0, ssem0, rsem0, d, t, depth)
    second = LineScatter(feed, got1, ssem1, rsem1, d, t, depth)

    def dp_copies(src, dst, send, recv):
        return [
            pltpu.make_async_remote_copy(
                src_ref=src,
                dst_ref=dst.at[d],
                send_sem=send.at[mask - 1],
                recv_sem=recv.at[mask - 1],
                device_id=(d ^ mask, t),
                device_id_type=MESH,
            )
            for mask in range(1, 8)
        ]

    small_copies = dp_copies(small, small_all, qsend, qrecv)
    for c in small_copies:
        c.start()
    first.step(0)
    for g in scatters:
        g.start()
    for g in scatters[:-1]:
        g.first()
        g.second()
    first.step(1)
    for g in scatters[:-1]:
        g.third()
    scatters[-1].first()
    first.step(2)
    second.step(0)
    scatters[-1].second()
    first.step(3)
    first.total(input_grad)
    seqs = act.shape[0]
    pack[1:2, :] = mlp_part[...]
    for s in range(seqs):
        change, gain_part = norm_back(act[s].astype(F32), gain[...], input_grad[s])
        input_grad[s] = change + grad_middle[s]
        if s == 0:
            pack[0:1, :] = gain_part
        else:
            pack[0:1, :] += gain_part
    pack_copies = dp_copies(pack, packs, psend, precv)
    for c in pack_copies:
        c.start()
    scatters[-1].third()
    second.step(1)
    packs[d] = pack[...]
    small_all[d] = small[...]
    for c in pack_copies:
        c.wait_recv()
    sum_ = packs[0]
    for i in range(1, 8):
        sum_ = sum_ + packs[i]
    line_pack[...] = sum_
    z_copies = [
        pltpu.make_async_remote_copy(
            src_ref=line_pack,
            dst_ref=line_packs.at[t],
            send_sem=zsend.at[step - 1],
            recv_sem=zrecv.at[step - 1],
            device_id=(d, lax.rem(t + step, depth)),
            device_id_type=MESH,
        )
        for step in range(1, depth)
    ]
    for c in z_copies:
        c.start()
    line_packs[t] = sum_
    second.step(2)
    for g in scatters[:-1]:
        g.end()
    second.step(3)
    second.total(total)
    output[...] = (total[...] + middle[...]).astype(BF16)
    for c in small_copies:
        c.wait_recv()
    sum_ = small_all[0]
    for i in range(1, 8):
        sum_ = sum_ + small_all[i]
    smalls[...] = sum_
    for c in z_copies:
        c.wait_recv()
    sum_ = line_packs[0]
    for i in range(1, depth):
        sum_ = sum_ + line_packs[i]
    gains[...] = sum_
    scatters[-1].end()
    for c in small_copies + pack_copies + z_copies:
        c.wait_send()
    first.end()
    second.end()


def last_phase(part, feed, act, gain, middle, grad_middle, mlp_part, small, grads, depth):
    seqs, rows, width = act.shape
    n = len(grads)
    shapes = [g.shape[1:] for g in grads]
    outs = [
        shaped(act.shape, BF16, VMEM),
        shaped(act.shape, F32, VMEM),
        shaped((8, width), F32, VMEM),
        shaped(small.shape, F32, VMEM),
    ] + [shaped(s, F32, VMEM) for s in shapes]
    scratch = (
        line_scatter_scratch(seqs, rows, width, depth) * 2
        + [
            pltpu.VMEM((8, width), F32),
            pltpu.VMEM((8, 8, width), F32),
            pltpu.VMEM((8,) + small.shape, F32),
            pltpu.VMEM((8, width), F32),
            pltpu.VMEM((depth, 8, width), F32),
        ]
        + [DMA((7,))] * 4
        + [DMA((depth - 1,))] * 2
        + [pltpu.VMEM(act.shape, F32)]
        + scatter_scratch(shapes)
    )
    res = call(
        functools.partial(last_kernel, depth, n),
        "last_phase",
        3,
        [VMEM] * 8 + [ANY] * n,
        outs,
        scratch,
        (part, feed, act, gain.reshape(1, width), middle, grad_middle, mlp_part, small)
        + tuple(grads),
    )
    return res[0], res[1], res[2], res[3], res[4:]


def scan_kernel(backward, rate_ref, drive_ref, out_ref):
    seqs, length, width = rate_ref.shape
    tile = 8
    row = lax.broadcasted_iota(jnp.int32, (tile, width), 0)

    def body(i, carried):
        k = length // tile - 1 - i if backward else i
        rows = pl.ds(pl.multiple_of(k * tile, tile), tile)
        ends = []
        for s in range(seqs):
            rate = rate_ref[s, rows, :]
            drive = drive_ref[s, rows, :]
            for shift in (1, 2, 4):
                turn = tile - shift if backward else shift
                inside = row < tile - shift if backward else row >= shift
                before = jnp.where(inside, pltpu.roll(drive, turn, 0), 0.0)
                drive = drive + rate * before
                rate = rate * jnp.where(inside, pltpu.roll(rate, turn, 0), 1.0)
            states = drive + rate * carried[s]
            out_ref[s, rows, :] = states
            ends.append(states[0:1] if backward else states[tile - 1 : tile])
        return tuple(ends)

    start = tuple(jnp.zeros((1, width), F32) for _ in range(seqs))
    lax.fori_loop(0, length // tile, body, start)


def recurrence(rate, drive, backward=False):
    return pl.pallas_call(
        functools.partial(scan_kernel, backward),
        name="recurrence",
        out_shape=jax.ShapeDtypeStruct(drive.shape, F32),
        in_specs=[VMEM, VMEM],
        out_specs=VMEM,
        compiler_params=pltpu.CompilerParams(vmem_limit_bytes=32 * 1024 * 1024),
    )(rate, drive)


def swapped(block, axis):
    count = lax.axis_size(axis)
    return lax.ppermute(block, axis, [(i, i ^ 1) for i in range(count)])


def normalize(value_entries, scale_gain):
    return (
        value_entries
        * lax.rsqrt(jnp.mean(value_entries * value_entries, axis=-1, keepdims=True) + EPS)
        * scale_gain
    )


def causal_conv(value_entries, kernel):
    summed = value_entries * kernel[0]
    for offset in range(1, kernel.shape[0]):
        shifted = jnp.concatenate(
            [jnp.zeros_like(value_entries[:, :offset]), value_entries[:, :-offset]], axis=1
        )
        summed = summed + shifted * kernel[offset]
    return summed


def decay_inputs(input_pre, decay_pre, conv_vals, decay_rate):
    log_decay = -8.0 * jax.nn.sigmoid(decay_pre) * decay_rate
    scaled = jnp.sqrt(-jnp.expm1(2.0 * log_decay))
    return (log_decay, scaled * jax.nn.sigmoid(input_pre) * conv_vals)


class Fast:
    @staticmethod
    def first(normed, cot, weights, depth):
        return gather_first(normed, cot, weights, depth)

    middle = staticmethod(middle_phase)
    back = staticmethod(back_phase)
    last = staticmethod(last_phase)


class Plain:
    @staticmethod
    def wide(block):
        return lax.all_gather(block, "tensor", axis=1, tiled=True)

    @staticmethod
    def narrow(part):
        return lax.psum_scatter(part, "tensor", scatter_dimension=1, tiled=True).astype(F32)

    @staticmethod
    def full(shard):
        return lax.all_gather(shard, "dp", axis=0, tiled=False)

    @staticmethod
    def own(grad):
        return lax.psum_scatter(grad, "dp", scatter_dimension=0, tiled=False).astype(F32)

    @classmethod
    def first(cls, normed, cot, weights, depth):
        return cls.wide(normed), cls.wide(cot), [cls.full(w) for w in weights]

    @classmethod
    def middle(cls, part, act, gain, w0, w1, depth):
        middle = act.astype(F32) + cls.narrow(part)
        wide = cls.wide(normalize(middle, gain).astype(BF16))
        return middle, wide, cls.full(w0), cls.full(w1)

    @classmethod
    def back(cls, part, middle, gain, cot, g0, g1, depth):
        _, back = jax.vjp(normalize, middle, gain)
        change, gain_grad = back(cls.narrow(part))
        grad = cot + change
        return grad, cls.wide(grad.astype(BF16)), gain_grad[None], cls.own(g0), cls.own(g1)

    @classmethod
    def last(cls, part, feed, act, gain, middle, grad_middle, mlp_part, small, grads, depth):
        _, back = jax.vjp(normalize, act.astype(F32), gain)
        change, gain_grad = back(cls.narrow(part))
        output = (middle + cls.narrow(feed)).astype(BF16)
        gains = lax.psum(jnp.concatenate([gain_grad[None], mlp_part]), ("dp", "tensor"))
        small = lax.psum(small, "dp")
        return output, grad_middle + change, gains, small, [cls.own(g) for g in grads]


def dot(spec, left, right):
    return jnp.einsum(spec, left, right, preferred_element_type=F32)


def shards(
    activations,
    norm_gain,
    gelu_proj,
    input_proj,
    conv_weight,
    gate_input,
    gate_decay,
    decay_rate,
    out_proj,
    mlp_gain,
    feed_gate,
    feed_up,
    feed_down,
    cotangent,
    lengths,
    batch_of,
):
    depth = lax.axis_size("tensor")
    dp_count = lax.axis_size("dp")
    moves = Fast if dp_count == 8 and depth == 4 else Plain
    tensor_index = lax.axis_index("tensor")
    data_index = lax.axis_index("dp")
    seq_count, row_count, model_width = activations.shape
    full_length = row_count * depth
    members = (batch_of[:, None] == jnp.arange(MICRO)[None, :]).astype(F32)
    counts = jnp.sum(members * lengths[:, None].astype(F32), axis=0)
    total_seqs = lengths.shape[0]
    per_batch = float(total_seqs * full_length) / (MICRO * counts)
    weight_all = jnp.sum(members * per_batch[None, :], axis=1)
    my_weight = lax.dynamic_slice_in_dim(weight_all, data_index * seq_count, seq_count)
    my_length = lax.dynamic_slice_in_dim(lengths, data_index * seq_count, seq_count)
    places = tensor_index * row_count + jnp.arange(row_count)
    valid_mask = (places[None, :] < my_length[:, None]).astype(F32)
    scaled_cot = cotangent.astype(F32) * (valid_mask * my_weight[:, None])[:, :, None]
    normed = normalize(activations.astype(F32), norm_gain).astype(BF16)

    normed_all, cot_all, weights = moves.first(
        normed,
        scaled_cot.astype(BF16),
        (gelu_proj, input_proj, gate_input, gate_decay, out_proj.T, feed_up),
        depth,
    )
    gelu_w, input_w, gate_in_w, gate_dec_w, out_w, up_w = (
        w.reshape(-1, w.shape[-1]) for w in weights
    )
    channels = gelu_w.shape[1]
    block_size = gate_in_w.shape[0]
    half_block = block_size // 2
    window_width = channels + half_block
    window_count = window_width // block_size
    parity = tensor_index % 2

    gelu_pre = dot("kqg,ga->kqa", normed_all, gelu_w)
    input_pre = dot("kqg,ga->kqa", normed_all, input_w)
    gelu_out, gelu_back = jax.vjp(jax.nn.gelu, gelu_pre)
    conv_out, conv_back = jax.vjp(causal_conv, input_pre, conv_weight)
    conv_bf = conv_out.astype(BF16)
    rim_send = lax.dynamic_slice_in_dim(
        conv_bf, (1 - parity) * (channels - half_block), half_block, 2
    )
    rim_recv = swapped(rim_send, "tensor")
    window = jnp.zeros((seq_count, full_length, window_width), BF16)
    window = lax.dynamic_update_slice_in_dim(window, conv_bf, parity * half_block, 2)
    window = lax.dynamic_update_slice_in_dim(window, rim_recv, (1 - parity) * channels, 2)
    tile_view = window.reshape(seq_count, full_length, window_count, block_size)
    gate_pair = jnp.stack([gate_in_w, gate_dec_w])
    placed = lax.dynamic_update_slice_in_dim(
        jnp.zeros((2, block_size, window_width), BF16), gate_pair, parity * half_block, 2
    )
    placed = placed.reshape(2, block_size, window_count, block_size)
    gate_wide = dot("slbk,gkbc->gslbc", tile_view, placed)
    gate_wide = gate_wide.reshape(2, seq_count, full_length, window_width)
    gate_own = lax.dynamic_slice_in_dim(gate_wide, parity * half_block, channels, 3)
    (log_decay, drive_in), gate_back = jax.vjp(
        decay_inputs, gate_own[0], gate_own[1], conv_bf.astype(F32), decay_rate
    )
    step_decay = jnp.exp(log_decay)
    states = recurrence(step_decay, drive_in)
    mixed = (gelu_out * states).astype(BF16)
    branch_part = dot("xgq,pq->xgp", mixed, out_w).astype(BF16)

    middle, normed_two_all, gate_w, down_w = moves.middle(
        branch_part, activations, mlp_gain, feed_gate, feed_down.T, depth
    )
    gate_w = gate_w.reshape(-1, gate_w.shape[-1])
    down_w = down_w.reshape(-1, down_w.shape[-1])
    gate_pre = dot("nwo,ob->nwb", normed_two_all, gate_w)
    lift_pre = dot("nwo,ob->nwb", normed_two_all, up_w)
    gate_act, activ_back = jax.vjp(jax.nn.gelu, gate_pre)
    hidden = (gate_act * lift_pre).astype(BF16)
    grad_hidden = dot("gre,eu->gru", cot_all, down_w)
    gate_grad = activ_back(grad_hidden * lift_pre)[0].astype(BF16)
    lift_grad = (grad_hidden * gate_act).astype(BF16)
    back_two = dot("mqa,ya->mqy", gate_grad, gate_w) + dot("mqa,ya->mqy", lift_grad, up_w)

    def weight_grad(left, right):
        total = dot("pkr,pku->ru", left, right).astype(BF16)
        return total.reshape(dp_count, -1, total.shape[-1])

    grad_down_part = weight_grad(cot_all, hidden)
    grad_gate_part = weight_grad(normed_two_all, gate_grad)
    grad_lift_part = weight_grad(normed_two_all, lift_grad)
    feed_part = dot("xav,tv->xat", hidden, down_w).astype(BF16)

    grad_middle, branch_grad_all, mlp_part, grad_down, grad_gate = moves.back(
        back_two.astype(BF16), middle, mlp_gain, scaled_cot, grad_down_part, grad_gate_part, depth
    )
    grad_mixed = dot("xtz,zm->xtm", branch_grad_all, out_w)
    grad_out_part = weight_grad(branch_grad_all, mixed)
    grad_states = grad_mixed * gelu_out
    gelu_pre_grad = gelu_back(grad_mixed * states)[0].astype(BF16)
    later = jnp.concatenate([step_decay[:, 1:], jnp.zeros_like(step_decay[:, :1])], axis=1)
    grad_drive = recurrence(later, grad_states, backward=True)
    earlier = jnp.concatenate([jnp.zeros_like(states[:, :1]), states[:, :-1]], axis=1)
    grad_log = grad_drive * step_decay * earlier
    grad_in_pre, grad_dec_pre, grad_conv_val, grad_rate = gate_back((grad_log, grad_drive))
    grad_pair = jnp.stack([grad_in_pre, grad_dec_pre]).astype(BF16)
    grad_wide = lax.dynamic_update_slice_in_dim(
        jnp.zeros((2, seq_count, full_length, window_width), BF16),
        grad_pair,
        parity * half_block,
        3,
    )
    grad_wide = grad_wide.reshape(2, seq_count, full_length, window_count, block_size)
    grad_window = dot("gslbc,gkbc->slbk", grad_wide, placed)
    grad_window = grad_window.reshape(seq_count, full_length, window_width)
    grad_placed = dot("slbk,gslbc->gkbc", tile_view, grad_wide)
    grad_placed = grad_placed.reshape(2, block_size, window_width)
    grad_gates = lax.dynamic_slice_in_dim(grad_placed, parity * half_block, channels, 2)
    rim_grad = lax.dynamic_slice_in_dim(grad_window, (1 - parity) * channels, half_block, 2)
    rim_return = swapped(rim_grad.astype(BF16), "tensor").astype(F32)
    grad_conv = grad_conv_val + lax.dynamic_slice_in_dim(
        grad_window, parity * half_block, channels, 2
    )
    rim_start = (1 - parity) * (channels - half_block)
    rim_sum = lax.dynamic_slice_in_dim(grad_conv, rim_start, half_block, 2) + rim_return
    grad_conv = lax.dynamic_update_slice_in_dim(grad_conv, rim_sum, rim_start, 2)
    input_pre_grad, grad_taps = conv_back(grad_conv)
    input_pre_grad = input_pre_grad.astype(BF16)
    grad_gelu_part = weight_grad(normed_all, gelu_pre_grad)
    grad_input_part = weight_grad(normed_all, input_pre_grad)
    back_one = dot("mzf,af->mza", gelu_pre_grad, gelu_w) + dot(
        "mzf,af->mza", input_pre_grad, input_w
    )
    gate_parts = grad_gates.astype(BF16).reshape(2, dp_count, -1, channels)
    small = jnp.concatenate([grad_rate[None], grad_taps, jnp.zeros((3, channels), F32)])

    output, input_grad, gains, small, grads = moves.last(
        back_one.astype(BF16),
        feed_part,
        activations,
        norm_gain,
        middle,
        grad_middle,
        mlp_part,
        small,
        (
            grad_gelu_part,
            grad_input_part,
            grad_out_part,
            gate_parts[0],
            gate_parts[1],
            grad_lift_part,
        ),
        depth,
    )
    return (
        output,
        input_grad,
        gains[0],
        grads[0],
        grads[1],
        small[1:5],
        grads[3],
        grads[4],
        small[0],
        grads[2].T,
        gains[1],
        grad_gate,
        grads[5],
        grad_down.T,
    )


def solution(mesh):
    placed = (
        P("dp", "tensor", None),
        P(),
        P("dp", "tensor"),
        P("dp", "tensor"),
        P(None, "tensor"),
        P("dp", "tensor"),
        P("dp", "tensor"),
        P("tensor"),
        P("tensor", "dp"),
        P(),
        P("dp", "tensor"),
        P("dp", "tensor"),
        P("tensor", "dp"),
        P("dp", "tensor", None),
        P(),
        P(),
    )
    return jax.shard_map(
        shards,
        mesh=mesh,
        in_specs=placed,
        out_specs=(
            P("dp", "tensor", None),
            P("dp", "tensor", None),
            P(),
            P("dp", "tensor"),
            P("dp", "tensor"),
            P(None, "tensor"),
            P("dp", "tensor"),
            P("dp", "tensor"),
            P("tensor"),
            P("tensor", "dp"),
            P(),
            P("dp", "tensor"),
            P("dp", "tensor"),
            P("tensor", "dp"),
        ),
        check_vma=False,
    )
```

time: 1500 us -> 745 us (0.50)
  waiting for transfers between devices: 1110 us -> 3.23 us
  Pallas kernels: 0 us -> 537 us
  other arithmetic: 112 us -> 19.8 us
  local copies, waits for them, and re-layouts: 87.9 us -> 44.4 us
  matrix products: 147 us -> 125 us
  blocking collectives: 20.3 us -> 0 us
    reduce_scatter x10 -> x0, waiting for transfers between devices: 554 us -> none  [the longest x1 81 us: reduce_feed(): lax.psum_scatter(grad_gate_w.astype(jnp.bfloat16), 'dp', scatter_dimensio...]
    pallas_call x0 -> x6, Pallas kernels: none -> 537 us  [the longest x4 534 us: call(): pl.pallas_call(kernel, name=name, out_shape=[o[0] for o in outs], in_spec...]
    all_gather x10 -> x0, waiting for transfers between devices: 384 us -> none  [the longest x1 61.2 us: shards(): lax.all_gather(feed_up, 'dp', axis=0, tiled=True)]
    psum x1 -> x0, waiting for transfers between devices: 124 us -> none  [shards(): lax.psum((grad_norm_gain, grad_mlp_gain, rate_full, taps_full), ('dp', 't...]
    reduce_sum x11 -> x1, other arithmetic: 60.7 us -> 0.77 us  [shards(): counts = jnp.sum(members * lengths[:, None].astype(F32), axis=0)]
    unnamed x25 -> x0, waiting for transfers between devices: 42.9 us -> none
    rev x3 -> x0, local copies, waits for them, and re-layouts: 25.8 us -> none  [the longest x1 10.8 us: shards(): jnp.flip(blocked_recurrence(jnp.flip(later_logs, 1), jnp.flip(grad_states...]
    dot_general x21, matrix products: 147 us -> 125 us  [dot(): return jnp.einsum(spec, left, right, preferred_element_type=F32)]
  transfers between devices with their start and end apart: 25 -> 2, of which waited for: 22 -> 2; matrix products, arithmetic and copies ran while one was open for 13% -> 1% of each run, Pallas kernels for 0% -> 0%
where the time goes in v1:
time: 745 us; the launch traced here: 732 us
  Pallas kernels  537 us (72%)
  matrix products  125 us (17%)
  local copies, waits for them, and re-layouts  44.4 us (6%)
  other arithmetic  19.8 us (3%)
    pallas_call x4, Pallas kernels, call(): pl.pallas_call(kernel, name=name, out_shape=[o[0] for o in outs], in_spec...  534 us
    dot_general x21, matrix products, dot(): return jnp.einsum(spec, left, right, preferred_element_type=F32)  125 us
    unnamed x126, local copies, waits for them, and re-layouts  28.2 us
  transfers between devices with their start and end apart: 2, of which 2 were waited for; matrix products, arithmetic and copies ran while one was open for 1% of the time, Pallas kernels for 0%

profile of v1, /device:TPU:0, one launch (start us, length us, event | category | flops | bytes accessed | tf_op | source)
XLA Modules:
  0.0 732.5 jit_solution(13471050100599513461)
XLA Ops:
  3.6 1.3 fusion.17
  5.9 3.1 convert_multiply_fusion.4
  9.1 122.5 %gather_first.1 = (bf16[2,256,2560]{2,1,0:T(8,128)(2,1)}, bf16[2,256,2560]{2,1,0:T(8,128)(2,1)}, bf16[8,320,640]{2,1,0:T(8,128)(2,1)}, bf16[8,320,640]{2,1,0:T(8...) custom-call(bf16[2,64,2560]{2,1,0:T(8,128)(2,1)} %get-tuple-element., ...), custom_call_target="tpu_custom_call" | custom-call | tf_op jit(solution)/shard_map/gather_first/pallas_call | solution.py:405
  131.6 4.9 fusion.50
  138.3 1.6 collective-permute-start
  144.9 1.5 copy.114
  147.5 3.3 convert_multiply_fusion.1
  150.7 1.3 recurrence.2
  152.7 3.3 multiply_convert_fusion.2
  156.0 3.7 convolution_convert_fusion.1.part
  159.7 124.9 %middle_phase.1 = (f32[2,64,2560]{2,1,0:T(8,128)}, bf16[2,256,2560]{2,1,0:T(8,128)(2,1)}, bf16[8,320,1920]{2,1,0:T(8,128)(2,1)}, bf16[8,320,1920]{2,1,0:T(8,128)(2,1)}) custom-call(bf16[2,256,2560]{2,1,0:T(8,128)(2,1)} %convolution_convert_fusion.1.part, bf16[2,64,2560]{2,1,0:T(8,128)(2,1)} %act.3, f32[1,2560]{1,0:T(1,128)} %reshape.201.gain, ...), custom_call_target="tpu_custom_call" | custom-call | tf_op jit(solution)/shard_map/middle_phase/pallas_call | solution.py:405
  284.6 11.5 %fusion.52 = f32[2,256,1920]{2,1,0:T(8,128)} fusion(bf16[2,256,2560]{2,1,0:T(8,128)(2,1)} %get-tuple-element.49, bf16[2560,1920,1]{1,0,2:T(8,128)(2,1)} %bitcast.199), kind=kOutput, calls=%fused_computation.120 | convolution fusion | flops 5033164800 | bytes 16384000 | tf_op jit(solution)/shard_map/nwo,ob->nwb/dot_general | solution.py:897
  296.1 7.6 %fusion.51 = f32[2,256,1920]{2,1,0:T(8,128)} fusion(bf16[2,256,2560]{2,1,0:T(8,128)(2,1)S(1)} %copy-done.38, bf16[2560,1920,1]{1,0,2:T(8,128)(2,1)S(1)} %bitcast.198), kind=kOutput, calls=%fused_computation.119 | convolution fusion | flops 5033164800 | bytes 16384000 | tf_op jit(solution)/shard_map/gre,eu->gru/dot_general | solution.py:897
  303.7 12.5 %multiply_convert_fusion = (bf16[2,256,1920]{2,1,0:T(8,128)(2,1)}, bf16[2,256,1920]{2,1,0:T(8,128)(2,1)S(1)}, bf16[2,256,1920]{2,1,0:T(8,128)(2,1)S(1)}) fusion(f32[2,256,1920]{2,1,0:T(8,128)} %fusion.52, f32[2,256,1920]{2,1,0:T(8,128)} %fusion.51, bf16[2,256,2560]{2,1,0:T(8,128)(2,1)} %get-tuple-element.49, bf16[2560,1920,1]{1,0,2:T(8,128)(2,1)S(1)} %bitcast.195), kind=kOutput, calls=%fused_computation.19 | convolution fusion | flops 5058723840 | bytes 26214400 | tf_op jit(solution)/shard_map/nwo,ob->nwb/dot_general | solution.py:897
  316.1 9.0 %fusion.53 = f32[2,256,2560]{2,1,0:T(8,128)S(1)} fusion(bf16[2,256,1920]{2,1,0:T(8,128)(2,1)S(1)} %get-tuple-element.81, bf16[2560,1920,1]{1,0,2:T(8,128)(2,1)} %bitcast.200), kind=kOutput, calls=%fused_computation.121 | convolution fusion | flops 5033164800 | bytes 17039360 | tf_op jit(solution)/shard_map/mqa,ya->mqy/dot_general | solution.py:897
  325.1 8.5 %bitcast_convert_fusion.1 = bf16[2560,1920]{1,0:T(8,128)(2,1)} fusion(bf16[2,256,2560]{2,1,0:T(8,128)(2,1)S(1)} %copy-done.40, bf16[2,256,1920]{2,1,0:T(8,128)(2,1)S(1)} %get-tuple-element.81), kind=kOutput, calls=%fused_computation.1 | convolution fusion | flops 5038080000 | bytes 14417920 | tf_op jit(solution)/shard_map/pkr,pku->ru/dot_general | solution.py:897
  333.7 1.6 copy-done.39
  335.4 8.1 %bitcast_convert_fusion.2 = bf16[2560,1920]{1,0:T(8,128)(2,1)} fusion(bf16[2,256,2560]{2,1,0:T(8,128)(2,1)S(1)} %copy-done.39, bf16[2,256,1920]{2,1,0:T(8,128)(2,1)S(1)} %copy-done.49), kind=kOutput, calls=%fused_computation.2 | convolution fusion | flops 5038080000 | bytes 14417920 | tf_op jit(solution)/shard_map/pkr,pku->ru/dot_general | solution.py:897
  344.7 7.0 add_convert_fusion.1.part
  351.6 123.6 %back_phase.1 = (f32[2,64,2560]{2,1,0:T(8,128)}, bf16[2,256,2560]{2,1,0:T(8,128)(2,1)}, f32[1,2560]{1,0:T(1,128)}, f32[320,1920]{1,0:T(8,128)}, f32[320,1920]{1,0:T(8,128)}) custom-call(bf16[2,256,2560]{2,1,0:T(8,128)(2,1)} %add_convert_fusion.1.part, f32[2,64,2560]{2,1,0:T(8,128)} %get-tuple-element.52.middle, f32[1,2560]{1,0:T(1,128)} %reshape.201.gain, ...), custom_call_target="tpu_custom_call" | custom-call | tf_op jit(solution)/shard_map/back_phase/pallas_call | solution.py:405
  475.3 6.5 fusion.46
  481.7 1.3 recurrence.3
  483.2 2.2 fusion.37
  485.8 1.2 pad_maximum_fusion
  487.0 1.6 copy.75
  490.7 1.4 copy-done.50
  492.1 11.2 %convolution_convert_fusion.feed = bf16[2,256,2560]{2,1,0:T(8,128)(2,1)} fusion(bf16[2,256,1920]{2,1,0:T(8,128)(2,1)S(1)} %copy-done.50, bf16[2560,1920,1]{1,0,2:T(8,128)(2,1)} %bitcast.197), kind=kOutput, calls=%fused_computation.10 | convolution fusion | flops 5034475520 | bytes 14417920 | tf_op jit(solution)/shard_map/xav,tv->xat/dot_general | solution.py:897
  503.3 4.6 fusion.54
  508.0 4.0 bitcast_convert_fusion.5
  511.9 4.0 bitcast_convert_fusion.3
  515.9 1.5 fusion.11
  518.5 8.4 %bitcast_convert_fusion = bf16[2560,1920]{1,0:T(8,128)(2,1)} fusion(bf16[2,256,2560]{2,1,0:T(8,128)(2,1)S(1)} %copy-done.41, bf16[2,256,1920]{2,1,0:T(8,128)(2,1)S(1)} %copy-done.48), kind=kOutput, calls=%fused_computation | convolution fusion | flops 5038080000 | bytes 14417920 | tf_op jit(solution)/shard_map/pkr,pku->ru/dot_general | solution.py:897
  526.9 1.5 copy.115
  528.3 3.4 multiply_add_fusion
  532.0 1.2 copy.86
  535.1 2.9 collective-permute-done.1
  538.5 1.2 copy-done.2
  541.4 3.9 bitcast_convert_fusion.4
  545.4 3.8 add_convert_fusion.part
  549.9 163.0 %last_phase.1 = (bf16[2,64,2560]{2,1,0:T(8,128)(2,1)}, f32[2,64,2560]{2,1,0:T(8,128)}, f32[8,2560]{1,0:T(8,128)}, f32[8,640]{1,0:T(8,128)}, f32[320,640]{1,0:T(8...) custom-call(bf16[2,256,2560]{2,1,0:T(8,128)(2,1)} %add_convert_fusio, ...), custom_call_target="tpu_custom_call" | custom-call | tf_op jit(solution)/shard_map/last_phase/pallas_call | solution.py:405
  713.0 1.4 slice.67
  714.4 1.3 slice_reduce_fusion.2
  715.7 1.6 slice_reduce_fusion
  717.4 2.0 copy.148
  725.4 1.4 copy.155
  726.9 1.1 copy-done.14
  728.0 1.4 copy.156
  730.6 1.4 copy.157
  (174 shorter events, 29.6 us)
Async XLA Ops:
  5.8 130.7 %copy-start.24 = (f32[640]{0:T(1024)}, f32[640]{0:T(1024)S(1)}, u32[]{:S(2)}) copy-start(f32[640]{0:T(1024)S(1)} %get-tuple-element.75) | copy-start | bytes 7684
  137.6 2.7 copy-start.5
  137.6 2.5 copy-start.26
  138.3 5.2 collective-permute-start
  140.2 1.5 copy-start.19
  140.2 1.6 copy-start.28
  147.5 337.9 %copy-start.3 = (f32[1,2,256,640]{3,2,1,0:T(8,128)}, f32[1,2,256,640]{3,2,1,0:T(8,128)S(1)}, u32[]{:S(2)}) copy-start(f32[1,2,256,640]{3,2,1,0:T(8,128)S(1)} %copy.113) | copy-start | bytes 3932164
  147.5 4.6 copy-start.35
  150.7 1.9 copy-start.32
  152.7 3.3 copy-start.34
  156.0 3.7 copy-start.45
  284.5 11.5 %copy-start.30 = (bf16[8,320,1920]{2,1,0:T(8,128)(2,1)S(1)}, bf16[8,320,1920]{2,1,0:T(8,128)(2,1)}, u32[]{:S(2)}) copy-start(bf16[8,320,1920]{2,1,0:T(8,128)(2,1)} %get-tuple-element.48) | copy-start | bytes 29491204
  284.6 11.5 %copy-start.38 = (bf16[2,256,2560]{2,1,0:T(8,128)(2,1)S(1)}, bf16[2,256,2560]{2,1,0:T(8,128)(2,1)}, u32[]{:S(2)}) copy-start(bf16[2,256,2560]{2,1,0:T(8,128)(2,1)} %get-tuple-element.41) | copy-start | bytes 7864324
  284.6 19.1 %slice-start = ((s8[9830400]{0:T(1024)(128)(4,1)}), s8[4194304]{0:T(1024)(128)(4,1)S(1)}, s32[]{:S(2)}) async-start(s8[9830400]{0:T(1024)(128)(4,1)} %bitcast.193), calls=%async_computation | async-start | bytes 8388608
  284.6 19.1 %slice-start.1 = ((s8[9830400]{0:T(1024)(128)(4,1)}), s8[4194304]{0:T(1024)(128)(4,1)S(1)}, s32[]{:S(2)}) async-start(s8[9830400]{0:T(1024)(128)(4,1)} %bitcast.193), calls=%async_computation.1 | async-start | bytes 8388608
  296.1 7.6 %slice-start.2 = ((s8[9830400]{0:T(1024)(128)(4,1)}), s8[1441792]{0:T(1024)(128)(4,1)S(1)}, s32[]{:S(2)}) async-start(s8[9830400]{0:T(1024)(128)(4,1)} %bitcast.193), calls=%async_computation.2 | async-start | bytes 2883584
  316.1 28.6 %copy-start.47 = (bf16[2,256,1920]{2,1,0:T(8,128)(2,1)}, bf16[2,256,1920]{2,1,0:T(8,128)(2,1)S(1)}, u32[]{:S(2)}) copy-start(bf16[2,256,1920]{2,1,0:T(8,128)(2,1)S(1)} %get-tuple-element.82) | copy-start | bytes 5898244
  316.1 9.0 %copy-start.40 = (bf16[2,256,2560]{2,1,0:T(8,128)(2,1)S(1)}, bf16[2,256,2560]{2,1,0:T(8,128)(2,1)}, u32[]{:S(2)}) copy-start(bf16[2,256,2560]{2,1,0:T(8,128)(2,1)} %get-tuple-element.49) | copy-start | bytes 7864324
  325.1 8.6 %copy-start.49 = (bf16[2,256,1920]{2,1,0:T(8,128)(2,1)S(1)}, bf16[2,256,1920]{2,1,0:T(8,128)(2,1)}, u32[]{:S(2)}) copy-start(bf16[2,256,1920]{2,1,0:T(8,128)(2,1)} %get-tuple-element.80) | copy-start | bytes 5898244
  333.6 1.7 copy-start.39
  351.6 123.6 %copy-start.44 = (f32[2,256,640]{2,1,0:T(8,128)S(1)}, f32[2,256,640]{2,1,0:T(8,128)}, u32[]{:S(2)}) copy-start(f32[2,256,640]{2,1,0:T(8,128)} %get-tuple-element.96) | copy-start | bytes 3932164
  475.2 6.5 copy-start
  481.7 1.5 copy-start.7
  483.2 2.2 copy-start.27
  490.6 1.5 copy-start.50
  492.1 11.2 %copy-start.33 = (bf16[8,320,640]{2,1,0:T(8,128)(2,1)S(1)}, bf16[8,320,640]{2,1,0:T(8,128)(2,1)}, u32[]{:S(2)}) copy-start(bf16[8,320,640]{2,1,0:T(8,128)(2,1)} %get-tuple-element.43) | copy-start | bytes 9830404
  492.1 11.2 %copy-start.43 = (bf16[2,256,640]{2,1,0:T(8,128)(2,1)S(1)}, bf16[2,256,640]{2,1,0:T(8,128)(2,1)}, u32[]{:S(2)}) copy-start(bf16[2,256,640]{2,1,0:T(8,128)(2,1)} %get-tuple-element.87) | copy-start | bytes 1966084
  503.3 4.6 copy-start.36
  508.0 4.0 copy-start.42
  508.0 4.0 copy-start.46
  511.9 4.0 copy-start.11
  515.9 2.0 copy-start.41
  515.9 2.6 copy-start.48
  531.9 6.1 collective-permute-start.1
  533.3 4.8 copy-start.25
  539.7 1.7 copy-start.37
  539.7 5.7 slice-start.3
  541.4 4.0 copy-start.31
  541.4 4.0 slice-start.4
  545.4 3.9 copy-start.29
  713.0 6.4 copy-start.15
  719.3 1.6 copy-start.18
  720.9 2.3 copy-start.22
  720.9 3.0 copy-start.21
  720.9 3.6 copy-start.16
  722.4 3.1 copy-start.13
  725.4 2.6 copy-start.14
  728.0 2.6 copy-start.12
  (10 other events, 11.3 us)

commit v2 on v1

--- a/solution.py
+++ b/solution.py
@@ -89,14 +89,12 @@
         self.own = pltpu.make_async_copy(shard, out.at[d], local)
 
     def start(self):
-        for i in (0, 1, 2, 3):
+        for i in (0, 1, 2, 3, 6, 7):
             self.copies[i].start()
         self.own.start()
 
     def relay(self):
         c = self.copies
-        for i in (6, 7):
-            c[i].start()
         c[0].wait_recv()
         c[4].start()
         c[1].wait_recv()
@@ -328,42 +326,43 @@
             device_id_type=MESH,
         )
 
-    def move(self, way, j):
+    def block(self, j, s):
+        return self.part.at[s, pl.ds(pl.multiple_of(j * self.rows, self.rows), self.rows)]
+
+    def start(self):
         t, depth = self.t, self.depth
-        rows = pl.ds(j * self.rows, self.rows)
-        if way == 0:
-            source, hears, sends, to = t == 0, (t > 0) & (j >= t), j > t, t + 1
-        else:
-            source, hears, sends, to = t == depth - 1, (t < depth - 1) & (j <= t), j < t, t - 1
+
+        @pl.when(t == 0)
+        def _():
+            for j in range(depth - 1, 0, -1):
+                for s in range(self.seqs):
+                    self.copy(0, j, s, self.block(j, s), t + 1).start()
+
+        @pl.when(t == depth - 1)
+        def _():
+            for j in range(depth - 1):
+                for s in range(self.seqs):
+                    self.copy(1, j, s, self.block(j, s), t - 1).start()
+
+    def pass_on(self, way, j, to):
         for s in range(self.seqs):
             mine = self.got.at[way, j, s]
-
-            @pl.when(hears)
-            def _():
-                self.copy(way, j, s, mine, t).wait_recv()
-
-            @pl.when(sends & source)
-            def _():
-                self.copy(way, j, s, self.part.at[s, rows], to).start()
-
-            @pl.when(sends & jnp.logical_not(source))
-            def _():
-                add_rows(mine, self.part.at[s, rows], self.rows)
-                self.copy(way, j, s, mine, to).start()
+            self.copy(way, j, s, mine, self.t).wait_recv()
+            add_rows(mine, self.block(j, s), self.rows)
+            self.copy(way, j, s, mine, to).start()
 
     def step(self, k):
-        depth, t = self.depth, self.t
-        right, left = depth - 1 - k, k
-
-        @pl.when(t < depth // 2)
+        t, depth = self.t, self.depth
+        right = depth - 1 - k + t
+        left = k - (depth - 1 - t)
+
+        @pl.when((t > 0) & (t < right) & (right < depth))
         def _():
-            self.move(0, right)
-
-        self.move(1, left)
-
-        @pl.when(t >= depth // 2)
+            self.pass_on(0, right, t + 1)
+
+        @pl.when((left >= 0) & (left < t) & (t < depth - 1))
         def _():
-            self.move(0, right)
+            self.pass_on(1, left, t - 1)
 
     def total(self, out):
         t, depth = self.t, self.depth
@@ -372,10 +371,14 @@
 
         @pl.when(t > 0)
         def _():
+            for s in range(self.seqs):
+                self.copy(0, t, s, self.got.at[0, t, s], t).wait_recv()
             out[...] += self.got[0, t].astype(F32)
 
         @pl.when(t < depth - 1)
         def _():
+            for s in range(self.seqs):
+                self.copy(1, t, s, self.got.at[1, t, s], t).wait_recv()
             out[...] += self.got[1, t].astype(F32)
 
     def end(self):
@@ -436,29 +439,31 @@
         WeightGather(shards[i], full[i], local.at[i], send.at[i], recv.at[i], d, t)
         for i in range(n_weights)
     ]
+    one, two, three = gathers[:-2], gathers[-2], gathers[-1]
     lines[0].step(0)
-    for g in gathers:
+    for g in one:
         g.start()
-    early, late = gathers[:-1], gathers[-1:]
+    lines[1].step(0)
+    for g in one:
+        g.relay()
+    two.start()
     lines[0].step(1)
-    for g in early:
-        g.relay()
-    lines[0].step(2)
-    lines[1].step(0)
-    for g in early:
+    for g in one:
         g.relay_two()
-    lines[0].step(3)
-    for g in early:
+    for g in one:
         g.relay_last()
     lines[1].step(1)
-    for g in late:
-        g.relay()
+    two.relay()
+    three.start()
+    two.relay_two()
+    two.relay_last()
+    lines[0].step(2)
+    three.relay()
     lines[1].step(2)
-    for g in late:
-        g.relay_two()
+    three.relay_two()
+    lines[0].step(3)
+    three.relay_last()
     lines[1].step(3)
-    for g in late:
-        g.relay_last()
     for g in gathers:
         g.end()
     for line in lines:
@@ -475,7 +480,7 @@
         functools.partial(gather_kernel, depth, n),
         "gather_first",
         0,
-        [ANY] * (2 + n),
+        [VMEM] * (2 + n),
         outs,
         scratch,
         (normed, cot) + tuple(weights),
@@ -495,14 +500,14 @@
         for i, (w, f) in enumerate(((w0, f0), (w1, f1)))
     ]
     scatter = LineScatter(part, got, ssem, rsem, d, t, depth)
-    scatter.step(0)
-    for g in gathers:
-        g.start()
+    scatter.start()
+    gathers[0].start()
+    gathers[0].relay()
+    gathers[1].start()
     scatter.step(1)
-    gathers[0].relay()
+    gathers[0].relay_two()
     scatter.step(2)
-    gathers[0].relay_two()
-    scatter.step(3)
+    gathers[0].relay_last()
     scatter.total(middle)
     seqs, rows, width = act.shape
     for s in range(seqs):
@@ -512,7 +517,6 @@
         block[s] = (value * inverse * gain[...]).astype(BF16)
     line = LineGather(block, wide, *lsem, d, t, depth)
     line.step(0)
-    gathers[0].relay_last()
     gathers[1].relay()
     line.step(1)
     gathers[1].relay_two()
@@ -543,7 +547,7 @@
         functools.partial(middle_kernel, depth),
         "middle_phase",
         1,
-        [VMEM, VMEM, VMEM, ANY, ANY],
+        [VMEM] * 5,
         outs,
         scratch,
         (part, act, gain.reshape(1, width), w0, w1),
@@ -566,17 +570,16 @@
     greet(d, t, depth)
     scatters = make_scatters((g0, g1), (o0, o1), scratch[7:], d, t)
     scatter = LineScatter(part, got, ssem, rsem, d, t, depth)
-    scatter.step(0)
+    scatter.start()
     for g in scatters:
         g.start()
     scatters[0].first()
     scatters[0].second()
     scatter.step(1)
-    scatters[1].first()
     scatters[0].third()
     scatter.step(2)
+    scatters[1].first()
     scatters[1].second()
-    scatter.step(3)
     scatter.total(grad)
     seqs, rows, width = middle.shape
     for s in range(seqs):
@@ -590,9 +593,9 @@
             gain_grad[...] += gain_part
     line = LineGather(block, wide, *lsem, d, t, depth)
     line.step(0)
+    scatters[0].end()
+    line.step(1)
     scatters[1].third()
-    line.step(1)
-    scatters[0].end()
     line.step(2)
     line.step(3)
     scatters[1].end()
@@ -659,37 +662,44 @@
     small_copies = dp_copies(small, small_all, qsend, qrecv)
     for c in small_copies:
         c.start()
-    first.step(0)
-    for g in scatters:
+    big, rest = scatters[-1], scatters[:-1]
+    first.start()
+    big.start()
+    second.start()
+    for g in rest:
         g.start()
-    for g in scatters[:-1]:
+    big.first()
+    big.second()
+    first.step(1)
+    big.third()
+    first.step(2)
+    for g in rest:
         g.first()
+    for g in rest:
         g.second()
-    first.step(1)
-    for g in scatters[:-1]:
-        g.third()
-    scatters[-1].first()
-    first.step(2)
-    second.step(0)
-    scatters[-1].second()
-    first.step(3)
     first.total(input_grad)
     seqs = act.shape[0]
-    pack[1:2, :] = mlp_part[...]
+    quarter = pack.shape[1]
+    for i in range(4):
+        pack[4 + i : 5 + i, :] = mlp_part[:, i * quarter : (i + 1) * quarter]
     for s in range(seqs):
         change, gain_part = norm_back(act[s].astype(F32), gain[...], input_grad[s])
         input_grad[s] = change + grad_middle[s]
-        if s == 0:
-            pack[0:1, :] = gain_part
-        else:
-            pack[0:1, :] += gain_part
+        for i in range(4):
+            piece = gain_part[:, i * quarter : (i + 1) * quarter]
+            if s == 0:
+                pack[i : i + 1, :] = piece
+            else:
+                pack[i : i + 1, :] += piece
     pack_copies = dp_copies(pack, packs, psend, precv)
     for c in pack_copies:
         c.start()
-    scatters[-1].third()
-    second.step(1)
+    big.end()
     packs[d] = pack[...]
     small_all[d] = small[...]
+    second.step(1)
+    for g in rest:
+        g.third()
     for c in pack_copies:
         c.wait_recv()
     sum_ = packs[0]
@@ -707,13 +717,12 @@
         )
         for step in range(1, depth)
     ]
+    second.step(2)
     for c in z_copies:
         c.start()
     line_packs[t] = sum_
-    second.step(2)
-    for g in scatters[:-1]:
+    for g in rest:
         g.end()
-    second.step(3)
     second.total(total)
     output[...] = (total[...] + middle[...]).astype(BF16)
     for c in small_copies:
@@ -728,7 +737,6 @@
     for i in range(1, depth):
         sum_ = sum_ + line_packs[i]
     gains[...] = sum_
-    scatters[-1].end()
     for c in small_copies + pack_copies + z_copies:
         c.wait_send()
     first.end()
@@ -742,17 +750,17 @@
     outs = [
         shaped(act.shape, BF16, VMEM),
         shaped(act.shape, F32, VMEM),
-        shaped((8, width), F32, VMEM),
+        shaped((8, width // 4), F32, VMEM),
         shaped(small.shape, F32, VMEM),
     ] + [shaped(s, F32, VMEM) for s in shapes]
     scratch = (
         line_scatter_scratch(seqs, rows, width, depth) * 2
         + [
-            pltpu.VMEM((8, width), F32),
-            pltpu.VMEM((8, 8, width), F32),
+            pltpu.VMEM((8, width // 4), F32),
+            pltpu.VMEM((8, 8, width // 4), F32),
             pltpu.VMEM((8,) + small.shape, F32),
-            pltpu.VMEM((8, width), F32),
-            pltpu.VMEM((depth, 8, width), F32),
+            pltpu.VMEM((8, width // 4), F32),
+            pltpu.VMEM((depth, 8, width // 4), F32),
         ]
         + [DMA((7,))] * 4
         + [DMA((depth - 1,))] * 2
@@ -769,7 +777,7 @@
         (part, feed, act, gain.reshape(1, width), middle, grad_middle, mlp_part, small)
         + tuple(grads),
     )
-    return res[0], res[1], res[2], res[3], res[4:]
+    return res[0], res[1], res[2].reshape(2, width), res[3], res[4:]
 
 
 def scan_kernel(backward, rate_ref, drive_ref, out_ref):

time: 745 us -> 596 us (0.80)
  Pallas kernels: 537 us -> 390 us
    pallas_call x4, Pallas kernels: 534 us -> 388 us  [call(): pl.pallas_call(kernel, name=name, out_shape=[o[0] for o in outs], in_spec...]
where the time goes in v2:
time: 596 us; the launch traced here: 586 us
  Pallas kernels  390 us (65%)
  matrix products  125 us (21%)
  local copies, waits for them, and re-layouts  44.8 us (8%)
  other arithmetic  19.8 us (3%)
    pallas_call x4, Pallas kernels, call(): pl.pallas_call(kernel, name=name, out_shape=[o[0] for o in outs], in_spec...  388 us
    dot_general x21, matrix products, dot(): return jnp.einsum(spec, left, right, preferred_element_type=F32)  125 us
    unnamed x126, local copies, waits for them, and re-layouts  28.2 us
  transfers between devices with their start and end apart: 2, of which 2 were waited for; matrix products, arithmetic and copies ran while one was open for 1% of the time, Pallas kernels for 0%

profile of v2, /device:TPU:0, one launch (start us, length us, event | category | flops | bytes accessed | tf_op | source)
XLA Modules:
  0.0 586.4 jit_solution(13450904654654847634)
XLA Ops:
  3.6 1.3 fusion.17
  5.9 3.1 convert_multiply_fusion.4
  9.1 93.5 %gather_first.1 = (bf16[2,256,2560]{2,1,0:T(8,128)(2,1)}, bf16[2,256,2560]{2,1,0:T(8,128)(2,1)}, bf16[8,320,640]{2,1,0:T(8,128)(2,1)}, bf16[8,320,640]{2,1,0:T(8...) custom-call(bf16[2,64,2560]{2,1,0:T(8,128)(2,1)} %get-tuple-element., ...), custom_call_target="tpu_custom_call" | custom-call | tf_op jit(solution)/shard_map/gather_first/pallas_call | solution.py:408
  102.6 4.9 fusion.51
  109.2 1.6 collective-permute-start
  116.6 1.5 copy.114
  119.2 3.3 convert_multiply_fusion.1
  122.5 1.3 recurrence.2
  124.4 3.3 multiply_convert_fusion.2
  127.7 3.7 convolution_convert_fusion.1.part
  131.4 94.7 %middle_phase.1 = (f32[2,64,2560]{2,1,0:T(8,128)}, bf16[2,256,2560]{2,1,0:T(8,128)(2,1)}, bf16[8,320,1920]{2,1,0:T(8,128)(2,1)}, bf16[8,320,1920]{2,1,0:T(8,128)(2,1)}) custom-call(bf16[2,256,2560]{2,1,0:T(8,128)(2,1)} %convolution_convert_fusion.1.part, bf16[2,64,2560]{2,1,0:T(8,128)(2,1)} %act.3, f32[1,2560]{1,0:T(1,128)} %reshape.206.gain, ...), custom_call_target="tpu_custom_call" | custom-call | tf_op jit(solution)/shard_map/middle_phase/pallas_call | solution.py:408
  226.1 11.5 %fusion.53 = f32[2,256,1920]{2,1,0:T(8,128)} fusion(bf16[2,256,2560]{2,1,0:T(8,128)(2,1)} %get-tuple-element.49, bf16[2560,1920,1]{1,0,2:T(8,128)(2,1)} %bitcast.199), kind=kOutput, calls=%fused_computation.119 | convolution fusion | flops 5033164800 | bytes 16384000 | tf_op jit(solution)/shard_map/nwo,ob->nwb/dot_general | solution.py:905
  237.6 7.5 %fusion.52 = f32[2,256,1920]{2,1,0:T(8,128)} fusion(bf16[2,256,2560]{2,1,0:T(8,128)(2,1)S(1)} %copy-done.38, bf16[2560,1920,1]{1,0,2:T(8,128)(2,1)S(1)} %bitcast.198), kind=kOutput, calls=%fused_computation.118 | convolution fusion | flops 5033164800 | bytes 16384000 | tf_op jit(solution)/shard_map/gre,eu->gru/dot_general | solution.py:905
  245.1 12.5 %multiply_convert_fusion = (bf16[2,256,1920]{2,1,0:T(8,128)(2,1)}, bf16[2,256,1920]{2,1,0:T(8,128)(2,1)S(1)}, bf16[2,256,1920]{2,1,0:T(8,128)(2,1)S(1)}) fusion(f32[2,256,1920]{2,1,0:T(8,128)} %fusion.53, f32[2,256,1920]{2,1,0:T(8,128)} %fusion.52, bf16[2,256,2560]{2,1,0:T(8,128)(2,1)} %get-tuple-element.49, bf16[2560,1920,1]{1,0,2:T(8,128)(2,1)S(1)} %bitcast.195), kind=kOutput, calls=%fused_computation.19 | convolution fusion | flops 5058723840 | bytes 26214400 | tf_op jit(solution)/shard_map/nwo,ob->nwb/dot_general | solution.py:905
  257.6 9.0 %fusion.54 = f32[2,256,2560]{2,1,0:T(8,128)S(1)} fusion(bf16[2,256,1920]{2,1,0:T(8,128)(2,1)S(1)} %get-tuple-element.79, bf16[2560,1920,1]{1,0,2:T(8,128)(2,1)} %bitcast.200), kind=kOutput, calls=%fused_computation.120 | convolution fusion | flops 5033164800 | bytes 17039360 | tf_op jit(solution)/shard_map/mqa,ya->mqy/dot_general | solution.py:905
  266.6 8.5 %bitcast_convert_fusion.1 = bf16[2560,1920]{1,0:T(8,128)(2,1)} fusion(bf16[2,256,2560]{2,1,0:T(8,128)(2,1)S(1)} %copy-done.40, bf16[2,256,1920]{2,1,0:T(8,128)(2,1)S(1)} %get-tuple-element.79), kind=kOutput, calls=%fused_computation.1 | convolution fusion | flops 5038080000 | bytes 14417920 | tf_op jit(solution)/shard_map/pkr,pku->ru/dot_general | solution.py:905
  275.2 1.6 copy-done.39
  276.9 8.2 %bitcast_convert_fusion.2 = bf16[2560,1920]{1,0:T(8,128)(2,1)} fusion(bf16[2,256,2560]{2,1,0:T(8,128)(2,1)S(1)} %copy-done.39, bf16[2,256,1920]{2,1,0:T(8,128)(2,1)S(1)} %copy-done.49), kind=kOutput, calls=%fused_computation.2 | convolution fusion | flops 5038080000 | bytes 14417920 | tf_op jit(solution)/shard_map/pkr,pku->ru/dot_general | solution.py:905
  285.0 1.1 concatenate.21.rate_ref
  286.2 7.0 %add_convert_fusion.1.part = bf16[2,256,2560]{2,1,0:T(8,128)(2,1)} fusion(f32[2,256,2560]{2,1,0:T(8,128)S(1)} %fusion.54, bf16[2,256,1920]{2,1,0:T(8,128)(2,1)S(1)} %get-tuple-element.80, bf16[2560,1920,1]{1,0,2:T(8,128)(2,1)S(1)} %bitcast.196), kind=kOutput, calls=%fused_computation.9 | convolution fusion | flops 5035786240 | bytes 19660800 | tf_op jit(solution)/shard_map/mqa,ya->mqy/dot_general | solution.py:905
  293.2 96.7 %back_phase.1 = (f32[2,64,2560]{2,1,0:T(8,128)}, bf16[2,256,2560]{2,1,0:T(8,128)(2,1)}, f32[1,2560]{1,0:T(1,128)}, f32[320,1920]{1,0:T(8,128)}, f32[320,1920]{1,0:T(8,128)}) custom-call(bf16[2,256,2560]{2,1,0:T(8,128)(2,1)} %add_convert_fusion.1.part, f32[2,64,2560]{2,1,0:T(8,128)} %get-tuple-element.52.middle, f32[1,2560]{1,0:T(1,128)} %reshape.206.gain, ...), custom_call_target="tpu_custom_call" | custom-call | tf_op jit(solution)/shard_map/back_phase/pallas_call | solution.py:408
  389.9 6.5 %fusion.46 = (f32[2,256,640]{2,1,0:T(8,128)S(1)}, bf16[2,256,640]{2,1,0:T(8,128)(2,1)}) fusion(f32[2,256,640]{2,1,0:T(8,128)S(1)} %copy-done.44, f32[2,256,640]{2,1,0:T(8,128)S(1)} %recurrence.2, bf16[2,256,2560]{2,1,0:T(8,128)(2,1)} %get-tuple-element.53, bf16[2560,640,1]{1,0,2:T(8,128)(2,1)} %bitcast.205), kind=kOutput, calls=%fused_computation.89 | convolution fusion | flops 1685258240 | bytes 10485760 | tf_op jit(solution)/shard_map/xtz,zm->xtm/dot_general | solution.py:905
  396.4 1.3 recurrence.3
  397.9 2.2 fusion.37
  400.5 1.2 pad_maximum_fusion
  401.7 1.6 copy.75
  405.4 1.4 copy-done.50
  406.8 11.2 %convolution_convert_fusion.feed = bf16[2,256,2560]{2,1,0:T(8,128)(2,1)} fusion(bf16[2,256,1920]{2,1,0:T(8,128)(2,1)S(1)} %copy-done.50, bf16[2560,1920,1]{1,0,2:T(8,128)(2,1)} %bitcast.197), kind=kOutput, calls=%fused_computation.10 | convolution fusion | flops 5034475520 | bytes 14417920 | tf_op jit(solution)/shard_map/xav,tv->xat/dot_general | solution.py:905
  418.0 4.6 fusion.55
  422.6 4.0 bitcast_convert_fusion.5
  426.6 4.0 bitcast_convert_fusion.3
  430.6 1.5 fusion.11
  433.2 8.4 %bitcast_convert_fusion = bf16[2560,1920]{1,0:T(8,128)(2,1)} fusion(bf16[2,256,2560]{2,1,0:T(8,128)(2,1)S(1)} %copy-done.41, bf16[2,256,1920]{2,1,0:T(8,128)(2,1)S(1)} %copy-done.48), kind=kOutput, calls=%fused_computation | convolution fusion | flops 5038080000 | bytes 14417920 | tf_op jit(solution)/shard_map/pkr,pku->ru/dot_general | solution.py:905
  441.6 1.5 copy.115
  443.1 3.4 multiply_add_fusion
  446.7 1.2 copy.86
  449.8 1.8 collective-permute-done.1
  452.1 1.2 copy-done.2
  455.0 4.0 bitcast_convert_fusion.4
  459.0 3.8 add_convert_fusion.part
  463.6 102.8 %last_phase.1 = (bf16[2,64,2560]{2,1,0:T(8,128)(2,1)}, f32[2,64,2560]{2,1,0:T(8,128)}, f32[8,640]{1,0:T(8,128)}, f32[8,640]{1,0:T(8,128)}, f32[320,640]{1,0:T(8,...) custom-call(bf16[2,256,2560]{2,1,0:T(8,128)(2,1)} %add_convert_fusio, ...), custom_call_target="tpu_custom_call" | custom-call | tf_op jit(solution)/shard_map/last_phase/pallas_call | solution.py:408
  566.4 1.4 slice.69
  567.9 1.3 slice_reduce_fusion
  571.2 2.0 copy.148
  579.3 1.4 copy.155
  580.8 1.1 copy-done.14
  581.9 1.4 copy.156
  584.5 1.4 copy.157
  (176 shorter events, 31.3 us)
Async XLA Ops:
  5.8 101.6 %copy-start.24 = (f32[640]{0:T(1024)}, f32[640]{0:T(1024)S(1)}, u32[]{:S(2)}) copy-start(f32[640]{0:T(1024)S(1)} %get-tuple-element.73) | copy-start | bytes 7684
  108.5 2.7 copy-start.5
  108.5 2.5 copy-start.26
  109.2 6.0 %collective-permute-start = (bf16[2,256,128]{2,1,0:T(8,128)(2,1)}, bf16[2,256,128]{2,1,0:T(8,128)(2,1)S(1)}, u32[]{:S(2)}, u32[]{:S(2)}) collective-permute-start(bf16[2,256,128]{2,1,0:T(8,128)(2,1)} %constant_dynamic-slice_fusion.4), channel_id=1, source_target_pairs={{0,1},{1,0},{2,3},{3,2},{4,5},{5,4},{6,7},{7,6},{8,9},{9,8},{10,11... | collective-permute-start | bytes 393224 | tf_op jit(solution)/shard_map/ppermute | solution.py:823
  111.1 1.6 copy-start.28
  114.0 1.9 copy-start.8
  119.2 280.8 %copy-start.3 = (f32[1,2,256,640]{3,2,1,0:T(8,128)}, f32[1,2,256,640]{3,2,1,0:T(8,128)S(1)}, u32[]{:S(2)}) copy-start(f32[1,2,256,640]{3,2,1,0:T(8,128)S(1)} %copy.113) | copy-start | bytes 3932164
  119.2 4.6 copy-start.35
  122.5 1.9 copy-start.32
  124.4 3.3 copy-start.34
  127.7 3.7 copy-start.45
  226.1 11.5 %copy-start.30 = (bf16[8,320,1920]{2,1,0:T(8,128)(2,1)S(1)}, bf16[8,320,1920]{2,1,0:T(8,128)(2,1)}, u32[]{:S(2)}) copy-start(bf16[8,320,1920]{2,1,0:T(8,128)(2,1)} %get-tuple-element.48) | copy-start | bytes 29491204
  226.1 11.5 %copy-start.38 = (bf16[2,256,2560]{2,1,0:T(8,128)(2,1)S(1)}, bf16[2,256,2560]{2,1,0:T(8,128)(2,1)}, u32[]{:S(2)}) copy-start(bf16[2,256,2560]{2,1,0:T(8,128)(2,1)} %get-tuple-element.41) | copy-start | bytes 7864324
  226.1 19.0 %slice-start = ((s8[9830400]{0:T(1024)(128)(4,1)}), s8[4194304]{0:T(1024)(128)(4,1)S(1)}, s32[]{:S(2)}) async-start(s8[9830400]{0:T(1024)(128)(4,1)} %bitcast.193), calls=%async_computation | async-start | bytes 8388608
  226.1 19.0 %slice-start.1 = ((s8[9830400]{0:T(1024)(128)(4,1)}), s8[4194304]{0:T(1024)(128)(4,1)S(1)}, s32[]{:S(2)}) async-start(s8[9830400]{0:T(1024)(128)(4,1)} %bitcast.193), calls=%async_computation.1 | async-start | bytes 8388608
  237.6 7.6 %slice-start.2 = ((s8[9830400]{0:T(1024)(128)(4,1)}), s8[1441792]{0:T(1024)(128)(4,1)S(1)}, s32[]{:S(2)}) async-start(s8[9830400]{0:T(1024)(128)(4,1)} %bitcast.193), calls=%async_computation.2 | async-start | bytes 2883584
  257.6 28.6 %copy-start.47 = (bf16[2,256,1920]{2,1,0:T(8,128)(2,1)}, bf16[2,256,1920]{2,1,0:T(8,128)(2,1)S(1)}, u32[]{:S(2)}) copy-start(bf16[2,256,1920]{2,1,0:T(8,128)(2,1)S(1)} %get-tuple-element.80) | copy-start | bytes 5898244
  257.6 9.0 %copy-start.40 = (bf16[2,256,2560]{2,1,0:T(8,128)(2,1)S(1)}, bf16[2,256,2560]{2,1,0:T(8,128)(2,1)}, u32[]{:S(2)}) copy-start(bf16[2,256,2560]{2,1,0:T(8,128)(2,1)} %get-tuple-element.49) | copy-start | bytes 7864324
  266.6 8.6 %copy-start.49 = (bf16[2,256,1920]{2,1,0:T(8,128)(2,1)S(1)}, bf16[2,256,1920]{2,1,0:T(8,128)(2,1)}, u32[]{:S(2)}) copy-start(bf16[2,256,1920]{2,1,0:T(8,128)(2,1)} %get-tuple-element.78) | copy-start | bytes 5898244
  275.1 1.7 copy-start.39
  293.2 96.7 %copy-start.44 = (f32[2,256,640]{2,1,0:T(8,128)S(1)}, f32[2,256,640]{2,1,0:T(8,128)}, u32[]{:S(2)}) copy-start(f32[2,256,640]{2,1,0:T(8,128)} %get-tuple-element.96) | copy-start | bytes 3932164
  389.9 6.5 %copy-start = (f32[2,256,640]{2,1,0:T(8,128)S(1)}, f32[2,256,640]{2,1,0:T(8,128)}, u32[]{:S(2)}) copy-start(f32[2,256,640]{2,1,0:T(8,128)} %concatenate.21.rate_ref) | copy-start | bytes 3932164
  396.4 1.5 copy-start.7
  397.9 2.2 copy-start.27
  405.3 1.5 copy-start.50
  406.8 11.2 %copy-start.33 = (bf16[8,320,640]{2,1,0:T(8,128)(2,1)S(1)}, bf16[8,320,640]{2,1,0:T(8,128)(2,1)}, u32[]{:S(2)}) copy-start(bf16[8,320,640]{2,1,0:T(8,128)(2,1)} %get-tuple-element.43) | copy-start | bytes 9830404
  406.8 11.2 %copy-start.43 = (bf16[2,256,640]{2,1,0:T(8,128)(2,1)S(1)}, bf16[2,256,640]{2,1,0:T(8,128)(2,1)}, u32[]{:S(2)}) copy-start(bf16[2,256,640]{2,1,0:T(8,128)(2,1)} %get-tuple-element.85) | copy-start | bytes 1966084
  418.0 4.6 copy-start.36
  422.6 4.0 copy-start.42
  422.6 4.0 copy-start.46
  426.6 4.0 copy-start.11
  430.6 2.0 copy-start.41
  430.6 2.6 copy-start.48
  446.6 5.0 collective-permute-start.1
  448.0 3.7 copy-start.25
  453.3 1.7 copy-start.37
  453.3 5.7 slice-start.3
  455.0 4.0 copy-start.31
  455.0 4.0 slice-start.4
  459.0 3.9 copy-start.29
  566.4 6.8 %copy-start.15 = (f32[2,64,2560]{2,1,0:T(8,128)S(1)}, f32[2,64,2560]{2,1,0:T(8,128)}, u32[]{:S(2)}) copy-start(f32[2,64,2560]{2,1,0:T(8,128)} %get-tuple-element.113) | copy-start | bytes 3932164
  573.2 1.6 copy-start.18
  574.8 2.3 copy-start.22
  574.8 3.0 copy-start.21
  574.8 3.6 copy-start.16
  576.3 3.1 copy-start.13
  579.3 2.6 copy-start.14
  581.9 2.6 copy-start.12
  (10 other events, 11.7 us)

commit v3 on v2

v3 whole, which is shorter than its diff:
```python
import functools

import jax
import jax.numpy as jnp
from jax import lax
from jax.experimental import pallas as pl
from jax.experimental.pallas import tpu as pltpu
from jax.sharding import PartitionSpec as P

MICRO = 4
EPS = 1e-06
MESH = pl.DeviceIdType.MESH
ANY = pl.BlockSpec(memory_space=pl.ANY)
VMEM = pl.BlockSpec(memory_space=pltpu.VMEM)
DMA = pltpu.SemaphoreType.DMA
BF16 = jnp.bfloat16
F32 = jnp.float32


def place():
    return lax.axis_index("dp"), lax.axis_index("tensor")


def greet(d, t, depth, dp_masks=(1, 2, 4), z_all=False):
    barrier = pltpu.get_barrier_semaphore()
    for mask in dp_masks:
        pl.semaphore_signal(barrier, inc=1, device_id=(d ^ mask, t), device_id_type=MESH)
    if z_all:
        for step in range(1, depth):
            pl.semaphore_signal(
                barrier, inc=1, device_id=(d, lax.rem(t + step, depth)), device_id_type=MESH
            )
        pl.semaphore_wait(barrier, len(dp_masks) + depth - 1)
        return

    @pl.when(t > 0)
    def _():
        pl.semaphore_signal(barrier, inc=1, device_id=(d, t - 1), device_id_type=MESH)

    @pl.when(t < depth - 1)
    def _():
        pl.semaphore_signal(barrier, inc=1, device_id=(d, t + 1), device_id_type=MESH)

    ends = jnp.where((t == 0) | (t == depth - 1), 1, 2)
    pl.semaphore_wait(barrier, len(dp_masks) + ends)


def add_rows(total, term, rows, step=32):
    step = min(step, rows)

    @pl.loop(0, rows, step=step)
    def _(start):
        part = pl.ds(pl.multiple_of(start, step), step)
        total[part, :] = (total[part, :].astype(F32) + term[part, :].astype(F32)).astype(BF16)


class WeightGather:
    def __init__(self, shard, out, local, send, recv, d, t):
        rows = shard.shape[0]
        half = rows // 2

        def view(slot, start, size):
            if len(out.shape) == 3:
                return out.at[slot, pl.ds(start, size)]
            return out.at[pl.ds(pl.multiple_of(slot * rows + start, 16), size)]

        top, low = (0, half), (half, half)
        plan = [
            (None, d, top, 2),
            (None, d, low, 4),
            (None, d, low, 2),
            (None, d, top, 4),
            (2, d ^ 2, top, 4),
            (4, d ^ 4, low, 2),
            (None, d, top, 1),
            (None, d, low, 1),
            (2, d ^ 2, top, 1),
            (4, d ^ 4, low, 1),
            (2, d ^ 2, low, 1),
            (4, d ^ 4, top, 1),
            (6, d ^ 6, top, 1),
            (6, d ^ 6, low, 1),
        ]
        self.copies = [
            pltpu.make_async_remote_copy(
                src_ref=shard.at[pl.ds(*part)] if came is None else view(slot, *part),
                dst_ref=view(slot, *part),
                send_sem=send.at[i],
                recv_sem=recv.at[i],
                device_id=(d ^ mask, t),
                device_id_type=MESH,
            )
            for i, (came, slot, part, mask) in enumerate(plan)
        ]
        self.own = pltpu.make_async_copy(shard, view(d, 0, rows), local)

    def start(self):
        for i in (0, 1, 2, 3, 6, 7):
            self.copies[i].start()
        self.own.start()

    def relay(self):
        c = self.copies
        c[0].wait_recv()
        c[4].start()
        c[1].wait_recv()
        c[5].start()
        c[8].start()
        c[9].start()

    def relay_two(self):
        c = self.copies
        c[2].wait_recv()
        c[10].start()
        c[3].wait_recv()
        c[11].start()

    def relay_last(self):
        c = self.copies
        c[4].wait_recv()
        c[12].start()
        c[5].wait_recv()
        c[13].start()

    def arrive(self):
        for i in range(6, 14):
            self.copies[i].wait_recv()
        self.own.wait()

    def end(self):
        for i in range(14):
            self.copies[i].wait_send()


def gather_scratch(count):
    return [DMA((count,)), DMA((count, 14)), DMA((count, 14))]


class GradScatter:
    ORDER = (6, 2, 4, 0)

    def __init__(self, grad, out, own, core, diag, last, local, send, recv, d, t):
        self.out, self.core, self.diag, self.last = out, core, diag, last
        self.rows = rows = out.shape[0]
        half = rows // 2
        self.half = half
        self.top, self.low = pl.ds(0, half), pl.ds(half, half)

        def block(slot, start=0, size=rows):
            return grad.at[pl.ds(pl.multiple_of(slot * rows + start, 16), size)]

        if own is None:
            self.loads = []
            self.mine = lambda i, start=0, size=rows: block(d ^ self.ORDER[i], start, size)
        else:
            self.loads = [
                pltpu.make_async_copy(block(d ^ r), own.at[i], local.at[i])
                for i, r in enumerate(self.ORDER)
            ]
            self.mine = lambda i, start=0, size=rows: own.at[i, pl.ds(start, size)]
        mine, top, low = self.mine, self.top, self.low
        plan = [(block(d ^ 1 ^ r), core.at[i], 1) for i, r in enumerate(self.ORDER)] + [
            (mine(0, 0, half), diag.at[0], 2),
            (mine(0, half, half), diag.at[1], 4),
            (mine(1, 0, half), last.at[0, top], 2),
            (mine(2, half, half), last.at[1, low], 4),
            (mine(2, 0, half), last.at[1, top], 4),
            (mine(1, half, half), last.at[0, low], 2),
        ]
        self.copies = [
            pltpu.make_async_remote_copy(
                src_ref=src,
                dst_ref=dst,
                send_sem=send.at[i],
                recv_sem=recv.at[i],
                device_id=(d ^ mask, t),
                device_id_type=MESH,
            )
            for i, (src, dst, mask) in enumerate(plan)
        ]

    def start(self):
        for i in range(4):
            self.copies[i].start()
        for load in self.loads:
            load.start()

    def pair(self, i):
        if self.loads:
            self.loads[i].wait()
        self.copies[i].wait_recv()
        add_rows(self.mine(i), self.core.at[i], self.rows)

    def first(self):
        self.pair(0)
        self.copies[4].start()
        self.copies[5].start()

    def second(self):
        self.pair(1)
        self.copies[6].start()
        self.pair(2)
        self.copies[7].start()
        self.pair(3)

    def third(self):
        c = self.copies
        c[4].wait_recv()
        add_rows(self.mine(2, 0, self.half), self.diag.at[0], self.half)
        c[8].start()
        c[5].wait_recv()
        add_rows(self.mine(1, self.half, self.half), self.diag.at[1], self.half)
        c[9].start()

    def end(self):
        for i in (6, 7, 8, 9):
            self.copies[i].wait_recv()
        step = 16
        own = self.mine(3)

        @pl.loop(0, self.rows, step=step)
        def _(start):
            part = pl.ds(pl.multiple_of(start, step), step)
            self.out[part, :] = (
                own[part, :].astype(F32)
                + self.last[0, part, :].astype(F32)
                + self.last[1, part, :].astype(F32)
            )

        for i in range(10):
            self.copies[i].wait_send()


def scatter_scratch(shapes, loaded):
    own = [pltpu.VMEM((4,) + s, BF16) for s, far in zip(shapes, loaded) if far]
    core = [pltpu.VMEM((4,) + s, BF16) for s in shapes]
    diag = [pltpu.VMEM((2, s[0] // 2, s[1]), BF16) for s in shapes]
    last = [pltpu.VMEM((2,) + s, BF16) for s in shapes]
    n = len(shapes)
    return own + core + diag + last + [DMA((n, 4)), DMA((n, 10)), DMA((n, 10))]


def make_scatters(grads, outs, loaded, scratch, d, t):
    n = len(grads)
    scratch = list(scratch)
    own = [scratch.pop(0) if far else None for far in loaded]
    core, diag, last = (scratch[i * n : (i + 1) * n] for i in range(3))
    local, send, recv = scratch[3 * n :]
    return [
        GradScatter(
            grads[i],
            outs[i],
            own[i],
            core[i],
            diag[i],
            last[i],
            local.at[i],
            send.at[i],
            recv.at[i],
            d,
            t,
        )
        for i in range(n)
    ]


class LineGather:
    def __init__(self, block, out, local, send, recv, d, t, depth):
        self.block, self.out, self.send, self.recv = block, out, send, recv
        self.d, self.t, self.depth = d, t, depth
        self.rows = block.shape[1]
        self.own = pltpu.make_async_copy(block, self.slot(t), local)

    def slot(self, j):
        return self.out.at[:, pl.ds(pl.multiple_of(j * self.rows, self.rows), self.rows)]

    def copy(self, way, step, j, to):
        return pltpu.make_async_remote_copy(
            src_ref=self.block if step == 0 else self.slot(j),
            dst_ref=self.slot(j),
            send_sem=self.send.at[way, step],
            recv_sem=self.recv.at[way, step],
            device_id=(self.d, to),
            device_id_type=MESH,
        )

    def step(self, s):
        t, depth = self.t, self.depth
        if s == 0:
            self.own.start()
        if s > 0:

            @pl.when(t - s >= 0)
            def _():
                self.copy(0, s - 1, t, t).wait_recv()

        if s < depth - 1:

            @pl.when((t - s >= 0) & (t < depth - 1))
            def _():
                self.copy(0, s, t - s, t + 1).start()

        if s > 0:

            @pl.when(t + s < depth)
            def _():
                self.copy(1, s - 1, t, t).wait_recv()

        if s < depth - 1:

            @pl.when((t + s < depth) & (t > 0))
            def _():
                self.copy(1, s, t + s, t - 1).start()

    def end(self):
        t, depth = self.t, self.depth
        for s in range(depth - 1):

            @pl.when((t - s >= 0) & (t < depth - 1))
            def _():
                self.copy(0, s, t, t).wait_send()

            @pl.when((t + s < depth) & (t > 0))
            def _():
                self.copy(1, s, t, t).wait_send()


def line_gather_scratch(depth):
    return [DMA, DMA((2, depth - 1)), DMA((2, depth - 1))]


class LineScatter:
    def __init__(self, part, got, send, recv, d, t, depth):
        self.part, self.got, self.send, self.recv = part, got, send, recv
        self.d, self.t, self.depth = d, t, depth
        self.seqs = part.shape[0]
        self.rows = part.shape[1] // depth

    def slot(self, way, j, s):
        return self.got.at[way, j - 1 if way == 0 else j, s]

    def copy(self, way, j, s, src, to):
        return pltpu.make_async_remote_copy(
            src_ref=src,
            dst_ref=self.slot(way, j, s),
            send_sem=self.send.at[way, j, s],
            recv_sem=self.recv.at[way, j, s],
            device_id=(self.d, to),
            device_id_type=MESH,
        )

    def block(self, j, s):
        return self.part.at[s, pl.ds(pl.multiple_of(j * self.rows, self.rows), self.rows)]

    def start(self, first=0, last=None):
        t, depth = self.t, self.depth
        steps = range(first, depth - 1 if last is None else last)

        @pl.when(t == 0)
        def _():
            for k in steps:
                for s in range(self.seqs):
                    j = depth - 1 - k
                    self.copy(0, j, s, self.block(j, s), t + 1).start()

        @pl.when(t == depth - 1)
        def _():
            for j in steps:
                for s in range(self.seqs):
                    self.copy(1, j, s, self.block(j, s), t - 1).start()

    def pass_on(self, way, j, to):
        for s in range(self.seqs):
            mine = self.slot(way, j, s)
            self.copy(way, j, s, mine, self.t).wait_recv()
            add_rows(mine, self.block(j, s), self.rows)
            self.copy(way, j, s, mine, to).start()

    def step(self, k):
        t, depth = self.t, self.depth
        right = depth - 1 - k + t
        left = k - (depth - 1 - t)

        @pl.when((t > 0) & (t < right) & (right < depth))
        def _():
            self.pass_on(0, right, t + 1)

        @pl.when((left >= 0) & (left < t) & (t < depth - 1))
        def _():
            self.pass_on(1, left, t - 1)

    def total(self, out):
        t, depth = self.t, self.depth
        mine = pl.ds(pl.multiple_of(t * self.rows, self.rows), self.rows)
        out[...] = self.part[:, mine, :].astype(F32)

        @pl.when(t > 0)
        def _():
            for s in range(self.seqs):
                self.copy(0, t, s, self.slot(0, t, s), t).wait_recv()
            out[...] += self.got[0, t - 1].astype(F32)

        @pl.when(t < depth - 1)
        def _():
            for s in range(self.seqs):
                self.copy(1, t, s, self.slot(1, t, s), t).wait_recv()
            out[...] += self.got[1, t].astype(F32)

    def end(self):
        t, depth = self.t, self.depth
        for j in range(depth):
            for s in range(self.seqs):
                if j > 0:

                    @pl.when(j > t)
                    def _():
                        self.copy(0, j, s, self.slot(0, j, s), t).wait_send()

                if j < depth - 1:

                    @pl.when(j < t)
                    def _():
                        self.copy(1, j, s, self.slot(1, j, s), t).wait_send()


def line_scatter_scratch(seqs, rows, width, depth):
    return [
        pltpu.VMEM((2, depth - 1, seqs, rows, width), BF16),
        DMA((2, depth, seqs)),
        DMA((2, depth, seqs)),
    ]


def call(kernel, name, number, ins, outs, scratch, args, vmem=60 * 1024 * 1024):
    return pl.pallas_call(
        kernel,
        name=name,
        out_shape=[o[0] for o in outs],
        in_specs=ins,
        out_specs=[o[1] for o in outs],
        scratch_shapes=scratch,
        compiler_params=pltpu.CompilerParams(
            collective_id=number, has_side_effects=True, vmem_limit_bytes=vmem
        ),
    )(*args)


def shaped(shape, dtype, spec):
    return (jax.ShapeDtypeStruct(shape, dtype), spec)


def sigmoid(x):
    return 1.0 / (1.0 + jnp.exp(-x))


def one_less_exp(y):
    series = 1.0 + y / 6.0 * (1.0 + y / 7.0)
    for k in (5.0, 4.0, 3.0, 2.0):
        series = 1.0 + y / k * series
    return jnp.where(y > -0.5, -y * series, 1.0 - jnp.exp(y))


GELU_SCALE = 0.7978845608028654
GELU_CUBE = 0.044715


def gelu(x):
    return 0.5 * x * (1.0 + jnp.tanh(GELU_SCALE * (x + GELU_CUBE * x * x * x)))


def gelu_both(x):
    square = x * x
    bent = jnp.tanh(GELU_SCALE * (x + GELU_CUBE * square * x))
    half = 0.5 * (1.0 + bent)
    slope = half + 0.5 * x * (1.0 - bent * bent) * (
        GELU_SCALE * (1.0 + 3.0 * GELU_CUBE * square)
    )
    return x * half, slope


def rows_of(index, size):
    return pl.ds(pl.multiple_of(index * size, size), size)


def contract(left, right, dims):
    return lax.dot_general(left, right, ((dims[:1], dims[1:]), ((), ())), preferred_element_type=F32)


def scan_rows(rate, out, seqs, length, base=0, backward=False):
    tile = 8
    width = out.shape[1]
    row = lax.broadcasted_iota(jnp.int32, (tile, width), 0)

    def body(i, carried):
        k = length // tile - 1 - i if backward else i
        ends = []
        for s in range(seqs):
            start = pl.multiple_of(s * length + k * tile, tile)
            rows = pl.ds(start, tile)
            if backward:
                pair = rate[pl.ds(start, 2 * tile), :]
                step = pltpu.roll(pair, 2 * tile - 1, 0)[:tile]
                step = jnp.where((row == tile - 1) & (i == 0), 0.0, step)
            else:
                step = rate[rows, :]
            held = pl.ds(pl.multiple_of(base + start, tile), tile)
            drive = out[held, :]
            for shift in (1, 2, 4):
                turn = tile - shift if backward else shift
                inside = row < tile - shift if backward else row >= shift
                before = jnp.where(inside, pltpu.roll(drive, turn, 0), 0.0)
                drive = drive + step * before
                step = step * jnp.where(inside, pltpu.roll(step, turn, 0), 1.0)
            states = drive + step * carried[s]
            out[held, :] = states
            ends.append(states[0:1] if backward else states[tile - 1 : tile])
        return tuple(ends)

    start = tuple(jnp.zeros((1, width), F32) for _ in range(seqs))
    lax.fori_loop(0, length // tile, body, start)


STRIP = 16


def gate_blocks(parity, width, block):
    half = block // 2
    shift = parity * half
    blocks = []
    for k in range((width + half) // block):
        low, high = k * block - shift, (k + 1) * block - shift
        blocks.append((k, max(low, 0), min(high, width)))
    return blocks


def first_kernel(
    depth,
    normed_block,
    cot_block,
    gelu_shard,
    input_shard,
    gate_in_shard,
    gate_dec_shard,
    out_shard,
    up_shard,
    taps,
    rate,
    normed_out,
    cot_out,
    gelu_full,
    input_full,
    gate_in_full,
    gate_dec_full,
    out_full,
    up_full,
    gelu_pre_out,
    input_pre_out,
    conv_out,
    window_out,
    gate_in_out,
    gate_dec_out,
    states_out,
    mixed_out,
    part_out,
    *scratch,
):
    normed, gelu_w, input_w, gate_in_w, gate_dec_w, out_w = scratch[:6]
    gelu_pre, input_pre, conv, window, gate_in, gate_dec, decay, states, mixed, part = scratch[6:16]
    local, send, recv = scratch[16:19]
    line_sems = scratch[19:25]
    rim_send, rim_recv, save_sem = scratch[25:28]
    d, t = place()
    parity = lax.rem(t, 2)
    even = parity == 0
    odd = parity == 1
    greet(d, t, depth)
    seqs, length, _ = normed.shape
    tokens = seqs * length
    width = conv.shape[1]
    block = gate_in_w.shape[0]
    half = block // 2
    lines = [
        LineGather(normed_block, normed, *line_sems[:3], d, t, depth),
        LineGather(cot_block, cot_out, *line_sems[3:], d, t, depth),
    ]
    pairs = (
        (gelu_shard, gelu_w),
        (input_shard, input_w),
        (gate_in_shard, gate_in_w),
        (gate_dec_shard, gate_dec_w),
        (out_shard, out_w),
        (up_shard, up_full),
    )
    gathers = [
        WeightGather(shard, full, local.at[i], send.at[i], recv.at[i], d, t)
        for i, (shard, full) in enumerate(pairs)
    ]
    saves = []

    def save(src, dst):
        copy = pltpu.make_async_copy(src, dst, save_sem.at[len(saves)])
        copy.start()
        saves.append(copy)

    one, two, three = gathers[:-2], gathers[-2], gathers[-1]
    lines[0].step(0)
    for g in one:
        g.start()
    for g in one:
        g.relay()
    two.start()
    lines[0].step(1)
    for g in one:
        g.relay_two()
    lines[0].step(2)
    for g in one:
        g.relay_last()
    two.relay()
    three.start()
    two.relay_two()
    two.relay_last()
    lines[0].step(3)
    lines[0].own.wait()
    lines[1].step(0)
    for g in one:
        g.arrive()
    save(normed, normed_out)
    save(gelu_w, gelu_full)
    save(input_w, input_full)
    save(gate_in_w, gate_in_full)
    save(gate_dec_w, gate_dec_full)

    for s in range(seqs):
        rows = pl.ds(s * length, length)
        input_pre[s, 0:8, :] = jnp.zeros((8, width), F32)
        input_pre[s, 8 : 8 + length, :] = contract(normed[s], input_w[...], (1, 0))
        gelu_pre[rows, :] = contract(normed[s], gelu_w[...], (1, 0))

    for s in range(seqs):

        @pl.loop(0, length // STRIP)
        def _(i):
            near = input_pre[s, pl.ds(pl.multiple_of(i * STRIP, STRIP), STRIP + 8), :]
            total = taps[0:1, :] * near[8:]
            for k in range(1, taps.shape[0]):
                total = total + taps[k : k + 1, :] * pltpu.roll(near, k, 0)[8:]
            rows = pl.ds(pl.multiple_of(s * length + i * STRIP, STRIP), STRIP)
            conv[rows, :] = total.astype(BF16)

    def rim(to, src, dst):
        return pltpu.make_async_remote_copy(
            src_ref=conv.at[:, pl.ds(src, half)],
            dst_ref=window.at[:, pl.ds(dst, half)],
            send_sem=rim_send,
            recv_sem=rim_recv,
            device_id=(d, to),
            device_id_type=MESH,
        )

    @pl.when(even)
    def _():
        rim(t + 1, width - half, 0).start()
        window[:, 0:width] = conv[...]

    @pl.when(odd)
    def _():
        rim(t - 1, 0, width).start()
        window[:, half : half + width] = conv[...]

    def gates(blocks):
        for k, low, high in blocks:
            near = window[:, k * block : (k + 1) * block]
            gate_in[:, low:high] = contract(near, gate_in_w[:, low:high], (1, 0))
            gate_dec[:, low:high] = contract(near, gate_dec_w[:, low:high], (1, 0))

    even_blocks, odd_blocks = gate_blocks(0, width, block), gate_blocks(1, width, block)

    @pl.when(even)
    def _():
        gates(even_blocks[:-1])

    @pl.when(odd)
    def _():
        gates(odd_blocks[1:])

    three.relay()

    @pl.when(even)
    def _():
        rim(t + 1, width - half, width).wait_recv()
        gates(even_blocks[-1:])

    @pl.when(odd)
    def _():
        rim(t - 1, 0, 0).wait_recv()
        gates(odd_blocks[:1])

    lines[1].step(1)

    @pl.loop(0, tokens // STRIP)
    def _(i):
        rows = rows_of(i, STRIP)
        log = -8.0 * sigmoid(gate_dec[rows, :]) * rate[...]
        decay[rows, :] = jnp.exp(log)
        drive = jnp.sqrt(one_less_exp(2.0 * log)) * sigmoid(gate_in[rows, :])
        held = pl.ds(pl.multiple_of(i * STRIP + 8, 8), STRIP)
        states[held, :] = drive * conv[rows, :].astype(F32)

    states[0:8, :] = jnp.zeros((8, width), F32)
    scan_rows(decay, states, seqs, length, base=8)

    @pl.loop(0, tokens // STRIP)
    def _(i):
        rows = rows_of(i, STRIP)
        held = pl.ds(pl.multiple_of(i * STRIP + 8, 8), STRIP)
        mixed[rows, :] = (gelu(gelu_pre[rows, :]) * states[held, :]).astype(BF16)

    save(gelu_pre, gelu_pre_out)
    save(input_pre, input_pre_out)
    save(conv, conv_out)
    save(window, window_out)
    save(gate_in, gate_in_out)
    save(gate_dec, gate_dec_out)
    save(states, states_out)
    save(mixed, mixed_out)
    three.relay_two()
    two.arrive()
    save(out_w, out_full)
    panel = 512

    @pl.loop(0, out_w.shape[0] // panel)
    def _(i):
        columns = rows_of(i, panel)
        value = contract(mixed[...], out_w[columns, :], (1, 1)).astype(BF16)
        for s in range(seqs):
            part[s, :, columns] = value[s * length : (s + 1) * length]

    save(part, part_out)
    lines[1].step(2)
    three.relay_last()
    lines[1].step(3)
    lines[1].own.wait()
    three.arrive()

    @pl.when(even)
    def _():
        rim(t + 1, width - half, 0).wait_send()

    @pl.when(odd)
    def _():
        rim(t - 1, 0, width).wait_send()

    for g in gathers:
        g.end()
    for line in lines:
        line.end()
    for copy in saves:
        copy.wait()


def first_phase(normed, cot, weights, taps, rate, depth):
    seqs, rows, model = normed.shape
    length = rows * depth
    tokens = seqs * length
    n = len(weights)
    block, width = weights[2].shape[0] * 8, weights[0].shape[1]
    wide = block // 2 + width
    wide_rows = (seqs, length, model)
    mixers = [(model, width), (model, width), (block, width), (block, width), (model, width)]
    saved = [
        ((tokens, width), F32),
        ((seqs, length + 8, width), F32),
        ((tokens, width), BF16),
        ((tokens, wide), BF16),
        ((tokens, width), F32),
        ((tokens, width), F32),
        ((tokens + 8, width), F32),
        ((tokens, width), BF16),
        (wide_rows, BF16),
    ]
    outs = [shaped(wide_rows, BF16, ANY)] * 2
    outs += [shaped(shape, BF16, ANY) for shape in mixers]
    outs += [shaped((8,) + weights[-1].shape, BF16, ANY)]
    outs += [shaped(shape, dtype, ANY) for shape, dtype in saved]
    saved_scratch = saved[:6] + [((tokens, width), F32)] + saved[6:]
    scratch = [pltpu.VMEM(wide_rows, BF16)]
    scratch += [pltpu.VMEM(shape, BF16) for shape in mixers]
    scratch += [pltpu.VMEM(shape, dtype) for shape, dtype in saved_scratch]
    scratch += gather_scratch(n) + line_gather_scratch(depth) * 2 + [DMA, DMA, DMA((16,))]
    res = call(
        functools.partial(first_kernel, depth),
        "first_phase",
        0,
        [VMEM] * (4 + n),
        outs,
        scratch,
        (normed, cot) + tuple(weights) + (taps, rate.reshape(1, width)),
    )
    return res[0], res[1], res[2 : 2 + n], res[2 + n : -1], res[-1]


def middle_kernel(depth, part, act, gain, w0, w1, middle, wide, f0, f1, *scratch):
    local, send, recv = scratch[:3]
    got, ssem, rsem = scratch[3:6]
    block = scratch[6]
    lsem = scratch[7:10]
    d, t = place()
    greet(d, t, depth)
    gathers = [
        WeightGather(w, f, local.at[i], send.at[i], recv.at[i], d, t)
        for i, (w, f) in enumerate(((w0, f0), (w1, f1)))
    ]
    scatter = LineScatter(part, got, ssem, rsem, d, t, depth)
    scatter.start()
    gathers[0].start()
    gathers[0].relay()
    gathers[1].start()
    scatter.step(1)
    gathers[0].relay_two()
    scatter.step(2)
    gathers[0].relay_last()
    scatter.total(middle)
    seqs, rows, width = act.shape
    for s in range(seqs):
        value = middle[s] + act[s].astype(F32)
        middle[s] = value
        inverse = lax.rsqrt(jnp.mean(value * value, axis=-1, keepdims=True) + EPS)
        block[s] = (value * inverse * gain[...]).astype(BF16)
    line = LineGather(block, wide, *lsem, d, t, depth)
    line.step(0)
    gathers[1].relay()
    line.step(1)
    gathers[1].relay_two()
    line.step(2)
    gathers[1].relay_last()
    line.step(3)
    for g in gathers:
        g.arrive()
        g.end()
    scatter.end()
    line.own.wait()
    line.end()


def middle_phase(part, act, gain, w0, w1, depth):
    seqs, rows, width = act.shape
    outs = [
        shaped(act.shape, F32, VMEM),
        shaped((seqs, rows * depth, width), BF16, ANY),
        shaped((8,) + w0.shape, BF16, ANY),
        shaped((8,) + w1.shape, BF16, ANY),
    ]
    scratch = (
        gather_scratch(2)
        + line_scatter_scratch(seqs, rows, width, depth)
        + [pltpu.VMEM(act.shape, BF16)]
        + line_gather_scratch(depth)
    )
    return call(
        functools.partial(middle_kernel, depth),
        "middle_phase",
        1,
        [VMEM] * 5,
        outs,
        scratch,
        (part, act, gain.reshape(1, width), w0, w1),
    )


def norm_back(value, gain, error):
    inverse = lax.rsqrt(jnp.mean(value * value, axis=-1, keepdims=True) + EPS)
    scaled = error * gain
    mean = jnp.mean(scaled * value, axis=-1, keepdims=True)
    grad = inverse * scaled - value * (inverse * inverse * inverse * mean)
    return grad, jnp.sum(error * value * inverse, axis=0, keepdims=True)


def back_kernel(depth, part, middle, gain, cot, g0, g1, grad, wide, gain_grad, o0, o1, *scratch):
    got, ssem, rsem = scratch[:3]
    block = scratch[3]
    lsem = scratch[4:7]
    d, t = place()
    greet(d, t, depth)
    scatters = make_scatters((g0, g1), (o0, o1), (True, True), scratch[7:], d, t)
    scatter = LineScatter(part, got, ssem, rsem, d, t, depth)
    scatter.start()
    for g in scatters:
        g.start()
    scatters[0].first()
    scatters[0].second()
    scatter.step(1)
    scatters[0].third()
    scatter.step(2)
    scatters[1].first()
    scatters[1].second()
    scatter.total(grad)
    seqs, rows, width = middle.shape
    for s in range(seqs):
        change, gain_part = norm_back(middle[s], gain[...], grad[s])
        change = change + cot[s]
        grad[s] = change
        block[s] = change.astype(BF16)
        if s == 0:
            gain_grad[...] = gain_part
        else:
            gain_grad[...] += gain_part
    line = LineGather(block, wide, *lsem, d, t, depth)
    line.step(0)
    scatters[0].end()
    line.step(1)
    scatters[1].third()
    line.step(2)
    line.step(3)
    scatters[1].end()
    scatter.end()
    line.own.wait()
    line.end()


def back_phase(part, middle, gain, cot, g0, g1, depth):
    seqs, rows, width = middle.shape
    shapes = [(g.shape[0] // 8, g.shape[1]) for g in (g0, g1)]
    outs = [
        shaped(middle.shape, F32, VMEM),
        shaped((seqs, rows * depth, width), BF16, ANY),
        shaped((1, width), F32, VMEM),
        shaped(shapes[0], F32, VMEM),
        shaped(shapes[1], F32, VMEM),
    ]
    scratch = (
        line_scatter_scratch(seqs, rows, width, depth)
        + [pltpu.VMEM(middle.shape, BF16)]
        + line_gather_scratch(depth)
        + scatter_scratch(shapes, (True, True))
    )
    return call(
        functools.partial(back_kernel, depth),
        "back_phase",
        2,
        [VMEM, VMEM, VMEM, VMEM, ANY, ANY],
        outs,
        scratch,
        (part, middle, gain.reshape(1, width), cot, g0, g1),
    )


def mixer_back_kernel(
    depth,
    branch_in,
    out_w_in,
    gelu_pre_in,
    input_pre_in,
    conv_in,
    window_in,
    gate_in_in,
    gate_dec_in,
    states_in,
    gelu_w_in,
    input_w_in,
    gate_in_w_in,
    gate_dec_w_in,
    up_in,
    feed,
    middle,
    taps,
    rate,
    part_out,
    gelu_grad_out,
    input_grad_out,
    gate_in_grad_out,
    gate_dec_grad_out,
    small,
    output,
    up_out,
    *scratch,
):
    branch, weight, input_w = scratch[:3]
    gelu_pre, input_pre, conv, window, gate_in, gate_dec, states, gate_in_w, gate_dec_w = scratch[3:12]
    grad, decay, grad_conv, gelu_grad, input_grad, grad_in, grad_dec = scratch[12:19]
    rim_out, rim_in, gate_in_grad, gate_dec_grad, part, sums, total = scratch[19:26]
    got, ssem, rsem = scratch[26:29]
    rim_send, rim_recv, load_sem, save_sem = scratch[29:33]
    d, t = place()
    parity = lax.rem(t, 2)
    even = parity == 0
    odd = parity == 1
    greet(d, t, depth)
    seqs, length, _ = branch.shape
    tokens = seqs * length
    width = conv.shape[1]
    block = gate_in_w.shape[0]
    half = block // 2
    even_blocks, odd_blocks = gate_blocks(0, width, block), gate_blocks(1, width, block)
    (scatter,) = make_scatters((up_in,), (up_out,), (True,), scratch[33:], d, t)
    line = LineScatter(feed, got, ssem, rsem, d, t, depth)
    saves = []

    def save(src, dst):
        copy = pltpu.make_async_copy(src, dst, save_sem.at[len(saves)])
        copy.start()
        saves.append(copy)

    def load(i, src, dst):
        copy = pltpu.make_async_copy(src, dst, load_sem.at[i])
        copy.start()
        return copy

    early = [load(0, branch_in, branch), load(1, out_w_in, weight)]
    next_ = [
        load(2, gelu_pre_in, gelu_pre),
        load(3, states_in, states),
        load(4, gate_dec_in, gate_dec),
    ]
    line.start(0, 1)
    scatter.start()
    then = [
        load(5, gate_in_in, gate_in),
        load(6, conv_in, conv),
        load(7, window_in, window),
        load(8, gate_in_w_in, gate_in_w),
        load(9, gate_dec_w_in, gate_dec_w),
        load(10, input_pre_in, input_pre),
        load(11, input_w_in, input_w),
    ]
    for copy in early:
        copy.wait()
    for s in range(seqs):
        rows = pl.ds(s * length, length)
        grad[rows, :] = contract(branch[s], weight[...], (1, 0))
    reload = load(0, gelu_w_in, weight)
    scatter.first()
    for copy in next_:
        copy.wait()

    @pl.loop(0, tokens // STRIP)
    def _(i):
        rows = rows_of(i, STRIP)
        held = pl.ds(pl.multiple_of(i * STRIP + 8, 8), STRIP)
        act, slope = gelu_both(gelu_pre[rows, :])
        came = grad[rows, :]
        gelu_grad[rows, :] = (came * states[held, :] * slope).astype(BF16)
        grad[rows, :] = came * act
        decay[rows, :] = jnp.exp(-8.0 * sigmoid(gate_dec[rows, :]) * rate[...])

    decay[tokens : tokens + 8, :] = jnp.zeros((8, width), F32)
    save(gelu_grad, gelu_grad_out)
    scatter.second()
    scan_rows(decay, grad, seqs, length, backward=True)
    for copy in then:
        copy.wait()
    sums[...] = jnp.zeros(sums.shape, F32)

    def fold(value):
        return value[0:8] + value[8:16]

    first_row = lax.broadcasted_iota(jnp.int32, (STRIP, width), 0) == 0
    for s in range(seqs):

        @pl.loop(0, length // STRIP)
        def _(i):
            start = pl.multiple_of(s * length + i * STRIP, STRIP)
            rows = pl.ds(start, STRIP)
            earlier = pltpu.roll(states[pl.ds(start, STRIP + 8), :], 1, 0)[8:]
            earlier = jnp.where(first_row & (i == 0), 0.0, earlier)
            came = grad[rows, :]
            open_in = sigmoid(gate_in[rows, :])
            open_dec = sigmoid(gate_dec[rows, :])
            slow = -8.0 * rate[...]
            lost = one_less_exp(2.0 * open_dec * slow)
            root = jnp.sqrt(lost)
            value = conv[rows, :].astype(F32)
            step = decay[rows, :]
            through = came * open_in
            grad_log = step * (came * earlier - through * value * step / root)
            sums[0] += fold(grad_log * (-8.0 * open_dec))
            through = through * root
            grad_conv[s, pl.ds(pl.multiple_of(i * STRIP, STRIP), STRIP), :] = through
            grad_in[rows, :] = (through * value * (1.0 - open_in)).astype(BF16)
            grad_dec[rows, :] = (grad_log * slow * open_dec * (1.0 - open_dec)).astype(BF16)

        grad_conv[s, length : length + 8, :] = jnp.zeros((8, width), F32)

    def gates_back(k, low, high):
        return contract(grad_in[:, low:high], gate_in_w[:, low:high], (1, 1)) + contract(
            grad_dec[:, low:high], gate_dec_w[:, low:high], (1, 1)
        )

    def add_conv(low, high, value):
        for s in range(seqs):
            grad_conv[s, 0:length, low:high] += value[s * length : (s + 1) * length]

    def rim(to):
        return pltpu.make_async_remote_copy(
            src_ref=rim_out,
            dst_ref=rim_in,
            send_sem=rim_send,
            recv_sem=rim_recv,
            device_id=(d, to),
            device_id_type=MESH,
        )

    @pl.when(even)
    def _():
        value = gates_back(*even_blocks[-1])
        rim_out[...] = value[:, half:].astype(BF16)
        rim(t + 1).start()
        add_conv(width - half, width, value[:, :half])

    @pl.when(odd)
    def _():
        value = gates_back(*odd_blocks[0])
        rim_out[...] = value[:, :half].astype(BF16)
        rim(t - 1).start()
        add_conv(0, half, value[:, half:])

    line.start(1)
    line.step(1)

    def inner(blocks):
        for k, low, high in blocks:
            add_conv(low, high, gates_back(k, low, high))

    def gate_grads(blocks):
        for k, low, high in blocks:
            near = window[:, k * block : (k + 1) * block]
            gate_in_grad[:, low:high] = contract(near, grad_in[:, low:high], (0, 0)).astype(BF16)
            gate_dec_grad[:, low:high] = contract(near, grad_dec[:, low:high], (0, 0)).astype(BF16)

    @pl.when(even)
    def _():
        inner(even_blocks[:-1])
        gate_grads(even_blocks)

    @pl.when(odd)
    def _():
        inner(odd_blocks[1:])
        gate_grads(odd_blocks)

    save(gate_in_grad, gate_in_grad_out)
    save(gate_dec_grad, gate_dec_grad_out)
    scatter.third()

    @pl.when(even)
    def _():
        rim(t + 1).wait()
        add_conv(width - half, width, rim_in[...].astype(F32))

    @pl.when(odd)
    def _():
        rim(t - 1).wait()
        add_conv(0, half, rim_in[...].astype(F32))

    for s in range(seqs):

        @pl.loop(0, length // STRIP)
        def _(i):
            near = pl.ds(pl.multiple_of(i * STRIP, STRIP), STRIP + 8)
            later = grad_conv[s, near, :]
            before = input_pre[s, near, :]
            here = later[:STRIP]
            value = taps[0:1, :] * here
            sums[1] += fold(here * before[8:])
            for k in range(1, taps.shape[0]):
                value = value + taps[k : k + 1, :] * pltpu.roll(later, STRIP + 8 - k, 0)[:STRIP]
                sums[1 + k] += fold(here * pltpu.roll(before, k, 0)[8:])
            rows = pl.ds(pl.multiple_of(s * length + i * STRIP, STRIP), STRIP)
            input_grad[rows, :] = value.astype(BF16)

    save(input_grad, input_grad_out)
    for k in range(sums.shape[0]):
        small[k : k + 1, :] = jnp.sum(sums[k], axis=0, keepdims=True)
    small[sums.shape[0] :, :] = jnp.zeros((8 - sums.shape[0], width), F32)
    reload.wait()
    panel = 512

    @pl.loop(0, weight.shape[0] // panel)
    def _(i):
        columns = rows_of(i, panel)
        value = contract(gelu_grad[...], weight[columns, :], (1, 1))
        value = (value + contract(input_grad[...], input_w[columns, :], (1, 1))).astype(BF16)
        for s in range(seqs):
            part[s, :, columns] = value[s * length : (s + 1) * length]

    save(part, part_out)
    line.step(2)
    scatter.end()
    line.total(total)
    output[...] = (total[...] + middle[...]).astype(BF16)
    line.end()
    for copy in saves:
        copy.wait()


def mixer_back_phase(branch, saved, weights, up, feed, middle, taps, rate, depth):
    seqs, length, model = branch.shape
    tokens = seqs * length
    gelu_w, input_w, gate_in_w, gate_dec_w, out_w = weights[:5]
    gelu_pre, input_pre, conv, window, gate_in, gate_dec, states, mixed = saved
    width = out_w.shape[1]
    block = gate_in_w.shape[0]
    half = block // 2
    up_shape = (up.shape[0] // 8, up.shape[1])
    flat = (tokens, width)
    outs = [
        shaped(branch.shape, BF16, ANY),
        shaped(flat, BF16, ANY),
        shaped(flat, BF16, ANY),
        shaped(gate_in_w.shape, BF16, ANY),
        shaped(gate_in_w.shape, BF16, ANY),
        shaped((8, width), F32, VMEM),
        shaped(middle.shape, BF16, VMEM),
        shaped(up_shape, F32, VMEM),
    ]
    scratch = [
        pltpu.VMEM(x.shape, x.dtype)
        for x in (
            branch,
            out_w,
            input_w,
            gelu_pre,
            input_pre,
            conv,
            window,
            gate_in,
            gate_dec,
            states,
            gate_in_w,
            gate_dec_w,
        )
    ]
    scratch += [
        pltpu.VMEM(flat, F32),
        pltpu.VMEM((tokens + 8, width), F32),
        pltpu.VMEM((seqs, length + 8, width), F32),
    ]
    scratch += [pltpu.VMEM(flat, BF16)] * 4
    scratch += [pltpu.VMEM((tokens, half), BF16)] * 2
    scratch += [pltpu.VMEM(gate_in_w.shape, BF16)] * 2
    scratch += [
        pltpu.VMEM(branch.shape, BF16),
        pltpu.VMEM((1 + taps.shape[0], 8, width), F32),
        pltpu.VMEM(middle.shape, F32),
    ]
    scratch += line_scatter_scratch(seqs, length // depth, model, depth)
    scratch += [DMA, DMA, DMA((12,)), DMA((8,))]
    scratch += scatter_scratch([up_shape], (True,))
    return call(
        functools.partial(mixer_back_kernel, depth),
        "mixer_back_phase",
        3,
        [ANY] * 14 + [VMEM] * 4,
        outs,
        scratch,
        (
            branch,
            out_w,
            gelu_pre,
            input_pre,
            conv,
            window,
            gate_in,
            gate_dec,
            states,
            gelu_w,
            input_w,
            gate_in_w,
            gate_dec_w,
            up,
            feed,
            middle,
            taps,
            rate.reshape(1, width),
        ),
    )


def last_kernel(
    depth,
    part,
    act,
    gain,
    grad_middle,
    mlp_part,
    small,
    branch_in,
    normed_in,
    mixed_in,
    gelu_grad_in,
    input_grad_in,
    gate_in_grad,
    gate_dec_grad,
    input_grad,
    gains,
    smalls,
    out_out,
    gelu_out,
    input_out,
    gate_in_out,
    gate_dec_out,
    *scratch,
):
    got, ssem, rsem = scratch[:3]
    pack, packs, small_all, line_pack, line_packs = scratch[3:8]
    psend, precv, qsend, qrecv, zsend, zrecv = scratch[8:14]
    branch, normed, mixed, gelu_grad, input_rows = scratch[14:19]
    out_w_grad, gelu_w_grad, input_w_grad, load_sem = scratch[19:23]
    d, t = place()
    greet(d, t, depth, dp_masks=(1, 2, 3, 4, 5, 6, 7), z_all=True)
    scatters = make_scatters(
        (out_w_grad, gelu_w_grad, input_w_grad, gate_in_grad, gate_dec_grad),
        (out_out, gelu_out, input_out, gate_in_out, gate_dec_out),
        (False, False, False, True, True),
        scratch[23:],
        d,
        t,
    )
    line = LineScatter(part, got, ssem, rsem, d, t, depth)

    def load(i, src, dst):
        copy = pltpu.make_async_copy(src, dst, load_sem.at[i])
        copy.start()
        return copy

    loads = [
        load(0, branch_in, branch),
        load(1, mixed_in, mixed),
        load(2, normed_in, normed),
        load(3, gelu_grad_in, gelu_grad),
        load(4, input_grad_in, input_rows),
    ]

    def dp_copies(src, dst, send, recv):
        return [
            pltpu.make_async_remote_copy(
                src_ref=src,
                dst_ref=dst.at[d],
                send_sem=send.at[mask - 1],
                recv_sem=recv.at[mask - 1],
                device_id=(d ^ mask, t),
                device_id_type=MESH,
            )
            for mask in range(1, 8)
        ]

    line.start()
    small_copies = dp_copies(small, small_all, qsend, qrecv)
    for c in small_copies:
        c.start()
    small_all[d] = small[...]
    for g in scatters[3:]:
        g.start()
    seqs, length, model = branch.shape
    panel = 512

    def weight_grad(left, right, out):
        @pl.loop(0, model // panel)
        def _(i):
            columns = rows_of(i, panel)
            value = contract(left[0, :, columns], right[0:length, :], (0, 0))
            for s in range(1, seqs):
                value = value + contract(
                    left[s, :, columns], right[s * length : (s + 1) * length, :], (0, 0)
                )
            out[columns, :] = value.astype(BF16)

    loads[0].wait()
    loads[1].wait()
    weight_grad(branch, mixed, out_w_grad)
    scatters[0].start()
    loads[2].wait()
    loads[3].wait()
    weight_grad(normed, gelu_grad, gelu_w_grad)
    scatters[1].start()
    scatters[0].first()
    scatters[0].second()
    loads[4].wait()
    weight_grad(normed, input_rows, input_w_grad)
    scatters[2].start()
    line.step(1)
    scatters[1].first()
    scatters[1].second()
    scatters[0].third()
    scatters[2].first()
    scatters[2].second()
    line.step(2)
    for g in scatters[3:]:
        g.first()
        g.second()
    scatters[1].third()
    scatters[0].end()
    line.total(input_grad)
    quarter = pack.shape[1]
    for i in range(4):
        pack[4 + i : 5 + i, :] = mlp_part[:, i * quarter : (i + 1) * quarter]
    for s in range(seqs):
        change, gain_part = norm_back(act[s].astype(F32), gain[...], input_grad[s])
        input_grad[s] = change + grad_middle[s]
        for i in range(4):
            piece = gain_part[:, i * quarter : (i + 1) * quarter]
            if s == 0:
                pack[i : i + 1, :] = piece
            else:
                pack[i : i + 1, :] += piece
    pack_copies = dp_copies(pack, packs, psend, precv)
    for c in pack_copies:
        c.start()
    packs[d] = pack[...]
    for g in scatters[2:]:
        g.third()
    for c in small_copies:
        c.wait_recv()
    sum_ = small_all[0]
    for i in range(1, 8):
        sum_ = sum_ + small_all[i]
    smalls[...] = sum_
    for c in pack_copies:
        c.wait_recv()
    sum_ = packs[0]
    for i in range(1, 8):
        sum_ = sum_ + packs[i]
    line_pack[...] = sum_
    z_copies = [
        pltpu.make_async_remote_copy(
            src_ref=line_pack,
            dst_ref=line_packs.at[t],
            send_sem=zsend.at[step - 1],
            recv_sem=zrecv.at[step - 1],
            device_id=(d, lax.rem(t + step, depth)),
            device_id_type=MESH,
        )
        for step in range(1, depth)
    ]
    for c in z_copies:
        c.start()
    line_packs[t] = sum_
    for g in scatters[1:]:
        g.end()
    for c in z_copies:
        c.wait_recv()
    sum_ = line_packs[0]
    for i in range(1, depth):
        sum_ = sum_ + line_packs[i]
    gains[...] = sum_
    for c in small_copies + pack_copies + z_copies:
        c.wait_send()
    line.end()


def last_phase(
    part, act, gain, grad_middle, mlp_part, small, branch, normed, mixed, gelu_grad, input_grad,
    gate_in_grad, gate_dec_grad, depth,
):
    seqs, rows, model = act.shape
    width = mixed.shape[1]
    mixer, gate = (model // 8, width), (gate_in_grad.shape[0] // 8, width)
    shapes = [mixer] * 3 + [gate] * 2
    pack = (8, model // 4)
    outs = [
        shaped(act.shape, F32, VMEM),
        shaped(pack, F32, VMEM),
        shaped(small.shape, F32, VMEM),
    ] + [shaped(s, F32, VMEM) for s in shapes]
    scratch = (
        line_scatter_scratch(seqs, rows, model, depth)
        + [
            pltpu.VMEM(pack, F32),
            pltpu.VMEM((8,) + pack, F32),
            pltpu.VMEM((8,) + small.shape, F32),
            pltpu.VMEM(pack, F32),
            pltpu.VMEM((depth,) + pack, F32),
        ]
        + [DMA((7,))] * 4
        + [DMA((depth - 1,))] * 2
        + [
            pltpu.VMEM(x.shape, BF16) for x in (branch, normed, mixed, gelu_grad, input_grad)
        ]
        + [pltpu.VMEM((model, width), BF16)] * 3
        + [DMA((5,))]
        + scatter_scratch(shapes, (False, False, False, True, True))
    )
    res = call(
        functools.partial(last_kernel, depth),
        "last_phase",
        4,
        [VMEM] * 6 + [ANY] * 7,
        outs,
        scratch,
        (
            part,
            act,
            gain.reshape(1, model),
            grad_middle,
            mlp_part,
            small,
            branch,
            normed,
            mixed,
            gelu_grad,
            input_grad,
            gate_in_grad,
            gate_dec_grad,
        ),
    )
    return res[0], res[1].reshape(2, model), res[2], res[3:]


def swapped(block, axis):
    count = lax.axis_size(axis)
    return lax.ppermute(block, axis, [(i, i ^ 1) for i in range(count)])


def normalize(value_entries, scale_gain):
    return (
        value_entries
        * lax.rsqrt(jnp.mean(value_entries * value_entries, axis=-1, keepdims=True) + EPS)
        * scale_gain
    )


def causal_conv(value_entries, kernel):
    summed = value_entries * kernel[0]
    for offset in range(1, kernel.shape[0]):
        shifted = jnp.concatenate(
            [jnp.zeros_like(value_entries[:, :offset]), value_entries[:, :-offset]], axis=1
        )
        summed = summed + shifted * kernel[offset]
    return summed


def decay_inputs(input_pre, decay_pre, conv_vals, decay_rate):
    log_decay = -8.0 * jax.nn.sigmoid(decay_pre) * decay_rate
    scaled = jnp.sqrt(-jnp.expm1(2.0 * log_decay))
    return (log_decay, scaled * jax.nn.sigmoid(input_pre) * conv_vals)


def recurrence(rate, drive):
    def join(left, right):
        return left[0] * right[0], left[1] * right[0] + right[1]

    return lax.associative_scan(join, (rate, drive), axis=1)[1]


def dot(spec, left, right):
    return jnp.einsum(spec, left, right, preferred_element_type=F32)


def weight_grad(left, right):
    return dot("pkr,pku->ru", left, right).astype(BF16)


class Fast:
    def __init__(self, depth, taps, rate):
        self.depth, self.taps, self.rate = depth, taps, rate

    def first(self, normed, cot, weights):
        normed_all, cot_all, weights, saved, part = first_phase(
            normed, cot, weights, self.taps, self.rate, self.depth
        )
        self.saved, self.weights, self.normed = saved, weights, normed_all
        return cot_all, weights[5].reshape(-1, weights[5].shape[-1]), part

    def middle(self, part, act, gain, w0, w1):
        middle, wide, w0, w1 = middle_phase(part, act, gain, w0, w1, self.depth)
        return middle, wide, w0.reshape(-1, w0.shape[-1]), w1.reshape(-1, w1.shape[-1])

    def back(self, part, middle, gain, cot, g0, g1):
        return back_phase(part, middle, gain, cot, g0, g1, self.depth)

    def last(self, branch, up, feed, act, gain, middle, grad_middle, mlp_part):
        part, gelu_grad, input_rows, gate_in, gate_dec, small, output, up = mixer_back_phase(
            branch, self.saved, self.weights, up, feed, middle, self.taps, self.rate, self.depth
        )
        input_grad, gains, small, grads = last_phase(
            part,
            act,
            gain,
            grad_middle,
            mlp_part,
            small,
            branch,
            self.normed,
            self.saved[-1],
            gelu_grad,
            input_rows,
            gate_in,
            gate_dec,
            self.depth,
        )
        return output, input_grad, gains, small, grads, up


class Plain:
    def __init__(self, depth, taps, rate):
        self.depth, self.taps, self.rate = depth, taps, rate

    @staticmethod
    def wide(block):
        return lax.all_gather(block, "tensor", axis=1, tiled=True)

    @staticmethod
    def narrow(part):
        return lax.psum_scatter(part, "tensor", scatter_dimension=1, tiled=True).astype(F32)

    @staticmethod
    def full(shard):
        return lax.all_gather(shard, "dp", axis=0, tiled=True)

    @staticmethod
    def own(grad):
        return lax.psum_scatter(grad, "dp", scatter_dimension=0, tiled=True).astype(F32)

    def first(self, normed, cot, weights):
        gelu_w, input_w, gate_in_w, gate_dec_w, out_w, up_w = (self.full(w) for w in weights)
        normed_all = self.wide(normed)
        seqs, length, _ = normed_all.shape
        channels = gelu_w.shape[1]
        block = gate_in_w.shape[0]
        half = block // 2
        width = channels + half
        parity = lax.axis_index("tensor") % 2
        gelu_pre = dot("kqg,ga->kqa", normed_all, gelu_w)
        input_pre = dot("kqg,ga->kqa", normed_all, input_w)
        gelu_out, gelu_back = jax.vjp(jax.nn.gelu, gelu_pre)
        conv_out, conv_back = jax.vjp(causal_conv, input_pre, self.taps)
        conv_bf = conv_out.astype(BF16)
        rim = lax.dynamic_slice_in_dim(conv_bf, (1 - parity) * (channels - half), half, 2)
        window = jnp.zeros((seqs, length, width), BF16)
        window = lax.dynamic_update_slice_in_dim(window, conv_bf, parity * half, 2)
        window = lax.dynamic_update_slice_in_dim(
            window, swapped(rim, "tensor"), (1 - parity) * channels, 2
        )
        tiles = window.reshape(seqs, length, width // block, block)
        placed = lax.dynamic_update_slice_in_dim(
            jnp.zeros((2, block, width), BF16), jnp.stack([gate_in_w, gate_dec_w]), parity * half, 2
        ).reshape(2, block, width // block, block)
        gates = dot("slbk,gkbc->gslbc", tiles, placed).reshape(2, seqs, length, width)
        gates = lax.dynamic_slice_in_dim(gates, parity * half, channels, 3)
        (log_decay, drive), gate_back = jax.vjp(
            decay_inputs, gates[0], gates[1], conv_bf.astype(F32), self.rate
        )
        decay = jnp.exp(log_decay)
        states = recurrence(decay, drive)
        mixed = (gelu_out * states).astype(BF16)
        self.kept = (
            normed_all, gelu_w, input_w, out_w, gelu_out, gelu_back, conv_back, tiles, placed,
            gate_back, decay, states, mixed,
        )
        part = dot("xgq,pq->xgp", mixed, out_w).astype(BF16)
        return self.wide(cot), up_w, part

    def middle(self, part, act, gain, w0, w1):
        middle = act.astype(F32) + self.narrow(part)
        wide = self.wide(normalize(middle, gain).astype(BF16))
        return middle, wide, self.full(w0), self.full(w1)

    def back(self, part, middle, gain, cot, g0, g1):
        _, back = jax.vjp(normalize, middle, gain)
        change, gain_grad = back(self.narrow(part))
        grad = cot + change
        return grad, self.wide(grad.astype(BF16)), gain_grad[None], self.own(g0), self.own(g1)

    def last(self, branch, up, feed, act, gain, middle, grad_middle, mlp_part):
        (
            normed_all, gelu_w, input_w, out_w, gelu_out, gelu_back, conv_back, tiles, placed,
            gate_back, decay, states, mixed,
        ) = self.kept
        seqs, length, channels = states.shape
        block = tiles.shape[-1]
        half = block // 2
        width = channels + half
        parity = lax.axis_index("tensor") % 2
        grad_mixed = dot("xtz,zm->xtm", branch, out_w)
        gelu_grad = gelu_back(grad_mixed * states)[0].astype(BF16)
        later = jnp.concatenate([decay[:, 1:], jnp.zeros_like(decay[:, :1])], axis=1)
        grad_drive = jnp.flip(
            recurrence(jnp.flip(later, 1), jnp.flip(grad_mixed * gelu_out, 1)), 1
        )
        earlier = jnp.concatenate([jnp.zeros_like(states[:, :1]), states[:, :-1]], axis=1)
        grad_in, grad_dec, grad_conv, grad_rate = gate_back(
            (grad_drive * decay * earlier, grad_drive)
        )
        grads = lax.dynamic_update_slice_in_dim(
            jnp.zeros((2, seqs, length, width), BF16),
            jnp.stack([grad_in, grad_dec]).astype(BF16),
            parity * half,
            3,
        ).reshape(2, seqs, length, width // block, block)
        grad_window = dot("gslbc,gkbc->slbk", grads, placed).reshape(seqs, length, width)
        grad_placed = dot("slbk,gslbc->gkbc", tiles, grads).reshape(2, block, width)
        grad_gates = lax.dynamic_slice_in_dim(grad_placed, parity * half, channels, 2)
        rim = lax.dynamic_slice_in_dim(grad_window, (1 - parity) * channels, half, 2)
        rim = swapped(rim.astype(BF16), "tensor").astype(F32)
        grad_conv = grad_conv + lax.dynamic_slice_in_dim(grad_window, parity * half, channels, 2)
        start = (1 - parity) * (channels - half)
        rim = lax.dynamic_slice_in_dim(grad_conv, start, half, 2) + rim
        grad_conv = lax.dynamic_update_slice_in_dim(grad_conv, rim, start, 2)
        input_rows, grad_taps = conv_back(grad_conv)
        input_rows = input_rows.astype(BF16)
        part = dot("mzf,af->mza", gelu_grad, gelu_w) + dot("mzf,af->mza", input_rows, input_w)
        _, back = jax.vjp(normalize, act.astype(F32), gain)
        change, gain_grad = back(self.narrow(part.astype(BF16)))
        output = (middle + self.narrow(feed)).astype(BF16)
        gains = lax.psum(jnp.concatenate([gain_grad[None], mlp_part]), ("dp", "tensor"))
        small = lax.psum(jnp.concatenate([grad_rate[None], grad_taps]), "dp")
        parts = (
            weight_grad(branch, mixed),
            weight_grad(normed_all, gelu_grad),
            weight_grad(normed_all, input_rows),
            grad_gates[0].astype(BF16),
            grad_gates[1].astype(BF16),
        )
        own = [self.own(g) for g in parts]
        return output, grad_middle + change, gains, small, own, self.own(up)


def shards(
    activations,
    norm_gain,
    gelu_proj,
    input_proj,
    conv_weight,
    gate_input,
    gate_decay,
    decay_rate,
    out_proj,
    mlp_gain,
    feed_gate,
    feed_up,
    feed_down,
    cotangent,
    lengths,
    batch_of,
):
    depth = lax.axis_size("tensor")
    fast = lax.axis_size("dp") == 8 and depth == 4
    run = (Fast if fast else Plain)(depth, conv_weight, decay_rate)
    tensor_index = lax.axis_index("tensor")
    data_index = lax.axis_index("dp")
    seq_count, row_count, _ = activations.shape
    full_length = row_count * depth
    members = (batch_of[:, None] == jnp.arange(MICRO)[None, :]).astype(F32)
    counts = jnp.sum(members * lengths[:, None].astype(F32), axis=0)
    total_seqs = lengths.shape[0]
    per_batch = float(total_seqs * full_length) / (MICRO * counts)
    weight_all = jnp.sum(members * per_batch[None, :], axis=1)
    my_weight = lax.dynamic_slice_in_dim(weight_all, data_index * seq_count, seq_count)
    my_length = lax.dynamic_slice_in_dim(lengths, data_index * seq_count, seq_count)
    places = tensor_index * row_count + jnp.arange(row_count)
    valid_mask = (places[None, :] < my_length[:, None]).astype(F32)
    scaled_cot = cotangent.astype(F32) * (valid_mask * my_weight[:, None])[:, :, None]
    normed = normalize(activations.astype(F32), norm_gain).astype(BF16)

    cot_all, up_w, branch_part = run.first(
        normed,
        scaled_cot.astype(BF16),
        (gelu_proj, input_proj, gate_input, gate_decay, out_proj.T, feed_up),
    )
    middle, normed_two_all, gate_w, down_w = run.middle(
        branch_part, activations, mlp_gain, feed_gate, feed_down.T
    )
    gate_pre = dot("nwo,ob->nwb", normed_two_all, gate_w)
    lift_pre = dot("nwo,ob->nwb", normed_two_all, up_w)
    gate_act, activ_back = jax.vjp(jax.nn.gelu, gate_pre)
    hidden = (gate_act * lift_pre).astype(BF16)
    grad_hidden = dot("gre,eu->gru", cot_all, down_w)
    gate_grad = activ_back(grad_hidden * lift_pre)[0].astype(BF16)
    lift_grad = (grad_hidden * gate_act).astype(BF16)
    back_two = dot("mqa,ya->mqy", gate_grad, gate_w) + dot("mqa,ya->mqy", lift_grad, up_w)
    grad_down_part = weight_grad(cot_all, hidden)
    grad_gate_part = weight_grad(normed_two_all, gate_grad)
    grad_lift_part = weight_grad(normed_two_all, lift_grad)
    feed_part = dot("xav,tv->xat", hidden, down_w).astype(BF16)

    grad_middle, branch_grad_all, mlp_part, grad_down, grad_gate = run.back(
        back_two.astype(BF16), middle, mlp_gain, scaled_cot, grad_down_part, grad_gate_part
    )
    output, input_grad, gains, small, grads, grad_up = run.last(
        branch_grad_all,
        grad_lift_part,
        feed_part,
        activations,
        norm_gain,
        middle,
        grad_middle,
        mlp_part,
    )
    return (
        output,
        input_grad,
        gains[0],
        grads[1],
        grads[2],
        small[1:5],
        grads[3],
        grads[4],
        small[0],
        grads[0].T,
        gains[1],
        grad_gate,
        grad_up,
        grad_down.T,
    )


def solution(mesh):
    placed = (
        P("dp", "tensor", None),
        P(),
        P("dp", "tensor"),
        P("dp", "tensor"),
        P(None, "tensor"),
        P("dp", "tensor"),
        P("dp", "tensor"),
        P("tensor"),
        P("tensor", "dp"),
        P(),
        P("dp", "tensor"),
        P("dp", "tensor"),
        P("tensor", "dp"),
        P("dp", "tensor", None),
        P(),
        P(),
    )
    return jax.shard_map(
        shards,
        mesh=mesh,
        in_specs=placed,
        out_specs=(
            P("dp", "tensor", None),
            P("dp", "tensor", None),
            P(),
            P("dp", "tensor"),
            P("dp", "tensor"),
            P(None, "tensor"),
            P("dp", "tensor"),
            P("dp", "tensor"),
            P("tensor"),
            P("tensor", "dp"),
            P(),
            P("dp", "tensor"),
            P("dp", "tensor"),
            P("tensor", "dp"),
        ),
        check_vma=False,
    )
```

time: 596 us -> 537 us (0.901)
  matrix products: 125 us -> 87.9 us
  local copies, waits for them, and re-layouts: 44.8 us -> 21.3 us
  Pallas kernels: 390 us -> 413 us
  other arithmetic: 19.8 us -> 6.71 us
    dot_general x21 -> x9, matrix products: 125 us -> 87.9 us  [dot(): return jnp.einsum(spec, left, right, preferred_element_type=F32)]
    pallas_call x4 -> x5, Pallas kernels: 388 us -> 413 us  [call(): pl.pallas_call(kernel, name=name, out_shape=[o[0] for o in outs], in_spec...]
    unnamed x126 -> x58, local copies, waits for them, and re-layouts: 28.2 us -> 14 us
  transfers between devices with their start and end apart: 2 -> 0, of which waited for: 2 -> 0; matrix products, arithmetic and copies ran while one was open for 1% -> 0% of each run, Pallas kernels for 0% -> 0%
where the time goes in v3:
time: 537 us; the launch traced here: 530 us
  Pallas kernels  413 us (77%)
  matrix products  87.9 us (16%)
  local copies, waits for them, and re-layouts  21.3 us (4%)
  other arithmetic  6.71 us (1%)
    pallas_call x5, Pallas kernels, call(): pl.pallas_call(kernel, name=name, out_shape=[o[0] for o in outs], in_spec...  413 us
    dot_general x9, matrix products, dot(): return jnp.einsum(spec, left, right, preferred_element_type=F32)  87.9 us
    unnamed x58, local copies, waits for them, and re-layouts  14 us

profile of v3, /device:TPU:0, one launch (start us, length us, event | category | flops | bytes accessed | tf_op | source)
XLA Modules:
  0.0 530.3 jit_solution(17873265180148974739)
XLA Ops:
  0.7 0.7 convert_element_type.45
  1.3 0.8 select_reduce_fusion.1
  2.1 0.7 select_reduce_fusion
  2.8 0.1 dynamic_slice.7
  2.9 0.7 dynamic_slice.6
  3.7 0.1 compare_select_fusion
  3.7 1.3 fusion.7
  5.0 3.1 convert_multiply_fusion.2
  8.2 0.6 reshape.117.rate
  8.8 102.9 %first_phase.1 = (bf16[2,256,2560]{2,1,0:T(8,128)(2,1)}, bf16[2,256,2560]{2,1,0:T(8,128)(2,1)}, bf16[2560,640]{1,0:T(8,128)(2,1)}, bf16[2560,640]{1,0:T(8,128)(2...) custom-call(bf16[2,64,2560]{2,1,0:T(8,128)(2,1)} %get-tuple-element., ...), custom_call_target="tpu_custom_call" | custom-call | tf_op jit(solution)/shard_map/first_phase/pallas_call | solution.py:435
  111.7 0.6 reshape.118.gain
  112.3 92.8 %middle_phase.1 = (f32[2,64,2560]{2,1,0:T(8,128)}, bf16[2,256,2560]{2,1,0:T(8,128)(2,1)}, bf16[8,320,1920]{2,1,0:T(8,128)(2,1)}, bf16[8,320,1920]{2,1,0:T(8,128)(2,1)}) custom-call(bf16[2,256,2560]{2,1,0:T(8,128)(2,1)} %get-tuple-element.57.part, bf16[2,64,2560]{2,1,0:T(8,128)(2,1)} %act.3, f32[1,2560]{1,0:T(1,128)} %reshape.118.gain, bf16[320,1920]{1,0:T(8,128)(2,1)} %w0.1, ...), custom_call_target="tpu_custom_call" | custom-call | tf_op jit(solution)/shard_map/middle_phase/pallas_call | solution.py:435
  205.1 0.0 slice-start
  205.2 0.0 slice-start.1
  205.2 11.7 %fusion.13 = f32[2,256,1920]{2,1,0:T(8,128)} fusion(bf16[2,256,2560]{2,1,0:T(8,128)(2,1)} %get-tuple-element.59, bf16[2560,1920,1]{1,0,2:T(8,128)(2,1)} %bitcast.47), kind=kOutput, calls=%fused_computation.34 | convolution fusion | flops 5033164800 | bytes 16384000 | tf_op jit(solution)/shard_map/nwo,ob->nwb/dot_general | solution.py:1544
  216.9 0.0 slice-start.3
  216.9 0.0 slice-start.4
  216.9 7.5 %fusion.12 = f32[2,256,1920]{2,1,0:T(8,128)} fusion(bf16[2,256,2560]{2,1,0:T(8,128)(2,1)S(1)} %copy-done.13, bf16[2560,1920,1]{1,0,2:T(8,128)(2,1)S(1)} %bitcast.42), kind=kOutput, calls=%fused_computation.33 | convolution fusion | flops 5033164800 | bytes 16384000 | tf_op jit(solution)/shard_map/gre,eu->gru/dot_general | solution.py:1544
  224.5 0.0 slice-start.5
  224.5 13.2 %multiply_convert_fusion = (bf16[2,256,1920]{2,1,0:T(8,128)(2,1)}, bf16[2,256,1920]{2,1,0:T(8,128)(2,1)}, bf16[2,256,1920]{2,1,0:T(8,128)(2,1)}) fusion(f32[2,256,1920]{2,1,0:T(8,128)} %fusion.13, f32[2,256,1920]{2,1,0:T(8,128)} %fusion.12, bf16[2,256,2560]{2,1,0:T(8,128)(2,1)} %get-tuple-element.59, bf16[2560,1920,1]{1,0,2:T(8,128)(2,1)S(1)} %bitcast.45), kind=kOutput, calls=%fused_computation.14 | convolution fusion | flops 5058723840 | bytes 26214400 | tf_op jit(solution)/shard_map/nwo,ob->nwb/dot_general | solution.py:1544
  237.7 8.7 %fusion.14 = f32[2,256,2560]{2,1,0:T(8,128)} fusion(bf16[2,256,1920]{2,1,0:T(8,128)(2,1)} %get-tuple-element.99, bf16[2560,1920,1]{1,0,2:T(8,128)(2,1)S(1)} %bitcast.50), kind=kOutput, calls=%fused_computation.35 | convolution fusion | flops 5033164800 | bytes 17039360 | tf_op jit(solution)/shard_map/mqa,ya->mqy/dot_general | solution.py:1544
  246.4 9.5 %add_convert_fusion.part = bf16[2,256,2560]{2,1,0:T(8,128)(2,1)} fusion(f32[2,256,2560]{2,1,0:T(8,128)} %fusion.14, bf16[2,256,1920]{2,1,0:T(8,128)(2,1)} %get-tuple-element.100, bf16[2560,1920,1]{1,0,2:T(8,128)(2,1)S(1)} %bitcast.46), kind=kOutput, calls=%fused_computation.5 | convolution fusion | flops 5035786240 | bytes 19660800 | tf_op jit(solution)/shard_map/mqa,ya->mqy/dot_general | solution.py:1544
  255.9 8.5 %bitcast_convert_fusion.2.g0 = bf16[2560,1920]{1,0:T(8,128)(2,1)} fusion(bf16[2,256,2560]{2,1,0:T(8,128)(2,1)S(1)} %copy-done.13, bf16[2,256,1920]{2,1,0:T(8,128)(2,1)S(1)} %copy-done.16), kind=kOutput, calls=%fused_computation.2 | convolution fusion | flops 5038080000 | bytes 14417920 | tf_op jit(solution)/shard_map/pkr,pku->ru/dot_general | solution.py:1544
  264.4 8.1 %bitcast_convert_fusion.1.g1 = bf16[2560,1920]{1,0:T(8,128)(2,1)} fusion(bf16[2,256,2560]{2,1,0:T(8,128)(2,1)S(1)} %copy-done.14, bf16[2,256,1920]{2,1,0:T(8,128)(2,1)S(1)} %copy-done.15), kind=kOutput, calls=%fused_computation.1 | convolution fusion | flops 5038080000 | bytes 14417920 | tf_op jit(solution)/shard_map/pkr,pku->ru/dot_general | solution.py:1544
  272.6 94.1 %back_phase.1 = (f32[2,64,2560]{2,1,0:T(8,128)}, bf16[2,256,2560]{2,1,0:T(8,128)(2,1)}, f32[1,2560]{1,0:T(1,128)}, f32[320,1920]{1,0:T(8,128)}, f32[320,1920]{1,0:T(8,128)}) custom-call(bf16[2,256,2560]{2,1,0:T(8,128)(2,1)} %add_convert_fusion.part, f32[2,64,2560]{2,1,0:T(8,128)} %get-tuple-element.62.middle, f32[1,2560]{1,0:T(1,128)} %reshape.118.gain, ...), custom_call_target="tpu_custom_call" | custom-call | tf_op jit(solution)/shard_map/back_phase/pallas_call | solution.py:435
  366.7 0.0 copy-start.17
  366.7 9.7 %bitcast_convert_fusion.up_in = bf16[2560,1920]{1,0:T(8,128)(2,1)} fusion(bf16[2,256,2560]{2,1,0:T(8,128)(2,1)S(1)} %copy-done.14, bf16[2,256,1920]{2,1,0:T(8,128)(2,1)} %get-tuple-element.100), kind=kOutput, calls=%fused_computation | convolution fusion | flops 5038080000 | bytes 14417920 | tf_op jit(solution)/shard_map/pkr,pku->ru/dot_general | solution.py:1544
  376.5 10.9 %convolution_convert_fusion.feed = bf16[2,256,2560]{2,1,0:T(8,128)(2,1)} fusion(bf16[2,256,1920]{2,1,0:T(8,128)(2,1)S(1)} %copy-done.17, bf16[2560,1920,1]{1,0,2:T(8,128)(2,1)} %bitcast.41), kind=kOutput, calls=%fused_computation.6 | convolution fusion | flops 5034475520 | bytes 14417920 | tf_op jit(solution)/shard_map/xav,tv->xat/dot_general | solution.py:1544
  387.3 62.0 %mixer_back_phase.1 = (bf16[2,256,2560]{2,1,0:T(8,128)(2,1)}, bf16[512,640]{1,0:T(8,128)(2,1)}, bf16[512,640]{1,0:T(8,128)(2,1)}, bf16[256,640]{1,0:T(8,128)(2,1...) custom-call(bf16[2,256,2560]{2,1,0:T(8,128)(2,1)} %get-tuple-element.63.bra, ...), custom_call_target="tpu_custom_call" | custom-call | tf_op jit(solution)/shard_map/mixer_back_phase/pallas_call | solution.py:435
  449.4 0.6 reshape.122.gain
  450.0 61.4 %last_phase.1 = (f32[2,64,2560]{2,1,0:T(8,128)}, f32[8,640]{1,0:T(8,128)}, f32[8,640]{1,0:T(8,128)}, f32[320,640]{1,0:T(8,128)}, f32[320,640]{1,0:T(8,128)}, /*i...) custom-call(bf16[2,256,2560]{2,1,0:T(8,128)(2,1)} %get-tuple-element.77.part, bf16[2,64,2560]{2,1,0:T(8,128)(2,1)} %act.3, ...), custom_call_target="tpu_custom_call" | custom-call | tf_op jit(solution)/shard_map/last_phase/pallas_call | solution.py:435
  511.4 0.8 fusion.11
  512.3 0.6 squeeze.9
  512.9 1.3 slice.15
  514.2 1.3 slice_reduce_fusion
  515.5 0.6 squeeze.11
  516.1 0.8 copy.49
  517.0 2.5 copy.50
  519.5 0.9 copy.51
  520.4 0.9 copy.52
  521.3 0.6 copy.53
  522.0 0.6 copy.54
  522.6 0.9 copy.55
  523.5 1.4 copy.56
  524.9 1.1 copy-done.2
  526.1 1.4 copy.57
  527.5 1.1 copy-done
  528.7 1.4 copy.58
  (45 shorter events, 0.1 us)
Async XLA Ops:
  0.6 7.5 %copy-start.11 = (f32[640]{0:T(1024)S(1)}, f32[640]{0:T(1024)}, u32[]{:S(2)}) copy-start(f32[640]{0:T(1024)} %param.23) | copy-start | bytes 7684
  8.2 103.5 %copy-start.10 = (f32[2560]{0:T(1024)S(1)}, f32[2560]{0:T(1024)}, u32[]{:S(2)}) copy-start(f32[2560]{0:T(1024)} %param.25) | copy-start | bytes 30724
  205.1 11.8 %copy-start.12 = (bf16[8,320,1920]{2,1,0:T(8,128)(2,1)S(1)}, bf16[8,320,1920]{2,1,0:T(8,128)(2,1)}, u32[]{:S(2)}) copy-start(bf16[8,320,1920]{2,1,0:T(8,128)(2,1)} %get-tuple-element.58) | copy-start | bytes 29491204
  205.1 11.8 %copy-start.13 = (bf16[2,256,2560]{2,1,0:T(8,128)(2,1)S(1)}, bf16[2,256,2560]{2,1,0:T(8,128)(2,1)}, u32[]{:S(2)}) copy-start(bf16[2,256,2560]{2,1,0:T(8,128)(2,1)} %get-tuple-element.56) | copy-start | bytes 7864324
  205.1 19.3 %slice-start = ((s8[9830400]{0:T(1024)(128)(4,1)}), s8[4194304]{0:T(1024)(128)(4,1)S(1)}, s32[]{:S(2)}) async-start(s8[9830400]{0:T(1024)(128)(4,1)} %bitcast.43), calls=%async_computation | async-start | bytes 8388608
  205.2 19.3 %slice-start.1 = ((s8[9830400]{0:T(1024)(128)(4,1)}), s8[4194304]{0:T(1024)(128)(4,1)S(1)}, s32[]{:S(2)}) async-start(s8[9830400]{0:T(1024)(128)(4,1)} %bitcast.43), calls=%async_computation.1 | async-start | bytes 8388608
  216.9 7.6 %slice-start.2 = ((s8[9830400]{0:T(1024)(128)(4,1)}), s8[1441792]{0:T(1024)(128)(4,1)S(1)}, s32[]{:S(2)}) async-start(s8[9830400]{0:T(1024)(128)(4,1)} %bitcast.43), calls=%async_computation.2 | async-start | bytes 2883584
  216.9 20.7 %slice-start.3 = ((s8[9830400]{0:T(1024)(128)(4,1)}), s8[4194304]{0:T(1024)(128)(4,1)S(1)}, s32[]{:S(2)}) async-start(s8[9830400]{0:T(1024)(128)(4,1)} %bitcast.48), calls=%async_computation.3 | async-start | bytes 8388608
  216.9 20.7 %slice-start.4 = ((s8[9830400]{0:T(1024)(128)(4,1)}), s8[4194304]{0:T(1024)(128)(4,1)S(1)}, s32[]{:S(2)}) async-start(s8[9830400]{0:T(1024)(128)(4,1)} %bitcast.48), calls=%async_computation.4 | async-start | bytes 8388608
  224.5 13.2 %slice-start.5 = ((s8[9830400]{0:T(1024)(128)(4,1)}), s8[1441792]{0:T(1024)(128)(4,1)S(1)}, s32[]{:S(2)}) async-start(s8[9830400]{0:T(1024)(128)(4,1)} %bitcast.48), calls=%async_computation.5 | async-start | bytes 2883584
  246.4 9.5 %copy-start.16 = (bf16[2,256,1920]{2,1,0:T(8,128)(2,1)S(1)}, bf16[2,256,1920]{2,1,0:T(8,128)(2,1)}, u32[]{:S(2)}) copy-start(bf16[2,256,1920]{2,1,0:T(8,128)(2,1)} %get-tuple-element.98) | copy-start | bytes 5898244
  255.9 8.5 %copy-start.14 = (bf16[2,256,2560]{2,1,0:T(8,128)(2,1)S(1)}, bf16[2,256,2560]{2,1,0:T(8,128)(2,1)}, u32[]{:S(2)}) copy-start(bf16[2,256,2560]{2,1,0:T(8,128)(2,1)} %get-tuple-element.59) | copy-start | bytes 7864324
  255.9 8.5 %copy-start.15 = (bf16[2,256,1920]{2,1,0:T(8,128)(2,1)S(1)}, bf16[2,256,1920]{2,1,0:T(8,128)(2,1)}, u32[]{:S(2)}) copy-start(bf16[2,256,1920]{2,1,0:T(8,128)(2,1)} %get-tuple-element.99) | copy-start | bytes 5898244
  366.7 9.8 %copy-start.17 = (bf16[2,256,1920]{2,1,0:T(8,128)(2,1)S(1)}, bf16[2,256,1920]{2,1,0:T(8,128)(2,1)}, u32[]{:S(2)}) copy-start(bf16[2,256,1920]{2,1,0:T(8,128)(2,1)} %get-tuple-element.98) | copy-start | bytes 5898244
  387.3 62.0 %copy-start.9 = (f32[2560]{0:T(1024)S(1)}, f32[2560]{0:T(1024)}, u32[]{:S(2)}) copy-start(f32[2560]{0:T(1024)} %param.17) | copy-start | bytes 30724
  450.0 66.1 %copy-start.6 = (bf16[2,64,2560]{2,1,0:T(8,128)(2,1)S(1)}, bf16[2,64,2560]{2,1,0:T(8,128)(2,1)}, u32[]{:S(2)}) copy-start(bf16[2,64,2560]{2,1,0:T(8,128)(2,1)} %get-tuple-element.120) | copy-start | bytes 1966084
  511.4 8.1 %copy-start.5 = (f32[320,640]{1,0:T(8,128)S(1)}, f32[320,640]{1,0:T(8,128)}, u32[]{:S(2)}) copy-start(f32[320,640]{1,0:T(8,128)} %get-tuple-element.123) | copy-start | bytes 2457604
  516.1 4.3 copy-start.4
  517.0 4.3 copy-start.8
  517.0 5.0 copy-start.7
  517.0 5.6 %copy-start.3 = (f32[320,640]{1,0:T(8,128)S(1)}, f32[320,640]{1,0:T(8,128)}, u32[]{:S(2)}) copy-start(f32[320,640]{1,0:T(8,128)} %get-tuple-element.94) | copy-start | bytes 2457604
  519.5 4.0 copy-start.1
  523.5 2.6 copy-start.2
  526.1 2.6 copy-start

commit v4 on v3

--- a/solution.py
+++ b/solution.py
@@ -141,6 +141,10 @@
 
     def __init__(self, grad, out, own, core, diag, last, local, send, recv, d, t):
         self.out, self.core, self.diag, self.last = out, core, diag, last
+        self.grad, self.d, self.t = grad, d, t
+        self.credit = None
+        self.reused = self.again = False
+        self.before = self.flush = None
         self.rows = rows = out.shape[0]
         half = rows // 2
         self.half = half
@@ -180,6 +184,8 @@
         ]
 
     def start(self):
+        if self.reused:
+            pl.semaphore_wait(self.credit.at[0], 1)
         for i in range(4):
             self.copies[i].start()
         for load in self.loads:
@@ -193,7 +199,11 @@
 
     def first(self):
         self.pair(0)
+        if self.reused:
+            pl.semaphore_wait(self.credit.at[1], 1)
         self.copies[4].start()
+        if self.reused:
+            pl.semaphore_wait(self.credit.at[2], 1)
         self.copies[5].start()
 
     def second(self):
@@ -217,6 +227,8 @@
             self.copies[i].wait_recv()
         step = 16
         own = self.mine(3)
+        if self.before is not None:
+            self.before.flush.wait()
 
         @pl.loop(0, self.rows, step=step)
         def _(start):
@@ -227,8 +239,61 @@
                 + self.last[1, part, :].astype(F32)
             )
 
+        if self.flush is not None:
+            self.flush.start()
         for i in range(10):
             self.copies[i].wait_send()
+        if self.again:
+            for i, mask in enumerate((1, 2, 4)):
+                pl.semaphore_signal(
+                    self.credit.at[i], inc=1, device_id=(self.d ^ mask, self.t), device_id_type=MESH
+                )
+
+
+class PanelRing:
+    def __init__(self, outs, scratch, d, t):
+        grads, core, diag, last, stage, send, recv, credit, flush = scratch
+        self.slots = slots = grads.shape[0]
+        self.panels = []
+        for i, out in enumerate(outs):
+            q = i % slots
+            panel = GradScatter(
+                grads.at[q],
+                stage.at[q],
+                None,
+                core.at[q],
+                diag.at[q],
+                last.at[q],
+                None,
+                send.at[q],
+                recv.at[q],
+                d,
+                t,
+            )
+            panel.credit = credit.at[q]
+            panel.reused = i >= slots
+            panel.again = i + slots < len(outs)
+            panel.before = self.panels[i - slots] if i >= slots else None
+            panel.flush = pltpu.make_async_copy(stage.at[q], out, flush.at[q])
+            self.panels.append(panel)
+
+    def end(self):
+        for panel in self.panels[-self.slots :]:
+            panel.flush.wait()
+
+
+def ring_scratch(slots, rows, n):
+    return [
+        pltpu.VMEM((slots, 8 * rows, n), BF16),
+        pltpu.VMEM((slots, 4, rows, n), BF16),
+        pltpu.VMEM((slots, 2, rows // 2, n), BF16),
+        pltpu.VMEM((slots, 2, rows, n), BF16),
+        pltpu.VMEM((slots, rows, n), F32),
+        DMA((slots, 10)),
+        DMA((slots, 10)),
+        pltpu.SemaphoreType.REGULAR((slots, 3)),
+        DMA((slots,)),
+    ]
 
 
 def scatter_scratch(shapes, loaded):
@@ -268,11 +333,12 @@
     def __init__(self, block, out, local, send, recv, d, t, depth):
         self.block, self.out, self.send, self.recv = block, out, send, recv
         self.d, self.t, self.depth = d, t, depth
-        self.rows = block.shape[1]
+        self.rows = block.shape[-2]
         self.own = pltpu.make_async_copy(block, self.slot(t), local)
 
     def slot(self, j):
-        return self.out.at[:, pl.ds(pl.multiple_of(j * self.rows, self.rows), self.rows)]
+        rows = pl.ds(pl.multiple_of(j * self.rows, self.rows), self.rows)
+        return self.out.at[:, rows] if len(self.out.shape) == 3 else self.out.at[rows]
 
     def copy(self, way, step, j, to):
         return pltpu.make_async_remote_copy(
@@ -330,10 +396,10 @@
 
 
 class LineScatter:
-    def __init__(self, part, got, send, recv, d, t, depth):
+    def __init__(self, part, got, send, recv, d, t, depth, which=None):
         self.part, self.got, self.send, self.recv = part, got, send, recv
         self.d, self.t, self.depth = d, t, depth
-        self.seqs = part.shape[0]
+        self.which = range(part.shape[0]) if which is None else which
         self.rows = part.shape[1] // depth
 
     def slot(self, way, j, s):
@@ -359,18 +425,18 @@
         @pl.when(t == 0)
         def _():
             for k in steps:
-                for s in range(self.seqs):
+                for s in self.which:
                     j = depth - 1 - k
                     self.copy(0, j, s, self.block(j, s), t + 1).start()
 
         @pl.when(t == depth - 1)
         def _():
             for j in steps:
-                for s in range(self.seqs):
+                for s in self.which:
                     self.copy(1, j, s, self.block(j, s), t - 1).start()
 
     def pass_on(self, way, j, to):
-        for s in range(self.seqs):
+        for s in self.which:
             mine = self.slot(way, j, s)
             self.copy(way, j, s, mine, self.t).wait_recv()
             add_rows(mine, self.block(j, s), self.rows)
@@ -392,24 +458,25 @@
     def total(self, out):
         t, depth = self.t, self.depth
         mine = pl.ds(pl.multiple_of(t * self.rows, self.rows), self.rows)
-        out[...] = self.part[:, mine, :].astype(F32)
+        for s in self.which:
+            out[s] = self.part[s, mine, :].astype(F32)
 
         @pl.when(t > 0)
         def _():
-            for s in range(self.seqs):
+            for s in self.which:
                 self.copy(0, t, s, self.slot(0, t, s), t).wait_recv()
-            out[...] += self.got[0, t - 1].astype(F32)
+                out[s] += self.got[0, t - 1, s].astype(F32)
 
         @pl.when(t < depth - 1)
         def _():
-            for s in range(self.seqs):
+            for s in self.which:
                 self.copy(1, t, s, self.slot(1, t, s), t).wait_recv()
-            out[...] += self.got[1, t].astype(F32)
+                out[s] += self.got[1, t, s].astype(F32)
 
     def end(self):
         t, depth = self.t, self.depth
         for j in range(depth):
-            for s in range(self.seqs):
+            for s in self.which:
                 if j > 0:
 
                     @pl.when(j > t)
@@ -521,6 +588,7 @@
 
 
 STRIP = 16
+PANEL = 640
 
 
 def gate_blocks(parity, width, block):
@@ -533,7 +601,7 @@
     return blocks
 
 
-def first_kernel(
+def front_kernel(
     depth,
     normed_block,
     cot_block,
@@ -542,16 +610,24 @@
     gate_in_shard,
     gate_dec_shard,
     out_shard,
+    down_shard,
+    gate_shard,
     up_shard,
     taps,
     rate,
+    act,
+    gain,
+    middle,
     normed_out,
     cot_out,
+    normed_two_out,
     gelu_full,
     input_full,
     gate_in_full,
     gate_dec_full,
     out_full,
+    down_full,
+    gate_full,
     up_full,
     gelu_pre_out,
     input_pre_out,
@@ -561,34 +637,47 @@
     gate_dec_out,
     states_out,
     mixed_out,
-    part_out,
+    grad_hidden_out,
+    gate_pre_out,
     *scratch,
 ):
     normed, gelu_w, input_w, gate_in_w, gate_dec_w, out_w = scratch[:6]
     gelu_pre, input_pre, conv, window, gate_in, gate_dec, decay, states, mixed, part = scratch[6:16]
     local, send, recv = scratch[16:19]
-    line_sems = scratch[19:25]
-    rim_send, rim_recv, save_sem = scratch[25:28]
+    line_sems = [scratch[19 + 3 * i : 22 + 3 * i] for i in range(5)]
+    rim_send, rim_recv, save_sem = scratch[34:37]
+    cot, normed_two, block_two, panel_w, product = scratch[37:42]
+    panel_sem, product_sem = scratch[42:44]
+    got, ssem, rsem = scratch[44:47]
     d, t = place()
     parity = lax.rem(t, 2)
     even = parity == 0
     odd = parity == 1
     greet(d, t, depth)
-    seqs, length, _ = normed.shape
+    seqs, length, model = normed.shape
     tokens = seqs * length
     width = conv.shape[1]
     block = gate_in_w.shape[0]
     half = block // 2
-    lines = [
-        LineGather(normed_block, normed, *line_sems[:3], d, t, depth),
-        LineGather(cot_block, cot_out, *line_sems[3:], d, t, depth),
+    spans = [pl.ds(s * length, length) for s in range(seqs)]
+    first_line = LineGather(normed_block, normed, *line_sems[0], d, t, depth)
+    cots = [
+        LineGather(cot_block.at[s], cot.at[spans[s]], *line_sems[1 + s], d, t, depth)
+        for s in range(seqs)
     ]
+    twos = [
+        LineGather(block_two.at[s], normed_two.at[spans[s]], *line_sems[3 + s], d, t, depth)
+        for s in range(seqs)
+    ]
+    scatters = [LineScatter(part, got, ssem, rsem, d, t, depth, (s,)) for s in range(seqs)]
     pairs = (
         (gelu_shard, gelu_w),
         (input_shard, input_w),
         (gate_in_shard, gate_in_w),
         (gate_dec_shard, gate_dec_w),
         (out_shard, out_w),
+        (down_shard, down_full),
+        (gate_shard, gate_full),
         (up_shard, up_full),
     )
     gathers = [
@@ -602,26 +691,27 @@
         copy.start()
         saves.append(copy)
 
-    one, two, three = gathers[:-2], gathers[-2], gathers[-1]
-    lines[0].step(0)
+    one = gathers[:4]
+    out_g, down_g, gate_g, up_g = gathers[4:]
+    first_line.step(0)
     for g in one:
         g.start()
     for g in one:
         g.relay()
-    two.start()
-    lines[0].step(1)
+    out_g.start()
+    first_line.step(1)
     for g in one:
         g.relay_two()
-    lines[0].step(2)
     for g in one:
         g.relay_last()
-    two.relay()
-    three.start()
-    two.relay_two()
-    two.relay_last()
-    lines[0].step(3)
-    lines[0].own.wait()
-    lines[1].step(0)
+    first_line.step(2)
+    out_g.relay()
+    down_g.start()
+    out_g.relay_two()
+    out_g.relay_last()
+    first_line.step(3)
+    first_line.own.wait()
+    cots[0].step(0)
     for g in one:
         g.arrive()
     save(normed, normed_out)
@@ -683,7 +773,9 @@
     def _():
         gates(odd_blocks[1:])
 
-    three.relay()
+    cots[0].step(1)
+    down_g.relay()
+    gate_g.start()
 
     @pl.when(even)
     def _():
@@ -694,8 +786,6 @@
     def _():
         rim(t - 1, 0, 0).wait_recv()
         gates(odd_blocks[:1])
-
-    lines[1].step(1)
 
     @pl.loop(0, tokens // STRIP)
     def _(i):
@@ -707,6 +797,7 @@
         states[held, :] = drive * conv[rows, :].astype(F32)
 
     states[0:8, :] = jnp.zeros((8, width), F32)
+    cots[0].step(2)
     scan_rows(decay, states, seqs, length, base=8)
 
     @pl.loop(0, tokens // STRIP)
@@ -715,6 +806,22 @@
         held = pl.ds(pl.multiple_of(i * STRIP + 8, 8), STRIP)
         mixed[rows, :] = (gelu(gelu_pre[rows, :]) * states[held, :]).astype(BF16)
 
+    panel = 512
+    out_g.arrive()
+    for s in range(seqs):
+
+        @pl.loop(0, model // panel)
+        def _(i):
+            columns = rows_of(i, panel)
+            part[s, :, columns] = contract(mixed[spans[s], :], out_w[columns, :], (1, 1)).astype(
+                BF16
+            )
+
+        scatters[s].start()
+    cots[0].step(3)
+    cots[1].step(0)
+    down_g.relay_two()
+    scatters[0].step(1)
     save(gelu_pre, gelu_pre_out)
     save(input_pre, input_pre_out)
     save(conv, conv_out)
@@ -723,24 +830,88 @@
     save(gate_dec, gate_dec_out)
     save(states, states_out)
     save(mixed, mixed_out)
-    three.relay_two()
-    two.arrive()
     save(out_w, out_full)
-    panel = 512
-
-    @pl.loop(0, out_w.shape[0] // panel)
-    def _(i):
-        columns = rows_of(i, panel)
-        value = contract(mixed[...], out_w[columns, :], (1, 1)).astype(BF16)
+    scatters[0].step(2)
+    down_g.relay_last()
+
+    def norm_step(s):
+        scatters[s].total(middle)
+        value = middle[s] + act[s].astype(F32)
+        middle[s] = value
+        inverse = lax.rsqrt(jnp.mean(value * value, axis=-1, keepdims=True) + EPS)
+        block_two[s] = (value * inverse * gain[...]).astype(BF16)
+        twos[s].step(0)
+
+    norm_step(0)
+    gate_g.relay()
+    up_g.start()
+    scatters[1].step(1)
+    twos[0].step(1)
+    scatters[1].step(2)
+    gate_g.relay_two()
+    norm_step(1)
+    cots[1].step(1)
+    gate_g.relay_last()
+    twos[0].step(2)
+    cots[1].step(2)
+    twos[1].step(1)
+    cots[1].step(3)
+    for s in range(seqs):
+        cots[s].own.wait()
+    save(cot, cot_out)
+    up_g.relay()
+    panels = down_full.shape[1] // PANEL
+
+    def load_panel(full, i):
+        columns = pl.ds(i % panels * PANEL, PANEL)
+        copy = pltpu.make_async_copy(full.at[:, columns], panel_w.at[i % 2], panel_sem.at[i % 2])
+        copy.start()
+        return copy
+
+    results = []
+
+    def multiply(left, full, out, i, following):
+        nonlocal loaded
+        loaded.wait()
+        if following is not None:
+            loaded = load_panel(*following)
+        if len(results) >= 2:
+            results[-2].wait()
         for s in range(seqs):
-            part[s, :, columns] = value[s * length : (s + 1) * length]
-
-    save(part, part_out)
-    lines[1].step(2)
-    three.relay_last()
-    lines[1].step(3)
-    lines[1].own.wait()
-    three.arrive()
+            product[i % 2, spans[s], :] = contract(left[spans[s], :], panel_w[i % 2], (1, 0))
+        columns = pl.ds(i % panels * PANEL, PANEL)
+        copy = pltpu.make_async_copy(product.at[i % 2], out.at[:, columns], product_sem.at[i % 2])
+        copy.start()
+        results.append(copy)
+
+    down_g.arrive()
+    gate_g.arrive()
+    loaded = load_panel(down_full, 0)
+    for i in range(panels):
+        multiply(
+            cot,
+            down_full,
+            grad_hidden_out,
+            i,
+            (down_full, i + 1) if i < panels - 1 else (gate_full, panels),
+        )
+    twos[0].step(3)
+    twos[1].step(2)
+    up_g.relay_two()
+    twos[1].step(3)
+    for s in range(seqs):
+        twos[s].own.wait()
+    save(normed_two, normed_two_out)
+    for i in range(panels, 2 * panels):
+        multiply(
+            normed_two,
+            gate_full,
+            gate_pre_out,
+            i,
+            (gate_full, i + 1) if i < 2 * panels - 1 else None,
+        )
+    up_g.relay_last()
+    up_g.arrive()
 
     @pl.when(even)
     def _():
@@ -752,18 +923,19 @@
 
     for g in gathers:
         g.end()
-    for line in lines:
+    for line in [first_line] + cots + twos + scatters:
         line.end()
-    for copy in saves:
+    for copy in saves + results[-2:]:
         copy.wait()
 
 
-def first_phase(normed, cot, weights, taps, rate, depth):
+def front_phase(normed, cot, weights, taps, rate, act, gain, depth):
     seqs, rows, model = normed.shape
     length = rows * depth
     tokens = seqs * length
     n = len(weights)
     block, width = weights[2].shape[0] * 8, weights[0].shape[1]
+    units = weights[-1].shape[1]
     wide = block // 2 + width
     wide_rows = (seqs, length, model)
     mixers = [(model, width), (model, width), (block, width), (block, width), (model, width)]
@@ -776,95 +948,38 @@
         ((tokens, width), F32),
         ((tokens + 8, width), F32),
         ((tokens, width), BF16),
-        (wide_rows, BF16),
     ]
-    outs = [shaped(wide_rows, BF16, ANY)] * 2
+    outs = [shaped(act.shape, F32, VMEM)]
+    outs += [shaped(wide_rows, BF16, ANY)] + [shaped((tokens, model), BF16, ANY)] * 2
     outs += [shaped(shape, BF16, ANY) for shape in mixers]
-    outs += [shaped((8,) + weights[-1].shape, BF16, ANY)]
+    outs += [shaped((model, units), BF16, ANY)] * 3
     outs += [shaped(shape, dtype, ANY) for shape, dtype in saved]
-    saved_scratch = saved[:6] + [((tokens, width), F32)] + saved[6:]
+    outs += [shaped((tokens, units), F32, ANY)] * 2
+    saved_scratch = saved[:6] + [((tokens, width), F32)] + saved[6:] + [(wide_rows, BF16)]
     scratch = [pltpu.VMEM(wide_rows, BF16)]
     scratch += [pltpu.VMEM(shape, BF16) for shape in mixers]
     scratch += [pltpu.VMEM(shape, dtype) for shape, dtype in saved_scratch]
-    scratch += gather_scratch(n) + line_gather_scratch(depth) * 2 + [DMA, DMA, DMA((16,))]
+    scratch += gather_scratch(n) + line_gather_scratch(depth) * 5 + [DMA, DMA, DMA((16,))]
+    scratch += [
+        pltpu.VMEM((tokens, model), BF16),
+        pltpu.VMEM((tokens, model), BF16),
+        pltpu.VMEM(act.shape, BF16),
+        pltpu.VMEM((2, model, PANEL), BF16),
+        pltpu.VMEM((2, tokens, PANEL), F32),
+        DMA((2,)),
+        DMA((2,)),
+    ]
+    scratch += line_scatter_scratch(seqs, rows, model, depth)
     res = call(
-        functools.partial(first_kernel, depth),
-        "first_phase",
+        functools.partial(front_kernel, depth),
+        "front_phase",
         0,
-        [VMEM] * (4 + n),
+        [VMEM] * (6 + n),
         outs,
         scratch,
-        (normed, cot) + tuple(weights) + (taps, rate.reshape(1, width)),
+        (normed, cot) + tuple(weights) + (taps, rate.reshape(1, width), act, gain.reshape(1, model)),
     )
-    return res[0], res[1], res[2 : 2 + n], res[2 + n : -1], res[-1]
-
-
-def middle_kernel(depth, part, act, gain, w0, w1, middle, wide, f0, f1, *scratch):
-    local, send, recv = scratch[:3]
-    got, ssem, rsem = scratch[3:6]
-    block = scratch[6]
-    lsem = scratch[7:10]
-    d, t = place()
-    greet(d, t, depth)
-    gathers = [
-        WeightGather(w, f, local.at[i], send.at[i], recv.at[i], d, t)
-        for i, (w, f) in enumerate(((w0, f0), (w1, f1)))
-    ]
-    scatter = LineScatter(part, got, ssem, rsem, d, t, depth)
-    scatter.start()
-    gathers[0].start()
-    gathers[0].relay()
-    gathers[1].start()
-    scatter.step(1)
-    gathers[0].relay_two()
-    scatter.step(2)
-    gathers[0].relay_last()
-    scatter.total(middle)
-    seqs, rows, width = act.shape
-    for s in range(seqs):
-        value = middle[s] + act[s].astype(F32)
-        middle[s] = value
-        inverse = lax.rsqrt(jnp.mean(value * value, axis=-1, keepdims=True) + EPS)
-        block[s] = (value * inverse * gain[...]).astype(BF16)
-    line = LineGather(block, wide, *lsem, d, t, depth)
-    line.step(0)
-    gathers[1].relay()
-    line.step(1)
-    gathers[1].relay_two()
-    line.step(2)
-    gathers[1].relay_last()
-    line.step(3)
-    for g in gathers:
-        g.arrive()
-        g.end()
-    scatter.end()
-    line.own.wait()
-    line.end()
-
-
-def middle_phase(part, act, gain, w0, w1, depth):
-    seqs, rows, width = act.shape
-    outs = [
-        shaped(act.shape, F32, VMEM),
-        shaped((seqs, rows * depth, width), BF16, ANY),
-        shaped((8,) + w0.shape, BF16, ANY),
-        shaped((8,) + w1.shape, BF16, ANY),
-    ]
-    scratch = (
-        gather_scratch(2)
-        + line_scatter_scratch(seqs, rows, width, depth)
-        + [pltpu.VMEM(act.shape, BF16)]
-        + line_gather_scratch(depth)
-    )
-    return call(
-        functools.partial(middle_kernel, depth),
-        "middle_phase",
-        1,
-        [VMEM] * 5,
-        outs,
-        scratch,
-        (part, act, gain.reshape(1, width), w0, w1),
-    )
+    return res[0], res[1:4], res[4:9], res[9:12], res[12:20], res[20:]
 
 
 def norm_back(value, gain, error):
@@ -875,78 +990,285 @@
     return grad, jnp.sum(error * value * inverse, axis=0, keepdims=True)
 
 
-def back_kernel(depth, part, middle, gain, cot, g0, g1, grad, wide, gain_grad, o0, o1, *scratch):
-    got, ssem, rsem = scratch[:3]
-    block = scratch[3]
-    lsem = scratch[4:7]
+HOSTED = 5
+
+
+def feed_kernel(
+    depth,
+    normed_in,
+    cot_in,
+    gate_in,
+    up_in,
+    down_in,
+    grad_hidden_in,
+    gate_pre_in,
+    middle,
+    gain,
+    cot_own,
+    grad,
+    wide,
+    gain_grad,
+    feed_out,
+    *refs,
+):
+    panels = gate_in.shape[1] // PANEL
+    n_panels = 3 * panels
+    outs, refs = refs[:n_panels], refs[n_panels:]
+    normed, cot, hidden, gate_rows, lift_rows = refs[:5]
+    gate_w, up_w, down_w, gate_pre, lift_pre, grad_hidden, acc, part, block, stage = refs[5:15]
+    got, ssem, rsem = refs[15:18]
+    load_sem, weight_sem, save_sem = refs[18:21]
+    lines = refs[21:24], refs[24:27]
     d, t = place()
     greet(d, t, depth)
-    scatters = make_scatters((g0, g1), (o0, o1), (True, True), scratch[7:], d, t)
-    scatter = LineScatter(part, got, ssem, rsem, d, t, depth)
-    scatter.start()
-    for g in scatters:
-        g.start()
-    scatters[0].first()
-    scatters[0].second()
-    scatter.step(1)
-    scatters[0].third()
-    scatter.step(2)
-    scatters[1].first()
-    scatters[1].second()
-    scatter.total(grad)
-    seqs, rows, width = middle.shape
-    for s in range(seqs):
+    seqs = middle.shape[0]
+    tokens, model = normed_in.shape
+    length = tokens // seqs
+    tile = 512
+    ring = PanelRing(outs[:HOSTED], refs[27:], d, t)
+    scatters = [LineScatter(part, got, ssem, rsem, d, t, depth, (s,)) for s in range(seqs)]
+    gathers = [
+        LineGather(block.at[s], wide.at[s], *lines[s], d, t, depth) for s in range(seqs)
+    ]
+
+    def load(i, src, dst):
+        copy = pltpu.make_async_copy(src, dst, load_sem.at[i])
+        copy.start()
+        return copy
+
+    def weight(i, src, dst, p):
+        copy = pltpu.make_async_copy(
+            src.at[:, pl.ds(p * PANEL, PANEL)], dst, weight_sem.at[i]
+        )
+        copy.start()
+        return copy
+
+    def held_rows(s, p):
+        rows, columns = pl.ds(s * length, length), pl.ds(p * PANEL, PANEL)
+        q = (s * panels + p) % 2
+        return [
+            load(2 + q, gate_pre_in.at[rows, columns], gate_pre.at[q]),
+            load(4 + q, grad_hidden_in.at[rows, columns], grad_hidden.at[q]),
+        ]
+
+    normed_load = load(0, normed_in, normed)
+    ups = (up_w, down_w)
+    up_load = weight(1, up_in, up_w, 0)
+    row_loads = held_rows(0, 0)
+    gate_load = weight(0, gate_in, gate_w, 0)
+    cot_load = load(1, cot_in, cot)
+
+    def forward(s, p, more):
+        nonlocal gate_load, up_load, row_loads
+        rows = pl.ds(s * length, length)
+        columns = pl.ds(p * PANEL, PANEL)
+        q = (s * panels + p) % 2
+        if s == 0 and p == 0:
+            normed_load.wait()
+        up = ups[q]
+        up_load.wait()
+        if more is not None:
+            up_load = weight(2 - q, up_in, ups[1 - q], more)
+        lift_pre[...] = contract(normed[rows, :], up[...], (1, 0))
+        for copy in row_loads:
+            copy.wait()
+        if more is not None:
+            row_loads = held_rows(*((s, more) if more > p else (s + 1, more)))
+
+        @pl.loop(0, length // STRIP)
+        def _(i):
+            strip = rows_of(i, STRIP)
+            held = pl.ds(pl.multiple_of(s * length + i * STRIP, STRIP), STRIP)
+            act, slope = gelu_both(gate_pre[q, strip, :])
+            lift = lift_pre[strip, :]
+            came = grad_hidden[q, strip, :]
+            hidden[held, columns] = (act * lift).astype(BF16)
+            gate_rows[held, columns] = (came * lift * slope).astype(BF16)
+            lift_rows[held, columns] = (came * act).astype(BF16)
+
+        gate_load.wait()
+
+        @pl.loop(0, model // tile)
+        def _(i):
+            out = rows_of(i, tile)
+            value = contract(gate_rows[rows, columns], gate_w[out, :], (1, 1))
+            value = value + contract(lift_rows[rows, columns], up[out, :], (1, 1))
+            if p == 0:
+                acc[:, out] = value
+            elif p < panels - 1:
+                acc[:, out] += value
+            else:
+                part[s, :, out] = (acc[:, out] + value).astype(BF16)
+
+        if more is not None:
+            gate_load = weight(0, gate_in, gate_w, more)
+
+    kinds = ((cot, hidden), (normed, gate_rows), (normed, lift_rows))
+
+    def weight_grad(i, out):
+        left, right = kinds[i // panels]
+        columns = pl.ds(i % panels * PANEL, PANEL)
+
+        @pl.loop(0, model // tile)
+        def _(k):
+            rows = rows_of(k, tile)
+            out[rows, :] = contract(left[:, rows], right[:, columns], (0, 0)).astype(BF16)
+
+    def begin(i):
+        panel = ring.panels[i]
+        weight_grad(i, panel.grad)
+        panel.start()
+        panel.first()
+        panel.second()
+
+    def norm_step(s):
+        scatters[s].total(grad)
         change, gain_part = norm_back(middle[s], gain[...], grad[s])
-        change = change + cot[s]
+        change = change + cot_own[s]
         grad[s] = change
         block[s] = change.astype(BF16)
         if s == 0:
             gain_grad[...] = gain_part
         else:
             gain_grad[...] += gain_part
-    line = LineGather(block, wide, *lsem, d, t, depth)
-    line.step(0)
-    scatters[0].end()
-    line.step(1)
-    scatters[1].third()
-    line.step(2)
-    line.step(3)
-    scatters[1].end()
-    scatter.end()
-    line.own.wait()
-    line.end()
-
-
-def back_phase(part, middle, gain, cot, g0, g1, depth):
-    seqs, rows, width = middle.shape
-    shapes = [(g.shape[0] // 8, g.shape[1]) for g in (g0, g1)]
+
+    for p in range(panels):
+        forward(0, p, (p + 1) % panels)
+    scatters[0].start()
+    forward(1, 0, 1)
+    scatters[0].step(1)
+    cot_load.wait()
+    begin(0)
+    forward(1, 1, 2)
+    scatters[0].step(2)
+    ring.panels[0].third()
+    begin(1)
+    forward(1, 2, None)
+    down_loads = [weight(0, down_in, gate_w, 0), weight(1, down_in, up_w, 1)]
+    down_loads.append(weight(2, down_in, down_w, 2))
+    scatters[1].start()
+    norm_step(0)
+    gathers[0].step(0)
+    ring.panels[0].end()
+    ring.panels[1].third()
+    begin(2)
+    scatters[1].step(1)
+    gathers[0].step(1)
+    ring.panels[1].end()
+    ring.panels[2].third()
+    begin(3)
+    scatters[1].step(2)
+    gathers[0].step(2)
+    ring.panels[2].end()
+    ring.panels[3].third()
+    begin(4)
+    norm_step(1)
+    gathers[1].step(0)
+    gathers[0].step(3)
+    pending = {}
+
+    def keep(key, src, dst):
+        if key in pending:
+            pending[key].wait()
+        pending[key] = pltpu.make_async_copy(src, dst, save_sem.at[key])
+        pending[key].start()
+
+    def feed(s):
+        rows = pl.ds(s * length, length)
+        if pending:
+            pending.pop(0).wait()
+        downs = (gate_w, up_w, down_w)
+
+        @pl.loop(0, model // tile)
+        def _(i):
+            out = rows_of(i, tile)
+            value = contract(hidden[rows, 0:PANEL], downs[0][out, :], (1, 1))
+            for p in range(1, panels):
+                columns = pl.ds(p * PANEL, PANEL)
+                value = value + contract(hidden[rows, columns], downs[p][out, :], (1, 1))
+            stage[:, out] = value.astype(BF16)
+
+        keep(0, stage, feed_out.at[s])
+
+    def store_grad(i):
+        q = i % ring.slots
+        if 1 + q in pending:
+            pending.pop(1 + q).wait()
+        weight_grad(i, ring.panels[q].grad)
+        keep(1 + q, ring.panels[q].grad, outs[i])
+
+    for copy in down_loads:
+        copy.wait()
+    feed(0)
+    gathers[1].step(1)
+    ring.panels[3].end()
+    ring.panels[4].third()
+    feed(1)
+    gathers[1].step(2)
+    store_grad(5)
+    store_grad(6)
+    ring.panels[4].end()
+    gathers[1].step(3)
+    store_grad(7)
+    store_grad(8)
+    ring.end()
+    for copy in pending.values():
+        copy.wait()
+    for line in scatters:
+        line.end()
+    for line in gathers:
+        line.own.wait()
+        line.end()
+
+
+def feed_phase(normed, cot, weights, held, middle, gain, cot_own, depth):
+    down_w, gate_w, up_w = weights
+    seqs, rows, model = middle.shape
+    tokens = normed.shape[0]
+    length = tokens // seqs
+    wide_rows = (seqs, length, model)
+    units = gate_w.shape[1]
+    count = 3 * (units // PANEL)
     outs = [
         shaped(middle.shape, F32, VMEM),
-        shaped((seqs, rows * depth, width), BF16, ANY),
-        shaped((1, width), F32, VMEM),
-        shaped(shapes[0], F32, VMEM),
-        shaped(shapes[1], F32, VMEM),
+        shaped(wide_rows, BF16, ANY),
+        shaped((1, model), F32, VMEM),
+        shaped(wide_rows, BF16, ANY),
     ]
-    scratch = (
-        line_scatter_scratch(seqs, rows, width, depth)
-        + [pltpu.VMEM(middle.shape, BF16)]
-        + line_gather_scratch(depth)
-        + scatter_scratch(shapes, (True, True))
-    )
-    return call(
-        functools.partial(back_kernel, depth),
-        "back_phase",
+    outs += [shaped((model // 8, PANEL), F32, ANY)] * HOSTED
+    outs += [shaped((model, PANEL), BF16, ANY)] * (count - HOSTED)
+    scratch = [pltpu.VMEM((tokens, model), BF16)] * 2
+    scratch += [pltpu.VMEM((tokens, units), BF16)] * 3
+    scratch += [pltpu.VMEM((model, PANEL), BF16)] * 3
+    scratch += [pltpu.VMEM((2, length, PANEL), F32), pltpu.VMEM((length, PANEL), F32)]
+    scratch += [pltpu.VMEM((2, length, PANEL), F32)]
+    scratch += [
+        pltpu.VMEM((length, model), F32),
+        pltpu.VMEM(wide_rows, BF16),
+        pltpu.VMEM(middle.shape, BF16),
+        pltpu.VMEM((length, model), BF16),
+    ]
+    scratch += line_scatter_scratch(seqs, rows, model, depth)
+    scratch += [DMA((6,)), DMA((3,)), DMA((8,))]
+    scratch += line_gather_scratch(depth) * 2
+    scratch += ring_scratch(3, model // 8, PANEL)
+    res = call(
+        functools.partial(feed_kernel, depth),
+        "feed_phase",
         2,
-        [VMEM, VMEM, VMEM, VMEM, ANY, ANY],
+        [ANY] * 7 + [VMEM] * 3,
         outs,
         scratch,
-        (part, middle, gain.reshape(1, width), cot, g0, g1),
+        (normed, cot, gate_w, up_w, down_w) + tuple(held) + (middle, gain.reshape(1, model), cot_own),
     )
+    return res[0], res[1], res[2], res[3], res[4:]
 
 
 def mixer_back_kernel(
     depth,
+    n_panels,
     branch_in,
+    normed_in,
     out_w_in,
     gelu_pre_in,
     input_pre_in,
@@ -955,64 +1277,114 @@
     gate_in_in,
     gate_dec_in,
     states_in,
+    mixed_in,
     gelu_w_in,
     input_w_in,
     gate_in_w_in,
     gate_dec_w_in,
-    up_in,
     feed,
     middle,
     taps,
     rate,
-    part_out,
-    gelu_grad_out,
-    input_grad_out,
-    gate_in_grad_out,
-    gate_dec_grad_out,
-    small,
-    output,
-    up_out,
-    *scratch,
+    act,
+    gain,
+    grad_middle,
+    mlp_part,
+    *refs,
 ):
+    panels_in, refs = refs[:n_panels], refs[n_panels:]
+    n_sums = n_panels + 3
+    output, input_grad, gains, smalls, gate_in_out, gate_dec_out = refs[:6]
+    panels_out, scratch = refs[6 : 6 + n_sums], refs[6 + n_sums :]
     branch, weight, input_w = scratch[:3]
     gelu_pre, input_pre, conv, window, gate_in, gate_dec, states, gate_in_w, gate_dec_w = scratch[3:12]
-    grad, decay, grad_conv, gelu_grad, input_grad, grad_in, grad_dec = scratch[12:19]
-    rim_out, rim_in, gate_in_grad, gate_dec_grad, part, sums, total = scratch[19:26]
-    got, ssem, rsem = scratch[26:29]
-    rim_send, rim_recv, load_sem, save_sem = scratch[29:33]
+    grad, decay, grad_conv, gelu_grad, input_rows, grad_in, grad_dec, mixed = scratch[12:20]
+    rim_out, rim_in, gate_in_grad, gate_dec_grad, part, sums, total = scratch[20:27]
+    got, ssem, rsem = scratch[27:30]
+    last_got, last_ssem, last_rsem = scratch[30:33]
+    rim_send, rim_recv, load_sem, panel_sem = scratch[33:37]
+    small, small_all, pack, packs, line_pack, line_packs = scratch[37:43]
+    psend, precv, qsend, qrecv, zsend, zrecv = scratch[43:49]
+    ring = PanelRing(panels_out, scratch[49:58], *place())
     d, t = place()
     parity = lax.rem(t, 2)
     even = parity == 0
     odd = parity == 1
-    greet(d, t, depth)
-    seqs, length, _ = branch.shape
+    greet(d, t, depth, dp_masks=(1, 2, 3, 4, 5, 6, 7), z_all=True)
+    seqs, length, model = branch_in.shape
     tokens = seqs * length
     width = conv.shape[1]
     block = gate_in_w.shape[0]
     half = block // 2
     even_blocks, odd_blocks = gate_blocks(0, width, block), gate_blocks(1, width, block)
-    (scatter,) = make_scatters((up_in,), (up_out,), (True,), scratch[33:], d, t)
+    gate_scatters = make_scatters(
+        (gate_in_grad, gate_dec_grad),
+        (gate_in_out, gate_dec_out),
+        (False, False),
+        scratch[58:],
+        d,
+        t,
+    )
     line = LineScatter(feed, got, ssem, rsem, d, t, depth)
-    saves = []
-
-    def save(src, dst):
-        copy = pltpu.make_async_copy(src, dst, save_sem.at[len(saves)])
-        copy.start()
-        saves.append(copy)
+    last_line = LineScatter(part, last_got, last_ssem, last_rsem, d, t, depth)
 
     def load(i, src, dst):
         copy = pltpu.make_async_copy(src, dst, load_sem.at[i])
         copy.start()
         return copy
 
-    early = [load(0, branch_in, branch), load(1, out_w_in, weight)]
+    def load_wide(i, src):
+        return [
+            load(i + s, src.at[s], branch.at[pl.ds(s * length, length)]) for s in range(seqs)
+        ]
+
+    early = [load(0, out_w_in, weight)] + load_wide(12, branch_in)
     next_ = [
         load(2, gelu_pre_in, gelu_pre),
         load(3, states_in, states),
         load(4, gate_dec_in, gate_dec),
     ]
     line.start(0, 1)
-    scatter.start()
+    panel_loads = [
+        pltpu.make_async_copy(src, panel.grad, panel_sem.at[i])
+        for i, (src, panel) in enumerate(zip(panels_in, ring.panels))
+    ]
+
+    def weight_grad(left, right, out):
+        panel = 512
+
+        @pl.loop(0, model // panel)
+        def _(i):
+            columns = rows_of(i, panel)
+            out[columns, :] = contract(left[:, columns], right[...], (0, 0)).astype(BF16)
+
+    def dp_copies(src, dst, send, recv):
+        return [
+            pltpu.make_async_remote_copy(
+                src_ref=src,
+                dst_ref=dst.at[d],
+                send_sem=send.at[mask - 1],
+                recv_sem=recv.at[mask - 1],
+                device_id=(d ^ mask, t),
+                device_id_type=MESH,
+            )
+            for mask in range(1, 8)
+        ]
+
+    def begin(i):
+        if i < n_panels:
+            panel_loads[i].wait()
+        ring.panels[i].start()
+        ring.panels[i].first()
+        ring.panels[i].second()
+
+    def finish(i):
+        ring.panels[i].end()
+        if i + ring.slots < n_panels:
+            panel_loads[i + ring.slots].start()
+
+    for i in range(ring.slots):
+        panel_loads[i].start()
     then = [
         load(5, gate_in_in, gate_in),
         load(6, conv_in, conv),
@@ -1021,14 +1393,15 @@
         load(9, gate_dec_w_in, gate_dec_w),
         load(10, input_pre_in, input_pre),
         load(11, input_w_in, input_w),
+        load(1, mixed_in, mixed),
     ]
     for copy in early:
         copy.wait()
     for s in range(seqs):
         rows = pl.ds(s * length, length)
-        grad[rows, :] = contract(branch[s], weight[...], (1, 0))
+        grad[rows, :] = contract(branch[rows, :], weight[...], (1, 0))
     reload = load(0, gelu_w_in, weight)
-    scatter.first()
+    begin(0)
     for copy in next_:
         copy.wait()
 
@@ -1043,8 +1416,8 @@
         decay[rows, :] = jnp.exp(-8.0 * sigmoid(gate_dec[rows, :]) * rate[...])
 
     decay[tokens : tokens + 8, :] = jnp.zeros((8, width), F32)
-    save(gelu_grad, gelu_grad_out)
-    scatter.second()
+    begin(1)
+    ring.panels[0].third()
     scan_rows(decay, grad, seqs, length, backward=True)
     for copy in then:
         copy.wait()
@@ -1115,6 +1488,8 @@
 
     line.start(1)
     line.step(1)
+    finish(0)
+    ring.panels[1].third()
 
     def inner(blocks):
         for k, low, high in blocks:
@@ -1136,9 +1511,9 @@
         inner(odd_blocks[1:])
         gate_grads(odd_blocks)
 
-    save(gate_in_grad, gate_in_grad_out)
-    save(gate_dec_grad, gate_dec_grad_out)
-    scatter.third()
+    for g in gate_scatters:
+        g.start()
+    begin(2)
 
     @pl.when(even)
     def _():
@@ -1164,12 +1539,17 @@
                 value = value + taps[k : k + 1, :] * pltpu.roll(later, STRIP + 8 - k, 0)[:STRIP]
                 sums[1 + k] += fold(here * pltpu.roll(before, k, 0)[8:])
             rows = pl.ds(pl.multiple_of(s * length + i * STRIP, STRIP), STRIP)
-            input_grad[rows, :] = value.astype(BF16)
-
-    save(input_grad, input_grad_out)
+            input_rows[rows, :] = value.astype(BF16)
+
+    finish(1)
+    ring.panels[2].third()
     for k in range(sums.shape[0]):
         small[k : k + 1, :] = jnp.sum(sums[k], axis=0, keepdims=True)
     small[sums.shape[0] :, :] = jnp.zeros((8 - sums.shape[0], width), F32)
+    small_copies = dp_copies(small, small_all, qsend, qrecv)
+    for c in small_copies:
+        c.start()
+    small_all[d] = small[...]
     reload.wait()
     panel = 512
 
@@ -1177,218 +1557,40 @@
     def _(i):
         columns = rows_of(i, panel)
         value = contract(gelu_grad[...], weight[columns, :], (1, 1))
-        value = (value + contract(input_grad[...], input_w[columns, :], (1, 1))).astype(BF16)
+        value = (value + contract(input_rows[...], input_w[columns, :], (1, 1))).astype(BF16)
         for s in range(seqs):
             part[s, :, columns] = value[s * length : (s + 1) * length]
 
-    save(part, part_out)
+    last_line.start()
+    begin(3)
+    for g in gate_scatters:
+        g.first()
+        g.second()
     line.step(2)
-    scatter.end()
+    finish(2)
+    ring.panels[3].third()
+    weight_grad(branch, mixed, ring.panels[4].grad)
+    wide_loads = load_wide(12, normed_in)
+    begin(4)
+    for g in gate_scatters:
+        g.third()
     line.total(total)
     output[...] = (total[...] + middle[...]).astype(BF16)
-    line.end()
-    for copy in saves:
+    finish(3)
+    ring.panels[4].third()
+    for copy in wide_loads:
         copy.wait()
-
-
-def mixer_back_phase(branch, saved, weights, up, feed, middle, taps, rate, depth):
-    seqs, length, model = branch.shape
-    tokens = seqs * length
-    gelu_w, input_w, gate_in_w, gate_dec_w, out_w = weights[:5]
-    gelu_pre, input_pre, conv, window, gate_in, gate_dec, states, mixed = saved
-    width = out_w.shape[1]
-    block = gate_in_w.shape[0]
-    half = block // 2
-    up_shape = (up.shape[0] // 8, up.shape[1])
-    flat = (tokens, width)
-    outs = [
-        shaped(branch.shape, BF16, ANY),
-        shaped(flat, BF16, ANY),
-        shaped(flat, BF16, ANY),
-        shaped(gate_in_w.shape, BF16, ANY),
-        shaped(gate_in_w.shape, BF16, ANY),
-        shaped((8, width), F32, VMEM),
-        shaped(middle.shape, BF16, VMEM),
-        shaped(up_shape, F32, VMEM),
-    ]
-    scratch = [
-        pltpu.VMEM(x.shape, x.dtype)
-        for x in (
-            branch,
-            out_w,
-            input_w,
-            gelu_pre,
-            input_pre,
-            conv,
-            window,
-            gate_in,
-            gate_dec,
-            states,
-            gate_in_w,
-            gate_dec_w,
-        )
-    ]
-    scratch += [
-        pltpu.VMEM(flat, F32),
-        pltpu.VMEM((tokens + 8, width), F32),
-        pltpu.VMEM((seqs, length + 8, width), F32),
-    ]
-    scratch += [pltpu.VMEM(flat, BF16)] * 4
-    scratch += [pltpu.VMEM((tokens, half), BF16)] * 2
-    scratch += [pltpu.VMEM(gate_in_w.shape, BF16)] * 2
-    scratch += [
-        pltpu.VMEM(branch.shape, BF16),
-        pltpu.VMEM((1 + taps.shape[0], 8, width), F32),
-        pltpu.VMEM(middle.shape, F32),
-    ]
-    scratch += line_scatter_scratch(seqs, length // depth, model, depth)
-    scratch += [DMA, DMA, DMA((12,)), DMA((8,))]
-    scratch += scatter_scratch([up_shape], (True,))
-    return call(
-        functools.partial(mixer_back_kernel, depth),
-        "mixer_back_phase",
-        3,
-        [ANY] * 14 + [VMEM] * 4,
-        outs,
-        scratch,
-        (
-            branch,
-            out_w,
-            gelu_pre,
-            input_pre,
-            conv,
-            window,
-            gate_in,
-            gate_dec,
-            states,
-            gelu_w,
-            input_w,
-            gate_in_w,
-            gate_dec_w,
-            up,
-            feed,
-            middle,
-            taps,
-            rate.reshape(1, width),
-        ),
-    )
-
-
-def last_kernel(
-    depth,
-    part,
-    act,
-    gain,
-    grad_middle,
-    mlp_part,
-    small,
-    branch_in,
-    normed_in,
-    mixed_in,
-    gelu_grad_in,
-    input_grad_in,
-    gate_in_grad,
-    gate_dec_grad,
-    input_grad,
-    gains,
-    smalls,
-    out_out,
-    gelu_out,
-    input_out,
-    gate_in_out,
-    gate_dec_out,
-    *scratch,
-):
-    got, ssem, rsem = scratch[:3]
-    pack, packs, small_all, line_pack, line_packs = scratch[3:8]
-    psend, precv, qsend, qrecv, zsend, zrecv = scratch[8:14]
-    branch, normed, mixed, gelu_grad, input_rows = scratch[14:19]
-    out_w_grad, gelu_w_grad, input_w_grad, load_sem = scratch[19:23]
-    d, t = place()
-    greet(d, t, depth, dp_masks=(1, 2, 3, 4, 5, 6, 7), z_all=True)
-    scatters = make_scatters(
-        (out_w_grad, gelu_w_grad, input_w_grad, gate_in_grad, gate_dec_grad),
-        (out_out, gelu_out, input_out, gate_in_out, gate_dec_out),
-        (False, False, False, True, True),
-        scratch[23:],
-        d,
-        t,
-    )
-    line = LineScatter(part, got, ssem, rsem, d, t, depth)
-
-    def load(i, src, dst):
-        copy = pltpu.make_async_copy(src, dst, load_sem.at[i])
-        copy.start()
-        return copy
-
-    loads = [
-        load(0, branch_in, branch),
-        load(1, mixed_in, mixed),
-        load(2, normed_in, normed),
-        load(3, gelu_grad_in, gelu_grad),
-        load(4, input_grad_in, input_rows),
-    ]
-
-    def dp_copies(src, dst, send, recv):
-        return [
-            pltpu.make_async_remote_copy(
-                src_ref=src,
-                dst_ref=dst.at[d],
-                send_sem=send.at[mask - 1],
-                recv_sem=recv.at[mask - 1],
-                device_id=(d ^ mask, t),
-                device_id_type=MESH,
-            )
-            for mask in range(1, 8)
-        ]
-
-    line.start()
-    small_copies = dp_copies(small, small_all, qsend, qrecv)
-    for c in small_copies:
-        c.start()
-    small_all[d] = small[...]
-    for g in scatters[3:]:
-        g.start()
-    seqs, length, model = branch.shape
-    panel = 512
-
-    def weight_grad(left, right, out):
-        @pl.loop(0, model // panel)
-        def _(i):
-            columns = rows_of(i, panel)
-            value = contract(left[0, :, columns], right[0:length, :], (0, 0))
-            for s in range(1, seqs):
-                value = value + contract(
-                    left[s, :, columns], right[s * length : (s + 1) * length, :], (0, 0)
-                )
-            out[columns, :] = value.astype(BF16)
-
-    loads[0].wait()
-    loads[1].wait()
-    weight_grad(branch, mixed, out_w_grad)
-    scatters[0].start()
-    loads[2].wait()
-    loads[3].wait()
-    weight_grad(normed, gelu_grad, gelu_w_grad)
-    scatters[1].start()
-    scatters[0].first()
-    scatters[0].second()
-    loads[4].wait()
-    weight_grad(normed, input_rows, input_w_grad)
-    scatters[2].start()
-    line.step(1)
-    scatters[1].first()
-    scatters[1].second()
-    scatters[0].third()
-    scatters[2].first()
-    scatters[2].second()
-    line.step(2)
-    for g in scatters[3:]:
-        g.first()
-        g.second()
-    scatters[1].third()
-    scatters[0].end()
-    line.total(input_grad)
+    weight_grad(branch, gelu_grad, ring.panels[5].grad)
+    begin(5)
+    last_line.step(1)
+    finish(4)
+    ring.panels[5].third()
+    weight_grad(branch, input_rows, ring.panels[6].grad)
+    begin(6)
+    last_line.step(2)
+    finish(5)
+    ring.panels[6].third()
+    last_line.total(input_grad)
     quarter = pack.shape[1]
     for i in range(4):
         pack[4 + i : 5 + i, :] = mlp_part[:, i * quarter : (i + 1) * quarter]
@@ -1405,14 +1607,14 @@
     for c in pack_copies:
         c.start()
     packs[d] = pack[...]
-    for g in scatters[2:]:
-        g.third()
     for c in small_copies:
         c.wait_recv()
     sum_ = small_all[0]
     for i in range(1, 8):
         sum_ = sum_ + small_all[i]
     smalls[...] = sum_
+    for g in gate_scatters:
+        g.end()
     for c in pack_copies:
         c.wait_recv()
     sum_ = packs[0]
@@ -1433,8 +1635,7 @@
     for c in z_copies:
         c.start()
     line_packs[t] = sum_
-    for g in scatters[1:]:
-        g.end()
+    finish(6)
     for c in z_copies:
         c.wait_recv()
     sum_ = line_packs[0]
@@ -1443,65 +1644,115 @@
     gains[...] = sum_
     for c in small_copies + pack_copies + z_copies:
         c.wait_send()
+    ring.end()
     line.end()
-
-
-def last_phase(
-    part, act, gain, grad_middle, mlp_part, small, branch, normed, mixed, gelu_grad, input_grad,
-    gate_in_grad, gate_dec_grad, depth,
+    last_line.end()
+
+
+def mixer_back_phase(
+    branch, normed, saved, weights, panels, feed, middle, taps, rate, act, gain, grad_middle,
+    mlp_part, depth,
 ):
-    seqs, rows, model = act.shape
-    width = mixed.shape[1]
-    mixer, gate = (model // 8, width), (gate_in_grad.shape[0] // 8, width)
-    shapes = [mixer] * 3 + [gate] * 2
+    seqs, length, model = branch.shape
+    tokens = seqs * length
+    gelu_w, input_w, gate_in_w, gate_dec_w, out_w = weights[:5]
+    gelu_pre, input_pre, conv, window, gate_in, gate_dec, states, mixed = saved
+    width = out_w.shape[1]
+    block = gate_in_w.shape[0]
+    half = block // 2
+    n = len(panels)
+    panel = (panels[0].shape[0] // 8, panels[0].shape[1])
+    gate = (block // 8, width)
     pack = (8, model // 4)
+    small = (8, width)
+    flat = (tokens, width)
     outs = [
-        shaped(act.shape, F32, VMEM),
+        shaped(middle.shape, BF16, VMEM),
+        shaped(middle.shape, F32, VMEM),
         shaped(pack, F32, VMEM),
-        shaped(small.shape, F32, VMEM),
-    ] + [shaped(s, F32, VMEM) for s in shapes]
-    scratch = (
-        line_scatter_scratch(seqs, rows, model, depth)
-        + [
-            pltpu.VMEM(pack, F32),
-            pltpu.VMEM((8,) + pack, F32),
-            pltpu.VMEM((8,) + small.shape, F32),
-            pltpu.VMEM(pack, F32),
-            pltpu.VMEM((depth,) + pack, F32),
-        ]
-        + [DMA((7,))] * 4
-        + [DMA((depth - 1,))] * 2
-        + [
-            pltpu.VMEM(x.shape, BF16) for x in (branch, normed, mixed, gelu_grad, input_grad)
-        ]
-        + [pltpu.VMEM((model, width), BF16)] * 3
-        + [DMA((5,))]
-        + scatter_scratch(shapes, (False, False, False, True, True))
-    )
+        shaped(small, F32, VMEM),
+        shaped(gate, F32, VMEM),
+        shaped(gate, F32, VMEM),
+    ] + [shaped(panel, F32, ANY)] * (n + 3)
+    scratch = [pltpu.VMEM((tokens, model), BF16)]
+    scratch += [
+        pltpu.VMEM(x.shape, x.dtype)
+        for x in (
+            out_w,
+            input_w,
+            gelu_pre,
+            input_pre,
+            conv,
+            window,
+            gate_in,
+            gate_dec,
+            states,
+            gate_in_w,
+            gate_dec_w,
+        )
+    ]
+    scratch += [
+        pltpu.VMEM(flat, F32),
+        pltpu.VMEM((tokens + 8, width), F32),
+        pltpu.VMEM((seqs, length + 8, width), F32),
+    ]
+    scratch += [pltpu.VMEM(flat, BF16)] * 5
+    scratch += [pltpu.VMEM((tokens, half), BF16)] * 2
+    scratch += [pltpu.VMEM(gate_in_w.shape, BF16)] * 2
+    scratch += [
+        pltpu.VMEM(branch.shape, BF16),
+        pltpu.VMEM((1 + taps.shape[0], 8, width), F32),
+        pltpu.VMEM(middle.shape, F32),
+    ]
+    scratch += line_scatter_scratch(seqs, length // depth, model, depth) * 2
+    scratch += [DMA, DMA, DMA((12 + seqs,)), DMA((n,))]
+    scratch += [
+        pltpu.VMEM(small, F32),
+        pltpu.VMEM((8,) + small, F32),
+        pltpu.VMEM(pack, F32),
+        pltpu.VMEM((8,) + pack, F32),
+        pltpu.VMEM(pack, F32),
+        pltpu.VMEM((depth,) + pack, F32),
+    ]
+    scratch += [DMA((7,))] * 4 + [DMA((depth - 1,))] * 2
+    scratch += ring_scratch(2, *panel)
+    scratch += scatter_scratch([gate] * 2, (False, False))
     res = call(
-        functools.partial(last_kernel, depth),
-        "last_phase",
-        4,
-        [VMEM] * 6 + [ANY] * 7,
+        functools.partial(mixer_back_kernel, depth, n),
+        "mixer_back_phase",
+        3,
+        [ANY] * 15 + [VMEM] * 8 + [ANY] * n,
         outs,
         scratch,
         (
-            part,
+            branch,
+            normed,
+            out_w,
+            gelu_pre,
+            input_pre,
+            conv,
+            window,
+            gate_in,
+            gate_dec,
+            states,
+            mixed,
+            gelu_w,
+            input_w,
+            gate_in_w,
+            gate_dec_w,
+            feed,
+            middle,
+            taps,
+            rate.reshape(1, width),
             act,
             gain.reshape(1, model),
             grad_middle,
             mlp_part,
-            small,
-            branch,
-            normed,
-            mixed,
-            gelu_grad,
-            input_grad,
-            gate_in_grad,
-            gate_dec_grad,
-        ),
+        )
+        + tuple(panels),
+        vmem=63 * 1024 * 1024,
     )
-    return res[0], res[1].reshape(2, model), res[2], res[3:]
+    return res[0], res[1], res[2].reshape(2, model), res[3], res[4:6], res[6:]
 
 
 def swapped(block, axis):
@@ -1552,41 +1803,43 @@
     def __init__(self, depth, taps, rate):
         self.depth, self.taps, self.rate = depth, taps, rate
 
-    def first(self, normed, cot, weights):
-        normed_all, cot_all, weights, saved, part = first_phase(
-            normed, cot, weights, self.taps, self.rate, self.depth
-        )
-        self.saved, self.weights, self.normed = saved, weights, normed_all
-        return cot_all, weights[5].reshape(-1, weights[5].shape[-1]), part
-
-    def middle(self, part, act, gain, w0, w1):
-        middle, wide, w0, w1 = middle_phase(part, act, gain, w0, w1, self.depth)
-        return middle, wide, w0.reshape(-1, w0.shape[-1]), w1.reshape(-1, w1.shape[-1])
-
-    def back(self, part, middle, gain, cot, g0, g1):
-        return back_phase(part, middle, gain, cot, g0, g1, self.depth)
-
-    def last(self, branch, up, feed, act, gain, middle, grad_middle, mlp_part):
-        part, gelu_grad, input_rows, gate_in, gate_dec, small, output, up = mixer_back_phase(
-            branch, self.saved, self.weights, up, feed, middle, self.taps, self.rate, self.depth
-        )
-        input_grad, gains, small, grads = last_phase(
-            part,
+    def front(self, normed, cot, weights, act, gain):
+        middle, rows, self.weights, self.feeds, self.saved, self.held = front_phase(
+            normed, cot, weights, self.taps, self.rate, act, gain, self.depth
+        )
+        self.normed, self.cot, self.normed_two = rows
+        return middle
+
+    def feed(self, middle, gain, cot_own):
+        return feed_phase(
+            self.normed_two, self.cot, self.feeds, self.held, middle, gain, cot_own, self.depth
+        )
+
+    def last(self, branch, panels, feed, act, gain, middle, grad_middle, mlp_part):
+        output, input_grad, gains, small, gates, rest = mixer_back_phase(
+            branch,
+            self.normed,
+            self.saved,
+            self.weights,
+            panels[HOSTED:],
+            feed,
+            middle,
+            self.taps,
+            self.rate,
             act,
             gain,
             grad_middle,
             mlp_part,
-            small,
-            branch,
-            self.normed,
-            self.saved[-1],
-            gelu_grad,
-            input_rows,
-            gate_in,
-            gate_dec,
             self.depth,
         )
-        return output, input_grad, gains, small, grads, up
+        grads = list(rest[-3:]) + list(gates)
+        rest = rest[:-3]
+        panels = list(panels[:HOSTED]) + list(rest)
+        third = len(panels) // 3
+        feeds = [
+            jnp.concatenate(panels[i * third : (i + 1) * third], axis=1) for i in range(3)
+        ]
+        return output, input_grad, gains, small, grads, feeds
 
 
 class Plain:
@@ -1609,8 +1862,9 @@
     def own(grad):
         return lax.psum_scatter(grad, "dp", scatter_dimension=0, tiled=True).astype(F32)
 
-    def first(self, normed, cot, weights):
-        gelu_w, input_w, gate_in_w, gate_dec_w, out_w, up_w = (self.full(w) for w in weights)
+    def front(self, normed, cot, weights, act, gain):
+        gelu_w, input_w, gate_in_w, gate_dec_w, out_w = (self.full(w) for w in weights[:5])
+        self.feeds = tuple(self.full(w) for w in weights[5:])
         normed_all = self.wide(normed)
         seqs, length, _ = normed_all.shape
         channels = gelu_w.shape[1]
@@ -1646,20 +1900,32 @@
             gate_back, decay, states, mixed,
         )
         part = dot("xgq,pq->xgp", mixed, out_w).astype(BF16)
-        return self.wide(cot), up_w, part
-
-    def middle(self, part, act, gain, w0, w1):
+        self.cot = self.wide(cot)
         middle = act.astype(F32) + self.narrow(part)
-        wide = self.wide(normalize(middle, gain).astype(BF16))
-        return middle, wide, self.full(w0), self.full(w1)
-
-    def back(self, part, middle, gain, cot, g0, g1):
+        self.normed_two = self.wide(normalize(middle, gain).astype(BF16))
+        return middle
+
+    def feed(self, middle, gain, cot_own):
+        down_w, gate_w, up_w = self.feeds
+        normed, cot = self.normed_two, self.cot
+        gate_pre = dot("nwo,ob->nwb", normed, gate_w)
+        lift_pre = dot("nwo,ob->nwb", normed, up_w)
+        gate_act, activ_back = jax.vjp(jax.nn.gelu, gate_pre)
+        hidden = (gate_act * lift_pre).astype(BF16)
+        grad_hidden = dot("gre,eu->gru", cot, down_w)
+        gate_grad = activ_back(grad_hidden * lift_pre)[0].astype(BF16)
+        lift_grad = (grad_hidden * gate_act).astype(BF16)
+        part = dot("mqa,ya->mqy", gate_grad, gate_w) + dot("mqa,ya->mqy", lift_grad, up_w)
         _, back = jax.vjp(normalize, middle, gain)
-        change, gain_grad = back(self.narrow(part))
-        grad = cot + change
-        return grad, self.wide(grad.astype(BF16)), gain_grad[None], self.own(g0), self.own(g1)
-
-    def last(self, branch, up, feed, act, gain, middle, grad_middle, mlp_part):
+        change, gain_grad = back(self.narrow(part.astype(BF16)))
+        grad = cot_own + change
+        panels = (
+            weight_grad(cot, hidden), weight_grad(normed, gate_grad), weight_grad(normed, lift_grad)
+        )
+        feed = dot("xav,tv->xat", hidden, down_w).astype(BF16)
+        return grad, self.wide(grad.astype(BF16)), gain_grad[None], feed, panels
+
+    def last(self, branch, panels, feed, act, gain, middle, grad_middle, mlp_part):
         (
             normed_all, gelu_w, input_w, out_w, gelu_out, gelu_back, conv_back, tiles, placed,
             gate_back, decay, states, mixed,
@@ -1710,7 +1976,8 @@
             grad_gates[1].astype(BF16),
         )
         own = [self.own(g) for g in parts]
-        return output, grad_middle + change, gains, small, own, self.own(up)
+        feeds = [self.own(g) for g in panels]
+        return output, grad_middle + change, gains, small, own, feeds
 
 
 def shards(
@@ -1750,33 +2017,16 @@
     scaled_cot = cotangent.astype(F32) * (valid_mask * my_weight[:, None])[:, :, None]
     normed = normalize(activations.astype(F32), norm_gain).astype(BF16)
 
-    cot_all, up_w, branch_part = run.first(
-        normed,
-        scaled_cot.astype(BF16),
-        (gelu_proj, input_proj, gate_input, gate_decay, out_proj.T, feed_up),
+    weights = (
+        gelu_proj, input_proj, gate_input, gate_decay, out_proj.T, feed_down.T, feed_gate, feed_up
     )
-    middle, normed_two_all, gate_w, down_w = run.middle(
-        branch_part, activations, mlp_gain, feed_gate, feed_down.T
+    middle = run.front(normed, scaled_cot.astype(BF16), weights, activations, mlp_gain)
+    grad_middle, branch_grad_all, mlp_part, feed_part, panels = run.feed(
+        middle, mlp_gain, scaled_cot
     )
-    gate_pre = dot("nwo,ob->nwb", normed_two_all, gate_w)
-    lift_pre = dot("nwo,ob->nwb", normed_two_all, up_w)
-    gate_act, activ_back = jax.vjp(jax.nn.gelu, gate_pre)
-    hidden = (gate_act * lift_pre).astype(BF16)
-    grad_hidden = dot("gre,eu->gru", cot_all, down_w)
-    gate_grad = activ_back(grad_hidden * lift_pre)[0].astype(BF16)
-    lift_grad = (grad_hidden * gate_act).astype(BF16)
-    back_two = dot("mqa,ya->mqy", gate_grad, gate_w) + dot("mqa,ya->mqy", lift_grad, up_w)
-    grad_down_part = weight_grad(cot_all, hidden)
-    grad_gate_part = weight_grad(normed_two_all, gate_grad)
-    grad_lift_part = weight_grad(normed_two_all, lift_grad)
-    feed_part = dot("xav,tv->xat", hidden, down_w).astype(BF16)
-
-    grad_middle, branch_grad_all, mlp_part, grad_down, grad_gate = run.back(
-        back_two.astype(BF16), middle, mlp_gain, scaled_cot, grad_down_part, grad_gate_part
-    )
-    output, input_grad, gains, small, grads, grad_up = run.last(
+    output, input_grad, gains, small, grads, feeds = run.last(
         branch_grad_all,
-        grad_lift_part,
+        panels,
         feed_part,
         activations,
         norm_gain,
@@ -1796,9 +2046,9 @@
         small[0],
         grads[0].T,
         gains[1],
-        grad_gate,
-        grad_up,
-        grad_down.T,
+        feeds[1],
+        feeds[2],
+        feeds[0].T,
     )
 
 

time: 537 us -> 498 us (0.927)
  matrix products: 87.9 us -> 0 us
  Pallas kernels: 413 us -> 465 us
  local copies, waits for them, and re-layouts: 21.3 us -> 10.9 us
  other arithmetic: 6.71 us -> 14.9 us
    dot_general x9 -> x0, matrix products: 87.9 us -> none  [dot(): return jnp.einsum(spec, left, right, preferred_element_type=F32)]
    pallas_call x5 -> x3, Pallas kernels: 413 us -> 465 us  [call(): pl.pallas_call(kernel, name=name, out_shape=[o[0] for o in outs], in_spec...]
    unnamed x58 -> x37, local copies, waits for them, and re-layouts: 14 us -> 5.9 us
where the time goes in v4:
time: 498 us; the launch traced here: 492 us
  Pallas kernels  465 us (93%)
  other arithmetic  14.9 us (3%)
  local copies, waits for them, and re-layouts  10.9 us (2%)
    pallas_call x3, Pallas kernels, call(): pl.pallas_call(kernel, name=name, out_shape=[o[0] for o in outs], in_spec...  465 us

profile of v4, /device:TPU:0, one launch (start us, length us, event | category | flops | bytes accessed | tf_op | source)
XLA Modules:
  0.0 491.7 jit_solution(16112591929650683427)
XLA Ops:
  0.6 0.0 copy-start.12
  0.7 0.0 copy-start.14
  0.7 0.7 dynamic_slice.6
  1.4 0.7 convert_element_type.21
  2.1 0.8 select_reduce_fusion.1
  2.8 0.7 select_reduce_fusion
  3.6 0.1 dynamic_slice.7
  3.7 0.1 compare_select_fusion
  3.7 1.3 fusion
  5.1 3.1 convert_multiply_fusion.2
  8.2 0.0 copy-done.12
  8.2 0.6 reshape.109.gain
  8.8 0.0 copy-done.14
  8.8 0.6 reshape.108.rate
  9.4 203.8 %front_phase.1 = (f32[2,64,2560]{2,1,0:T(8,128)}, bf16[2,256,2560]{2,1,0:T(8,128)(2,1)}, bf16[512,2560]{1,0:T(8,128)(2,1)}, bf16[512,2560]{1,0:T(8,128)(2,1)}, b...) custom-call(bf16[2,64,2560]{2,1,0:T(8,128)(2,1)} %get-tuple-element., ...), custom_call_target="tpu_custom_call" | custom-call | tf_op jit(solution)/shard_map/front_phase/pallas_call | solution.py:502
  213.2 135.2 %feed_phase.1 = (f32[2,64,2560]{2,1,0:T(8,128)}, bf16[2,256,2560]{2,1,0:T(8,128)(2,1)}, f32[1,2560]{1,0:T(1,128)}, bf16[2,256,2560]{2,1,0:T(8,128)(2,1)}, f32[32...) custom-call(bf16[512,2560]{1,0:T(8,128)(2,1)} %get-tuple-element.62., ...), custom_call_target="tpu_custom_call" | custom-call | tf_op jit(solution)/shard_map/feed_phase/pallas_call | solution.py:502
  348.3 0.0 copy-start.10
  348.3 3.2 maximum_bitcast_fusion
  351.6 0.0 copy-done.10
  351.6 0.6 reshape.110.gain
  352.2 125.9 %mixer_back_phase.1 = (bf16[2,64,2560]{2,1,0:T(8,128)(2,1)}, f32[2,64,2560]{2,1,0:T(8,128)}, f32[8,640]{1,0:T(8,128)}, f32[8,640]{1,0:T(8,128)}, f32[32,640]{1,0...) custom-call(bf16[2,256,2560]{2,1,0:T(8,128)(2,1)} %get-tuple-element, ...), custom_call_target="tpu_custom_call" | custom-call | tf_op jit(solution)/shard_map/mixer_back_phase/pallas_call | solution.py:502
  478.1 0.0 copy-start.1
  478.1 0.0 copy-start.2
  478.1 0.0 copy-start.3
  478.1 3.4 pad_maximum_fusion.1
  481.5 0.0 copy-done.1
  481.5 0.0 copy-done.2
  481.5 0.0 copy-done.3
  481.5 0.0 copy-start.11
  481.5 0.0 copy-start.13
  481.6 0.0 copy-start.7
  481.6 0.0 copy-start
  481.6 1.6 pad_maximum_fusion
  483.2 0.0 copy-done.11
  483.2 0.6 squeeze.11
  483.8 0.6 squeeze.9
  484.4 0.0 copy-done.13
  484.4 0.6 slice.15
  485.0 0.6 slice_reduce_fusion
  485.6 0.0 copy-done.7
  485.6 0.8 copy.37
  486.5 0.0 copy-done
  486.5 1.1 copy.38
  487.5 0.9 copy.39
  488.4 0.9 copy.40
  489.3 0.6 copy.41
  490.0 0.6 copy.42
  490.6 0.9 copy.43
  (14 shorter events, 0.0 us)
Async XLA Ops:
  0.6 7.5 %copy-start.12 = (f32[2560]{0:T(1024)S(1)}, f32[2560]{0:T(1024)}, u32[]{:S(2)}) copy-start(f32[2560]{0:T(1024)} %param.25) | copy-start | bytes 30724
  0.7 8.1 %copy-start.14 = (f32[640]{0:T(1024)S(1)}, f32[640]{0:T(1024)}, u32[]{:S(2)}) copy-start(f32[640]{0:T(1024)} %param.23) | copy-start | bytes 7684
  348.3 3.3 copy-start.10
  478.1 3.4 copy-start.1
  478.1 3.4 copy-start.2
  478.1 3.4 copy-start.3
  481.5 1.6 copy-start.11
  481.5 2.9 copy-start.13
  481.6 4.1 copy-start.7
  481.6 4.9 copy-start
  483.2 4.4 copy-start.6
  485.6 2.8 copy-start.5
  486.5 2.9 copy-start.9
  486.5 3.5 copy-start.8
  486.5 4.1 copy-start.4

commit v5 on v4

--- a/solution.py
+++ b/solution.py
@@ -21,7 +21,7 @@
     return lax.axis_index("dp"), lax.axis_index("tensor")
 
 
-def greet(d, t, depth, dp_masks=(1, 2, 4), z_all=False):
+def greet(d, t, depth, dp_masks=(1, 2, 4), z_all=False, meanwhile=None):
     barrier = pltpu.get_barrier_semaphore()
     for mask in dp_masks:
         pl.semaphore_signal(barrier, inc=1, device_id=(d ^ mask, t), device_id_type=MESH)
@@ -30,6 +30,8 @@
             pl.semaphore_signal(
                 barrier, inc=1, device_id=(d, lax.rem(t + step, depth)), device_id_type=MESH
             )
+        if meanwhile is not None:
+            meanwhile()
         pl.semaphore_wait(barrier, len(dp_masks) + depth - 1)
         return
 
@@ -41,6 +43,8 @@
     def _():
         pl.semaphore_signal(barrier, inc=1, device_id=(d, t + 1), device_id_type=MESH)
 
+    if meanwhile is not None:
+        meanwhile()
     ends = jnp.where((t == 0) | (t == depth - 1), 1, 2)
     pl.semaphore_wait(barrier, len(dp_masks) + ends)
 
@@ -350,33 +354,48 @@
             device_id_type=MESH,
         )
 
+    def open(self, k):
+        t, depth = self.t, self.depth
+        if k == 0:
+            self.own.start()
+
+        @pl.when(t == k)
+        def _():
+            self.copy(0, 0, t, t + 1).start()
+
+        @pl.when(t == depth - 1 - k)
+        def _():
+            self.copy(1, 0, t, t - 1).start()
+
     def step(self, s):
         t, depth = self.t, self.depth
         if s == 0:
-            self.own.start()
-        if s > 0:
-
-            @pl.when(t - s >= 0)
+            for k in range(depth - 1):
+                self.open(k)
+            return
+
+        @pl.when((t - s >= 0) & (t < depth - 1))
+        def _():
+            self.copy(0, s - 1, t, t).wait_recv()
+            self.copy(0, s, t - s, t + 1).start()
+
+        @pl.when((t + s < depth) & (t > 0))
+        def _():
+            self.copy(1, s - 1, t, t).wait_recv()
+            self.copy(1, s, t + s, t - 1).start()
+
+    def finish(self):
+        t, depth = self.t, self.depth
+        self.own.wait()
+        for s in range(depth - 1):
+
+            @pl.when(t == depth - 1)
             def _():
-                self.copy(0, s - 1, t, t).wait_recv()
-
-        if s < depth - 1:
-
-            @pl.when((t - s >= 0) & (t < depth - 1))
+                self.copy(0, s, t, t).wait_recv()
+
+            @pl.when(t == 0)
             def _():
-                self.copy(0, s, t - s, t + 1).start()
-
-        if s > 0:
-
-            @pl.when(t + s < depth)
-            def _():
-                self.copy(1, s - 1, t, t).wait_recv()
-
-        if s < depth - 1:
-
-            @pl.when((t + s < depth) & (t > 0))
-            def _():
-                self.copy(1, s, t + s, t - 1).start()
+                self.copy(1, s, t, t).wait_recv()
 
     def end(self):
         t, depth = self.t, self.depth
@@ -396,11 +415,12 @@
 
 
 class LineScatter:
-    def __init__(self, part, got, send, recv, d, t, depth, which=None):
+    def __init__(self, part, got, send, recv, d, t, depth, which=None, first_row=None):
         self.part, self.got, self.send, self.recv = part, got, send, recv
         self.d, self.t, self.depth = d, t, depth
         self.which = range(part.shape[0]) if which is None else which
-        self.rows = part.shape[1] // depth
+        self.first_row = first_row
+        self.rows = got.shape[3]
 
     def slot(self, way, j, s):
         return self.got.at[way, j - 1 if way == 0 else j, s]
@@ -416,7 +436,11 @@
         )
 
     def block(self, j, s):
-        return self.part.at[s, pl.ds(pl.multiple_of(j * self.rows, self.rows), self.rows)]
+        start = j * self.rows
+        if self.first_row is not None:
+            start = pl.multiple_of(self.first_row + start, self.rows)
+            return self.part.at[pl.ds(start, self.rows)]
+        return self.part.at[s, pl.ds(pl.multiple_of(start, self.rows), self.rows)]
 
     def start(self, first=0, last=None):
         t, depth = self.t, self.depth
@@ -457,21 +481,20 @@
 
     def total(self, out):
         t, depth = self.t, self.depth
-        mine = pl.ds(pl.multiple_of(t * self.rows, self.rows), self.rows)
         for s in self.which:
-            out[s] = self.part[s, mine, :].astype(F32)
+            out[s][...] = self.block(t, s)[...].astype(F32)
 
         @pl.when(t > 0)
         def _():
             for s in self.which:
                 self.copy(0, t, s, self.slot(0, t, s), t).wait_recv()
-                out[s] += self.got[0, t - 1, s].astype(F32)
+                out[s][...] += self.got[0, t - 1, s].astype(F32)
 
         @pl.when(t < depth - 1)
         def _():
             for s in self.which:
                 self.copy(1, t, s, self.slot(1, t, s), t).wait_recv()
-                out[s] += self.got[1, t, s].astype(F32)
+                out[s][...] += self.got[1, t, s].astype(F32)
 
     def end(self):
         t, depth = self.t, self.depth
@@ -553,7 +576,7 @@
     return lax.dot_general(left, right, ((dims[:1], dims[1:]), ((), ())), preferred_element_type=F32)
 
 
-def scan_rows(rate, out, seqs, length, base=0, backward=False):
+def scan_rows(rate, out, which, length, base=0, backward=False):
     tile = 8
     width = out.shape[1]
     row = lax.broadcasted_iota(jnp.int32, (tile, width), 0)
@@ -561,7 +584,7 @@
     def body(i, carried):
         k = length // tile - 1 - i if backward else i
         ends = []
-        for s in range(seqs):
+        for at, s in enumerate(which):
             start = pl.multiple_of(s * length + k * tile, tile)
             rows = pl.ds(start, tile)
             if backward:
@@ -578,13 +601,13 @@
                 before = jnp.where(inside, pltpu.roll(drive, turn, 0), 0.0)
                 drive = drive + step * before
                 step = step * jnp.where(inside, pltpu.roll(step, turn, 0), 1.0)
-            states = drive + step * carried[s]
+            states = drive + step * carried[at]
             out[held, :] = states
             ends.append(states[0:1] if backward else states[tile - 1 : tile])
         return tuple(ends)
 
-    start = tuple(jnp.zeros((1, width), F32) for _ in range(seqs))
-    lax.fori_loop(0, length // tile, body, start)
+    start = tuple(jnp.zeros((1, width), F32) for _ in which)
+    lax.fori_loop(0, length // tile, body, start, unroll=2)
 
 
 STRIP = 16
@@ -603,8 +626,8 @@
 
 def front_kernel(
     depth,
-    normed_block,
-    cot_block,
+    cotangent,
+    token_weight,
     gelu_shard,
     input_shard,
     gate_in_shard,
@@ -617,6 +640,7 @@
     rate,
     act,
     gain,
+    first_gain,
     middle,
     normed_out,
     cot_out,
@@ -644,23 +668,35 @@
     normed, gelu_w, input_w, gate_in_w, gate_dec_w, out_w = scratch[:6]
     gelu_pre, input_pre, conv, window, gate_in, gate_dec, decay, states, mixed, part = scratch[6:16]
     local, send, recv = scratch[16:19]
-    line_sems = [scratch[19 + 3 * i : 22 + 3 * i] for i in range(5)]
-    rim_send, rim_recv, save_sem = scratch[34:37]
-    cot, normed_two, block_two, panel_w, product = scratch[37:42]
-    panel_sem, product_sem = scratch[42:44]
-    got, ssem, rsem = scratch[44:47]
+    line_sems = [scratch[19 + 3 * i : 22 + 3 * i] for i in range(6)]
+    rim_send, rim_recv, save_sem = scratch[37:40]
+    cot, normed_two, block_two, panel_w, product = scratch[40:45]
+    panel_sem, product_sem = scratch[45:47]
+    got, ssem, rsem = scratch[47:50]
+    normed_block, cot_block = scratch[50:52]
     d, t = place()
     parity = lax.rem(t, 2)
     even = parity == 0
     odd = parity == 1
-    greet(d, t, depth)
+
+    def prepare():
+        for s in range(act.shape[0]):
+            value = act[s].astype(F32)
+            inverse = lax.rsqrt(jnp.mean(value * value, axis=-1, keepdims=True) + EPS)
+            normed_block[s] = (value * inverse * first_gain[...]).astype(BF16)
+            cot_block[s] = (cotangent[s].astype(F32) * token_weight[s]).astype(BF16)
+
+    greet(d, t, depth, meanwhile=prepare)
     seqs, length, model = normed.shape
     tokens = seqs * length
     width = conv.shape[1]
     block = gate_in_w.shape[0]
     half = block // 2
     spans = [pl.ds(s * length, length) for s in range(seqs)]
-    first_line = LineGather(normed_block, normed, *line_sems[0], d, t, depth)
+    firsts = [
+        LineGather(normed_block.at[s], normed.at[s], *line_sems[5 * s], d, t, depth)
+        for s in range(seqs)
+    ]
     cots = [
         LineGather(cot_block.at[s], cot.at[spans[s]], *line_sems[1 + s], d, t, depth)
         for s in range(seqs)
@@ -691,42 +727,23 @@
         copy.start()
         saves.append(copy)
 
-    one = gathers[:4]
+    one = [gathers[1], gathers[0], gathers[2], gathers[3]]
     out_g, down_g, gate_g, up_g = gathers[4:]
-    first_line.step(0)
-    for g in one:
-        g.start()
-    for g in one:
-        g.relay()
-    out_g.start()
-    first_line.step(1)
-    for g in one:
-        g.relay_two()
-    for g in one:
-        g.relay_last()
-    first_line.step(2)
-    out_g.relay()
-    down_g.start()
-    out_g.relay_two()
-    out_g.relay_last()
-    first_line.step(3)
-    first_line.own.wait()
-    cots[0].step(0)
-    for g in one:
-        g.arrive()
-    save(normed, normed_out)
-    save(gelu_w, gelu_full)
-    save(input_w, input_full)
-    save(gate_in_w, gate_in_full)
-    save(gate_dec_w, gate_dec_full)
-
-    for s in range(seqs):
-        rows = pl.ds(s * length, length)
+    even_blocks, odd_blocks = gate_blocks(0, width, block), gate_blocks(1, width, block)
+
+    def rim(s, to, src, dst):
+        return pltpu.make_async_remote_copy(
+            src_ref=conv.at[spans[s], pl.ds(src, half)],
+            dst_ref=window.at[spans[s], pl.ds(dst, half)],
+            send_sem=rim_send.at[s],
+            recv_sem=rim_recv.at[s],
+            device_id=(d, to),
+            device_id_type=MESH,
+        )
+
+    def convolve(s):
         input_pre[s, 0:8, :] = jnp.zeros((8, width), F32)
         input_pre[s, 8 : 8 + length, :] = contract(normed[s], input_w[...], (1, 0))
-        gelu_pre[rows, :] = contract(normed[s], gelu_w[...], (1, 0))
-
-    for s in range(seqs):
 
         @pl.loop(0, length // STRIP)
         def _(i):
@@ -737,78 +754,64 @@
             rows = pl.ds(pl.multiple_of(s * length + i * STRIP, STRIP), STRIP)
             conv[rows, :] = total.astype(BF16)
 
-    def rim(to, src, dst):
-        return pltpu.make_async_remote_copy(
-            src_ref=conv.at[:, pl.ds(src, half)],
-            dst_ref=window.at[:, pl.ds(dst, half)],
-            send_sem=rim_send,
-            recv_sem=rim_recv,
-            device_id=(d, to),
-            device_id_type=MESH,
-        )
-
-    @pl.when(even)
-    def _():
-        rim(t + 1, width - half, 0).start()
-        window[:, 0:width] = conv[...]
-
-    @pl.when(odd)
-    def _():
-        rim(t - 1, 0, width).start()
-        window[:, half : half + width] = conv[...]
-
-    def gates(blocks):
+        @pl.when(even)
+        def _():
+            rim(s, t + 1, width - half, 0).start()
+            window[spans[s], 0:width] = conv[spans[s], :]
+
+        @pl.when(odd)
+        def _():
+            rim(s, t - 1, 0, width).start()
+            window[spans[s], half : half + width] = conv[spans[s], :]
+
+    def gates(s, blocks):
         for k, low, high in blocks:
-            near = window[:, k * block : (k + 1) * block]
-            gate_in[:, low:high] = contract(near, gate_in_w[:, low:high], (1, 0))
-            gate_dec[:, low:high] = contract(near, gate_dec_w[:, low:high], (1, 0))
-
-    even_blocks, odd_blocks = gate_blocks(0, width, block), gate_blocks(1, width, block)
-
-    @pl.when(even)
-    def _():
-        gates(even_blocks[:-1])
-
-    @pl.when(odd)
-    def _():
-        gates(odd_blocks[1:])
-
-    cots[0].step(1)
-    down_g.relay()
-    gate_g.start()
-
-    @pl.when(even)
-    def _():
-        rim(t + 1, width - half, width).wait_recv()
-        gates(even_blocks[-1:])
-
-    @pl.when(odd)
-    def _():
-        rim(t - 1, 0, 0).wait_recv()
-        gates(odd_blocks[:1])
-
-    @pl.loop(0, tokens // STRIP)
-    def _(i):
-        rows = rows_of(i, STRIP)
-        log = -8.0 * sigmoid(gate_dec[rows, :]) * rate[...]
-        decay[rows, :] = jnp.exp(log)
-        drive = jnp.sqrt(one_less_exp(2.0 * log)) * sigmoid(gate_in[rows, :])
-        held = pl.ds(pl.multiple_of(i * STRIP + 8, 8), STRIP)
-        states[held, :] = drive * conv[rows, :].astype(F32)
-
-    states[0:8, :] = jnp.zeros((8, width), F32)
-    cots[0].step(2)
-    scan_rows(decay, states, seqs, length, base=8)
-
-    @pl.loop(0, tokens // STRIP)
-    def _(i):
-        rows = rows_of(i, STRIP)
-        held = pl.ds(pl.multiple_of(i * STRIP + 8, 8), STRIP)
-        mixed[rows, :] = (gelu(gelu_pre[rows, :]) * states[held, :]).astype(BF16)
-
-    panel = 512
-    out_g.arrive()
-    for s in range(seqs):
+            near = window[spans[s], k * block : (k + 1) * block]
+            gate_in[spans[s], low:high] = contract(near, gate_in_w[:, low:high], (1, 0))
+            gate_dec[spans[s], low:high] = contract(near, gate_dec_w[:, low:high], (1, 0))
+
+    def inner_gates(s):
+        gelu_pre[spans[s], :] = contract(normed[s], gelu_w[...], (1, 0))
+
+        @pl.when(even)
+        def _():
+            gates(s, even_blocks[:-1])
+
+        @pl.when(odd)
+        def _():
+            gates(s, odd_blocks[1:])
+
+    def recur(s):
+        @pl.when(even)
+        def _():
+            rim(s, t + 1, width - half, width).wait_recv()
+            gates(s, even_blocks[-1:])
+
+        @pl.when(odd)
+        def _():
+            rim(s, t - 1, 0, 0).wait_recv()
+            gates(s, odd_blocks[:1])
+
+        @pl.loop(0, length // STRIP)
+        def _(i):
+            start = pl.multiple_of(s * length + i * STRIP, STRIP)
+            rows = pl.ds(start, STRIP)
+            log = -8.0 * sigmoid(gate_dec[rows, :]) * rate[...]
+            decay[rows, :] = jnp.exp(log)
+            drive = jnp.sqrt(one_less_exp(2.0 * log)) * sigmoid(gate_in[rows, :])
+            held = pl.ds(pl.multiple_of(start + 8, 8), STRIP)
+            states[held, :] = drive * conv[rows, :].astype(F32)
+
+        scan_rows(decay, states, (s,), length, base=8)
+
+    def mix(s):
+        @pl.loop(0, length // STRIP)
+        def _(i):
+            start = pl.multiple_of(s * length + i * STRIP, STRIP)
+            rows, held = pl.ds(start, STRIP), pl.ds(pl.multiple_of(start + 8, 8), STRIP)
+            mixed[rows, :] = (gelu(gelu_pre[rows, :]) * states[held, :]).astype(BF16)
+
+        panel = 512
 
         @pl.loop(0, model // panel)
         def _(i):
@@ -817,11 +820,71 @@
                 BF16
             )
 
-        scatters[s].start()
-    cots[0].step(3)
-    cots[1].step(0)
-    down_g.relay_two()
+    def norm_step(s):
+        scatters[s].total([middle.at[i] for i in range(seqs)])
+        value = middle[s] + act[s].astype(F32)
+        middle[s] = value
+        inverse = lax.rsqrt(jnp.mean(value * value, axis=-1, keepdims=True) + EPS)
+        block_two[s] = (value * inverse * gain[...]).astype(BF16)
+        twos[s].step(0)
+
+    firsts[0].step(0)
+    for g in one:
+        g.start()
+    firsts[0].step(1)
+    firsts[1].step(0)
+    for g in one:
+        g.relay()
+    out_g.start()
+    firsts[0].step(2)
+    for line in cots:
+        line.open(0)
+    for g in one:
+        g.relay_two()
+    firsts[1].step(1)
+    for g in one:
+        g.relay_last()
+    firsts[0].finish()
+    for line in cots:
+        line.open(1)
+    one[0].arrive()
+    states[0:8, :] = jnp.zeros((8, width), F32)
+    convolve(0)
+    out_g.relay()
+    down_g.start()
+    gate_g.start()
+    for g in one[1:]:
+        g.arrive()
+    inner_gates(0)
+    out_g.relay_two()
+    firsts[1].step(2)
+    recur(0)
+    out_g.relay_last()
+    out_g.arrive()
+    mix(0)
+    firsts[1].finish()
+    scatters[0].start(0, 1)
+    for line in cots:
+        line.open(2)
+    convolve(1)
+    scatters[0].start(1)
+    for line in cots:
+        line.step(1)
+    inner_gates(1)
     scatters[0].step(1)
+    down_g.relay()
+    recur(1)
+    scatters[0].step(2)
+    mix(1)
+    scatters[1].start()
+    for line in cots:
+        line.step(2)
+    save(normed, normed_out)
+    save(gelu_w, gelu_full)
+    save(input_w, input_full)
+    save(gate_in_w, gate_in_full)
+    save(gate_dec_w, gate_dec_full)
+    save(out_w, out_full)
     save(gelu_pre, gelu_pre_out)
     save(input_pre, input_pre_out)
     save(conv, conv_out)
@@ -830,36 +893,27 @@
     save(gate_dec, gate_dec_out)
     save(states, states_out)
     save(mixed, mixed_out)
-    save(out_w, out_full)
-    scatters[0].step(2)
-    down_g.relay_last()
-
-    def norm_step(s):
-        scatters[s].total(middle)
-        value = middle[s] + act[s].astype(F32)
-        middle[s] = value
-        inverse = lax.rsqrt(jnp.mean(value * value, axis=-1, keepdims=True) + EPS)
-        block_two[s] = (value * inverse * gain[...]).astype(BF16)
-        twos[s].step(0)
-
+    down_g.relay_two()
+    scatters[1].step(1)
     norm_step(0)
     gate_g.relay()
     up_g.start()
-    scatters[1].step(1)
-    twos[0].step(1)
     scatters[1].step(2)
     gate_g.relay_two()
+    twos[0].step(1)
     norm_step(1)
-    cots[1].step(1)
+    twos[0].step(2)
+    down_g.relay_last()
+    twos[1].step(1)
+    twos[1].step(2)
     gate_g.relay_last()
-    twos[0].step(2)
-    cots[1].step(2)
-    twos[1].step(1)
-    cots[1].step(3)
-    for s in range(seqs):
-        cots[s].own.wait()
+    for line in cots:
+        line.finish()
     save(cot, cot_out)
     up_g.relay()
+    for line in twos:
+        line.finish()
+    save(normed_two, normed_two_out)
     panels = down_full.shape[1] // PANEL
 
     def load_panel(full, i):
@@ -895,13 +949,7 @@
             i,
             (down_full, i + 1) if i < panels - 1 else (gate_full, panels),
         )
-    twos[0].step(3)
-    twos[1].step(2)
     up_g.relay_two()
-    twos[1].step(3)
-    for s in range(seqs):
-        twos[s].own.wait()
-    save(normed_two, normed_two_out)
     for i in range(panels, 2 * panels):
         multiply(
             normed_two,
@@ -913,24 +961,26 @@
     up_g.relay_last()
     up_g.arrive()
 
-    @pl.when(even)
-    def _():
-        rim(t + 1, width - half, 0).wait_send()
-
-    @pl.when(odd)
-    def _():
-        rim(t - 1, 0, width).wait_send()
+    for s in range(seqs):
+
+        @pl.when(even)
+        def _():
+            rim(s, t + 1, width - half, 0).wait_send()
+
+        @pl.when(odd)
+        def _():
+            rim(s, t - 1, 0, width).wait_send()
 
     for g in gathers:
         g.end()
-    for line in [first_line] + cots + twos + scatters:
+    for line in firsts + cots + twos + scatters:
         line.end()
     for copy in saves + results[-2:]:
         copy.wait()
 
 
-def front_phase(normed, cot, weights, taps, rate, act, gain, depth):
-    seqs, rows, model = normed.shape
+def front_phase(cotangent, token_weight, weights, taps, rate, act, gain, first_gain, depth):
+    seqs, rows, model = act.shape
     length = rows * depth
     tokens = seqs * length
     n = len(weights)
@@ -959,7 +1009,7 @@
     scratch = [pltpu.VMEM(wide_rows, BF16)]
     scratch += [pltpu.VMEM(shape, BF16) for shape in mixers]
     scratch += [pltpu.VMEM(shape, dtype) for shape, dtype in saved_scratch]
-    scratch += gather_scratch(n) + line_gather_scratch(depth) * 5 + [DMA, DMA, DMA((16,))]
+    scratch += gather_scratch(n) + line_gather_scratch(depth) * 6 + [DMA((seqs,)), DMA((seqs,)), DMA((16,))]
     scratch += [
         pltpu.VMEM((tokens, model), BF16),
         pltpu.VMEM((tokens, model), BF16),
@@ -970,14 +1020,17 @@
         DMA((2,)),
     ]
     scratch += line_scatter_scratch(seqs, rows, model, depth)
+    scratch += [pltpu.VMEM(act.shape, BF16)] * 2
     res = call(
         functools.partial(front_kernel, depth),
         "front_phase",
         0,
-        [VMEM] * (6 + n),
+        [VMEM] * (7 + n),
         outs,
         scratch,
-        (normed, cot) + tuple(weights) + (taps, rate.reshape(1, width), act, gain.reshape(1, model)),
+        (cotangent, token_weight)
+        + tuple(weights)
+        + (taps, rate.reshape(1, width), act, gain.reshape(1, model), first_gain.reshape(1, model)),
     )
     return res[0], res[1:4], res[4:9], res[9:12], res[12:20], res[20:]
 
@@ -990,7 +1043,7 @@
     return grad, jnp.sum(error * value * inverse, axis=0, keepdims=True)
 
 
-HOSTED = 5
+HOSTED = 6
 
 
 def feed_kernel(
@@ -1004,29 +1057,36 @@
     gate_pre_in,
     middle,
     gain,
-    cot_own,
+    cotangent,
+    token_weight,
     grad,
     wide,
     gain_grad,
-    feed_out,
+    output,
     *refs,
 ):
     panels = gate_in.shape[1] // PANEL
     n_panels = 3 * panels
     outs, refs = refs[:n_panels], refs[n_panels:]
     normed, cot, hidden, gate_rows, lift_rows = refs[:5]
-    gate_w, up_w, down_w, gate_pre, lift_pre, grad_hidden, acc, part, block, stage = refs[5:15]
-    got, ssem, rsem = refs[15:18]
-    load_sem, weight_sem, save_sem = refs[18:21]
-    lines = refs[21:24], refs[24:27]
+    gate_w, up_w, down_w, gate_pre, lift_pre, grad_hidden, acc, part, block = refs[5:14]
+    got, ssem, rsem = refs[14:17]
+    feed_got, feed_ssem, feed_rsem = refs[17:20]
+    load_sem, weight_sem, save_sem = refs[20:23]
+    lines = refs[23:26], refs[26:29]
     d, t = place()
     greet(d, t, depth)
     seqs = middle.shape[0]
     tokens, model = normed_in.shape
     length = tokens // seqs
     tile = 512
-    ring = PanelRing(outs[:HOSTED], refs[27:], d, t)
+    ring = PanelRing(outs[:HOSTED], refs[29:], d, t)
     scatters = [LineScatter(part, got, ssem, rsem, d, t, depth, (s,)) for s in range(seqs)]
+    feeds = [
+        LineScatter(cot, feed_got, feed_ssem, feed_rsem, d, t, depth, (s,), s * length)
+        for s in range(seqs)
+    ]
+    own_rows = middle.shape[1]
     gathers = [
         LineGather(block.at[s], wide.at[s], *lines[s], d, t, depth) for s in range(seqs)
     ]
@@ -1118,19 +1178,51 @@
         panel = ring.panels[i]
         weight_grad(i, panel.grad)
         panel.start()
-        panel.first()
-        panel.second()
+
+    def push(i):
+        ring.panels[i].first()
+        ring.panels[i].second()
 
     def norm_step(s):
-        scatters[s].total(grad)
+        scatters[s].total([grad.at[i] for i in range(seqs)])
         change, gain_part = norm_back(middle[s], gain[...], grad[s])
-        change = change + cot_own[s]
+        change = change + cotangent[s].astype(F32) * token_weight[s]
         grad[s] = change
         block[s] = change.astype(BF16)
         if s == 0:
             gain_grad[...] = gain_part
         else:
             gain_grad[...] += gain_part
+
+    def feed(s):
+        rows = pl.ds(s * length, length)
+        downs = (gate_w, up_w, down_w)
+
+        @pl.loop(0, model // tile)
+        def _(i):
+            out = rows_of(i, tile)
+            value = contract(hidden[rows, 0:PANEL], downs[0][out, :], (1, 1))
+            for p in range(1, panels):
+                columns = pl.ds(p * PANEL, PANEL)
+                value = value + contract(hidden[rows, columns], downs[p][out, :], (1, 1))
+            cot[rows, out] = value.astype(BF16)
+
+        feeds[s].start()
+
+    def feed_end(s):
+        total = acc.at[pl.ds(s * own_rows, own_rows)]
+        feeds[s].total([total] * seqs)
+        output[s] = (total[...] + middle[s]).astype(BF16)
+
+    pending = {}
+
+    def store_grad(i):
+        q = i % ring.slots
+        if q in pending:
+            pending.pop(q).wait()
+        weight_grad(i, ring.panels[q].grad)
+        pending[q] = pltpu.make_async_copy(ring.panels[q].grad, outs[i], save_sem.at[q])
+        pending[q].start()
 
     for p in range(panels):
         forward(0, p, (p + 1) % panels)
@@ -1141,87 +1233,66 @@
     begin(0)
     forward(1, 1, 2)
     scatters[0].step(2)
-    ring.panels[0].third()
+    push(0)
     begin(1)
     forward(1, 2, None)
     down_loads = [weight(0, down_in, gate_w, 0), weight(1, down_in, up_w, 1)]
     down_loads.append(weight(2, down_in, down_w, 2))
     scatters[1].start()
+    ring.panels[0].third()
     norm_step(0)
     gathers[0].step(0)
-    ring.panels[0].end()
-    ring.panels[1].third()
+    push(1)
     begin(2)
     scatters[1].step(1)
     gathers[0].step(1)
-    ring.panels[1].end()
-    ring.panels[2].third()
-    begin(3)
+    ring.panels[0].end()
+    ring.panels[1].third()
+    push(2)
     scatters[1].step(2)
     gathers[0].step(2)
-    ring.panels[2].end()
-    ring.panels[3].third()
-    begin(4)
-    norm_step(1)
-    gathers[1].step(0)
-    gathers[0].step(3)
-    pending = {}
-
-    def keep(key, src, dst):
-        if key in pending:
-            pending[key].wait()
-        pending[key] = pltpu.make_async_copy(src, dst, save_sem.at[key])
-        pending[key].start()
-
-    def feed(s):
-        rows = pl.ds(s * length, length)
-        if pending:
-            pending.pop(0).wait()
-        downs = (gate_w, up_w, down_w)
-
-        @pl.loop(0, model // tile)
-        def _(i):
-            out = rows_of(i, tile)
-            value = contract(hidden[rows, 0:PANEL], downs[0][out, :], (1, 1))
-            for p in range(1, panels):
-                columns = pl.ds(p * PANEL, PANEL)
-                value = value + contract(hidden[rows, columns], downs[p][out, :], (1, 1))
-            stage[:, out] = value.astype(BF16)
-
-        keep(0, stage, feed_out.at[s])
-
-    def store_grad(i):
-        q = i % ring.slots
-        if 1 + q in pending:
-            pending.pop(1 + q).wait()
-        weight_grad(i, ring.panels[q].grad)
-        keep(1 + q, ring.panels[q].grad, outs[i])
-
     for copy in down_loads:
         copy.wait()
     feed(0)
+    begin(3)
+    ring.panels[1].end()
+    ring.panels[2].third()
+    norm_step(1)
+    gathers[1].step(0)
+    feed(1)
+    push(3)
+    begin(4)
+    feeds[0].step(1)
     gathers[1].step(1)
+    ring.panels[2].end()
+    ring.panels[3].third()
+    push(4)
+    begin(5)
+    feeds[0].step(2)
+    gathers[1].step(2)
     ring.panels[3].end()
     ring.panels[4].third()
-    feed(1)
-    gathers[1].step(2)
-    store_grad(5)
+    push(5)
     store_grad(6)
+    feeds[1].step(1)
     ring.panels[4].end()
-    gathers[1].step(3)
+    ring.panels[5].third()
     store_grad(7)
+    feeds[1].step(2)
+    feed_end(0)
+    ring.panels[5].end()
     store_grad(8)
+    feed_end(1)
+    for line in gathers:
+        line.finish()
     ring.end()
     for copy in pending.values():
         copy.wait()
-    for line in scatters:
+    for line in scatters + feeds + gathers:
         line.end()
-    for line in gathers:
-        line.own.wait()
-        line.end()
-
-
-def feed_phase(normed, cot, weights, held, middle, gain, cot_own, depth):
+
+
+def feed_phase(normed, cot, weights, held, middle, gain, cotangent, token_weight, depth):
     down_w, gate_w, up_w = weights
     seqs, rows, model = middle.shape
     tokens = normed.shape[0]
@@ -1233,7 +1304,7 @@
         shaped(middle.shape, F32, VMEM),
         shaped(wide_rows, BF16, ANY),
         shaped((1, model), F32, VMEM),
-        shaped(wide_rows, BF16, ANY),
+        shaped(middle.shape, BF16, VMEM),
     ]
     outs += [shaped((model // 8, PANEL), F32, ANY)] * HOSTED
     outs += [shaped((model, PANEL), BF16, ANY)] * (count - HOSTED)
@@ -1246,20 +1317,20 @@
         pltpu.VMEM((length, model), F32),
         pltpu.VMEM(wide_rows, BF16),
         pltpu.VMEM(middle.shape, BF16),
-        pltpu.VMEM((length, model), BF16),
     ]
-    scratch += line_scatter_scratch(seqs, rows, model, depth)
-    scratch += [DMA((6,)), DMA((3,)), DMA((8,))]
+    scratch += line_scatter_scratch(seqs, rows, model, depth) * 2
+    scratch += [DMA((6,)), DMA((3,)), DMA((3,))]
     scratch += line_gather_scratch(depth) * 2
     scratch += ring_scratch(3, model // 8, PANEL)
     res = call(
         functools.partial(feed_kernel, depth),
         "feed_phase",
         2,
-        [ANY] * 7 + [VMEM] * 3,
+        [ANY] * 7 + [VMEM] * 4,
         outs,
         scratch,
-        (normed, cot, gate_w, up_w, down_w) + tuple(held) + (middle, gain.reshape(1, model), cot_own),
+        (normed, cot, gate_w, up_w, down_w) + tuple(held) + (middle, gain.reshape(1, model), cotangent, token_weight),
+        vmem=63 * 1024 * 1024,
     )
     return res[0], res[1], res[2], res[3], res[4:]
 
@@ -1282,8 +1353,6 @@
     input_w_in,
     gate_in_w_in,
     gate_dec_w_in,
-    feed,
-    middle,
     taps,
     rate,
     act,
@@ -1294,19 +1363,18 @@
 ):
     panels_in, refs = refs[:n_panels], refs[n_panels:]
     n_sums = n_panels + 3
-    output, input_grad, gains, smalls, gate_in_out, gate_dec_out = refs[:6]
-    panels_out, scratch = refs[6 : 6 + n_sums], refs[6 + n_sums :]
+    input_grad, gains, smalls, gate_in_out, gate_dec_out = refs[:5]
+    panels_out, scratch = refs[5 : 5 + n_sums], refs[5 + n_sums :]
     branch, weight, input_w = scratch[:3]
     gelu_pre, input_pre, conv, window, gate_in, gate_dec, states, gate_in_w, gate_dec_w = scratch[3:12]
     grad, decay, grad_conv, gelu_grad, input_rows, grad_in, grad_dec, mixed = scratch[12:20]
-    rim_out, rim_in, gate_in_grad, gate_dec_grad, part, sums, total = scratch[20:27]
-    got, ssem, rsem = scratch[27:30]
-    last_got, last_ssem, last_rsem = scratch[30:33]
-    rim_send, rim_recv, load_sem, panel_sem = scratch[33:37]
-    small, small_all, pack, packs, line_pack, line_packs = scratch[37:43]
-    psend, precv, qsend, qrecv, zsend, zrecv = scratch[43:49]
-    ring = PanelRing(panels_out, scratch[49:58], *place())
+    rim_out, rim_in, gate_in_grad, gate_dec_grad, part, sums = scratch[20:26]
+    got, ssem, rsem = scratch[26:29]
+    rim_send, rim_recv, load_sem, panel_sem = scratch[29:33]
+    small, small_all, pack, packs, line_pack, line_packs = scratch[33:39]
+    psend, precv, qsend, qrecv, zsend, zrecv = scratch[39:45]
     d, t = place()
+    ring = PanelRing(panels_out, scratch[45:54], d, t)
     parity = lax.rem(t, 2)
     even = parity == 0
     odd = parity == 1
@@ -1321,12 +1389,11 @@
         (gate_in_grad, gate_dec_grad),
         (gate_in_out, gate_dec_out),
         (False, False),
-        scratch[58:],
+        scratch[54:],
         d,
         t,
     )
-    line = LineScatter(feed, got, ssem, rsem, d, t, depth)
-    last_line = LineScatter(part, last_got, last_ssem, last_rsem, d, t, depth)
+    lines = [LineScatter(part, got, ssem, rsem, d, t, depth, (s,)) for s in range(seqs)]
 
     def load(i, src, dst):
         copy = pltpu.make_async_copy(src, dst, load_sem.at[i])
@@ -1344,7 +1411,6 @@
         load(3, states_in, states),
         load(4, gate_dec_in, gate_dec),
     ]
-    line.start(0, 1)
     panel_loads = [
         pltpu.make_async_copy(src, panel.grad, panel_sem.at[i])
         for i, (src, panel) in enumerate(zip(panels_in, ring.panels))
@@ -1375,16 +1441,13 @@
         if i < n_panels:
             panel_loads[i].wait()
         ring.panels[i].start()
+
+    def push(i):
         ring.panels[i].first()
         ring.panels[i].second()
 
-    def finish(i):
-        ring.panels[i].end()
-        if i + ring.slots < n_panels:
-            panel_loads[i + ring.slots].start()
-
-    for i in range(ring.slots):
-        panel_loads[i].start()
+    for copy in panel_loads:
+        copy.start()
     then = [
         load(5, gate_in_in, gate_in),
         load(6, conv_in, conv),
@@ -1395,13 +1458,15 @@
         load(11, input_w_in, input_w),
         load(1, mixed_in, mixed),
     ]
+    for i in range(n_panels):
+        begin(i)
     for copy in early:
         copy.wait()
     for s in range(seqs):
         rows = pl.ds(s * length, length)
         grad[rows, :] = contract(branch[rows, :], weight[...], (1, 0))
     reload = load(0, gelu_w_in, weight)
-    begin(0)
+    push(0)
     for copy in next_:
         copy.wait()
 
@@ -1416,9 +1481,9 @@
         decay[rows, :] = jnp.exp(-8.0 * sigmoid(gate_dec[rows, :]) * rate[...])
 
     decay[tokens : tokens + 8, :] = jnp.zeros((8, width), F32)
-    begin(1)
+    push(1)
     ring.panels[0].third()
-    scan_rows(decay, grad, seqs, length, backward=True)
+    scan_rows(decay, grad, range(seqs), length, backward=True)
     for copy in then:
         copy.wait()
     sums[...] = jnp.zeros(sums.shape, F32)
@@ -1486,10 +1551,9 @@
         rim(t - 1).start()
         add_conv(0, half, value[:, half:])
 
-    line.start(1)
-    line.step(1)
-    finish(0)
+    ring.panels[0].end()
     ring.panels[1].third()
+    push(2)
 
     def inner(blocks):
         for k, low, high in blocks:
@@ -1513,7 +1577,9 @@
 
     for g in gate_scatters:
         g.start()
-    begin(2)
+    weight_grad(branch, mixed, ring.panels[3].grad)
+    begin(3)
+    wide_loads = load_wide(12, normed_in)
 
     @pl.when(even)
     def _():
@@ -1541,8 +1607,9 @@
             rows = pl.ds(pl.multiple_of(s * length + i * STRIP, STRIP), STRIP)
             input_rows[rows, :] = value.astype(BF16)
 
-    finish(1)
+    ring.panels[1].end()
     ring.panels[2].third()
+    push(3)
     for k in range(sums.shape[0]):
         small[k : k + 1, :] = jnp.sum(sums[k], axis=0, keepdims=True)
     small[sums.shape[0] :, :] = jnp.zeros((8 - sums.shape[0], width), F32)
@@ -1561,36 +1628,35 @@
         for s in range(seqs):
             part[s, :, columns] = value[s * length : (s + 1) * length]
 
-    last_line.start()
-    begin(3)
+    for line in lines:
+        line.start()
+    for copy in wide_loads:
+        copy.wait()
+    weight_grad(branch, gelu_grad, ring.panels[4].grad)
+    begin(4)
     for g in gate_scatters:
         g.first()
         g.second()
-    line.step(2)
-    finish(2)
+    ring.panels[2].end()
     ring.panels[3].third()
-    weight_grad(branch, mixed, ring.panels[4].grad)
-    wide_loads = load_wide(12, normed_in)
-    begin(4)
+    push(4)
+    lines[0].step(1)
+    weight_grad(branch, input_rows, ring.panels[5].grad)
+    begin(5)
     for g in gate_scatters:
         g.third()
-    line.total(total)
-    output[...] = (total[...] + middle[...]).astype(BF16)
-    finish(3)
+    lines[0].step(2)
+    ring.panels[3].end()
     ring.panels[4].third()
-    for copy in wide_loads:
-        copy.wait()
-    weight_grad(branch, gelu_grad, ring.panels[5].grad)
-    begin(5)
-    last_line.step(1)
-    finish(4)
+    push(5)
+    lines[1].step(1)
+    lines[1].step(2)
+    for g in gate_scatters:
+        g.end()
+    ring.panels[4].end()
     ring.panels[5].third()
-    weight_grad(branch, input_rows, ring.panels[6].grad)
-    begin(6)
-    last_line.step(2)
-    finish(5)
-    ring.panels[6].third()
-    last_line.total(input_grad)
+    for s in range(seqs):
+        lines[s].total([input_grad.at[i] for i in range(seqs)])
     quarter = pack.shape[1]
     for i in range(4):
         pack[4 + i : 5 + i, :] = mlp_part[:, i * quarter : (i + 1) * quarter]
@@ -1613,8 +1679,6 @@
     for i in range(1, 8):
         sum_ = sum_ + small_all[i]
     smalls[...] = sum_
-    for g in gate_scatters:
-        g.end()
     for c in pack_copies:
         c.wait_recv()
     sum_ = packs[0]
@@ -1635,7 +1699,7 @@
     for c in z_copies:
         c.start()
     line_packs[t] = sum_
-    finish(6)
+    ring.panels[5].end()
     for c in z_copies:
         c.wait_recv()
     sum_ = line_packs[0]
@@ -1645,13 +1709,12 @@
     for c in small_copies + pack_copies + z_copies:
         c.wait_send()
     ring.end()
-    line.end()
-    last_line.end()
+    for line in lines:
+        line.end()
 
 
 def mixer_back_phase(
-    branch, normed, saved, weights, panels, feed, middle, taps, rate, act, gain, grad_middle,
-    mlp_part, depth,
+    branch, normed, saved, weights, panels, taps, rate, act, gain, grad_middle, mlp_part, depth,
 ):
     seqs, length, model = branch.shape
     tokens = seqs * length
@@ -1667,8 +1730,7 @@
     small = (8, width)
     flat = (tokens, width)
     outs = [
-        shaped(middle.shape, BF16, VMEM),
-        shaped(middle.shape, F32, VMEM),
+        shaped(act.shape, F32, VMEM),
         shaped(pack, F32, VMEM),
         shaped(small, F32, VMEM),
         shaped(gate, F32, VMEM),
@@ -1702,9 +1764,8 @@
     scratch += [
         pltpu.VMEM(branch.shape, BF16),
         pltpu.VMEM((1 + taps.shape[0], 8, width), F32),
-        pltpu.VMEM(middle.shape, F32),
     ]
-    scratch += line_scatter_scratch(seqs, length // depth, model, depth) * 2
+    scratch += line_scatter_scratch(seqs, length // depth, model, depth)
     scratch += [DMA, DMA, DMA((12 + seqs,)), DMA((n,))]
     scratch += [
         pltpu.VMEM(small, F32),
@@ -1715,13 +1776,13 @@
         pltpu.VMEM((depth,) + pack, F32),
     ]
     scratch += [DMA((7,))] * 4 + [DMA((depth - 1,))] * 2
-    scratch += ring_scratch(2, *panel)
+    scratch += ring_scratch(3, *panel)
     scratch += scatter_scratch([gate] * 2, (False, False))
     res = call(
         functools.partial(mixer_back_kernel, depth, n),
         "mixer_back_phase",
         3,
-        [ANY] * 15 + [VMEM] * 8 + [ANY] * n,
+        [ANY] * 15 + [VMEM] * 6 + [ANY] * n,
         outs,
         scratch,
         (
@@ -1740,8 +1801,6 @@
             input_w,
             gate_in_w,
             gate_dec_w,
-            feed,
-            middle,
             taps,
             rate.reshape(1, width),
             act,
@@ -1752,7 +1811,7 @@
         + tuple(panels),
         vmem=63 * 1024 * 1024,
     )
-    return res[0], res[1], res[2].reshape(2, model), res[3], res[4:6], res[6:]
+    return res[0], res[1].reshape(2, model), res[2], res[3:5], res[5:]
 
 
 def swapped(block, axis):
@@ -1803,27 +1862,27 @@
     def __init__(self, depth, taps, rate):
         self.depth, self.taps, self.rate = depth, taps, rate
 
-    def front(self, normed, cot, weights, act, gain):
+    def front(self, cotangent, token_weight, weights, act, gain, first_gain):
         middle, rows, self.weights, self.feeds, self.saved, self.held = front_phase(
-            normed, cot, weights, self.taps, self.rate, act, gain, self.depth
+            cotangent, token_weight, weights, self.taps, self.rate, act, gain, first_gain,
+            self.depth,
         )
         self.normed, self.cot, self.normed_two = rows
         return middle
 
-    def feed(self, middle, gain, cot_own):
+    def feed(self, middle, gain, cotangent, token_weight):
         return feed_phase(
-            self.normed_two, self.cot, self.feeds, self.held, middle, gain, cot_own, self.depth
-        )
-
-    def last(self, branch, panels, feed, act, gain, middle, grad_middle, mlp_part):
-        output, input_grad, gains, small, gates, rest = mixer_back_phase(
+            self.normed_two, self.cot, self.feeds, self.held, middle, gain, cotangent,
+            token_weight, self.depth,
+        )
+
+    def last(self, branch, panels, act, gain, grad_middle, mlp_part):
+        input_grad, gains, small, gates, rest = mixer_back_phase(
             branch,
             self.normed,
             self.saved,
             self.weights,
             panels[HOSTED:],
-            feed,
-            middle,
             self.taps,
             self.rate,
             act,
@@ -1839,7 +1898,7 @@
         feeds = [
             jnp.concatenate(panels[i * third : (i + 1) * third], axis=1) for i in range(3)
         ]
-        return output, input_grad, gains, small, grads, feeds
+        return input_grad, gains, small, grads, feeds
 
 
 class Plain:
@@ -1862,7 +1921,9 @@
     def own(grad):
         return lax.psum_scatter(grad, "dp", scatter_dimension=0, tiled=True).astype(F32)
 
-    def front(self, normed, cot, weights, act, gain):
+    def front(self, cotangent, token_weight, weights, act, gain, first_gain):
+        cot = (cotangent.astype(F32) * token_weight).astype(BF16)
+        normed = normalize(act.astype(F32), first_gain).astype(BF16)
         gelu_w, input_w, gate_in_w, gate_dec_w, out_w = (self.full(w) for w in weights[:5])
         self.feeds = tuple(self.full(w) for w in weights[5:])
         normed_all = self.wide(normed)
@@ -1905,7 +1966,8 @@
         self.normed_two = self.wide(normalize(middle, gain).astype(BF16))
         return middle
 
-    def feed(self, middle, gain, cot_own):
+    def feed(self, middle, gain, cotangent, token_weight):
+        cot_own = cotangent.astype(F32) * token_weight
         down_w, gate_w, up_w = self.feeds
         normed, cot = self.normed_two, self.cot
         gate_pre = dot("nwo,ob->nwb", normed, gate_w)
@@ -1923,9 +1985,10 @@
             weight_grad(cot, hidden), weight_grad(normed, gate_grad), weight_grad(normed, lift_grad)
         )
         feed = dot("xav,tv->xat", hidden, down_w).astype(BF16)
-        return grad, self.wide(grad.astype(BF16)), gain_grad[None], feed, panels
-
-    def last(self, branch, panels, feed, act, gain, middle, grad_middle, mlp_part):
+        output = (middle + self.narrow(feed)).astype(BF16)
+        return grad, self.wide(grad.astype(BF16)), gain_grad[None], output, panels
+
+    def last(self, branch, panels, act, gain, grad_middle, mlp_part):
         (
             normed_all, gelu_w, input_w, out_w, gelu_out, gelu_back, conv_back, tiles, placed,
             gate_back, decay, states, mixed,
@@ -1965,7 +2028,6 @@
         part = dot("mzf,af->mza", gelu_grad, gelu_w) + dot("mzf,af->mza", input_rows, input_w)
         _, back = jax.vjp(normalize, act.astype(F32), gain)
         change, gain_grad = back(self.narrow(part.astype(BF16)))
-        output = (middle + self.narrow(feed)).astype(BF16)
         gains = lax.psum(jnp.concatenate([gain_grad[None], mlp_part]), ("dp", "tensor"))
         small = lax.psum(jnp.concatenate([grad_rate[None], grad_taps]), "dp")
         parts = (
@@ -1977,7 +2039,7 @@
         )
         own = [self.own(g) for g in parts]
         feeds = [self.own(g) for g in panels]
-        return output, grad_middle + change, gains, small, own, feeds
+        return grad_middle + change, gains, small, own, feeds
 
 
 def shards(
@@ -2014,25 +2076,17 @@
     my_length = lax.dynamic_slice_in_dim(lengths, data_index * seq_count, seq_count)
     places = tensor_index * row_count + jnp.arange(row_count)
     valid_mask = (places[None, :] < my_length[:, None]).astype(F32)
-    scaled_cot = cotangent.astype(F32) * (valid_mask * my_weight[:, None])[:, :, None]
-    normed = normalize(activations.astype(F32), norm_gain).astype(BF16)
+    token_weight = (valid_mask * my_weight[:, None])[:, :, None]
 
     weights = (
         gelu_proj, input_proj, gate_input, gate_decay, out_proj.T, feed_down.T, feed_gate, feed_up
     )
-    middle = run.front(normed, scaled_cot.astype(BF16), weights, activations, mlp_gain)
-    grad_middle, branch_grad_all, mlp_part, feed_part, panels = run.feed(
-        middle, mlp_gain, scaled_cot
+    middle = run.front(cotangent, token_weight, weights, activations, mlp_gain, norm_gain)
+    grad_middle, branch_grad_all, mlp_part, output, panels = run.feed(
+        middle, mlp_gain, cotangent, token_weight
     )
-    output, input_grad, gains, small, grads, feeds = run.last(
-        branch_grad_all,
-        panels,
-        feed_part,
-        activations,
-        norm_gain,
-        middle,
-        grad_middle,
-        mlp_part,
+    input_grad, gains, small, grads, feeds = run.last(
+        branch_grad_all, panels, activations, norm_gain, grad_middle, mlp_part
     )
     return (
         output,

time: 498 us -> 466 us (0.936)
  Pallas kernels: 465 us -> 434 us
  other arithmetic: 14.9 us -> 8.85 us
    pallas_call x3, Pallas kernels: 465 us -> 434 us  [call(): pl.pallas_call(kernel, name=name, out_shape=[o[0] for o in outs], in_spec...]
where the time goes in v5:
time: 466 us; the launch traced here: 459 us
  Pallas kernels  434 us (93%)
  local copies, waits for them, and re-layouts  15.5 us (3%)
  other arithmetic  8.85 us (2%)
    pallas_call x3, Pallas kernels, call(): pl.pallas_call(kernel, name=name, out_shape=[o[0] for o in outs], in_spec...  434 us

profile of v5, /device:TPU:0, one launch (start us, length us, event | category | flops | bytes accessed | tf_op | source)
XLA Modules:
  0.0 459.4 jit_solution(4746238463386811651)
XLA Ops:
  0.7 0.7 convert_element_type.6
  1.3 0.8 select_reduce_fusion.1
  2.1 0.7 select_reduce_fusion
  2.8 0.1 dynamic_slice.7
  2.9 0.7 dynamic_slice.6
  3.7 1.3 reshape.125.rate
  4.9 1.3 reshape.127.first_gain.gain
  6.2 1.3 reshape.126.gain
  7.5 0.7 compare_select_fusion.token_weight
  8.3 180.7 %front_phase.1 = (f32[2,64,2560]{2,1,0:T(8,128)}, bf16[2,256,2560]{2,1,0:T(8,128)(2,1)}, bf16[512,2560]{1,0:T(8,128)(2,1)}, bf16[512,2560]{1,0:T(8,128)(2,1)}, b...) custom-call(bf16[2,64,2560]{2,1,0:T(8,128)(2,1)} %cotangent.3, ...), custom_call_target="tpu_custom_call" | custom-call | tf_op jit(solution)/shard_map/front_phase/pallas_call | solution.py:525
  188.9 140.7 %feed_phase.1 = (f32[2,64,2560]{2,1,0:T(8,128)}, bf16[2,256,2560]{2,1,0:T(8,128)(2,1)}, f32[1,2560]{1,0:T(1,128)}, bf16[2,64,2560]{2,1,0:T(8,128)(2,1)}, f32[320...) custom-call(bf16[512,2560]{1,0:T(8,128)(2,1)} %get-tuple-element.60., ...), custom_call_target="tpu_custom_call" | custom-call | tf_op jit(solution)/shard_map/feed_phase/pallas_call | solution.py:525
  329.7 112.7 %mixer_back_phase.1 = (f32[2,64,2560]{2,1,0:T(8,128)}, f32[8,640]{1,0:T(8,128)}, f32[8,640]{1,0:T(8,128)}, f32[32,640]{1,0:T(8,128)}, f32[32,640]{1,0:T(8,128)},...) custom-call(bf16[2,256,2560]{2,1,0:T(8,128)(2,1)} %get-tuple-element, ...), custom_call_target="tpu_custom_call" | custom-call | tf_op jit(solution)/shard_map/mixer_back_phase/pallas_call | solution.py:525
  442.4 1.3 slice_reduce_fusion
  443.7 1.3 slice.15
  445.1 0.8 fusion
  445.9 0.6 squeeze.11
  446.5 0.6 squeeze.9
  447.1 0.0 copy-start.1
  447.1 0.0 copy-start.2
  447.1 0.0 copy-start.3
  447.1 0.0 copy-start.4
  447.1 0.0 copy-start.5
  447.1 0.0 copy-start.6
  447.1 3.4 pad_maximum_fusion.1
  450.5 0.0 copy-done.1
  450.5 0.0 copy-done.2
  450.5 0.0 copy-done.3
  450.5 0.0 copy-done.4
  450.5 0.0 copy-done.5
  450.5 0.2 copy-done.6
  450.8 0.0 copy-start.10
  450.8 0.0 copy-start
  450.8 2.6 pad_maximum_fusion
  453.3 0.0 copy-start.9
  453.3 0.0 copy-done.10
  453.3 0.8 copy.37
  454.2 0.0 copy-done
  454.2 1.1 copy.38
  455.2 0.0 copy-done.9
  455.2 0.9 copy.39
  456.1 0.0 copy-done.8
  456.1 0.9 copy.40
  457.0 0.0 copy-done.12
  457.0 0.6 copy.41
  457.7 0.0 copy-done.11
  457.7 0.6 copy.42
  458.3 0.0 copy-done.7
  458.3 0.9 copy.43
  (6 shorter events, 0.0 us)
Async XLA Ops:
  447.1 3.4 copy-start.1
  447.1 3.4 copy-start.2
  447.1 3.4 copy-start.3
  447.1 3.4 copy-start.4
  447.1 3.4 copy-start.5
  447.1 3.6 copy-start.6
  450.8 2.6 copy-start.10
  450.8 3.4 copy-start
  453.3 1.9 copy-start.9
  453.3 2.8 copy-start.8
  454.2 2.9 copy-start.12
  454.2 3.5 copy-start.11
  454.2 4.1 copy-start.7

commit v6 on v5

--- a/solution.py
+++ b/solution.py
@@ -49,13 +49,16 @@
     pl.semaphore_wait(barrier, len(dp_masks) + ends)
 
 
-def add_rows(total, term, rows, step=32):
+def add_rows(total, *terms, rows, step=32):
     step = min(step, rows)
 
     @pl.loop(0, rows, step=step)
     def _(start):
         part = pl.ds(pl.multiple_of(start, step), step)
-        total[part, :] = (total[part, :].astype(F32) + term[part, :].astype(F32)).astype(BF16)
+        value = total[part, :].astype(F32)
+        for term in terms:
+            value = value + term[part, :].astype(F32)
+        total[part, :] = value.astype(BF16)
 
 
 class WeightGather:
@@ -195,38 +198,42 @@
         for load in self.loads:
             load.start()
 
-    def pair(self, i):
+    def arrive(self, i):
         if self.loads:
             self.loads[i].wait()
         self.copies[i].wait_recv()
-        add_rows(self.mine(i), self.core.at[i], self.rows)
+
+    def add(self, i, start, *terms):
+        half = pl.ds(start, self.half)
+        add_rows(self.mine(i, start, self.half), self.core.at[i, half], *terms, rows=self.half)
 
     def first(self):
-        self.pair(0)
-        if self.reused:
-            pl.semaphore_wait(self.credit.at[1], 1)
-        self.copies[4].start()
-        if self.reused:
-            pl.semaphore_wait(self.credit.at[2], 1)
-        self.copies[5].start()
+        self.arrive(0)
+        for i, start in enumerate((0, self.half)):
+            self.add(0, start)
+            if self.reused:
+                pl.semaphore_wait(self.credit.at[1 + i], 1)
+            self.copies[4 + i].start()
 
     def second(self):
-        self.pair(1)
+        self.arrive(1)
+        self.add(1, 0)
         self.copies[6].start()
-        self.pair(2)
+        self.arrive(2)
+        self.add(2, self.half)
         self.copies[7].start()
-        self.pair(3)
 
     def third(self):
         c = self.copies
         c[4].wait_recv()
-        add_rows(self.mine(2, 0, self.half), self.diag.at[0], self.half)
+        self.add(2, 0, self.diag.at[0])
         c[8].start()
         c[5].wait_recv()
-        add_rows(self.mine(1, self.half, self.half), self.diag.at[1], self.half)
+        self.add(1, self.half, self.diag.at[1])
         c[9].start()
 
     def end(self):
+        self.arrive(3)
         for i in (6, 7, 8, 9):
             self.copies[i].wait_recv()
         step = 16
@@ -239,6 +246,7 @@
             part = pl.ds(pl.multiple_of(start, step), step)
             self.out[part, :] = (
                 own[part, :].astype(F32)
+                + self.core[3, part, :].astype(F32)
                 + self.last[0, part, :].astype(F32)
                 + self.last[1, part, :].astype(F32)
             )
@@ -463,7 +471,7 @@
         for s in self.which:
             mine = self.slot(way, j, s)
             self.copy(way, j, s, mine, self.t).wait_recv()
-            add_rows(mine, self.block(j, s), self.rows)
+            add_rows(mine, self.block(j, s), rows=self.rows)
             self.copy(way, j, s, mine, to).start()
 
     def step(self, k):
@@ -479,10 +487,11 @@
         def _():
             self.pass_on(1, left, t - 1)
 
-    def total(self, out):
+    def total(self, out, more=False):
         t, depth = self.t, self.depth
         for s in self.which:
-            out[s][...] = self.block(t, s)[...].astype(F32)
+            own = self.block(t, s)[...].astype(F32)
+            out[s][...] = out[s][...] + own if more else own
 
         @pl.when(t > 0)
         def _():
@@ -633,9 +642,9 @@
     gate_in_shard,
     gate_dec_shard,
     out_shard,
-    down_shard,
     gate_shard,
     up_shard,
+    down_shard,
     taps,
     rate,
     act,
@@ -650,19 +659,19 @@
     gate_in_full,
     gate_dec_full,
     out_full,
-    down_full,
     gate_full,
     up_full,
+    down_full,
     gelu_pre_out,
     input_pre_out,
-    conv_out,
     window_out,
     gate_in_out,
     gate_dec_out,
     states_out,
     mixed_out,
-    grad_hidden_out,
     gate_pre_out,
+    lift_pre_out,
+    hidden_out,
     *scratch,
 ):
     normed, gelu_w, input_w, gate_in_w, gate_dec_w, out_w = scratch[:6]
@@ -673,7 +682,7 @@
     cot, normed_two, block_two, panel_w, product = scratch[40:45]
     panel_sem, product_sem = scratch[45:47]
     got, ssem, rsem = scratch[47:50]
-    normed_block, cot_block = scratch[50:52]
+    normed_block, cot_block, hidden = scratch[50:53]
     d, t = place()
     parity = lax.rem(t, 2)
     even = parity == 0
@@ -683,7 +692,7 @@
         for s in range(act.shape[0]):
             value = act[s].astype(F32)
             inverse = lax.rsqrt(jnp.mean(value * value, axis=-1, keepdims=True) + EPS)
-            normed_block[s] = (value * inverse * first_gain[...]).astype(BF16)
+            normed_block[s] = (value * inverse * first_gain[...][None]).astype(BF16)
             cot_block[s] = (cotangent[s].astype(F32) * token_weight[s]).astype(BF16)
 
     greet(d, t, depth, meanwhile=prepare)
@@ -712,9 +721,9 @@
         (gate_in_shard, gate_in_w),
         (gate_dec_shard, gate_dec_w),
         (out_shard, out_w),
-        (down_shard, down_full),
         (gate_shard, gate_full),
         (up_shard, up_full),
+        (down_shard, down_full),
     )
     gathers = [
         WeightGather(shard, full, local.at[i], send.at[i], recv.at[i], d, t)
@@ -728,7 +737,7 @@
         saves.append(copy)
 
     one = [gathers[1], gathers[0], gathers[2], gathers[3]]
-    out_g, down_g, gate_g, up_g = gathers[4:]
+    out_g, gate_g, up_g, down_g = gathers[4:]
     even_blocks, odd_blocks = gate_blocks(0, width, block), gate_blocks(1, width, block)
 
     def rim(s, to, src, dst):
@@ -796,7 +805,7 @@
         def _(i):
             start = pl.multiple_of(s * length + i * STRIP, STRIP)
             rows = pl.ds(start, STRIP)
-            log = -8.0 * sigmoid(gate_dec[rows, :]) * rate[...]
+            log = -8.0 * sigmoid(gate_dec[rows, :]) * rate[...][None]
             decay[rows, :] = jnp.exp(log)
             drive = jnp.sqrt(one_less_exp(2.0 * log)) * sigmoid(gate_in[rows, :])
             held = pl.ds(pl.multiple_of(start + 8, 8), STRIP)
@@ -825,7 +834,7 @@
         value = middle[s] + act[s].astype(F32)
         middle[s] = value
         inverse = lax.rsqrt(jnp.mean(value * value, axis=-1, keepdims=True) + EPS)
-        block_two[s] = (value * inverse * gain[...]).astype(BF16)
+        block_two[s] = (value * inverse * gain[...][None]).astype(BF16)
         twos[s].step(0)
 
     firsts[0].step(0)
@@ -851,8 +860,8 @@
     states[0:8, :] = jnp.zeros((8, width), F32)
     convolve(0)
     out_g.relay()
-    down_g.start()
     gate_g.start()
+    up_g.start()
     for g in one[1:]:
         g.arrive()
     inner_gates(0)
@@ -868,17 +877,13 @@
         line.open(2)
     convolve(1)
     scatters[0].start(1)
-    for line in cots:
-        line.step(1)
     inner_gates(1)
     scatters[0].step(1)
-    down_g.relay()
+    gate_g.relay()
     recur(1)
     scatters[0].step(2)
     mix(1)
     scatters[1].start()
-    for line in cots:
-        line.step(2)
     save(normed, normed_out)
     save(gelu_w, gelu_full)
     save(input_w, input_full)
@@ -887,79 +892,89 @@
     save(out_w, out_full)
     save(gelu_pre, gelu_pre_out)
     save(input_pre, input_pre_out)
-    save(conv, conv_out)
     save(window, window_out)
     save(gate_in, gate_in_out)
     save(gate_dec, gate_dec_out)
     save(states, states_out)
     save(mixed, mixed_out)
-    down_g.relay_two()
+    gate_g.relay_two()
     scatters[1].step(1)
     norm_step(0)
-    gate_g.relay()
-    up_g.start()
+    up_g.relay()
+    down_g.start()
     scatters[1].step(2)
-    gate_g.relay_two()
+    up_g.relay_two()
     twos[0].step(1)
     norm_step(1)
     twos[0].step(2)
-    down_g.relay_last()
+    gate_g.relay_last()
     twos[1].step(1)
+    for line in cots:
+        line.step(1)
     twos[1].step(2)
-    gate_g.relay_last()
+    for line in cots:
+        line.step(2)
+    up_g.relay_last()
+    panels = down_full.shape[1] // PANEL
+
+    kinds = ((gate_full, gate_pre_out), (up_full, lift_pre_out))
+    order = [(s, p, i) for s in range(seqs) for p in range(panels) for i in range(2)]
+
+    def load_panel(at):
+        _, p, i = order[at]
+        columns = pl.ds(p * PANEL, PANEL)
+        copy = pltpu.make_async_copy(
+            kinds[i][0].at[:, columns], panel_w.at[at % 2], panel_sem.at[at % 2]
+        )
+        copy.start()
+        return copy
+
+    results = [[], []]
+
+    def store(src, out, s, p, i):
+        columns = pl.ds(p * PANEL, PANEL)
+        copy = pltpu.make_async_copy(src, out.at[spans[s], columns], product_sem.at[3 * s + i])
+        copy.start()
+        results[s].append(copy)
+
+    def multiply(s, p):
+        nonlocal loaded
+        while results[s]:
+            results[s].pop().wait()
+        for i, (_, out) in enumerate(kinds):
+            at = (s * panels + p) * 2 + i
+            loaded.wait()
+            if at + 1 < len(order):
+                loaded = load_panel(at + 1)
+            product[i, spans[s], :] = contract(normed_two[spans[s], :], panel_w[at % 2], (1, 0))
+            store(product.at[i, spans[s]], out, s, p, i)
+
+        @pl.loop(0, length // STRIP)
+        def _(k):
+            rows = pl.ds(pl.multiple_of(s * length + k * STRIP, STRIP), STRIP)
+            hidden[rows, :] = (gelu(product[0, rows, :]) * product[1, rows, :]).astype(BF16)
+
+        store(hidden.at[spans[s]], hidden_out, s, p, 2)
+
+    gate_g.arrive()
+    loaded = load_panel(0)
+    up_g.arrive()
+    twos[0].finish()
+    multiply(0, 0)
+    down_g.relay()
+    multiply(0, 1)
+    multiply(0, 2)
+    down_g.relay_two()
+    twos[1].finish()
+    multiply(1, 0)
+    multiply(1, 1)
+    multiply(1, 2)
+    save(normed_two, normed_two_out)
     for line in cots:
         line.finish()
     save(cot, cot_out)
-    up_g.relay()
-    for line in twos:
-        line.finish()
-    save(normed_two, normed_two_out)
-    panels = down_full.shape[1] // PANEL
-
-    def load_panel(full, i):
-        columns = pl.ds(i % panels * PANEL, PANEL)
-        copy = pltpu.make_async_copy(full.at[:, columns], panel_w.at[i % 2], panel_sem.at[i % 2])
-        copy.start()
-        return copy
-
-    results = []
-
-    def multiply(left, full, out, i, following):
-        nonlocal loaded
-        loaded.wait()
-        if following is not None:
-            loaded = load_panel(*following)
-        if len(results) >= 2:
-            results[-2].wait()
-        for s in range(seqs):
-            product[i % 2, spans[s], :] = contract(left[spans[s], :], panel_w[i % 2], (1, 0))
-        columns = pl.ds(i % panels * PANEL, PANEL)
-        copy = pltpu.make_async_copy(product.at[i % 2], out.at[:, columns], product_sem.at[i % 2])
-        copy.start()
-        results.append(copy)
-
+    down_g.relay_last()
     down_g.arrive()
-    gate_g.arrive()
-    loaded = load_panel(down_full, 0)
-    for i in range(panels):
-        multiply(
-            cot,
-            down_full,
-            grad_hidden_out,
-            i,
-            (down_full, i + 1) if i < panels - 1 else (gate_full, panels),
-        )
-    up_g.relay_two()
-    for i in range(panels, 2 * panels):
-        multiply(
-            normed_two,
-            gate_full,
-            gate_pre_out,
-            i,
-            (gate_full, i + 1) if i < 2 * panels - 1 else None,
-        )
-    up_g.relay_last()
-    up_g.arrive()
 
     for s in range(seqs):
 
@@ -975,7 +990,7 @@
         g.end()
     for line in firsts + cots + twos + scatters:
         line.end()
-    for copy in saves + results[-2:]:
+    for copy in saves + results[0] + results[1]:
         copy.wait()
 
 
@@ -992,7 +1007,6 @@
     saved = [
         ((tokens, width), F32),
         ((seqs, length + 8, width), F32),
-        ((tokens, width), BF16),
         ((tokens, wide), BF16),
         ((tokens, width), F32),
         ((tokens, width), F32),
@@ -1004,8 +1018,9 @@
     outs += [shaped(shape, BF16, ANY) for shape in mixers]
     outs += [shaped((model, units), BF16, ANY)] * 3
     outs += [shaped(shape, dtype, ANY) for shape, dtype in saved]
-    outs += [shaped((tokens, units), F32, ANY)] * 2
-    saved_scratch = saved[:6] + [((tokens, width), F32)] + saved[6:] + [(wide_rows, BF16)]
+    outs += [shaped((tokens, units), F32, ANY)] * 2 + [shaped((tokens, units), BF16, ANY)]
+    saved_scratch = saved[:2] + [((tokens, width), BF16)] + saved[2:5] + [((tokens, width), F32)]
+    saved_scratch += saved[5:] + [(wide_rows, BF16)]
     scratch = [pltpu.VMEM(wide_rows, BF16)]
     scratch += [pltpu.VMEM(shape, BF16) for shape in mixers]
     scratch += [pltpu.VMEM(shape, dtype) for shape, dtype in saved_scratch]
@@ -1017,10 +1032,10 @@
         pltpu.VMEM((2, model, PANEL), BF16),
         pltpu.VMEM((2, tokens, PANEL), F32),
         DMA((2,)),
-        DMA((2,)),
+        DMA((6,)),
     ]
     scratch += line_scatter_scratch(seqs, rows, model, depth)
-    scratch += [pltpu.VMEM(act.shape, BF16)] * 2
+    scratch += [pltpu.VMEM(act.shape, BF16)] * 2 + [pltpu.VMEM((tokens, PANEL), BF16)]
     res = call(
         functools.partial(front_kernel, depth),
         "front_phase",
@@ -1030,9 +1045,9 @@
         scratch,
         (cotangent, token_weight)
         + tuple(weights)
-        + (taps, rate.reshape(1, width), act, gain.reshape(1, model), first_gain.reshape(1, model)),
+        + (taps, rate, act, gain, first_gain),
     )
-    return res[0], res[1:4], res[4:9], res[9:12], res[12:20], res[20:]
+    return res[0], res[1:4], res[4:9], res[9:12], res[12:19], res[19:]
 
 
 def norm_back(value, gain, error):
@@ -1041,9 +1056,6 @@
     mean = jnp.mean(scaled * value, axis=-1, keepdims=True)
     grad = inverse * scaled - value * (inverse * inverse * inverse * mean)
     return grad, jnp.sum(error * value * inverse, axis=0, keepdims=True)
-
-
-HOSTED = 6
 
 
 def feed_kernel(
@@ -1053,8 +1065,9 @@
     gate_in,
     up_in,
     down_in,
-    grad_hidden_in,
     gate_pre_in,
+    lift_pre_in,
+    hidden_in,
     middle,
     gain,
     cotangent,
@@ -1062,31 +1075,32 @@
     grad,
     wide,
     gain_grad,
-    output,
+    feed_out,
+    lift_rows_out,
+    output_first,
+    down_out,
+    gate_out,
     *refs,
 ):
     panels = gate_in.shape[1] // PANEL
-    n_panels = 3 * panels
-    outs, refs = refs[:n_panels], refs[n_panels:]
+    outs = [
+        out.at[:, pl.ds(p * PANEL, PANEL)] for out in (down_out, gate_out) for p in range(panels)
+    ]
     normed, cot, hidden, gate_rows, lift_rows = refs[:5]
-    gate_w, up_w, down_w, gate_pre, lift_pre, grad_hidden, acc, part, block = refs[5:14]
-    got, ssem, rsem = refs[14:17]
-    feed_got, feed_ssem, feed_rsem = refs[17:20]
-    load_sem, weight_sem, save_sem = refs[20:23]
-    lines = refs[23:26], refs[26:29]
+    gate_w, up_w, down_w, gate_pre, lift_pre, grad_hidden, acc, part, block, feed_part = refs[5:15]
+    got, ssem, rsem = refs[15:18]
+    load_sem, weight_sem, save_sem = refs[18:21]
+    lines = refs[21:24], refs[24:27]
+    feed_got, feed_ssem, feed_rsem = refs[27:30]
     d, t = place()
     greet(d, t, depth)
     seqs = middle.shape[0]
     tokens, model = normed_in.shape
     length = tokens // seqs
     tile = 512
-    ring = PanelRing(outs[:HOSTED], refs[29:], d, t)
+    ring = PanelRing(outs, refs[30:], d, t)
     scatters = [LineScatter(part, got, ssem, rsem, d, t, depth, (s,)) for s in range(seqs)]
-    feeds = [
-        LineScatter(cot, feed_got, feed_ssem, feed_rsem, d, t, depth, (s,), s * length)
-        for s in range(seqs)
-    ]
-    own_rows = middle.shape[1]
+    early_feed = LineScatter(feed_part, feed_got, feed_ssem, feed_rsem, d, t, depth, (0,), 0)
     gathers = [
         LineGather(block.at[s], wide.at[s], *lines[s], d, t, depth) for s in range(seqs)
     ]
@@ -1108,31 +1122,26 @@
         q = (s * panels + p) % 2
         return [
             load(2 + q, gate_pre_in.at[rows, columns], gate_pre.at[q]),
-            load(4 + q, grad_hidden_in.at[rows, columns], grad_hidden.at[q]),
+            load(4 + q, lift_pre_in.at[rows, columns], lift_pre.at[q]),
         ]
 
+    hidden_load = load(6, hidden_in, hidden)
+    cot_load = load(1, cot_in, cot)
+    down_loads = [weight(p, down_in, w, p) for p, w in enumerate((gate_w, up_w, down_w))]
+    row_loads = held_rows(0, 0)
     normed_load = load(0, normed_in, normed)
-    ups = (up_w, down_w)
-    up_load = weight(1, up_in, up_w, 0)
-    row_loads = held_rows(0, 0)
-    gate_load = weight(0, gate_in, gate_w, 0)
-    cot_load = load(1, cot_in, cot)
 
     def forward(s, p, more):
-        nonlocal gate_load, up_load, row_loads
+        nonlocal down_load, gate_load, up_load, row_loads
         rows = pl.ds(s * length, length)
         columns = pl.ds(p * PANEL, PANEL)
         q = (s * panels + p) % 2
-        if s == 0 and p == 0:
-            normed_load.wait()
-        up = ups[q]
-        up_load.wait()
-        if more is not None:
-            up_load = weight(2 - q, up_in, ups[1 - q], more)
-        lift_pre[...] = contract(normed[rows, :], up[...], (1, 0))
+        down_load.wait()
+        grad_hidden[...] = contract(cot[rows, :], down_w[...], (1, 0))
         for copy in row_loads:
             copy.wait()
         if more is not None:
+            down_load = weight(2, down_in, down_w, more)
             row_loads = held_rows(*((s, more) if more > p else (s + 1, more)))
 
         @pl.loop(0, length // STRIP)
@@ -1140,19 +1149,19 @@
             strip = rows_of(i, STRIP)
             held = pl.ds(pl.multiple_of(s * length + i * STRIP, STRIP), STRIP)
             act, slope = gelu_both(gate_pre[q, strip, :])
-            lift = lift_pre[strip, :]
-            came = grad_hidden[q, strip, :]
-            hidden[held, columns] = (act * lift).astype(BF16)
+            lift = lift_pre[q, strip, :]
+            came = grad_hidden[strip, :]
             gate_rows[held, columns] = (came * lift * slope).astype(BF16)
             lift_rows[held, columns] = (came * act).astype(BF16)
 
         gate_load.wait()
+        up_load.wait()
 
         @pl.loop(0, model // tile)
         def _(i):
             out = rows_of(i, tile)
             value = contract(gate_rows[rows, columns], gate_w[out, :], (1, 1))
-            value = value + contract(lift_rows[rows, columns], up[out, :], (1, 1))
+            value = value + contract(lift_rows[rows, columns], up_w[out, :], (1, 1))
             if p == 0:
                 acc[:, out] = value
             elif p < panels - 1:
@@ -1162,6 +1171,7 @@
 
         if more is not None:
             gate_load = weight(0, gate_in, gate_w, more)
+            up_load = weight(1, up_in, up_w, more)
 
     kinds = ((cot, hidden), (normed, gate_rows), (normed, lift_rows))
 
@@ -1185,7 +1195,7 @@
 
     def norm_step(s):
         scatters[s].total([grad.at[i] for i in range(seqs)])
-        change, gain_part = norm_back(middle[s], gain[...], grad[s])
+        change, gain_part = norm_back(middle[s], gain[...][None], grad[s])
         change = change + cotangent[s].astype(F32) * token_weight[s]
         grad[s] = change
         block[s] = change.astype(BF16)
@@ -1194,156 +1204,150 @@
         else:
             gain_grad[...] += gain_part
 
-    def feed(s):
+    def feed(s, out):
         rows = pl.ds(s * length, length)
         downs = (gate_w, up_w, down_w)
 
         @pl.loop(0, model // tile)
         def _(i):
-            out = rows_of(i, tile)
-            value = contract(hidden[rows, 0:PANEL], downs[0][out, :], (1, 1))
+            columns = rows_of(i, tile)
+            value = contract(hidden[rows, 0:PANEL], downs[0][columns, :], (1, 1))
             for p in range(1, panels):
-                columns = pl.ds(p * PANEL, PANEL)
-                value = value + contract(hidden[rows, columns], downs[p][out, :], (1, 1))
-            cot[rows, out] = value.astype(BF16)
-
-        feeds[s].start()
-
-    def feed_end(s):
-        total = acc.at[pl.ds(s * own_rows, own_rows)]
-        feeds[s].total([total] * seqs)
-        output[s] = (total[...] + middle[s]).astype(BF16)
-
-    pending = {}
-
-    def store_grad(i):
-        q = i % ring.slots
-        if q in pending:
-            pending.pop(q).wait()
-        weight_grad(i, ring.panels[q].grad)
-        pending[q] = pltpu.make_async_copy(ring.panels[q].grad, outs[i], save_sem.at[q])
-        pending[q].start()
-
-    for p in range(panels):
-        forward(0, p, (p + 1) % panels)
+                units = pl.ds(p * PANEL, PANEL)
+                value = value + contract(hidden[rows, units], downs[p][columns, :], (1, 1))
+            out[:, columns] = value.astype(BF16)
+
+    saves = []
+
+    def save(i, src, dst):
+        copy = pltpu.make_async_copy(src, dst, save_sem.at[i])
+        copy.start()
+        saves.append(copy)
+
+    hidden_load.wait()
+    cot_load.wait()
+    begin(0)
+    for copy in down_loads:
+        copy.wait()
+    feed(0, feed_part)
+    early_feed.start()
+    down_load = weight(2, down_in, down_w, 0)
+    gate_load = weight(0, gate_in, gate_w, 0)
+    up_load = weight(1, up_in, up_w, 0)
+    push(0)
+    forward(0, 0, 1)
+    begin(1)
+    early_feed.step(1)
+    forward(0, 1, 2)
+    early_feed.step(2)
+    ring.panels[0].third()
+    push(1)
+    forward(0, 2, 0)
     scatters[0].start()
     forward(1, 0, 1)
     scatters[0].step(1)
-    cot_load.wait()
-    begin(0)
+    ring.panels[0].end()
+    ring.panels[1].third()
+    begin(2)
+    scatters[0].step(2)
     forward(1, 1, 2)
-    scatters[0].step(2)
-    push(0)
-    begin(1)
+    push(2)
+    norm_step(0)
+    gathers[0].step(0)
     forward(1, 2, None)
     down_loads = [weight(0, down_in, gate_w, 0), weight(1, down_in, up_w, 1)]
     down_loads.append(weight(2, down_in, down_w, 2))
     scatters[1].start()
-    ring.panels[0].third()
-    norm_step(0)
-    gathers[0].step(0)
-    push(1)
-    begin(2)
+    save(2, lift_rows, lift_rows_out)
+    gathers[0].step(1)
+    ring.panels[1].end()
+    ring.panels[2].third()
+    normed_load.wait()
+    begin(3)
     scatters[1].step(1)
-    gathers[0].step(1)
-    ring.panels[0].end()
-    ring.panels[1].third()
-    push(2)
+    gathers[0].step(2)
+    push(3)
+    begin(4)
     scatters[1].step(2)
-    gathers[0].step(2)
+    ring.panels[2].end()
+    ring.panels[3].third()
     for copy in down_loads:
         copy.wait()
-    feed(0)
-    begin(3)
-    ring.panels[1].end()
-    ring.panels[2].third()
+    feed(1, cot.at[pl.ds(length, length)])
+    save(1, cot.at[pl.ds(length, length)], feed_out)
+    push(4)
     norm_step(1)
     gathers[1].step(0)
-    feed(1)
-    push(3)
-    begin(4)
-    feeds[0].step(1)
+    ring.panels[3].end()
+    begin(5)
+    ring.panels[4].third()
+    total = acc.at[pl.ds(0, middle.shape[1])]
+    early_feed.total([total])
+    output_first[...] = (total[...] + middle[0]).astype(BF16)
     gathers[1].step(1)
-    ring.panels[2].end()
-    ring.panels[3].third()
-    push(4)
-    begin(5)
-    feeds[0].step(2)
+    push(5)
+    ring.panels[4].end()
     gathers[1].step(2)
-    ring.panels[3].end()
-    ring.panels[4].third()
-    push(5)
-    store_grad(6)
-    feeds[1].step(1)
-    ring.panels[4].end()
     ring.panels[5].third()
-    store_grad(7)
-    feeds[1].step(2)
-    feed_end(0)
-    ring.panels[5].end()
-    store_grad(8)
-    feed_end(1)
     for line in gathers:
         line.finish()
+    ring.panels[5].end()
     ring.end()
-    for copy in pending.values():
+    for copy in saves:
         copy.wait()
-    for line in scatters + feeds + gathers:
+    for line in scatters + gathers + [early_feed]:
         line.end()
 
 
 def feed_phase(normed, cot, weights, held, middle, gain, cotangent, token_weight, depth):
-    down_w, gate_w, up_w = weights
+    gate_w, up_w, down_w = weights
     seqs, rows, model = middle.shape
     tokens = normed.shape[0]
     length = tokens // seqs
     wide_rows = (seqs, length, model)
     units = gate_w.shape[1]
-    count = 3 * (units // PANEL)
     outs = [
         shaped(middle.shape, F32, VMEM),
         shaped(wide_rows, BF16, ANY),
         shaped((1, model), F32, VMEM),
-        shaped(middle.shape, BF16, VMEM),
-    ]
-    outs += [shaped((model // 8, PANEL), F32, ANY)] * HOSTED
-    outs += [shaped((model, PANEL), BF16, ANY)] * (count - HOSTED)
+        shaped((length, model), BF16, ANY),
+        shaped((tokens, units), BF16, ANY),
+        shaped(middle.shape[1:], BF16, VMEM),
+    ] + [shaped((model // 8, units), F32, ANY)] * 2
     scratch = [pltpu.VMEM((tokens, model), BF16)] * 2
     scratch += [pltpu.VMEM((tokens, units), BF16)] * 3
     scratch += [pltpu.VMEM((model, PANEL), BF16)] * 3
-    scratch += [pltpu.VMEM((2, length, PANEL), F32), pltpu.VMEM((length, PANEL), F32)]
-    scratch += [pltpu.VMEM((2, length, PANEL), F32)]
+    scratch += [pltpu.VMEM((2, length, PANEL), F32)] * 2 + [pltpu.VMEM((length, PANEL), F32)]
     scratch += [
         pltpu.VMEM((length, model), F32),
         pltpu.VMEM(wide_rows, BF16),
         pltpu.VMEM(middle.shape, BF16),
+        pltpu.VMEM((length, model), BF16),
     ]
-    scratch += line_scatter_scratch(seqs, rows, model, depth) * 2
-    scratch += [DMA((6,)), DMA((3,)), DMA((3,))]
+    scratch += line_scatter_scratch(seqs, rows, model, depth)
+    scratch += [DMA((7,)), DMA((3,)), DMA((3,))]
     scratch += line_gather_scratch(depth) * 2
+    scratch += line_scatter_scratch(1, rows, model, depth)
     scratch += ring_scratch(3, model // 8, PANEL)
-    res = call(
+    return call(
         functools.partial(feed_kernel, depth),
         "feed_phase",
         2,
-        [ANY] * 7 + [VMEM] * 4,
+        [ANY] * 8 + [VMEM] * 4,
         outs,
         scratch,
-        (normed, cot, gate_w, up_w, down_w) + tuple(held) + (middle, gain.reshape(1, model), cotangent, token_weight),
+        (normed, cot, gate_w, up_w, down_w) + tuple(held) + (middle, gain, cotangent, token_weight),
         vmem=63 * 1024 * 1024,
     )
-    return res[0], res[1], res[2], res[3], res[4:]
 
 
 def mixer_back_kernel(
     depth,
-    n_panels,
     branch_in,
     normed_in,
     out_w_in,
     gelu_pre_in,
     input_pre_in,
-    conv_in,
     window_in,
     gate_in_in,
     gate_dec_in,
@@ -1353,35 +1357,45 @@
     input_w_in,
     gate_in_w_in,
     gate_dec_w_in,
+    normed_two_in,
+    lift_rows_in,
+    feed_in,
+    middle_in,
     taps,
     rate,
     act,
     gain,
     grad_middle,
     mlp_part,
+    output_first,
     *refs,
 ):
-    panels_in, refs = refs[:n_panels], refs[n_panels:]
-    n_sums = n_panels + 3
-    input_grad, gains, smalls, gate_in_out, gate_dec_out = refs[:5]
-    panels_out, scratch = refs[5 : 5 + n_sums], refs[5 + n_sums :]
+    output, input_grad, norm_grad, mlp_grad, rate_grad, taps_grad = refs[:6]
+    gate_in_out, gate_dec_out, out_out, gelu_out, input_out, up_out = refs[6:12]
+    scratch = refs[12:]
+    panels = up_out.shape[1] // PANEL
+    ups = [up_out.at[:, pl.ds(p * PANEL, PANEL)] for p in range(panels)]
     branch, weight, input_w = scratch[:3]
-    gelu_pre, input_pre, conv, window, gate_in, gate_dec, states, gate_in_w, gate_dec_w = scratch[3:12]
-    grad, decay, grad_conv, gelu_grad, input_rows, grad_in, grad_dec, mixed = scratch[12:20]
-    rim_out, rim_in, gate_in_grad, gate_dec_grad, part, sums = scratch[20:26]
-    got, ssem, rsem = scratch[26:29]
-    rim_send, rim_recv, load_sem, panel_sem = scratch[29:33]
-    small, small_all, pack, packs, line_pack, line_packs = scratch[33:39]
-    psend, precv, qsend, qrecv, zsend, zrecv = scratch[39:45]
+    gelu_pre, input_pre, window, gate_in, gate_dec, states, gate_in_w, gate_dec_w = scratch[3:11]
+    grad, decay, gelu_grad, grad_in, grad_dec = scratch[11:16]
+    input_rows = grad_in
+    grad_conv = [decay.at[pl.ds(s * (decay.shape[0] // 2), decay.shape[0] // 2)] for s in range(2)]
+    rim_out, rim_in, gate_in_grad, gate_dec_grad, part, sums = scratch[16 : 22]
+    panel_sem = scratch[22]
+    got, ssem, rsem = scratch[23 : 26]
+    rim_send, rim_recv, load_sem, feed_sem = scratch[26 : 30]
+    small, small_all, pack, packs, line_pack, line_packs = scratch[30 : 36]
+    psend, precv, qsend, qrecv, zsend, zrecv = scratch[36 : 42]
     d, t = place()
-    ring = PanelRing(panels_out, scratch[45:54], d, t)
+    ring = PanelRing([out_out] + ups + [gelu_out, input_out], scratch[42 : 51], d, t)
+    feed, lift_rows, feed_got, feed_ssem, feed_rsem = scratch[51 : 56]
     parity = lax.rem(t, 2)
     even = parity == 0
     odd = parity == 1
     greet(d, t, depth, dp_masks=(1, 2, 3, 4, 5, 6, 7), z_all=True)
     seqs, length, model = branch_in.shape
     tokens = seqs * length
-    width = conv.shape[1]
+    width = gate_in.shape[1]
     block = gate_in_w.shape[0]
     half = block // 2
     even_blocks, odd_blocks = gate_blocks(0, width, block), gate_blocks(1, width, block)
@@ -1389,40 +1403,35 @@
         (gate_in_grad, gate_dec_grad),
         (gate_in_out, gate_dec_out),
         (False, False),
-        scratch[54:],
+        scratch[56:],
         d,
         t,
     )
-    lines = [LineScatter(part, got, ssem, rsem, d, t, depth, (s,)) for s in range(seqs)]
+    feed_line = LineScatter(feed, feed_got, feed_ssem, feed_rsem, d, t, depth, (0,), 0)
+    lines = [
+        LineScatter(part, got, ssem, rsem, d, t, depth, (s,), s * length) for s in range(seqs)
+    ]
 
     def load(i, src, dst):
         copy = pltpu.make_async_copy(src, dst, load_sem.at[i])
         copy.start()
         return copy
 
-    def load_wide(i, src):
+    def load_wide(i, src, dst):
+        spans = [pl.ds(s * length, length) for s in range(seqs)]
         return [
-            load(i + s, src.at[s], branch.at[pl.ds(s * length, length)]) for s in range(seqs)
+            load(i + s, src.at[s] if len(src.shape) == 3 else src.at[rows], dst.at[rows])
+            for s, rows in enumerate(spans)
         ]
 
-    early = [load(0, out_w_in, weight)] + load_wide(12, branch_in)
+    early = [load(0, out_w_in, weight)] + load_wide(12, branch_in, branch)
     next_ = [
         load(2, gelu_pre_in, gelu_pre),
         load(3, states_in, states),
         load(4, gate_dec_in, gate_dec),
     ]
-    panel_loads = [
-        pltpu.make_async_copy(src, panel.grad, panel_sem.at[i])
-        for i, (src, panel) in enumerate(zip(panels_in, ring.panels))
-    ]
-
-    def weight_grad(left, right, out):
-        panel = 512
-
-        @pl.loop(0, model // panel)
-        def _(i):
-            columns = rows_of(i, panel)
-            out[columns, :] = contract(left[:, columns], right[...], (0, 0)).astype(BF16)
+    feed_load = pltpu.make_async_copy(feed_in, feed, feed_sem)
+    feed_load.start()
 
     def dp_copies(src, dst, send, recv):
         return [
@@ -1437,36 +1446,57 @@
             for mask in range(1, 8)
         ]
 
-    def begin(i):
-        if i < n_panels:
-            panel_loads[i].wait()
+    def weight_grad(left, right, out):
+        panel = 512
+
+        @pl.loop(0, model // panel)
+        def _(i):
+            columns = rows_of(i, panel)
+            out[columns, :] = contract(left[:, columns], right[...], (0, 0)).astype(BF16)
+
+    def begin(i, left, right):
+        weight_grad(left, right, ring.panels[i].grad)
         ring.panels[i].start()
 
     def push(i):
         ring.panels[i].first()
         ring.panels[i].second()
 
-    for copy in panel_loads:
+    def load_lift(p):
+        copy = pltpu.make_async_copy(
+            lift_rows_in.at[:, pl.ds(p * PANEL, PANEL)], lift_rows, panel_sem
+        )
         copy.start()
+        return copy
+
+    mixed_load = load(1, mixed_in, lift_rows)
+    two_loads = load_wide(12 + seqs, normed_two_in, part)
     then = [
         load(5, gate_in_in, gate_in),
-        load(6, conv_in, conv),
         load(7, window_in, window),
         load(8, gate_in_w_in, gate_in_w),
         load(9, gate_dec_w_in, gate_dec_w),
         load(10, input_pre_in, input_pre),
         load(11, input_w_in, input_w),
-        load(1, mixed_in, mixed),
     ]
-    for i in range(n_panels):
-        begin(i)
     for copy in early:
         copy.wait()
+    feed_load.wait()
+    feed_line.start()
+    mixed_load.wait()
+    begin(0, branch, lift_rows)
+    lift_load = load_lift(0)
     for s in range(seqs):
         rows = pl.ds(s * length, length)
         grad[rows, :] = contract(branch[rows, :], weight[...], (1, 0))
     reload = load(0, gelu_w_in, weight)
+    wide_loads = load_wide(12, normed_in, branch)
     push(0)
+    for copy in two_loads:
+        copy.wait()
+    lift_load.wait()
+    begin(1, part, lift_rows)
+    lift_load = load_lift(1)
     for copy in next_:
         copy.wait()
 
@@ -1478,12 +1508,18 @@
         came = grad[rows, :]
         gelu_grad[rows, :] = (came * states[held, :] * slope).astype(BF16)
         grad[rows, :] = came * act
-        decay[rows, :] = jnp.exp(-8.0 * sigmoid(gate_dec[rows, :]) * rate[...])
+        decay[rows, :] = jnp.exp(-8.0 * sigmoid(gate_dec[rows, :]) * rate[...][None])
 
     decay[tokens : tokens + 8, :] = jnp.zeros((8, width), F32)
     push(1)
     ring.panels[0].third()
+    feed_line.step(1)
+    lift_load.wait()
+    begin(2, part, lift_rows)
+    lift_load = load_lift(2)
     scan_rows(decay, grad, range(seqs), length, backward=True)
+    feed_line.step(2)
+    push(2)
     for copy in then:
         copy.wait()
     sums[...] = jnp.zeros(sums.shape, F32)
@@ -1491,6 +1527,7 @@
     def fold(value):
         return value[0:8] + value[8:16]
 
+    own_columns = pl.ds(pl.multiple_of(parity * half, half), width)
     first_row = lax.broadcasted_iota(jnp.int32, (STRIP, width), 0) == 0
     for s in range(seqs):
 
@@ -1503,20 +1540,23 @@
             came = grad[rows, :]
             open_in = sigmoid(gate_in[rows, :])
             open_dec = sigmoid(gate_dec[rows, :])
-            slow = -8.0 * rate[...]
+            slow = -8.0 * rate[...][None]
             lost = one_less_exp(2.0 * open_dec * slow)
             root = jnp.sqrt(lost)
-            value = conv[rows, :].astype(F32)
-            step = decay[rows, :]
+            value = window[rows, own_columns].astype(F32)
+            step = jnp.exp(open_dec * slow)
             through = came * open_in
             grad_log = step * (came * earlier - through * value * step / root)
             sums[0] += fold(grad_log * (-8.0 * open_dec))
             through = through * root
-            grad_conv[s, pl.ds(pl.multiple_of(i * STRIP, STRIP), STRIP), :] = through
+            grad_conv[s][pl.ds(pl.multiple_of(i * STRIP, STRIP), STRIP), :] = through
             grad_in[rows, :] = (through * value * (1.0 - open_in)).astype(BF16)
             grad_dec[rows, :] = (grad_log * slow * open_dec * (1.0 - open_dec)).astype(BF16)
 
-        grad_conv[s, length : length + 8, :] = jnp.zeros((8, width), F32)
+        grad_conv[s][length : length + 8, :] = jnp.zeros((8, width), F32)
+
+    ring.panels[0].end()
+    ring.panels[1].third()
 
     def gates_back(k, low, high):
         return contract(grad_in[:, low:high], gate_in_w[:, low:high], (1, 1)) + contract(
@@ -1525,7 +1565,7 @@
 
     def add_conv(low, high, value):
         for s in range(seqs):
-            grad_conv[s, 0:length, low:high] += value[s * length : (s + 1) * length]
+            grad_conv[s][0:length, low:high] += value[s * length : (s + 1) * length]
 
     def rim(to):
         return pltpu.make_async_remote_copy(
@@ -1551,9 +1591,8 @@
         rim(t - 1).start()
         add_conv(0, half, value[:, half:])
 
-    ring.panels[0].end()
-    ring.panels[1].third()
-    push(2)
+    lift_load.wait()
+    begin(3, part, lift_rows)
 
     def inner(blocks):
         for k, low, high in blocks:
@@ -1577,9 +1616,9 @@
 
     for g in gate_scatters:
         g.start()
-    weight_grad(branch, mixed, ring.panels[3].grad)
-    begin(3)
-    wide_loads = load_wide(12, normed_in)
+    ring.panels[1].end()
+    ring.panels[2].third()
+    push(3)
 
     @pl.when(even)
     def _():
@@ -1596,7 +1635,7 @@
         @pl.loop(0, length // STRIP)
         def _(i):
             near = pl.ds(pl.multiple_of(i * STRIP, STRIP), STRIP + 8)
-            later = grad_conv[s, near, :]
+            later = grad_conv[s][near, :]
             before = input_pre[s, near, :]
             here = later[:STRIP]
             value = taps[0:1, :] * here
@@ -1607,9 +1646,6 @@
             rows = pl.ds(pl.multiple_of(s * length + i * STRIP, STRIP), STRIP)
             input_rows[rows, :] = value.astype(BF16)
 
-    ring.panels[1].end()
-    ring.panels[2].third()
-    push(3)
     for k in range(sums.shape[0]):
         small[k : k + 1, :] = jnp.sum(sums[k], axis=0, keepdims=True)
     small[sums.shape[0] :, :] = jnp.zeros((8 - sums.shape[0], width), F32)
@@ -1619,49 +1655,52 @@
     small_all[d] = small[...]
     reload.wait()
     panel = 512
-
-    @pl.loop(0, weight.shape[0] // panel)
-    def _(i):
-        columns = rows_of(i, panel)
-        value = contract(gelu_grad[...], weight[columns, :], (1, 1))
-        value = (value + contract(input_rows[...], input_w[columns, :], (1, 1))).astype(BF16)
-        for s in range(seqs):
-            part[s, :, columns] = value[s * length : (s + 1) * length]
-
-    for line in lines:
-        line.start()
+    for s in range(seqs):
+        rows = pl.ds(s * length, length)
+
+        @pl.loop(0, weight.shape[0] // panel)
+        def _(i):
+            columns = rows_of(i, panel)
+            value = contract(gelu_grad[rows, :], weight[columns, :], (1, 1))
+            value = value + contract(input_rows[rows, :], input_w[columns, :], (1, 1))
+            part[rows, columns] = value.astype(BF16)
+
+        lines[s].start()
+
+    middle_load = load(0, middle_in.at[1], input_grad.at[1])
+    ring.panels[2].end()
+    ring.panels[3].third()
     for copy in wide_loads:
         copy.wait()
-    weight_grad(branch, gelu_grad, ring.panels[4].grad)
-    begin(4)
+    begin(4, branch, gelu_grad)
     for g in gate_scatters:
         g.first()
         g.second()
-    ring.panels[2].end()
-    ring.panels[3].third()
     push(4)
     lines[0].step(1)
-    weight_grad(branch, input_rows, ring.panels[5].grad)
-    begin(5)
-    for g in gate_scatters:
-        g.third()
+    begin(5, branch, input_rows)
     lines[0].step(2)
     ring.panels[3].end()
     ring.panels[4].third()
     push(5)
+    for g in gate_scatters:
+        g.third()
+    middle_load.wait()
+    feed_line.total([input_grad.at[1]], more=True)
+    output[0] = output_first[...]
+    output[1] = input_grad[1].astype(BF16)
     lines[1].step(1)
+    ring.panels[4].end()
+    ring.panels[5].third()
     lines[1].step(2)
     for g in gate_scatters:
         g.end()
-    ring.panels[4].end()
-    ring.panels[5].third()
-    for s in range(seqs):
-        lines[s].total([input_grad.at[i] for i in range(seqs)])
     quarter = pack.shape[1]
     for i in range(4):
         pack[4 + i : 5 + i, :] = mlp_part[:, i * quarter : (i + 1) * quarter]
     for s in range(seqs):
-        change, gain_part = norm_back(act[s].astype(F32), gain[...], input_grad[s])
+        lines[s].total([input_grad.at[i] for i in range(seqs)])
+        change, gain_part = norm_back(act[s].astype(F32), gain[...][None], input_grad[s])
         input_grad[s] = change + grad_middle[s]
         for i in range(4):
             piece = gain_part[:, i * quarter : (i + 1) * quarter]
@@ -1678,7 +1717,8 @@
     sum_ = small_all[0]
     for i in range(1, 8):
         sum_ = sum_ + small_all[i]
-    smalls[...] = sum_
+    rate_grad[...] = sum_[0]
+    taps_grad[...] = sum_[1:5]
     for c in pack_copies:
         c.wait_recv()
     sum_ = packs[0]
@@ -1705,37 +1745,44 @@
     sum_ = line_packs[0]
     for i in range(1, depth):
         sum_ = sum_ + line_packs[i]
-    gains[...] = sum_
+    for i in range(4):
+        norm_grad[i * quarter : (i + 1) * quarter] = sum_[i]
+        mlp_grad[i * quarter : (i + 1) * quarter] = sum_[4 + i]
     for c in small_copies + pack_copies + z_copies:
         c.wait_send()
     ring.end()
-    for line in lines:
+    for line in lines + [feed_line]:
         line.end()
 
 
 def mixer_back_phase(
-    branch, normed, saved, weights, panels, taps, rate, act, gain, grad_middle, mlp_part, depth,
+    branch, normed, saved, weights, normed_two, lift_rows, feed, middle, taps, rate, act, gain,
+    grad_middle, mlp_part, output_first, depth,
 ):
     seqs, length, model = branch.shape
     tokens = seqs * length
+    units = lift_rows.shape[1]
     gelu_w, input_w, gate_in_w, gate_dec_w, out_w = weights[:5]
-    gelu_pre, input_pre, conv, window, gate_in, gate_dec, states, mixed = saved
+    gelu_pre, input_pre, window, gate_in, gate_dec, states, mixed = saved
     width = out_w.shape[1]
     block = gate_in_w.shape[0]
     half = block // 2
-    n = len(panels)
-    panel = (panels[0].shape[0] // 8, panels[0].shape[1])
+    panel = (model // 8, PANEL)
     gate = (block // 8, width)
     pack = (8, model // 4)
     small = (8, width)
     flat = (tokens, width)
     outs = [
+        shaped(act.shape, BF16, VMEM),
         shaped(act.shape, F32, VMEM),
-        shaped(pack, F32, VMEM),
-        shaped(small, F32, VMEM),
+        shaped((model,), F32, VMEM),
+        shaped((model,), F32, VMEM),
+        shaped((width,), F32, VMEM),
+        shaped(taps.shape, F32, VMEM),
         shaped(gate, F32, VMEM),
         shaped(gate, F32, VMEM),
-    ] + [shaped(panel, F32, ANY)] * (n + 3)
+    ]
+    outs += [shaped(panel, F32, ANY)] * 3 + [shaped((model // 8, units), F32, ANY)]
     scratch = [pltpu.VMEM((tokens, model), BF16)]
     scratch += [
         pltpu.VMEM(x.shape, x.dtype)
@@ -1744,7 +1791,6 @@
             input_w,
             gelu_pre,
             input_pre,
-            conv,
             window,
             gate_in,
             gate_dec,
@@ -1753,20 +1799,17 @@
             gate_dec_w,
         )
     ]
-    scratch += [
-        pltpu.VMEM(flat, F32),
-        pltpu.VMEM((tokens + 8, width), F32),
-        pltpu.VMEM((seqs, length + 8, width), F32),
-    ]
-    scratch += [pltpu.VMEM(flat, BF16)] * 5
+    scratch += [pltpu.VMEM(flat, F32), pltpu.VMEM((seqs * (length + 8), width), F32)]
+    scratch += [pltpu.VMEM(flat, BF16)] * 3
     scratch += [pltpu.VMEM((tokens, half), BF16)] * 2
     scratch += [pltpu.VMEM(gate_in_w.shape, BF16)] * 2
     scratch += [
-        pltpu.VMEM(branch.shape, BF16),
+        pltpu.VMEM((tokens, model), BF16),
         pltpu.VMEM((1 + taps.shape[0], 8, width), F32),
+        DMA,
     ]
     scratch += line_scatter_scratch(seqs, length // depth, model, depth)
-    scratch += [DMA, DMA, DMA((12 + seqs,)), DMA((n,))]
+    scratch += [DMA, DMA, DMA((12 + 2 * seqs,)), DMA]
     scratch += [
         pltpu.VMEM(small, F32),
         pltpu.VMEM((8,) + small, F32),
@@ -1777,12 +1820,14 @@
     ]
     scratch += [DMA((7,))] * 4 + [DMA((depth - 1,))] * 2
     scratch += ring_scratch(3, *panel)
+    scratch += [pltpu.VMEM((length, model), BF16), pltpu.VMEM((tokens, PANEL), BF16)]
+    scratch += line_scatter_scratch(1, length // depth, model, depth)
     scratch += scatter_scratch([gate] * 2, (False, False))
-    res = call(
-        functools.partial(mixer_back_kernel, depth, n),
+    return call(
+        functools.partial(mixer_back_kernel, depth),
         "mixer_back_phase",
         3,
-        [ANY] * 15 + [VMEM] * 6 + [ANY] * n,
+        [ANY] * 18 + [VMEM] * 7,
         outs,
         scratch,
         (
@@ -1791,7 +1836,6 @@
             out_w,
             gelu_pre,
             input_pre,
-            conv,
             window,
             gate_in,
             gate_dec,
@@ -1801,17 +1845,48 @@
             input_w,
             gate_in_w,
             gate_dec_w,
+            normed_two,
+            lift_rows,
+            feed,
+            middle,
             taps,
-            rate.reshape(1, width),
+            rate,
             act,
-            gain.reshape(1, model),
+            gain,
             grad_middle,
             mlp_part,
-        )
-        + tuple(panels),
+            output_first,
+        ),
         vmem=63 * 1024 * 1024,
     )
-    return res[0], res[1].reshape(2, model), res[2], res[3:5], res[5:]
+
+
+def finish_kernel(*refs):
+    n = (len(refs) - 2) // 3
+    ins, outs, held = refs[:n], refs[n : 2 * n], refs[2 * n : 3 * n]
+    load_sem, save_sem = refs[3 * n :]
+    loads = [pltpu.make_async_copy(ins[i], held[i], load_sem.at[i]) for i in range(n)]
+    saves = [pltpu.make_async_copy(held[i], outs[i], save_sem.at[i]) for i in range(n)]
+    for copy in loads:
+        copy.start()
+    for load, save in zip(loads, saves):
+        load.wait()
+        save.start()
+    for save in saves:
+        save.wait()
+
+
+def finish(arrays):
+    n = len(arrays)
+    return pl.pallas_call(
+        finish_kernel,
+        name="finish",
+        out_shape=[jax.ShapeDtypeStruct(x.shape, x.dtype) for x in arrays],
+        in_specs=[ANY] * n,
+        out_specs=[ANY] * n,
+        scratch_shapes=[pltpu.VMEM(x.shape, x.dtype) for x in arrays] + [DMA((n,))] * 2,
+        compiler_params=pltpu.CompilerParams(vmem_limit_bytes=62 * 1024 * 1024),
+    )(*arrays)
 
 
 def swapped(block, axis):
@@ -1870,35 +1945,24 @@
         self.normed, self.cot, self.normed_two = rows
         return middle
 
-    def feed(self, middle, gain, cotangent, token_weight):
-        return feed_phase(
+    def back(self, middle, gain, cotangent, token_weight, act, first_gain):
+        grad_middle, branch, mlp_part, feed, lift_rows, output, down_grad, gate_grad = feed_phase(
             self.normed_two, self.cot, self.feeds, self.held, middle, gain, cotangent,
             token_weight, self.depth,
         )
-
-    def last(self, branch, panels, act, gain, grad_middle, mlp_part):
-        input_grad, gains, small, gates, rest = mixer_back_phase(
-            branch,
-            self.normed,
-            self.saved,
-            self.weights,
-            panels[HOSTED:],
-            self.taps,
-            self.rate,
-            act,
-            gain,
-            grad_middle,
-            mlp_part,
-            self.depth,
+        res = mixer_back_phase(
+            branch, self.normed, self.saved, self.weights, self.normed_two, lift_rows, feed,
+            middle, self.taps, self.rate, act, first_gain, grad_middle, mlp_part,
+            output, self.depth,
         )
-        grads = list(rest[-3:]) + list(gates)
-        rest = rest[:-3]
-        panels = list(panels[:HOSTED]) + list(rest)
-        third = len(panels) // 3
-        feeds = [
-            jnp.concatenate(panels[i * third : (i + 1) * third], axis=1) for i in range(3)
-        ]
-        return input_grad, gains, small, grads, feeds
+        output, input_grad, norm_grad, mlp_grad, rate_grad, taps_grad = res[:6]
+        gate_in, gate_dec, out_grad, gelu_grad, input_w_grad, up_grad = res[6:]
+        results = (
+            output, input_grad, norm_grad, mlp_grad, rate_grad, taps_grad, gelu_grad, input_w_grad,
+            gate_in, gate_dec, out_grad, gate_grad, up_grad, down_grad,
+        )
+        results = finish(results)
+        return tuple(results[:6]) + (tuple(results[6:]),)
 
 
 class Plain:
@@ -1966,9 +2030,9 @@
         self.normed_two = self.wide(normalize(middle, gain).astype(BF16))
         return middle
 
-    def feed(self, middle, gain, cotangent, token_weight):
+    def back(self, middle, gain, cotangent, token_weight, act, first_gain):
         cot_own = cotangent.astype(F32) * token_weight
-        down_w, gate_w, up_w = self.feeds
+        gate_w, up_w, down_w = self.feeds
         normed, cot = self.normed_two, self.cot
         gate_pre = dot("nwo,ob->nwb", normed, gate_w)
         lift_pre = dot("nwo,ob->nwb", normed, up_w)
@@ -1986,9 +2050,7 @@
         )
         feed = dot("xav,tv->xat", hidden, down_w).astype(BF16)
         output = (middle + self.narrow(feed)).astype(BF16)
-        return grad, self.wide(grad.astype(BF16)), gain_grad[None], output, panels
-
-    def last(self, branch, panels, act, gain, grad_middle, mlp_part):
+        branch = self.wide(grad.astype(BF16))
         (
             normed_all, gelu_w, input_w, out_w, gelu_out, gelu_back, conv_back, tiles, placed,
             gate_back, decay, states, mixed,
@@ -2026,20 +2088,22 @@
         input_rows, grad_taps = conv_back(grad_conv)
         input_rows = input_rows.astype(BF16)
         part = dot("mzf,af->mza", gelu_grad, gelu_w) + dot("mzf,af->mza", input_rows, input_w)
-        _, back = jax.vjp(normalize, act.astype(F32), gain)
-        change, gain_grad = back(self.narrow(part.astype(BF16)))
-        gains = lax.psum(jnp.concatenate([gain_grad[None], mlp_part]), ("dp", "tensor"))
-        small = lax.psum(jnp.concatenate([grad_rate[None], grad_taps]), "dp")
+        _, back = jax.vjp(normalize, act.astype(F32), first_gain)
+        change, norm_grad = back(self.narrow(part.astype(BF16)))
+        gains = lax.psum((norm_grad, gain_grad), ("dp", "tensor"))
+        small = lax.psum((grad_rate, grad_taps), "dp")
         parts = (
-            weight_grad(branch, mixed),
             weight_grad(normed_all, gelu_grad),
             weight_grad(normed_all, input_rows),
             grad_gates[0].astype(BF16),
             grad_gates[1].astype(BF16),
+            weight_grad(branch, mixed),
+            panels[1],
+            panels[2],
+            panels[0],
         )
         own = [self.own(g) for g in parts]
-        feeds = [self.own(g) for g in panels]
-        return grad_middle + change, gains, small, own, feeds
+        return (output, grad + change) + gains + small + (tuple(own),)
 
 
 def shards(
@@ -2079,30 +2143,27 @@
     token_weight = (valid_mask * my_weight[:, None])[:, :, None]
 
     weights = (
-        gelu_proj, input_proj, gate_input, gate_decay, out_proj.T, feed_down.T, feed_gate, feed_up
+        gelu_proj, input_proj, gate_input, gate_decay, out_proj.T, feed_gate, feed_up, feed_down.T
     )
     middle = run.front(cotangent, token_weight, weights, activations, mlp_gain, norm_gain)
-    grad_middle, branch_grad_all, mlp_part, output, panels = run.feed(
-        middle, mlp_gain, cotangent, token_weight
-    )
-    input_grad, gains, small, grads, feeds = run.last(
-        branch_grad_all, panels, activations, norm_gain, grad_middle, mlp_part
+    output, input_grad, norm_grad, mlp_grad, rate_grad, taps_grad, grads = run.back(
+        middle, mlp_gain, cotangent, token_weight, activations, norm_gain
     )
     return (
         output,
         input_grad,
-        gains[0],
+        norm_grad,
+        grads[0],
         grads[1],
+        taps_grad,
         grads[2],
-        small[1:5],
         grads[3],
-        grads[4],
-        small[0],
-        grads[0].T,
-        gains[1],
-        feeds[1],
-        feeds[2],
-        feeds[0].T,
+        rate_grad,
+        grads[4].T,
+        mlp_grad,
+        grads[5],
+        grads[6],
+        grads[7].T,
     )
 
 

time: 466 us -> 433 us (0.929)
  local copies, waits for them, and re-layouts: 15.5 us -> 0.8 us
  Pallas kernels: 434 us -> 422 us
  other arithmetic: 8.85 us -> 2.9 us
    pallas_call x3, Pallas kernels: 434 us -> 413 us  [call(): pl.pallas_call(kernel, name=name, out_shape=[o[0] for o in outs], in_spec...]
    pallas_call x0 -> x1, Pallas kernels: none -> 8.82 us  [finish(): pl.pallas_call(finish_kernel, name='finish', out_shape=[jax.ShapeDtypeStr...]
    unnamed x33 -> x0, local copies, waits for them, and re-layouts: 6.1 us -> none
    concatenate x2 -> x0, other arithmetic: 5.95 us -> none  [last(): jnp.concatenate(panels[i * third:(i + 1) * third], axis=1)]
where the time goes in v6:
time: 433 us; the launch traced here: 427 us
  Pallas kernels  422 us (97%)
    pallas_call x3, Pallas kernels, call(): pl.pallas_call(kernel, name=name, out_shape=[o[0] for o in outs], in_spec...  413 us
    pallas_call x1, Pallas kernels, finish(): pl.pallas_call(finish_kernel, name='finish', out_shape=[jax.ShapeDtypeStr...  8.82 us

profile of v6, /device:TPU:0, one launch (start us, length us, event | category | flops | bytes accessed | tf_op | source)
XLA Modules:
  0.0 426.8 jit_solution(4734928894214281153)
XLA Ops:
  0.7 0.7 convert_element_type.6
  1.3 0.8 select_reduce_fusion.1
  2.1 0.7 select_reduce_fusion
  2.8 0.1 dynamic_slice.7
  2.9 0.7 dynamic_slice.6
  3.7 0.7 compare_select_fusion.token_weight
  4.4 179.9 %front_phase.1 = (f32[2,64,2560]{2,1,0:T(8,128)}, bf16[2,256,2560]{2,1,0:T(8,128)(2,1)}, bf16[512,2560]{1,0:T(8,128)(2,1)}, bf16[512,2560]{1,0:T(8,128)(2,1)}, b...) custom-call(bf16[2,64,2560]{2,1,0:T(8,128)(2,1)} %cotangent.3, ...), custom_call_target="tpu_custom_call" | custom-call | tf_op jit(solution)/shard_map/front_phase/pallas_call | solution.py:534
  184.3 118.7 %feed_phase.1 = (f32[2,64,2560]{2,1,0:T(8,128)}, bf16[2,256,2560]{2,1,0:T(8,128)(2,1)}, f32[1,2560]{1,0:T(1,128)}, bf16[256,2560]{1,0:T(8,128)(2,1)}, bf16[512,1...) custom-call(bf16[512,2560]{1,0:T(8,128)(2,1)} %get-tuple-element.70.normed_in.normed_two_, ...), custom_call_target="tpu_custom_call" | custom-call | tf_op jit(solution)/shard_map/feed_phase/pallas_call | solution.py:534
  303.0 114.8 %mixer_back_phase.1 = (bf16[2,64,2560]{2,1,0:T(8,128)(2,1)}, f32[2,64,2560]{2,1,0:T(8,128)}, f32[2560]{0:T(1024)}, f32[2560]{0:T(1024)}, f32[640]{0:T(1024)}, /*...) custom-call(bf16[2,256,2560]{2,1,0:T(8,128)(2,1)} %get-tuple-element, ...), custom_call_target="tpu_custom_call" | custom-call | tf_op jit(solution)/shard_map/mixer_back_phase/pallas_call | solution.py:534
  417.8 8.8 %finish.1 = (bf16[2,64,2560]{2,1,0:T(8,128)(2,1)}, f32[2,64,2560]{2,1,0:T(8,128)}, f32[2560]{0:T(1024)}, f32[2560]{0:T(1024)}, f32[640]{0:T(1024)}, /*index=5*/f...) custom-call(bf16[2,64,2560]{2,1,0:T(8,128)(2,1)} %get-tuple-element., ...), custom_call_target="tpu_custom_call" | custom-call | tf_op jit(solution)/shard_map/finish/pallas_call | solution.py:1881
  (2 shorter events, 0.0 us)

commit v7 on v6

--- a/solution.py
+++ b/solution.py
@@ -1378,7 +1378,7 @@
     branch, weight, input_w = scratch[:3]
     gelu_pre, input_pre, window, gate_in, gate_dec, states, gate_in_w, gate_dec_w = scratch[3:11]
     grad, decay, gelu_grad, grad_in, grad_dec = scratch[11:16]
-    input_rows = grad_in
+    input_rows = scratch[-1]
     grad_conv = [decay.at[pl.ds(s * (decay.shape[0] // 2), decay.shape[0] // 2)] for s in range(2)]
     rim_out, rim_in, gate_in_grad, gate_dec_grad, part, sums = scratch[16 : 22]
     panel_sem = scratch[22]
@@ -1403,7 +1403,7 @@
         (gate_in_grad, gate_dec_grad),
         (gate_in_out, gate_dec_out),
         (False, False),
-        scratch[56:],
+        scratch[56:-1],
         d,
         t,
     )
@@ -1499,29 +1499,7 @@
     lift_load = load_lift(1)
     for copy in next_:
         copy.wait()
-
-    @pl.loop(0, tokens // STRIP)
-    def _(i):
-        rows = rows_of(i, STRIP)
-        held = pl.ds(pl.multiple_of(i * STRIP + 8, 8), STRIP)
-        act, slope = gelu_both(gelu_pre[rows, :])
-        came = grad[rows, :]
-        gelu_grad[rows, :] = (came * states[held, :] * slope).astype(BF16)
-        grad[rows, :] = came * act
-        decay[rows, :] = jnp.exp(-8.0 * sigmoid(gate_dec[rows, :]) * rate[...][None])
-
-    decay[tokens : tokens + 8, :] = jnp.zeros((8, width), F32)
-    push(1)
-    ring.panels[0].third()
-    feed_line.step(1)
-    lift_load.wait()
-    begin(2, part, lift_rows)
-    lift_load = load_lift(2)
-    scan_rows(decay, grad, range(seqs), length, backward=True)
-    feed_line.step(2)
-    push(2)
-    for copy in then:
-        copy.wait()
+    spans = [pl.ds(s * length, length) for s in range(seqs)]
     sums[...] = jnp.zeros(sums.shape, F32)
 
     def fold(value):
@@ -1529,8 +1507,23 @@
 
     own_columns = pl.ds(pl.multiple_of(parity * half, half), width)
     first_row = lax.broadcasted_iota(jnp.int32, (STRIP, width), 0) == 0
-    for s in range(seqs):
-
+
+    def states_back(s):
+        @pl.loop(0, length // STRIP)
+        def _(i):
+            start = pl.multiple_of(s * length + i * STRIP, STRIP)
+            rows, held = pl.ds(start, STRIP), pl.ds(pl.multiple_of(start + 8, 8), STRIP)
+            act, slope = gelu_both(gelu_pre[rows, :])
+            came = grad[rows, :]
+            gelu_grad[rows, :] = (came * states[held, :] * slope).astype(BF16)
+            grad[rows, :] = came * act
+            decay[rows, :] = jnp.exp(-8.0 * sigmoid(gate_dec[rows, :]) * rate[...][None])
+
+        end = (s + 1) * length
+        decay[end : end + 8, :] = jnp.zeros((8, width), F32)
+        scan_rows(decay, grad, (s,), length, backward=True)
+
+    def drive_back(s):
         @pl.loop(0, length // STRIP)
         def _(i):
             start = pl.multiple_of(s * length + i * STRIP, STRIP)
@@ -1555,82 +1548,61 @@
 
         grad_conv[s][length : length + 8, :] = jnp.zeros((8, width), F32)
 
-    ring.panels[0].end()
-    ring.panels[1].third()
-
-    def gates_back(k, low, high):
-        return contract(grad_in[:, low:high], gate_in_w[:, low:high], (1, 1)) + contract(
-            grad_dec[:, low:high], gate_dec_w[:, low:high], (1, 1)
+    def gates_back(s, k, low, high):
+        rows = spans[s]
+        return contract(grad_in[rows, low:high], gate_in_w[:, low:high], (1, 1)) + contract(
+            grad_dec[rows, low:high], gate_dec_w[:, low:high], (1, 1)
         )
 
-    def add_conv(low, high, value):
-        for s in range(seqs):
-            grad_conv[s][0:length, low:high] += value[s * length : (s + 1) * length]
-
-    def rim(to):
+    def add_conv(s, low, high, value):
+        grad_conv[s][0:length, low:high] += value
+
+    def rim(s, to):
         return pltpu.make_async_remote_copy(
-            src_ref=rim_out,
-            dst_ref=rim_in,
-            send_sem=rim_send,
-            recv_sem=rim_recv,
+            src_ref=rim_out.at[spans[s]],
+            dst_ref=rim_in.at[spans[s]],
+            send_sem=rim_send.at[s],
+            recv_sem=rim_recv.at[s],
             device_id=(d, to),
             device_id_type=MESH,
         )
 
-    @pl.when(even)
-    def _():
-        value = gates_back(*even_blocks[-1])
-        rim_out[...] = value[:, half:].astype(BF16)
-        rim(t + 1).start()
-        add_conv(width - half, width, value[:, :half])
-
-    @pl.when(odd)
-    def _():
-        value = gates_back(*odd_blocks[0])
-        rim_out[...] = value[:, :half].astype(BF16)
-        rim(t - 1).start()
-        add_conv(0, half, value[:, half:])
-
-    lift_load.wait()
-    begin(3, part, lift_rows)
-
-    def inner(blocks):
-        for k, low, high in blocks:
-            add_conv(low, high, gates_back(k, low, high))
-
-    def gate_grads(blocks):
-        for k, low, high in blocks:
-            near = window[:, k * block : (k + 1) * block]
-            gate_in_grad[:, low:high] = contract(near, grad_in[:, low:high], (0, 0)).astype(BF16)
-            gate_dec_grad[:, low:high] = contract(near, grad_dec[:, low:high], (0, 0)).astype(BF16)
-
-    @pl.when(even)
-    def _():
-        inner(even_blocks[:-1])
-        gate_grads(even_blocks)
-
-    @pl.when(odd)
-    def _():
-        inner(odd_blocks[1:])
-        gate_grads(odd_blocks)
-
-    for g in gate_scatters:
-        g.start()
-    ring.panels[1].end()
-    ring.panels[2].third()
-    push(3)
-
-    @pl.when(even)
-    def _():
-        rim(t + 1).wait()
-        add_conv(width - half, width, rim_in[...].astype(F32))
-
-    @pl.when(odd)
-    def _():
-        rim(t - 1).wait()
-        add_conv(0, half, rim_in[...].astype(F32))
-
-    for s in range(seqs):
+    def rim_start(s):
+        @pl.when(even)
+        def _():
+            value = gates_back(s, *even_blocks[-1])
+            rim_out[spans[s], :] = value[:, half:].astype(BF16)
+            rim(s, t + 1).start()
+            add_conv(s, width - half, width, value[:, :half])
+
+        @pl.when(odd)
+        def _():
+            value = gates_back(s, *odd_blocks[0])
+            rim_out[spans[s], :] = value[:, :half].astype(BF16)
+            rim(s, t - 1).start()
+            add_conv(s, 0, half, value[:, half:])
+
+    def inner(s):
+        @pl.when(even)
+        def _():
+            for k, low, high in even_blocks[:-1]:
+                add_conv(s, low, high, gates_back(s, k, low, high))
+
+        @pl.when(odd)
+        def _():
+            for k, low, high in odd_blocks[1:]:
+                add_conv(s, low, high, gates_back(s, k, low, high))
+
+    def conv_back(s):
+        @pl.when(even)
+        def _():
+            rim(s, t + 1).wait()
+            add_conv(s, width - half, width, rim_in[spans[s], :].astype(F32))
+
+        @pl.when(odd)
+        def _():
+            rim(s, t - 1).wait()
+            add_conv(s, 0, half, rim_in[spans[s], :].astype(F32))
 
         @pl.loop(0, length // STRIP)
         def _(i):
@@ -1646,6 +1618,69 @@
             rows = pl.ds(pl.multiple_of(s * length + i * STRIP, STRIP), STRIP)
             input_rows[rows, :] = value.astype(BF16)
 
+    def project_back(s):
+        rows, panel = spans[s], 512
+
+        @pl.loop(0, weight.shape[0] // panel)
+        def _(i):
+            columns = rows_of(i, panel)
+            value = contract(gelu_grad[rows, :], weight[columns, :], (1, 1))
+            value = value + contract(input_rows[rows, :], input_w[columns, :], (1, 1))
+            part[rows, columns] = value.astype(BF16)
+
+    def gate_grads(blocks):
+        for k, low, high in blocks:
+            near = window[:, k * block : (k + 1) * block]
+            gate_in_grad[:, low:high] = contract(near, grad_in[:, low:high], (0, 0)).astype(BF16)
+            gate_dec_grad[:, low:high] = contract(near, grad_dec[:, low:high], (0, 0)).astype(BF16)
+
+    states_back(0)
+    feed_line.step(1)
+    push(1)
+    ring.panels[0].third()
+    for copy in then:
+        copy.wait()
+    drive_back(0)
+    rim_start(0)
+    feed_line.step(2)
+    inner(0)
+    lift_load.wait()
+    begin(2, part, lift_rows)
+    lift_load = load_lift(2)
+    conv_back(0)
+    push(2)
+    ring.panels[1].third()
+    ring.panels[0].end()
+    lift_load.wait()
+    begin(3, part, lift_rows)
+    reload.wait()
+    project_back(0)
+    lines[0].start(0, 1)
+    states_back(1)
+    ring.panels[2].third()
+    push(3)
+    drive_back(1)
+    rim_start(1)
+    lines[0].start(1)
+    lines[0].step(1)
+    inner(1)
+
+    @pl.when(even)
+    def _():
+        gate_grads(even_blocks)
+
+    @pl.when(odd)
+    def _():
+        gate_grads(odd_blocks)
+
+    for g in gate_scatters:
+        g.start()
+    conv_back(1)
+    lines[0].step(2)
+    project_back(1)
+    lines[1].start()
+    middle_load = load(0, middle_in.at[1], input_grad.at[1])
+    ring.panels[3].third()
     for k in range(sums.shape[0]):
         small[k : k + 1, :] = jnp.sum(sums[k], axis=0, keepdims=True)
     small[sums.shape[0] :, :] = jnp.zeros((8 - sums.shape[0], width), F32)
@@ -1653,48 +1688,27 @@
     for c in small_copies:
         c.start()
     small_all[d] = small[...]
-    reload.wait()
-    panel = 512
-    for s in range(seqs):
-        rows = pl.ds(s * length, length)
-
-        @pl.loop(0, weight.shape[0] // panel)
-        def _(i):
-            columns = rows_of(i, panel)
-            value = contract(gelu_grad[rows, :], weight[columns, :], (1, 1))
-            value = value + contract(input_rows[rows, :], input_w[columns, :], (1, 1))
-            part[rows, columns] = value.astype(BF16)
-
-        lines[s].start()
-
-    middle_load = load(0, middle_in.at[1], input_grad.at[1])
-    ring.panels[2].end()
-    ring.panels[3].third()
     for copy in wide_loads:
         copy.wait()
+    ring.panels[1].end()
     begin(4, branch, gelu_grad)
     for g in gate_scatters:
         g.first()
         g.second()
     push(4)
-    lines[0].step(1)
+    lines[1].step(1)
+    ring.panels[2].end()
     begin(5, branch, input_rows)
-    lines[0].step(2)
+    ring.panels[4].third()
+    lines[1].step(2)
+    push(5)
     ring.panels[3].end()
-    ring.panels[4].third()
-    push(5)
     for g in gate_scatters:
         g.third()
     middle_load.wait()
     feed_line.total([input_grad.at[1]], more=True)
     output[0] = output_first[...]
     output[1] = input_grad[1].astype(BF16)
-    lines[1].step(1)
-    ring.panels[4].end()
-    ring.panels[5].third()
-    lines[1].step(2)
-    for g in gate_scatters:
-        g.end()
     quarter = pack.shape[1]
     for i in range(4):
         pack[4 + i : 5 + i, :] = mlp_part[:, i * quarter : (i + 1) * quarter]
@@ -1711,6 +1725,10 @@
     pack_copies = dp_copies(pack, packs, psend, precv)
     for c in pack_copies:
         c.start()
+    ring.panels[5].third()
+    ring.panels[4].end()
+    for g in gate_scatters:
+        g.end()
     packs[d] = pack[...]
     for c in small_copies:
         c.wait_recv()
@@ -1809,7 +1827,7 @@
         DMA,
     ]
     scratch += line_scatter_scratch(seqs, length // depth, model, depth)
-    scratch += [DMA, DMA, DMA((12 + 2 * seqs,)), DMA]
+    scratch += [DMA((seqs,)), DMA((seqs,)), DMA((12 + 2 * seqs,)), DMA]
     scratch += [
         pltpu.VMEM(small, F32),
         pltpu.VMEM((8,) + small, F32),
@@ -1823,6 +1841,7 @@
     scratch += [pltpu.VMEM((length, model), BF16), pltpu.VMEM((tokens, PANEL), BF16)]
     scratch += line_scatter_scratch(1, length // depth, model, depth)
     scratch += scatter_scratch([gate] * 2, (False, False))
+    scratch += [pltpu.VMEM(flat, BF16)]
     return call(
         functools.partial(mixer_back_kernel, depth),
         "mixer_back_phase",

time: 433 us -> 429 us (level)
    pallas_call x3, Pallas kernels: 413 us -> 409 us  [call(): pl.pallas_call(kernel, name=name, out_shape=[o[0] for o in outs], in_spec...]
where the time goes in v7:
time: 429 us; the launch traced here: 422 us
  Pallas kernels  418 us (97%)
    pallas_call x3, Pallas kernels, call(): pl.pallas_call(kernel, name=name, out_shape=[o[0] for o in outs], in_spec...  409 us
    pallas_call x1, Pallas kernels, finish(): pl.pallas_call(finish_kernel, name='finish', out_shape=[jax.ShapeDtypeStr...  8.82 us

profile of v7, /device:TPU:0, one launch (start us, length us, event | category | flops | bytes accessed | tf_op | source)
XLA Modules:
  0.0 422.2 jit_solution(4180994443325230705)
XLA Ops:
  0.7 0.7 convert_element_type.6
  1.3 0.8 select_reduce_fusion.1
  2.1 0.7 select_reduce_fusion
  2.8 0.1 dynamic_slice.7
  2.9 0.7 dynamic_slice.6
  3.7 0.7 compare_select_fusion.token_weight
  4.4 179.9 %front_phase.1 = (f32[2,64,2560]{2,1,0:T(8,128)}, bf16[2,256,2560]{2,1,0:T(8,128)(2,1)}, bf16[512,2560]{1,0:T(8,128)(2,1)}, bf16[512,2560]{1,0:T(8,128)(2,1)}, b...) custom-call(bf16[2,64,2560]{2,1,0:T(8,128)(2,1)} %cotangent.3, ...), custom_call_target="tpu_custom_call" | custom-call | tf_op jit(solution)/shard_map/front_phase/pallas_call | solution.py:534
  184.3 118.7 %feed_phase.1 = (f32[2,64,2560]{2,1,0:T(8,128)}, bf16[2,256,2560]{2,1,0:T(8,128)(2,1)}, f32[1,2560]{1,0:T(1,128)}, bf16[256,2560]{1,0:T(8,128)(2,1)}, bf16[512,1...) custom-call(bf16[512,2560]{1,0:T(8,128)(2,1)} %get-tuple-element.70.normed_in.normed_two_, ...), custom_call_target="tpu_custom_call" | custom-call | tf_op jit(solution)/shard_map/feed_phase/pallas_call | solution.py:534
  303.0 110.1 %mixer_back_phase.1 = (bf16[2,64,2560]{2,1,0:T(8,128)(2,1)}, f32[2,64,2560]{2,1,0:T(8,128)}, f32[2560]{0:T(1024)}, f32[2560]{0:T(1024)}, f32[640]{0:T(1024)}, /*...) custom-call(bf16[2,256,2560]{2,1,0:T(8,128)(2,1)} %get-tuple-element, ...), custom_call_target="tpu_custom_call" | custom-call | tf_op jit(solution)/shard_map/mixer_back_phase/pallas_call | solution.py:534
  413.1 8.8 %finish.1 = (bf16[2,64,2560]{2,1,0:T(8,128)(2,1)}, f32[2,64,2560]{2,1,0:T(8,128)}, f32[2560]{0:T(1024)}, f32[2560]{0:T(1024)}, f32[640]{0:T(1024)}, /*index=5*/f...) custom-call(bf16[2,64,2560]{2,1,0:T(8,128)(2,1)} %get-tuple-element., ...), custom_call_target="tpu_custom_call" | custom-call | tf_op jit(solution)/shard_map/finish/pallas_call | solution.py:1900
  (2 shorter events, 0.0 us)

commit v8 on v7

--- a/solution.py
+++ b/solution.py
@@ -55,10 +55,10 @@
     @pl.loop(0, rows, step=step)
     def _(start):
         part = pl.ds(pl.multiple_of(start, step), step)
-        value = total[part, :].astype(F32)
+        value = total[part, :]
         for term in terms:
-            value = value + term[part, :].astype(F32)
-        total[part, :] = value.astype(BF16)
+            value = value + term[part, :]
+        total[part, :] = value
 
 
 class WeightGather:
@@ -642,9 +642,9 @@
     gate_in_shard,
     gate_dec_shard,
     out_shard,
-    gate_shard,
-    up_shard,
-    down_shard,
+    gate_in_place,
+    up_in_place,
+    down_in_place,
     taps,
     rate,
     act,
@@ -683,6 +683,14 @@
     panel_sem, product_sem = scratch[45:47]
     got, ssem, rsem = scratch[47:50]
     normed_block, cot_block, hidden = scratch[50:53]
+    gate_shard, up_shard, down_shard, shard_sem = scratch[53:57]
+    sources = (gate_in_place, up_in_place, down_in_place)
+    shard_loads = [
+        pltpu.make_async_copy(source, shard, shard_sem.at[i])
+        for i, (source, shard) in enumerate(zip(sources, (gate_shard, up_shard, down_shard)))
+    ]
+    for copy in shard_loads:
+        copy.start()
     d, t = place()
     parity = lax.rem(t, 2)
     even = parity == 0
@@ -860,6 +868,8 @@
     states[0:8, :] = jnp.zeros((8, width), F32)
     convolve(0)
     out_g.relay()
+    for copy in shard_loads:
+        copy.wait()
     gate_g.start()
     up_g.start()
     for g in one[1:]:
@@ -1036,11 +1046,12 @@
     ]
     scratch += line_scatter_scratch(seqs, rows, model, depth)
     scratch += [pltpu.VMEM(act.shape, BF16)] * 2 + [pltpu.VMEM((tokens, PANEL), BF16)]
+    scratch += [pltpu.VMEM(w.shape, BF16) for w in weights[-3:]] + [DMA((3,))]
     res = call(
         functools.partial(front_kernel, depth),
         "front_phase",
         0,
-        [VMEM] * (7 + n),
+        [VMEM] * (n - 1) + [ANY] * 3 + [VMEM] * 5,
         outs,
         scratch,
         (cotangent, token_weight)

time: 429 us -> 427 us (level)
  no operation moved by 1% of the time
where the time goes in v8:
time: 427 us; the launch traced here: 421 us
  Pallas kernels  416 us (97%)
    pallas_call x3, Pallas kernels, call(): pl.pallas_call(kernel, name=name, out_shape=[o[0] for o in outs], in_spec...  407 us
    pallas_call x1, Pallas kernels, finish(): pl.pallas_call(finish_kernel, name='finish', out_shape=[jax.ShapeDtypeStr...  8.82 us

profile of v8, /device:TPU:0, one launch (start us, length us, event | category | flops | bytes accessed | tf_op | source)
XLA Modules:
  0.0 420.6 jit_solution(3435547315487349745)
XLA Ops:
  0.7 0.7 convert_element_type.6
  1.3 0.8 select_reduce_fusion.1
  2.1 0.7 select_reduce_fusion
  2.8 0.1 dynamic_slice.7
  2.9 0.7 dynamic_slice.6
  3.7 0.7 compare_select_fusion.token_weight
  4.4 178.8 %front_phase.1 = (f32[2,64,2560]{2,1,0:T(8,128)}, bf16[2,256,2560]{2,1,0:T(8,128)(2,1)}, bf16[512,2560]{1,0:T(8,128)(2,1)}, bf16[512,2560]{1,0:T(8,128)(2,1)}, b...) custom-call(bf16[2,64,2560]{2,1,0:T(8,128)(2,1)} %cotangent.3, ...), custom_call_target="tpu_custom_call" | custom-call | tf_op jit(solution)/shard_map/front_phase/pallas_call | solution.py:534
  183.2 118.6 %feed_phase.1 = (f32[2,64,2560]{2,1,0:T(8,128)}, bf16[2,256,2560]{2,1,0:T(8,128)(2,1)}, f32[1,2560]{1,0:T(1,128)}, bf16[256,2560]{1,0:T(8,128)(2,1)}, bf16[512,1...) custom-call(bf16[512,2560]{1,0:T(8,128)(2,1)} %get-tuple-element.70.normed_in.normed_two_, ...), custom_call_target="tpu_custom_call" | custom-call | tf_op jit(solution)/shard_map/feed_phase/pallas_call | solution.py:534
  301.8 109.7 %mixer_back_phase.1 = (bf16[2,64,2560]{2,1,0:T(8,128)(2,1)}, f32[2,64,2560]{2,1,0:T(8,128)}, f32[2560]{0:T(1024)}, f32[2560]{0:T(1024)}, f32[640]{0:T(1024)}, /*...) custom-call(bf16[2,256,2560]{2,1,0:T(8,128)(2,1)} %get-tuple-element, ...), custom_call_target="tpu_custom_call" | custom-call | tf_op jit(solution)/shard_map/mixer_back_phase/pallas_call | solution.py:534
  411.5 8.8 %finish.1 = (bf16[2,64,2560]{2,1,0:T(8,128)(2,1)}, f32[2,64,2560]{2,1,0:T(8,128)}, f32[2560]{0:T(1024)}, f32[2560]{0:T(1024)}, f32[640]{0:T(1024)}, /*index=5*/f...) custom-call(bf16[2,64,2560]{2,1,0:T(8,128)(2,1)} %get-tuple-element., ...), custom_call_target="tpu_custom_call" | custom-call | tf_op jit(solution)/shard_map/finish/pallas_call | solution.py:1911
  (2 shorter events, 0.0 us)
